TPU v7x, 256 devices: a whole 4x4x8 slice. The times are simulated.
256 devices in a mesh: section: 16 (over z, core), dp: 16 (over y, x).
Axes of the slice: x: 4, y: 4, z: 8, core: 2. Of those that a mesh axis runs over, the one named last changes fastest.
Arguments:
- inputs: bfloat16 [2, 256, 1024], P(None, 'dp'), may hold values from -6 to 6, as said below
- norm_gain: float32 [16, 1024], P('section'), may hold values from 0.1 to 1.9
- w_query: bfloat16 [16, 1024, 8192], P('section', None, 'dp'), may hold values from -0.1875 to 0.1875
- w_key: bfloat16 [16, 1024, 8192], P('section', None, 'dp'), may hold values from -12.5 to 12.5
- w_value: bfloat16 [16, 1024, 8192], P('section', None, 'dp'), may hold values from -0.1875 to 0.1875
- w_output: bfloat16 [16, 8192, 1024], P('section', 'dp'), may hold values from -0.0625 to 0.0625
- segment_ids: int32 [2, 256], replicated, may hold values from 0 to 7, never falling along the last dimension, each value on 1 to 64 neighbouring positions
- prefix_lengths: int32 [2, 8], replicated, may hold values from 1 to 64
- batch_lengths: int32 [2], replicated, may hold values from 128 to 256, as said below
Outputs:
- stashed: bfloat16 [16, 2, 256, 1024], P('section', None, 'dp')
Inputs may be any that keep to these rules, and one draw needn't show every extreme that they name: inputs are of order one. `segment_ids`: ids never fall along a micro-batch; each of the 8 ids holds 1 to 64 slots. `batch_lengths`: slots from the length on are padding; some micro-batch is full.
All inputs are finite; a program needn't handle non-finite values.
Results may differ from a plain program's by a relative error of at most 0.04.
Values may be sent and summed in bfloat16 or wider, within the bound.
No kernel may reach another device: no remote copies, remote signals or barrier semaphores. Data moves between devices by JAX's collectives and lax.ppermute only.
A program may use at most 64 MiB of HBM per device.

v0:
```python
import jax
import jax.numpy as jnp
from jax import lax
from jax.sharding import PartitionSpec as P

DH = 128


def from_behind(value, axis, steps):
    count = lax.axis_size(axis)
    first, last = (max(0, -steps), min(count, count - steps))
    return lax.ppermute(value, axis, [(source, source + steps) for source in range(first, last)])


def rms_scale(hidden, norm_gain):
    wide = hidden.astype(jnp.float32)
    mean_square = jnp.mean(wide * wide, axis=-1, keepdims=True)
    return (wide * lax.rsqrt(mean_square + 1e-06) * norm_gain).astype(jnp.bfloat16)


def visible_keys(segments, prefixes, length):
    seq_len = segments.shape[0]
    count_seg = prefixes.shape[0]
    position = jnp.arange(seq_len, dtype=jnp.int32)
    member = segments[:, None] == jnp.arange(count_seg, dtype=jnp.int32)[None, :]
    seg_start = jnp.min(jnp.where(member, position[:, None], jnp.int32(seq_len)), axis=0)
    prefix_end = jnp.sum(jnp.where(member, (seg_start + prefixes)[None, :], jnp.int32(0)), axis=1)
    key_ok = (position[None, :] <= position[:, None]) | (position[None, :] < prefix_end[None, :])
    same_seg = segments[:, None] == segments[None, :]
    live_keys = (position[None, :] < length) | (position[None, :] == position[:, None])
    return same_seg & key_ok & live_keys


def head_terms(
    normed_all, query_here, key_here, value_here, output_here, segments, prefixes, length
):
    seq_len = normed_all.shape[0]
    width = query_here.shape[1]
    heads = width // DH
    queries = (
        jnp.dot(normed_all, query_here, preferred_element_type=jnp.float32)
        .astype(jnp.bfloat16)
        .reshape(seq_len, heads, DH)
    )
    keyed = (
        jnp.dot(normed_all, key_here, preferred_element_type=jnp.float32)
        .astype(jnp.bfloat16)
        .reshape(seq_len, heads, DH)
    )
    values = (
        jnp.dot(normed_all, value_here, preferred_element_type=jnp.float32)
        .astype(jnp.bfloat16)
        .reshape(seq_len, heads, DH)
    )
    scores = jnp.einsum(
        "qhd,khd->hqk", queries, keyed, preferred_element_type=jnp.float32
    ) * DH ** (-0.5)
    visible = visible_keys(segments, prefixes, length)
    scores = jnp.where(visible[None, :, :], scores, jnp.float32(-1e30))
    row_max = jnp.max(scores, axis=-1, keepdims=True)
    expo = jnp.exp(scores - row_max)
    weights = (expo / jnp.sum(expo, axis=-1, keepdims=True)).astype(jnp.bfloat16)
    context = jnp.einsum("hqk,khd->qhd", weights, values, preferred_element_type=jnp.float32)
    context = context.astype(jnp.bfloat16).reshape(seq_len, width)
    return jnp.dot(context, output_here, preferred_element_type=jnp.float32)


def shards(
    inputs, norm_gain, w_query, w_key, w_value, w_output, segment_ids, prefix_lengths, batch_lengths
):
    section_index = lax.axis_index("section")
    sections = lax.axis_size("section")
    groups = lax.axis_size("dp")
    group_index = lax.axis_index("dp")
    micro_count = inputs.shape[0]
    row_count = inputs.shape[1]
    model_width = inputs.shape[2]
    seq_len = row_count * groups
    gain_here = norm_gain[0]
    query_here = w_query[0]
    key_here = w_key[0]
    value_here = w_value[0]
    output_here = w_output[0]
    own_rows = group_index * row_count + jnp.arange(row_count, dtype=jnp.int32)
    tick_count = micro_count + sections - 1
    stash_start = jnp.zeros((micro_count, row_count, model_width), jnp.bfloat16)

    def run_heads(normed_all, micro, active):

        def busy(operand):
            return head_terms(
                operand,
                query_here,
                key_here,
                value_here,
                output_here,
                segment_ids[micro],
                prefix_lengths[micro],
                batch_lengths[micro],
            )

        def quiet(operand):
            return jnp.zeros((seq_len, model_width), jnp.float32)

        return lax.cond(active, busy, quiet, normed_all)

    def place_micro(tick_index):
        micro_raw = tick_index - section_index
        active = (micro_raw >= 0) & (micro_raw < micro_count)
        return (jnp.clip(micro_raw, 0, micro_count - 1), active)

    def finish_rows(layer_in, summed, micro):
        live_rows = own_rows < batch_lengths[micro]
        return (
            layer_in.astype(jnp.float32) + jnp.where(live_rows[:, None], summed, jnp.float32(0.0))
        ).astype(jnp.bfloat16)

    def keep_stash(stashed, layer_out, micro, active):
        written = lax.dynamic_update_index_in_dim(stashed, layer_out, micro, 0)
        return jnp.where(active, written, stashed)

    inputs_all = lax.all_gather(inputs, "dp", axis=1, tiled=True)

    def tick_whole(tick_index, loop_state):
        previous_all, stashed = loop_state
        incoming = from_behind(previous_all, "section", 1)
        micro, active = place_micro(tick_index)
        layer_in_all = jnp.where(section_index == 0, inputs_all[micro], incoming)
        normed_all = rms_scale(layer_in_all, gain_here)
        terms = run_heads(normed_all, micro, active)
        summed = lax.psum_scatter(
            terms.astype(jnp.bfloat16), "dp", scatter_dimension=0, tiled=True
        ).astype(jnp.float32)
        layer_in = lax.dynamic_slice_in_dim(layer_in_all, group_index * row_count, row_count, 0)
        layer_out = finish_rows(layer_in, summed, micro)
        layer_out_all = lax.all_gather(layer_out, "dp", axis=0, tiled=True)
        return (layer_out_all, keep_stash(stashed, layer_out, micro, active))

    first_all = jnp.zeros((seq_len, model_width), jnp.bfloat16)
    _, stashed = lax.fori_loop(0, tick_count, tick_whole, (first_all, stash_start))
    return stashed[None]


def solution(mesh):
    return jax.shard_map(
        shards,
        mesh=mesh,
        in_specs=(
            P(None, "dp", None),
            P("section", None),
            P("section", None, "dp"),
            P("section", None, "dp"),
            P("section", None, "dp"),
            P("section", "dp", None),
            P(),
            P(),
            P(),
        ),
        out_specs=P("section", None, "dp", None),
        check_vma=False,
    )
```

profile of v0, /device:TPU:224, one launch (start us, length us, event | category | flops | bytes accessed | tf_op | source)
XLA Modules:
  0.0 2079.0 jit_solution(12439683014642256525)
XLA Ops:
  7.3 50.7 %all-gather.2.cloned.1.call-done = bf16[2,256,1024]{2,1,0:T(8,128)(2,1)} async-done(((bf16[2,16,1024]{2,1,0:T(8,128)(2,1)}), bf16[2,256,1024]{2,1,0:T(8,128)(2,1)}) %all-gather.2.cloned.1.call-update) | async-done | bytes 1048592 | tf_op jit(solution)/shard_map/all_gather | solution.py:122
  58.7 2012.8 %while.18 = (s32[]{:T(128)}, bf16[256,1024]{1,0:T(8,128)(2,1)S(1)}, bf16[2,16,1024]{2,1,0:T(8,128)(2,1)S(1)}, pred[]{:T(512)}, s32[]{:T(128)}, /*index=5*/bf16[2...) while((s32[]{:T(128)}, bf16[256,1024]{1,0:T(8,128)(2,1)S(1)}, ...), condition=%wide.region_9.10_spmd.clone, body=%wide.region_0.9_spmd.clone.sunk | while | flops 1280620544 | bytes 37741856 | solution.py:140
  60.7 8.6 collective-permute-done
  73.3 76.6 %reduce-scatter.2.cloned.1.call-done = bf16[16,1024]{1,0:T(8,128)(2,1)} async-done(((bf16[256,1024]{1,0:T(8,128)(2,1)}), bf16[16,1024]{1,0:T(8,128)(2,1)}) %reduce-scatter.2.cloned.1.call-update) | async-done | bytes 32784 | tf_op jit(solution)/shard_map/while/body/eval_jaxpr/reduce_scatter | solution.py:131
  150.7 23.3 %all_gather.15 = bf16[256,1024]{1,0:T(8,128)(2,1)S(1)} all-gather(bf16[16,1024]{1,0:T(8,128)(2,1)S(1)} %get-tuple-element.565), channel_id=1, replica_groups=mesh['section'=16,'dp'=16] {'dp'}, dimensions={0}, use_global_device_ids=true | all-gather | bytes 557056 | tf_op jit(solution)/shard_map/while/body/eval_jaxpr/all_gather | solution.py:136
  176.0 8.6 collective-permute-done
  188.5 76.1 %reduce-scatter.2.cloned.1.call-done = bf16[16,1024]{1,0:T(8,128)(2,1)} async-done(((bf16[256,1024]{1,0:T(8,128)(2,1)}), bf16[16,1024]{1,0:T(8,128)(2,1)}) %reduce-scatter.2.cloned.1.call-update) | async-done | bytes 32784 | tf_op jit(solution)/shard_map/while/body/eval_jaxpr/reduce_scatter | solution.py:131
  265.4 23.3 %all_gather.15 = bf16[256,1024]{1,0:T(8,128)(2,1)S(1)} all-gather(bf16[16,1024]{1,0:T(8,128)(2,1)S(1)} %get-tuple-element.565), channel_id=1, replica_groups=mesh['section'=16,'dp'=16] {'dp'}, dimensions={0}, use_global_device_ids=true | all-gather | bytes 557056 | tf_op jit(solution)/shard_map/while/body/eval_jaxpr/all_gather | solution.py:136
  290.8 8.6 collective-permute-done
  303.3 78.1 %reduce-scatter.2.cloned.1.call-done = bf16[16,1024]{1,0:T(8,128)(2,1)} async-done(((bf16[256,1024]{1,0:T(8,128)(2,1)}), bf16[16,1024]{1,0:T(8,128)(2,1)}) %reduce-scatter.2.cloned.1.call-update) | async-done | bytes 32784 | tf_op jit(solution)/shard_map/while/body/eval_jaxpr/reduce_scatter | solution.py:131
  382.2 23.4 %all_gather.15 = bf16[256,1024]{1,0:T(8,128)(2,1)S(1)} all-gather(bf16[16,1024]{1,0:T(8,128)(2,1)S(1)} %get-tuple-element.565), channel_id=1, replica_groups=mesh['section'=16,'dp'=16] {'dp'}, dimensions={0}, use_global_device_ids=true | all-gather | bytes 557056 | tf_op jit(solution)/shard_map/while/body/eval_jaxpr/all_gather | solution.py:136
  407.6 8.6 collective-permute-done
  420.1 78.2 %reduce-scatter.2.cloned.1.call-done = bf16[16,1024]{1,0:T(8,128)(2,1)} async-done(((bf16[256,1024]{1,0:T(8,128)(2,1)}), bf16[16,1024]{1,0:T(8,128)(2,1)}) %reduce-scatter.2.cloned.1.call-update) | async-done | bytes 32784 | tf_op jit(solution)/shard_map/while/body/eval_jaxpr/reduce_scatter | solution.py:131
  499.1 23.3 %all_gather.15 = bf16[256,1024]{1,0:T(8,128)(2,1)S(1)} all-gather(bf16[16,1024]{1,0:T(8,128)(2,1)S(1)} %get-tuple-element.565), channel_id=1, replica_groups=mesh['section'=16,'dp'=16] {'dp'}, dimensions={0}, use_global_device_ids=true | all-gather | bytes 557056 | tf_op jit(solution)/shard_map/while/body/eval_jaxpr/all_gather | solution.py:136
  524.4 8.6 collective-permute-done
  537.0 79.1 %reduce-scatter.2.cloned.1.call-done = bf16[16,1024]{1,0:T(8,128)(2,1)} async-done(((bf16[256,1024]{1,0:T(8,128)(2,1)}), bf16[16,1024]{1,0:T(8,128)(2,1)}) %reduce-scatter.2.cloned.1.call-update) | async-done | bytes 32784 | tf_op jit(solution)/shard_map/while/body/eval_jaxpr/reduce_scatter | solution.py:131
  616.9 23.3 %all_gather.15 = bf16[256,1024]{1,0:T(8,128)(2,1)S(1)} all-gather(bf16[16,1024]{1,0:T(8,128)(2,1)S(1)} %get-tuple-element.565), channel_id=1, replica_groups=mesh['section'=16,'dp'=16] {'dp'}, dimensions={0}, use_global_device_ids=true | all-gather | bytes 557056 | tf_op jit(solution)/shard_map/while/body/eval_jaxpr/all_gather | solution.py:136
  642.3 8.6 collective-permute-done
  654.8 79.2 %reduce-scatter.2.cloned.1.call-done = bf16[16,1024]{1,0:T(8,128)(2,1)} async-done(((bf16[256,1024]{1,0:T(8,128)(2,1)}), bf16[16,1024]{1,0:T(8,128)(2,1)}) %reduce-scatter.2.cloned.1.call-update) | async-done | bytes 32784 | tf_op jit(solution)/shard_map/while/body/eval_jaxpr/reduce_scatter | solution.py:131
  734.8 23.3 %all_gather.15 = bf16[256,1024]{1,0:T(8,128)(2,1)S(1)} all-gather(bf16[16,1024]{1,0:T(8,128)(2,1)S(1)} %get-tuple-element.565), channel_id=1, replica_groups=mesh['section'=16,'dp'=16] {'dp'}, dimensions={0}, use_global_device_ids=true | all-gather | bytes 557056 | tf_op jit(solution)/shard_map/while/body/eval_jaxpr/all_gather | solution.py:136
  760.1 8.6 collective-permute-done
  772.6 80.2 %reduce-scatter.2.cloned.1.call-done = bf16[16,1024]{1,0:T(8,128)(2,1)} async-done(((bf16[256,1024]{1,0:T(8,128)(2,1)}), bf16[16,1024]{1,0:T(8,128)(2,1)}) %reduce-scatter.2.cloned.1.call-update) | async-done | bytes 32784 | tf_op jit(solution)/shard_map/while/body/eval_jaxpr/reduce_scatter | solution.py:131
  853.6 23.3 %all_gather.15 = bf16[256,1024]{1,0:T(8,128)(2,1)S(1)} all-gather(bf16[16,1024]{1,0:T(8,128)(2,1)S(1)} %get-tuple-element.565), channel_id=1, replica_groups=mesh['section'=16,'dp'=16] {'dp'}, dimensions={0}, use_global_device_ids=true | all-gather | bytes 557056 | tf_op jit(solution)/shard_map/while/body/eval_jaxpr/all_gather | solution.py:136
  878.9 8.6 collective-permute-done
  891.4 80.2 %reduce-scatter.2.cloned.1.call-done = bf16[16,1024]{1,0:T(8,128)(2,1)} async-done(((bf16[256,1024]{1,0:T(8,128)(2,1)}), bf16[16,1024]{1,0:T(8,128)(2,1)}) %reduce-scatter.2.cloned.1.call-update) | async-done | bytes 32784 | tf_op jit(solution)/shard_map/while/body/eval_jaxpr/reduce_scatter | solution.py:131
  972.5 23.3 %all_gather.15 = bf16[256,1024]{1,0:T(8,128)(2,1)S(1)} all-gather(bf16[16,1024]{1,0:T(8,128)(2,1)S(1)} %get-tuple-element.565), channel_id=1, replica_groups=mesh['section'=16,'dp'=16] {'dp'}, dimensions={0}, use_global_device_ids=true | all-gather | bytes 557056 | tf_op jit(solution)/shard_map/while/body/eval_jaxpr/all_gather | solution.py:136
  997.8 8.6 collective-permute-done
  1010.3 83.6 %reduce-scatter.2.cloned.1.call-done = bf16[16,1024]{1,0:T(8,128)(2,1)} async-done(((bf16[256,1024]{1,0:T(8,128)(2,1)}), bf16[16,1024]{1,0:T(8,128)(2,1)}) %reduce-scatter.2.cloned.1.call-update) | async-done | bytes 32784 | tf_op jit(solution)/shard_map/while/body/eval_jaxpr/reduce_scatter | solution.py:131
  1094.7 23.3 %all_gather.15 = bf16[256,1024]{1,0:T(8,128)(2,1)S(1)} all-gather(bf16[16,1024]{1,0:T(8,128)(2,1)S(1)} %get-tuple-element.565), channel_id=1, replica_groups=mesh['section'=16,'dp'=16] {'dp'}, dimensions={0}, use_global_device_ids=true | all-gather | bytes 557056 | tf_op jit(solution)/shard_map/while/body/eval_jaxpr/all_gather | solution.py:136
  1120.0 8.6 collective-permute-done
  1132.6 83.6 %reduce-scatter.2.cloned.1.call-done = bf16[16,1024]{1,0:T(8,128)(2,1)} async-done(((bf16[256,1024]{1,0:T(8,128)(2,1)}), bf16[16,1024]{1,0:T(8,128)(2,1)}) %reduce-scatter.2.cloned.1.call-update) | async-done | bytes 32784 | tf_op jit(solution)/shard_map/while/body/eval_jaxpr/reduce_scatter | solution.py:131
  1217.0 23.3 %all_gather.15 = bf16[256,1024]{1,0:T(8,128)(2,1)S(1)} all-gather(bf16[16,1024]{1,0:T(8,128)(2,1)S(1)} %get-tuple-element.565), channel_id=1, replica_groups=mesh['section'=16,'dp'=16] {'dp'}, dimensions={0}, use_global_device_ids=true | all-gather | bytes 557056 | tf_op jit(solution)/shard_map/while/body/eval_jaxpr/all_gather | solution.py:136
  1242.3 8.6 collective-permute-done
  1254.8 81.5 %reduce-scatter.2.cloned.1.call-done = bf16[16,1024]{1,0:T(8,128)(2,1)} async-done(((bf16[256,1024]{1,0:T(8,128)(2,1)}), bf16[16,1024]{1,0:T(8,128)(2,1)}) %reduce-scatter.2.cloned.1.call-update) | async-done | bytes 32784 | tf_op jit(solution)/shard_map/while/body/eval_jaxpr/reduce_scatter | solution.py:131
  1337.2 23.3 %all_gather.15 = bf16[256,1024]{1,0:T(8,128)(2,1)S(1)} all-gather(bf16[16,1024]{1,0:T(8,128)(2,1)S(1)} %get-tuple-element.565), channel_id=1, replica_groups=mesh['section'=16,'dp'=16] {'dp'}, dimensions={0}, use_global_device_ids=true | all-gather | bytes 557056 | tf_op jit(solution)/shard_map/while/body/eval_jaxpr/all_gather | solution.py:136
  1362.4 8.6 collective-permute-done
  1375.0 81.6 %reduce-scatter.2.cloned.1.call-done = bf16[16,1024]{1,0:T(8,128)(2,1)} async-done(((bf16[256,1024]{1,0:T(8,128)(2,1)}), bf16[16,1024]{1,0:T(8,128)(2,1)}) %reduce-scatter.2.cloned.1.call-update) | async-done | bytes 32784 | tf_op jit(solution)/shard_map/while/body/eval_jaxpr/reduce_scatter | solution.py:131
  1457.4 23.3 %all_gather.15 = bf16[256,1024]{1,0:T(8,128)(2,1)S(1)} all-gather(bf16[16,1024]{1,0:T(8,128)(2,1)S(1)} %get-tuple-element.565), channel_id=1, replica_groups=mesh['section'=16,'dp'=16] {'dp'}, dimensions={0}, use_global_device_ids=true | all-gather | bytes 557056 | tf_op jit(solution)/shard_map/while/body/eval_jaxpr/all_gather | solution.py:136
  1495.2 80.7 %reduce-scatter.2.cloned.1.call-done = bf16[16,1024]{1,0:T(8,128)(2,1)} async-done(((bf16[256,1024]{1,0:T(8,128)(2,1)}), bf16[16,1024]{1,0:T(8,128)(2,1)}) %reduce-scatter.2.cloned.1.call-update) | async-done | bytes 32784 | tf_op jit(solution)/shard_map/while/body/eval_jaxpr/reduce_scatter | solution.py:131
  1576.7 23.4 %all_gather.15 = bf16[256,1024]{1,0:T(8,128)(2,1)S(1)} all-gather(bf16[16,1024]{1,0:T(8,128)(2,1)S(1)} %get-tuple-element.565), channel_id=1, replica_groups=mesh['section'=16,'dp'=16] {'dp'}, dimensions={0}, use_global_device_ids=true | all-gather | bytes 557056 | tf_op jit(solution)/shard_map/while/body/eval_jaxpr/all_gather | solution.py:136
  1614.6 80.8 %reduce-scatter.2.cloned.1.call-done = bf16[16,1024]{1,0:T(8,128)(2,1)} async-done(((bf16[256,1024]{1,0:T(8,128)(2,1)}), bf16[16,1024]{1,0:T(8,128)(2,1)}) %reduce-scatter.2.cloned.1.call-update) | async-done | bytes 32784 | tf_op jit(solution)/shard_map/while/body/eval_jaxpr/reduce_scatter | solution.py:131
  1696.2 23.3 %all_gather.15 = bf16[256,1024]{1,0:T(8,128)(2,1)S(1)} all-gather(bf16[16,1024]{1,0:T(8,128)(2,1)S(1)} %get-tuple-element.565), channel_id=1, replica_groups=mesh['section'=16,'dp'=16] {'dp'}, dimensions={0}, use_global_device_ids=true | all-gather | bytes 557056 | tf_op jit(solution)/shard_map/while/body/eval_jaxpr/all_gather | solution.py:136
  1741.6 72.4 %reduce-scatter.2.cloned.1.call-done = bf16[16,1024]{1,0:T(8,128)(2,1)} async-done(((bf16[256,1024]{1,0:T(8,128)(2,1)}), bf16[16,1024]{1,0:T(8,128)(2,1)}) %reduce-scatter.2.cloned.1.call-update) | async-done | bytes 32784 | tf_op jit(solution)/shard_map/while/body/eval_jaxpr/reduce_scatter | solution.py:131
  1814.8 23.3 %all_gather.15 = bf16[256,1024]{1,0:T(8,128)(2,1)S(1)} all-gather(bf16[16,1024]{1,0:T(8,128)(2,1)S(1)} %get-tuple-element.565), channel_id=1, replica_groups=mesh['section'=16,'dp'=16] {'dp'}, dimensions={0}, use_global_device_ids=true | all-gather | bytes 557056 | tf_op jit(solution)/shard_map/while/body/eval_jaxpr/all_gather | solution.py:136
  1860.2 72.4 %reduce-scatter.2.cloned.1.call-done = bf16[16,1024]{1,0:T(8,128)(2,1)} async-done(((bf16[256,1024]{1,0:T(8,128)(2,1)}), bf16[16,1024]{1,0:T(8,128)(2,1)}) %reduce-scatter.2.cloned.1.call-update) | async-done | bytes 32784 | tf_op jit(solution)/shard_map/while/body/eval_jaxpr/reduce_scatter | solution.py:131
  1933.5 23.3 %all_gather.15 = bf16[256,1024]{1,0:T(8,128)(2,1)S(1)} all-gather(bf16[16,1024]{1,0:T(8,128)(2,1)S(1)} %get-tuple-element.565), channel_id=1, replica_groups=mesh['section'=16,'dp'=16] {'dp'}, dimensions={0}, use_global_device_ids=true | all-gather | bytes 557056 | tf_op jit(solution)/shard_map/while/body/eval_jaxpr/all_gather | solution.py:136
  1971.3 76.0 %reduce-scatter.2.cloned.1.call-done = bf16[16,1024]{1,0:T(8,128)(2,1)} async-done(((bf16[256,1024]{1,0:T(8,128)(2,1)}), bf16[16,1024]{1,0:T(8,128)(2,1)}) %reduce-scatter.2.cloned.1.call-update) | async-done | bytes 32784 | tf_op jit(solution)/shard_map/while/body/eval_jaxpr/reduce_scatter | solution.py:131
  2048.2 23.3 %all_gather.15 = bf16[256,1024]{1,0:T(8,128)(2,1)S(1)} all-gather(bf16[16,1024]{1,0:T(8,128)(2,1)S(1)} %get-tuple-element.565), channel_id=1, replica_groups=mesh['section'=16,'dp'=16] {'dp'}, dimensions={0}, use_global_device_ids=true | all-gather | bytes 557056 | tf_op jit(solution)/shard_map/while/body/eval_jaxpr/all_gather | solution.py:136
  (344 shorter events, 189.8 us)
Async XLA Ops:
  6.5 51.4 %all-gather.2.cloned.1.call-start = ((), (), s32[]{:S(2)}) async-start(), calls=%async_computation.1 | async-start | bytes 1114112 | tf_op jit(solution)/shard_map/all_gather | solution.py:122
  58.7 91.1 %reduce-scatter.2.cloned.1.call-start = ((), (), s32[]{:S(2)}) async-start(), calls=%async_computation.2 | async-start | bytes 557056 | tf_op jit(solution)/shard_map/while/body/eval_jaxpr/reduce_scatter | solution.py:131
  58.8 10.5 collective-permute-start
  69.3 1.7 copy-start.2
  174.0 90.6 %reduce-scatter.2.cloned.1.call-start = ((), (), s32[]{:S(2)}) async-start(), calls=%async_computation.2 | async-start | bytes 557056 | tf_op jit(solution)/shard_map/while/body/eval_jaxpr/reduce_scatter | solution.py:131
  174.0 10.5 collective-permute-start
  184.5 1.7 copy-start.2
  288.8 92.6 %reduce-scatter.2.cloned.1.call-start = ((), (), s32[]{:S(2)}) async-start(), calls=%async_computation.2 | async-start | bytes 557056 | tf_op jit(solution)/shard_map/while/body/eval_jaxpr/reduce_scatter | solution.py:131
  288.8 10.5 collective-permute-start
  299.3 1.7 copy-start.2
  405.6 92.7 %reduce-scatter.2.cloned.1.call-start = ((), (), s32[]{:S(2)}) async-start(), calls=%async_computation.2 | async-start | bytes 557056 | tf_op jit(solution)/shard_map/while/body/eval_jaxpr/reduce_scatter | solution.py:131
  405.6 10.5 collective-permute-start
  416.1 1.7 copy-start.2
  522.5 93.6 %reduce-scatter.2.cloned.1.call-start = ((), (), s32[]{:S(2)}) async-start(), calls=%async_computation.2 | async-start | bytes 557056 | tf_op jit(solution)/shard_map/while/body/eval_jaxpr/reduce_scatter | solution.py:131
  522.5 10.5 collective-permute-start
  533.0 1.7 copy-start.2
  640.3 93.7 %reduce-scatter.2.cloned.1.call-start = ((), (), s32[]{:S(2)}) async-start(), calls=%async_computation.2 | async-start | bytes 557056 | tf_op jit(solution)/shard_map/while/body/eval_jaxpr/reduce_scatter | solution.py:131
  640.3 10.5 collective-permute-start
  758.1 94.7 %reduce-scatter.2.cloned.1.call-start = ((), (), s32[]{:S(2)}) async-start(), calls=%async_computation.2 | async-start | bytes 557056 | tf_op jit(solution)/shard_map/while/body/eval_jaxpr/reduce_scatter | solution.py:131
  758.1 10.5 collective-permute-start
  768.6 1.7 copy-start.2
  876.9 94.7 %reduce-scatter.2.cloned.1.call-start = ((), (), s32[]{:S(2)}) async-start(), calls=%async_computation.2 | async-start | bytes 557056 | tf_op jit(solution)/shard_map/while/body/eval_jaxpr/reduce_scatter | solution.py:131
  877.0 10.5 collective-permute-start
  887.5 1.7 copy-start.2
  995.8 98.1 %reduce-scatter.2.cloned.1.call-start = ((), (), s32[]{:S(2)}) async-start(), calls=%async_computation.2 | async-start | bytes 557056 | tf_op jit(solution)/shard_map/while/body/eval_jaxpr/reduce_scatter | solution.py:131
  995.8 10.5 collective-permute-start
  1006.3 1.7 copy-start.2
  1118.1 98.1 %reduce-scatter.2.cloned.1.call-start = ((), (), s32[]{:S(2)}) async-start(), calls=%async_computation.2 | async-start | bytes 557056 | tf_op jit(solution)/shard_map/while/body/eval_jaxpr/reduce_scatter | solution.py:131
  1118.1 10.5 collective-permute-start
  1128.6 1.7 copy-start.2
  1240.3 96.1 %reduce-scatter.2.cloned.1.call-start = ((), (), s32[]{:S(2)}) async-start(), calls=%async_computation.2 | async-start | bytes 557056 | tf_op jit(solution)/shard_map/while/body/eval_jaxpr/reduce_scatter | solution.py:131
  1240.3 10.5 collective-permute-start
  1360.5 96.1 %reduce-scatter.2.cloned.1.call-start = ((), (), s32[]{:S(2)}) async-start(), calls=%async_computation.2 | async-start | bytes 557056 | tf_op jit(solution)/shard_map/while/body/eval_jaxpr/reduce_scatter | solution.py:131
  1360.5 10.5 collective-permute-start
  1480.7 95.2 %reduce-scatter.2.cloned.1.call-start = ((), (), s32[]{:S(2)}) async-start(), calls=%async_computation.2 | async-start | bytes 557056 | tf_op jit(solution)/shard_map/while/body/eval_jaxpr/reduce_scatter | solution.py:131
  1480.8 10.5 collective-permute-start
  1600.1 95.3 %reduce-scatter.2.cloned.1.call-start = ((), (), s32[]{:S(2)}) async-start(), calls=%async_computation.2 | async-start | bytes 557056 | tf_op jit(solution)/shard_map/while/body/eval_jaxpr/reduce_scatter | solution.py:131
  1600.1 10.5 collective-permute-start
  1719.5 94.5 %reduce-scatter.2.cloned.1.call-start = ((), (), s32[]{:S(2)}) async-start(), calls=%async_computation.2 | async-start | bytes 557056 | tf_op jit(solution)/shard_map/while/body/eval_jaxpr/reduce_scatter | solution.py:131
  1719.5 10.5 collective-permute-start
  1731.8 2.2 copy-start.3
  1736.8 2.1 copy-start.4
  1838.1 94.5 %reduce-scatter.2.cloned.1.call-start = ((), (), s32[]{:S(2)}) async-start(), calls=%async_computation.2 | async-start | bytes 557056 | tf_op jit(solution)/shard_map/while/body/eval_jaxpr/reduce_scatter | solution.py:131
  1838.2 10.5 collective-permute-start
  1850.4 2.2 copy-start.3
  1855.4 2.1 copy-start.4
  1956.8 90.5 %reduce-scatter.2.cloned.1.call-start = ((), (), s32[]{:S(2)}) async-start(), calls=%async_computation.2 | async-start | bytes 557056 | tf_op jit(solution)/shard_map/while/body/eval_jaxpr/reduce_scatter | solution.py:131
  1956.9 10.5 collective-permute-start
  (47 other events, 59.0 us)
Sparse Core Ops, SparseCore 0:
  9.8 48.1 all-gather.1
  72.0 77.8 reduce-scatter.1
  187.3 77.2 reduce-scatter.1
  302.0 79.3 reduce-scatter.1
  418.9 79.3 reduce-scatter.1
  535.7 80.3 reduce-scatter.1
  653.5 80.3 reduce-scatter.1
  771.4 81.3 reduce-scatter.1
  890.2 81.4 reduce-scatter.1
  1009.1 84.7 reduce-scatter.1
  1131.3 84.7 reduce-scatter.1
  1253.5 82.7 reduce-scatter.1
  1373.7 82.8 reduce-scatter.1
  1494.0 81.8 reduce-scatter.1
  1613.4 81.9 reduce-scatter.1
  1740.3 73.6 reduce-scatter.1
  1858.9 73.6 reduce-scatter.1
  1970.1 77.2 reduce-scatter.1
where the time goes:
time: 2080 us
  waiting for transfers between devices  1540 us (74%)
  blocking collectives  396 us (19%)
  other arithmetic  56.3 us (3%)
  starting transfers between devices  33.3 us (2%)
  local copies, waits for them, and re-layouts  29 us (1%)
    reduce_scatter x17, waiting for transfers between devices, tick_whole(): lax.psum_scatter(terms.astype(jnp.bfloat16), 'dp', scatter_dimension=0, t...  1340 us
    all_gather x17, blocking collectives, tick_whole(): layer_out_all = lax.all_gather(layer_out, 'dp', axis=0, tiled=True)  396 us
    ppermute x17, waiting for transfers between devices, from_behind(): lax.ppermute(value, axis, [(source, source + steps) for source in range(f...  145 us
    all_gather x1, waiting for transfers between devices, shards(): inputs_all = lax.all_gather(inputs, 'dp', axis=1, tiled=True)  50.7 us
  transfers between devices with their start and end apart: 35, of which 35 were waited for; matrix products, arithmetic and copies ran while one was open for 1% of the time, Pallas kernels for 0%

commit v1 on v0

--- a/solution.py
+++ b/solution.py
@@ -128,12 +128,14 @@
         layer_in_all = jnp.where(section_index == 0, inputs_all[micro], incoming)
         normed_all = rms_scale(layer_in_all, gain_here)
         terms = run_heads(normed_all, micro, active)
-        summed = lax.psum_scatter(
-            terms.astype(jnp.bfloat16), "dp", scatter_dimension=0, tiled=True
-        ).astype(jnp.float32)
+        pieces = lax.all_to_all(
+            terms.astype(jnp.bfloat16).reshape(groups, row_count, model_width), "dp", 0, 0
+        )
+        summed = jnp.sum(pieces.astype(jnp.float32), axis=0)
         layer_in = lax.dynamic_slice_in_dim(layer_in_all, group_index * row_count, row_count, 0)
         layer_out = finish_rows(layer_in, summed, micro)
-        layer_out_all = lax.all_gather(layer_out, "dp", axis=0, tiled=True)
+        copies = jnp.broadcast_to(layer_out[None], (groups, row_count, model_width))
+        layer_out_all = lax.all_to_all(copies, "dp", 0, 0).reshape(seq_len, model_width)
         return (layer_out_all, keep_stash(stashed, layer_out, micro, active))
 
     first_all = jnp.zeros((seq_len, model_width), jnp.bfloat16)

time: 2080 us -> 860 us (0.41)
  waiting for transfers between devices: 1540 us -> 586 us
  blocking collectives: 396 us -> 0 us
  starting transfers between devices: 33.3 us -> 155 us
    reduce_scatter x17 -> x0, waiting for transfers between devices: 1340 us -> none  [tick_whole(): lax.psum_scatter(terms.astype(jnp.bfloat16), 'dp', scatter_dimension=0, t...]
    all_gather x17 -> x0, blocking collectives: 396 us -> none  [tick_whole(): layer_out_all = lax.all_gather(layer_out, 'dp', axis=0, tiled=True)]
    all_to_all x0 -> x34, waiting for transfers between devices: none -> 326 us  [the longest x17 174 us: tick_whole(): lax.all_to_all(copies, 'dp', 0, 0).reshape(seq_len, model_width)]
    all_to_all x0 -> x34, starting transfers between devices: none -> 123 us  [the longest x17 62 us: tick_whole(): lax.all_to_all(terms.astype(jnp.bfloat16).reshape(groups, row_count, mode...]
    ppermute x17, waiting for transfers between devices: 145 us -> 208 us  [from_behind(): lax.ppermute(value, axis, [(source, source + steps) for source in range(f...]
  transfers between devices with their start and end apart: 35 -> 52, of which waited for: 35 -> 52; matrix products, arithmetic and copies ran while one was open for 1% -> 3% of each run, Pallas kernels for 0% -> 0%
where the time goes in v1:
time: 860 us; the launch traced here: 855 us
  waiting for transfers between devices  586 us (68%)
  starting transfers between devices  155 us (18%)
  other arithmetic  43.8 us (5%)
  local copies, waits for them, and re-layouts  41.9 us (5%)
  between operations  13.4 us (2%)
  matrix products  13 us (2%)
    ppermute x17, waiting for transfers between devices, from_behind(): lax.ppermute(value, axis, [(source, source + steps) for source in range(f...  208 us
    all_to_all x17, waiting for transfers between devices, tick_whole(): lax.all_to_all(copies, 'dp', 0, 0).reshape(seq_len, model_width)  174 us
    all_to_all x17, waiting for transfers between devices, tick_whole(): lax.all_to_all(terms.astype(jnp.bfloat16).reshape(groups, row_count, mode...  153 us
    all_to_all x17, starting transfers between devices, tick_whole(): lax.all_to_all(terms.astype(jnp.bfloat16).reshape(groups, row_count, mode...  62 us
    all_to_all x17, starting transfers between devices, tick_whole(): lax.all_to_all(copies, 'dp', 0, 0).reshape(seq_len, model_width)  60.7 us
    all_gather x1, waiting for transfers between devices, shards(): inputs_all = lax.all_gather(inputs, 'dp', axis=1, tiled=True)  50.7 us
    ppermute x17, starting transfers between devices, from_behind(): lax.ppermute(value, axis, [(source, source + steps) for source in range(f...  32.5 us
    reduce_sum x17, other arithmetic, rms_scale(): mean_square = jnp.mean(wide * wide, axis=-1, keepdims=True)  24.7 us
  transfers between devices with their start and end apart: 52, of which 52 were waited for; matrix products, arithmetic and copies ran while one was open for 3% of the time, Pallas kernels for 0%

profile of v1, /device:TPU:224, one launch (start us, length us, event | category | flops | bytes accessed | tf_op | source)
XLA Modules:
  0.0 854.8 jit_solution(5647398635196766579)
XLA Ops:
  7.3 50.7 %all-gather.2.cloned.1.call-done = bf16[2,256,1024]{2,1,0:T(8,128)(2,1)} async-done(((bf16[2,16,1024]{2,1,0:T(8,128)(2,1)}), bf16[2,256,1024]{2,1,0:T(8,128)(2,1)}) %all-gather.2.cloned.1.call-update) | async-done | bytes 1048592 | tf_op jit(solution)/shard_map/all_gather | solution.py:122
  58.7 788.6 %while.18 = (s32[]{:T(128)}, bf16[256,1024]{1,0:T(8,128)(2,1)S(1)}, bf16[2,16,1024]{2,1,0:T(8,128)(2,1)S(1)}, pred[]{:T(512)}, s32[]{:T(128)}, /*index=5*/bf16[2...) while((s32[]{:T(128)}, bf16[256,1024]{1,0:T(8,128)(2,1)S(1)}, ...), condition=%wide.region_9.10_spmd.clone, body=%wide.region_0.9_spmd.clone.sunk | while | flops 1281112064 | bytes 37741852 | solution.py:142
  60.7 8.6 %collective-permute-done = bf16[256,1024]{1,0:T(8,128)(2,1)S(1)} collective-permute-done((bf16[256,1024]{1,0:T(8,128)(2,1)S(1)}, bf16[256,1024]{1,0:T(8,128)(2,1)S(1)}, u32[]{:S(2)}, u32[]{:S(2)}) %collective-permute-start) | collective-permute-done | bytes 524320 | tf_op jit(solution)/shard_map/while/body/eval_jaxpr/ppermute | solution.py:12
  77.9 8.8 %all-to-all-done = bf16[16,16,1024]{2,1,0:T(8,128)(2,1)S(1)} async-done(((bf16[16,16,1024]{2,1,0:T(8,128)(2,1)}), bf16[16,16,1024]{2,1,0:T(8,128)(2,1)S(1)}, u32[]{:S(2)}, u32[]{:S(2)}) %all-to-all-start) | async-done | bytes 524320 | tf_op jit(solution)/shard_map/while/body/eval_jaxpr/all_to_all | solution.py:131
  91.4 10.1 %all-to-all-done.1 = bf16[16,16,1024]{2,1,0:T(8,128)(2,1)S(1)} async-done(((bf16[16,16,1024]{2,1,0:T(8,128)(2,1)}), bf16[16,16,1024]{2,1,0:T(8,128)(2,1)S(1)}, u32[]{:S(2)}, u32[]{:S(2)}) %all-to-all-start.1) | async-done | bytes 524320 | tf_op jit(solution)/shard_map/while/body/eval_jaxpr/all_to_all | solution.py:138
  103.4 8.6 %collective-permute-done = bf16[256,1024]{1,0:T(8,128)(2,1)S(1)} collective-permute-done((bf16[256,1024]{1,0:T(8,128)(2,1)S(1)}, bf16[256,1024]{1,0:T(8,128)(2,1)S(1)}, u32[]{:S(2)}, u32[]{:S(2)}) %collective-permute-start) | collective-permute-done | bytes 524320 | tf_op jit(solution)/shard_map/while/body/eval_jaxpr/ppermute | solution.py:12
  119.4 8.8 %all-to-all-done = bf16[16,16,1024]{2,1,0:T(8,128)(2,1)S(1)} async-done(((bf16[16,16,1024]{2,1,0:T(8,128)(2,1)}), bf16[16,16,1024]{2,1,0:T(8,128)(2,1)S(1)}, u32[]{:S(2)}, u32[]{:S(2)}) %all-to-all-start) | async-done | bytes 524320 | tf_op jit(solution)/shard_map/while/body/eval_jaxpr/all_to_all | solution.py:131
  132.8 10.1 %all-to-all-done.1 = bf16[16,16,1024]{2,1,0:T(8,128)(2,1)S(1)} async-done(((bf16[16,16,1024]{2,1,0:T(8,128)(2,1)}), bf16[16,16,1024]{2,1,0:T(8,128)(2,1)S(1)}, u32[]{:S(2)}, u32[]{:S(2)}) %all-to-all-start.1) | async-done | bytes 524320 | tf_op jit(solution)/shard_map/while/body/eval_jaxpr/all_to_all | solution.py:138
  144.9 8.6 %collective-permute-done = bf16[256,1024]{1,0:T(8,128)(2,1)S(1)} collective-permute-done((bf16[256,1024]{1,0:T(8,128)(2,1)S(1)}, bf16[256,1024]{1,0:T(8,128)(2,1)S(1)}, u32[]{:S(2)}, u32[]{:S(2)}) %collective-permute-start) | collective-permute-done | bytes 524320 | tf_op jit(solution)/shard_map/while/body/eval_jaxpr/ppermute | solution.py:12
  160.9 8.8 %all-to-all-done = bf16[16,16,1024]{2,1,0:T(8,128)(2,1)S(1)} async-done(((bf16[16,16,1024]{2,1,0:T(8,128)(2,1)}), bf16[16,16,1024]{2,1,0:T(8,128)(2,1)S(1)}, u32[]{:S(2)}, u32[]{:S(2)}) %all-to-all-start) | async-done | bytes 524320 | tf_op jit(solution)/shard_map/while/body/eval_jaxpr/all_to_all | solution.py:131
  174.3 10.1 %all-to-all-done.1 = bf16[16,16,1024]{2,1,0:T(8,128)(2,1)S(1)} async-done(((bf16[16,16,1024]{2,1,0:T(8,128)(2,1)}), bf16[16,16,1024]{2,1,0:T(8,128)(2,1)S(1)}, u32[]{:S(2)}, u32[]{:S(2)}) %all-to-all-start.1) | async-done | bytes 524320 | tf_op jit(solution)/shard_map/while/body/eval_jaxpr/all_to_all | solution.py:138
  186.3 8.6 %collective-permute-done = bf16[256,1024]{1,0:T(8,128)(2,1)S(1)} collective-permute-done((bf16[256,1024]{1,0:T(8,128)(2,1)S(1)}, bf16[256,1024]{1,0:T(8,128)(2,1)S(1)}, u32[]{:S(2)}, u32[]{:S(2)}) %collective-permute-start) | collective-permute-done | bytes 524320 | tf_op jit(solution)/shard_map/while/body/eval_jaxpr/ppermute | solution.py:12
  202.3 8.8 %all-to-all-done = bf16[16,16,1024]{2,1,0:T(8,128)(2,1)S(1)} async-done(((bf16[16,16,1024]{2,1,0:T(8,128)(2,1)}), bf16[16,16,1024]{2,1,0:T(8,128)(2,1)S(1)}, u32[]{:S(2)}, u32[]{:S(2)}) %all-to-all-start) | async-done | bytes 524320 | tf_op jit(solution)/shard_map/while/body/eval_jaxpr/all_to_all | solution.py:131
  215.7 10.1 %all-to-all-done.1 = bf16[16,16,1024]{2,1,0:T(8,128)(2,1)S(1)} async-done(((bf16[16,16,1024]{2,1,0:T(8,128)(2,1)}), bf16[16,16,1024]{2,1,0:T(8,128)(2,1)S(1)}, u32[]{:S(2)}, u32[]{:S(2)}) %all-to-all-start.1) | async-done | bytes 524320 | tf_op jit(solution)/shard_map/while/body/eval_jaxpr/all_to_all | solution.py:138
  227.8 8.6 %collective-permute-done = bf16[256,1024]{1,0:T(8,128)(2,1)S(1)} collective-permute-done((bf16[256,1024]{1,0:T(8,128)(2,1)S(1)}, bf16[256,1024]{1,0:T(8,128)(2,1)S(1)}, u32[]{:S(2)}, u32[]{:S(2)}) %collective-permute-start) | collective-permute-done | bytes 524320 | tf_op jit(solution)/shard_map/while/body/eval_jaxpr/ppermute | solution.py:12
  243.7 8.8 %all-to-all-done = bf16[16,16,1024]{2,1,0:T(8,128)(2,1)S(1)} async-done(((bf16[16,16,1024]{2,1,0:T(8,128)(2,1)}), bf16[16,16,1024]{2,1,0:T(8,128)(2,1)S(1)}, u32[]{:S(2)}, u32[]{:S(2)}) %all-to-all-start) | async-done | bytes 524320 | tf_op jit(solution)/shard_map/while/body/eval_jaxpr/all_to_all | solution.py:131
  257.2 10.1 %all-to-all-done.1 = bf16[16,16,1024]{2,1,0:T(8,128)(2,1)S(1)} async-done(((bf16[16,16,1024]{2,1,0:T(8,128)(2,1)}), bf16[16,16,1024]{2,1,0:T(8,128)(2,1)S(1)}, u32[]{:S(2)}, u32[]{:S(2)}) %all-to-all-start.1) | async-done | bytes 524320 | tf_op jit(solution)/shard_map/while/body/eval_jaxpr/all_to_all | solution.py:138
  269.2 8.6 %collective-permute-done = bf16[256,1024]{1,0:T(8,128)(2,1)S(1)} collective-permute-done((bf16[256,1024]{1,0:T(8,128)(2,1)S(1)}, bf16[256,1024]{1,0:T(8,128)(2,1)S(1)}, u32[]{:S(2)}, u32[]{:S(2)}) %collective-permute-start) | collective-permute-done | bytes 524320 | tf_op jit(solution)/shard_map/while/body/eval_jaxpr/ppermute | solution.py:12
  285.2 8.8 %all-to-all-done = bf16[16,16,1024]{2,1,0:T(8,128)(2,1)S(1)} async-done(((bf16[16,16,1024]{2,1,0:T(8,128)(2,1)}), bf16[16,16,1024]{2,1,0:T(8,128)(2,1)S(1)}, u32[]{:S(2)}, u32[]{:S(2)}) %all-to-all-start) | async-done | bytes 524320 | tf_op jit(solution)/shard_map/while/body/eval_jaxpr/all_to_all | solution.py:131
  298.6 10.1 %all-to-all-done.1 = bf16[16,16,1024]{2,1,0:T(8,128)(2,1)S(1)} async-done(((bf16[16,16,1024]{2,1,0:T(8,128)(2,1)}), bf16[16,16,1024]{2,1,0:T(8,128)(2,1)S(1)}, u32[]{:S(2)}, u32[]{:S(2)}) %all-to-all-start.1) | async-done | bytes 524320 | tf_op jit(solution)/shard_map/while/body/eval_jaxpr/all_to_all | solution.py:138
  310.6 8.6 %collective-permute-done = bf16[256,1024]{1,0:T(8,128)(2,1)S(1)} collective-permute-done((bf16[256,1024]{1,0:T(8,128)(2,1)S(1)}, bf16[256,1024]{1,0:T(8,128)(2,1)S(1)}, u32[]{:S(2)}, u32[]{:S(2)}) %collective-permute-start) | collective-permute-done | bytes 524320 | tf_op jit(solution)/shard_map/while/body/eval_jaxpr/ppermute | solution.py:12
  326.6 8.8 %all-to-all-done = bf16[16,16,1024]{2,1,0:T(8,128)(2,1)S(1)} async-done(((bf16[16,16,1024]{2,1,0:T(8,128)(2,1)}), bf16[16,16,1024]{2,1,0:T(8,128)(2,1)S(1)}, u32[]{:S(2)}, u32[]{:S(2)}) %all-to-all-start) | async-done | bytes 524320 | tf_op jit(solution)/shard_map/while/body/eval_jaxpr/all_to_all | solution.py:131
  340.1 10.1 %all-to-all-done.1 = bf16[16,16,1024]{2,1,0:T(8,128)(2,1)S(1)} async-done(((bf16[16,16,1024]{2,1,0:T(8,128)(2,1)}), bf16[16,16,1024]{2,1,0:T(8,128)(2,1)S(1)}, u32[]{:S(2)}, u32[]{:S(2)}) %all-to-all-start.1) | async-done | bytes 524320 | tf_op jit(solution)/shard_map/while/body/eval_jaxpr/all_to_all | solution.py:138
  352.1 8.6 %collective-permute-done = bf16[256,1024]{1,0:T(8,128)(2,1)S(1)} collective-permute-done((bf16[256,1024]{1,0:T(8,128)(2,1)S(1)}, bf16[256,1024]{1,0:T(8,128)(2,1)S(1)}, u32[]{:S(2)}, u32[]{:S(2)}) %collective-permute-start) | collective-permute-done | bytes 524320 | tf_op jit(solution)/shard_map/while/body/eval_jaxpr/ppermute | solution.py:12
  368.1 8.8 %all-to-all-done = bf16[16,16,1024]{2,1,0:T(8,128)(2,1)S(1)} async-done(((bf16[16,16,1024]{2,1,0:T(8,128)(2,1)}), bf16[16,16,1024]{2,1,0:T(8,128)(2,1)S(1)}, u32[]{:S(2)}, u32[]{:S(2)}) %all-to-all-start) | async-done | bytes 524320 | tf_op jit(solution)/shard_map/while/body/eval_jaxpr/all_to_all | solution.py:131
  381.5 10.1 %all-to-all-done.1 = bf16[16,16,1024]{2,1,0:T(8,128)(2,1)S(1)} async-done(((bf16[16,16,1024]{2,1,0:T(8,128)(2,1)}), bf16[16,16,1024]{2,1,0:T(8,128)(2,1)S(1)}, u32[]{:S(2)}, u32[]{:S(2)}) %all-to-all-start.1) | async-done | bytes 524320 | tf_op jit(solution)/shard_map/while/body/eval_jaxpr/all_to_all | solution.py:138
  393.5 8.6 %collective-permute-done = bf16[256,1024]{1,0:T(8,128)(2,1)S(1)} collective-permute-done((bf16[256,1024]{1,0:T(8,128)(2,1)S(1)}, bf16[256,1024]{1,0:T(8,128)(2,1)S(1)}, u32[]{:S(2)}, u32[]{:S(2)}) %collective-permute-start) | collective-permute-done | bytes 524320 | tf_op jit(solution)/shard_map/while/body/eval_jaxpr/ppermute | solution.py:12
  409.5 8.8 %all-to-all-done = bf16[16,16,1024]{2,1,0:T(8,128)(2,1)S(1)} async-done(((bf16[16,16,1024]{2,1,0:T(8,128)(2,1)}), bf16[16,16,1024]{2,1,0:T(8,128)(2,1)S(1)}, u32[]{:S(2)}, u32[]{:S(2)}) %all-to-all-start) | async-done | bytes 524320 | tf_op jit(solution)/shard_map/while/body/eval_jaxpr/all_to_all | solution.py:131
  423.0 10.1 %all-to-all-done.1 = bf16[16,16,1024]{2,1,0:T(8,128)(2,1)S(1)} async-done(((bf16[16,16,1024]{2,1,0:T(8,128)(2,1)}), bf16[16,16,1024]{2,1,0:T(8,128)(2,1)S(1)}, u32[]{:S(2)}, u32[]{:S(2)}) %all-to-all-start.1) | async-done | bytes 524320 | tf_op jit(solution)/shard_map/while/body/eval_jaxpr/all_to_all | solution.py:138
  435.0 8.6 %collective-permute-done = bf16[256,1024]{1,0:T(8,128)(2,1)S(1)} collective-permute-done((bf16[256,1024]{1,0:T(8,128)(2,1)S(1)}, bf16[256,1024]{1,0:T(8,128)(2,1)S(1)}, u32[]{:S(2)}, u32[]{:S(2)}) %collective-permute-start) | collective-permute-done | bytes 524320 | tf_op jit(solution)/shard_map/while/body/eval_jaxpr/ppermute | solution.py:12
  451.0 8.8 %all-to-all-done = bf16[16,16,1024]{2,1,0:T(8,128)(2,1)S(1)} async-done(((bf16[16,16,1024]{2,1,0:T(8,128)(2,1)}), bf16[16,16,1024]{2,1,0:T(8,128)(2,1)S(1)}, u32[]{:S(2)}, u32[]{:S(2)}) %all-to-all-start) | async-done | bytes 524320 | tf_op jit(solution)/shard_map/while/body/eval_jaxpr/all_to_all | solution.py:131
  464.4 10.1 %all-to-all-done.1 = bf16[16,16,1024]{2,1,0:T(8,128)(2,1)S(1)} async-done(((bf16[16,16,1024]{2,1,0:T(8,128)(2,1)}), bf16[16,16,1024]{2,1,0:T(8,128)(2,1)S(1)}, u32[]{:S(2)}, u32[]{:S(2)}) %all-to-all-start.1) | async-done | bytes 524320 | tf_op jit(solution)/shard_map/while/body/eval_jaxpr/all_to_all | solution.py:138
  492.4 8.8 %all-to-all-done = bf16[16,16,1024]{2,1,0:T(8,128)(2,1)S(1)} async-done(((bf16[16,16,1024]{2,1,0:T(8,128)(2,1)}), bf16[16,16,1024]{2,1,0:T(8,128)(2,1)S(1)}, u32[]{:S(2)}, u32[]{:S(2)}) %all-to-all-start) | async-done | bytes 524320 | tf_op jit(solution)/shard_map/while/body/eval_jaxpr/all_to_all | solution.py:131
  505.9 10.1 %all-to-all-done.1 = bf16[16,16,1024]{2,1,0:T(8,128)(2,1)S(1)} async-done(((bf16[16,16,1024]{2,1,0:T(8,128)(2,1)}), bf16[16,16,1024]{2,1,0:T(8,128)(2,1)S(1)}, u32[]{:S(2)}, u32[]{:S(2)}) %all-to-all-start.1) | async-done | bytes 524320 | tf_op jit(solution)/shard_map/while/body/eval_jaxpr/all_to_all | solution.py:138
  533.9 8.8 %all-to-all-done = bf16[16,16,1024]{2,1,0:T(8,128)(2,1)S(1)} async-done(((bf16[16,16,1024]{2,1,0:T(8,128)(2,1)}), bf16[16,16,1024]{2,1,0:T(8,128)(2,1)S(1)}, u32[]{:S(2)}, u32[]{:S(2)}) %all-to-all-start) | async-done | bytes 524320 | tf_op jit(solution)/shard_map/while/body/eval_jaxpr/all_to_all | solution.py:131
  547.3 10.1 %all-to-all-done.1 = bf16[16,16,1024]{2,1,0:T(8,128)(2,1)S(1)} async-done(((bf16[16,16,1024]{2,1,0:T(8,128)(2,1)}), bf16[16,16,1024]{2,1,0:T(8,128)(2,1)S(1)}, u32[]{:S(2)}, u32[]{:S(2)}) %all-to-all-start.1) | async-done | bytes 524320 | tf_op jit(solution)/shard_map/while/body/eval_jaxpr/all_to_all | solution.py:138
  575.3 8.8 %all-to-all-done = bf16[16,16,1024]{2,1,0:T(8,128)(2,1)S(1)} async-done(((bf16[16,16,1024]{2,1,0:T(8,128)(2,1)}), bf16[16,16,1024]{2,1,0:T(8,128)(2,1)S(1)}, u32[]{:S(2)}, u32[]{:S(2)}) %all-to-all-start) | async-done | bytes 524320 | tf_op jit(solution)/shard_map/while/body/eval_jaxpr/all_to_all | solution.py:131
  588.8 10.1 %all-to-all-done.1 = bf16[16,16,1024]{2,1,0:T(8,128)(2,1)S(1)} async-done(((bf16[16,16,1024]{2,1,0:T(8,128)(2,1)}), bf16[16,16,1024]{2,1,0:T(8,128)(2,1)S(1)}, u32[]{:S(2)}, u32[]{:S(2)}) %all-to-all-start.1) | async-done | bytes 524320 | tf_op jit(solution)/shard_map/while/body/eval_jaxpr/all_to_all | solution.py:138
  616.8 8.8 %all-to-all-done = bf16[16,16,1024]{2,1,0:T(8,128)(2,1)S(1)} async-done(((bf16[16,16,1024]{2,1,0:T(8,128)(2,1)}), bf16[16,16,1024]{2,1,0:T(8,128)(2,1)S(1)}, u32[]{:S(2)}, u32[]{:S(2)}) %all-to-all-start) | async-done | bytes 524320 | tf_op jit(solution)/shard_map/while/body/eval_jaxpr/all_to_all | solution.py:131
  630.2 10.1 %all-to-all-done.1 = bf16[16,16,1024]{2,1,0:T(8,128)(2,1)S(1)} async-done(((bf16[16,16,1024]{2,1,0:T(8,128)(2,1)}), bf16[16,16,1024]{2,1,0:T(8,128)(2,1)S(1)}, u32[]{:S(2)}, u32[]{:S(2)}) %all-to-all-start.1) | async-done | bytes 524320 | tf_op jit(solution)/shard_map/while/body/eval_jaxpr/all_to_all | solution.py:138
  642.2 45.5 %collective-permute-done = bf16[256,1024]{1,0:T(8,128)(2,1)S(1)} collective-permute-done((bf16[256,1024]{1,0:T(8,128)(2,1)S(1)}, bf16[256,1024]{1,0:T(8,128)(2,1)S(1)}, u32[]{:S(2)}, u32[]{:S(2)}) %collective-permute-start) | collective-permute-done | bytes 524320 | tf_op jit(solution)/shard_map/while/body/eval_jaxpr/ppermute | solution.py:12
  702.7 8.8 %all-to-all-done = bf16[16,16,1024]{2,1,0:T(8,128)(2,1)S(1)} async-done(((bf16[16,16,1024]{2,1,0:T(8,128)(2,1)}), bf16[16,16,1024]{2,1,0:T(8,128)(2,1)S(1)}, u32[]{:S(2)}, u32[]{:S(2)}) %all-to-all-start) | async-done | bytes 524320 | tf_op jit(solution)/shard_map/while/body/eval_jaxpr/all_to_all | solution.py:131
  716.1 10.1 %all-to-all-done.1 = bf16[16,16,1024]{2,1,0:T(8,128)(2,1)S(1)} async-done(((bf16[16,16,1024]{2,1,0:T(8,128)(2,1)}), bf16[16,16,1024]{2,1,0:T(8,128)(2,1)S(1)}, u32[]{:S(2)}, u32[]{:S(2)}) %all-to-all-start.1) | async-done | bytes 524320 | tf_op jit(solution)/shard_map/while/body/eval_jaxpr/all_to_all | solution.py:138
  728.2 34.3 %collective-permute-done = bf16[256,1024]{1,0:T(8,128)(2,1)S(1)} collective-permute-done((bf16[256,1024]{1,0:T(8,128)(2,1)S(1)}, bf16[256,1024]{1,0:T(8,128)(2,1)S(1)}, u32[]{:S(2)}, u32[]{:S(2)}) %collective-permute-start) | collective-permute-done | bytes 524320 | tf_op jit(solution)/shard_map/while/body/eval_jaxpr/ppermute | solution.py:12
  777.5 8.8 %all-to-all-done = bf16[16,16,1024]{2,1,0:T(8,128)(2,1)S(1)} async-done(((bf16[16,16,1024]{2,1,0:T(8,128)(2,1)}), bf16[16,16,1024]{2,1,0:T(8,128)(2,1)S(1)}, u32[]{:S(2)}, u32[]{:S(2)}) %all-to-all-start) | async-done | bytes 524320 | tf_op jit(solution)/shard_map/while/body/eval_jaxpr/all_to_all | solution.py:131
  791.0 10.1 %all-to-all-done.1 = bf16[16,16,1024]{2,1,0:T(8,128)(2,1)S(1)} async-done(((bf16[16,16,1024]{2,1,0:T(8,128)(2,1)}), bf16[16,16,1024]{2,1,0:T(8,128)(2,1)S(1)}, u32[]{:S(2)}, u32[]{:S(2)}) %all-to-all-start.1) | async-done | bytes 524320 | tf_op jit(solution)/shard_map/while/body/eval_jaxpr/all_to_all | solution.py:138
  819.0 11.8 %all-to-all-done = bf16[16,16,1024]{2,1,0:T(8,128)(2,1)S(1)} async-done(((bf16[16,16,1024]{2,1,0:T(8,128)(2,1)}), bf16[16,16,1024]{2,1,0:T(8,128)(2,1)S(1)}, u32[]{:S(2)}, u32[]{:S(2)}) %all-to-all-start) | async-done | bytes 524320 | tf_op jit(solution)/shard_map/while/body/eval_jaxpr/all_to_all | solution.py:131
  835.4 11.9 %all-to-all-done.1 = bf16[16,16,1024]{2,1,0:T(8,128)(2,1)S(1)} async-done(((bf16[16,16,1024]{2,1,0:T(8,128)(2,1)}), bf16[16,16,1024]{2,1,0:T(8,128)(2,1)S(1)}, u32[]{:S(2)}, u32[]{:S(2)}) %all-to-all-start.1) | async-done | bytes 524320 | tf_op jit(solution)/shard_map/while/body/eval_jaxpr/all_to_all | solution.py:138
  (344 shorter events, 327.2 us)
Async XLA Ops:
  6.5 51.4 %all-gather.2.cloned.1.call-start = ((), (), s32[]{:S(2)}) async-start(), calls=%async_computation.2 | async-start | bytes 1114112 | tf_op jit(solution)/shard_map/all_gather | solution.py:122
  58.7 10.5 %collective-permute-start = (bf16[256,1024]{1,0:T(8,128)(2,1)S(1)}, bf16[256,1024]{1,0:T(8,128)(2,1)S(1)}, u32[]{:S(2)}, u32[]{:S(2)}) collective-permute-start(bf16[256,1024]{1,0:T(8,128)(2,1)S(1)} %get-tuple-element.587), channel_id=1, source_target_pairs={{0,16},{16,32},{32,48},{48,64},{64,80},{80,96},{96,112},{112,128},... | collective-permute-start | bytes 1572872 | tf_op jit(solution)/shard_map/while/body/eval_jaxpr/ppermute | solution.py:12
  71.8 15.0 %all-to-all-start = ((bf16[16,16,1024]{2,1,0:T(8,128)(2,1)}), bf16[16,16,1024]{2,1,0:T(8,128)(2,1)S(1)}, u32[]{:S(2)}, u32[]{:S(2)}) async-start(bf16[16,16,1024]{2,1,0:T(8,128)(2,1)} %bitcast.63), calls=%async_computation | async-start | bytes 1048576 | tf_op jit(solution)/shard_map/while/body/eval_jaxpr/all_to_all | solution.py:131
  87.8 13.7 %all-to-all-start.1 = ((bf16[16,16,1024]{2,1,0:T(8,128)(2,1)}), bf16[16,16,1024]{2,1,0:T(8,128)(2,1)S(1)}, u32[]{:S(2)}, u32[]{:S(2)}) async-start(bf16[16,16,1024]{2,1,0:T(8,128)(2,1)} %broadcast_in_dim.149), calls=%async_computation.1 | async-start | bytes 1048576 | tf_op jit(solution)/shard_map/while/body/eval_jaxpr/all_to_all | solution.py:138
  101.5 10.5 %collective-permute-start = (bf16[256,1024]{1,0:T(8,128)(2,1)S(1)}, bf16[256,1024]{1,0:T(8,128)(2,1)S(1)}, u32[]{:S(2)}, u32[]{:S(2)}) collective-permute-start(bf16[256,1024]{1,0:T(8,128)(2,1)S(1)} %get-tuple-element.587), channel_id=1, source_target_pairs={{0,16},{16,32},{32,48},{48,64},{64,80},{80,96},{96,112},{112,128},... | collective-permute-start | bytes 1572872 | tf_op jit(solution)/shard_map/while/body/eval_jaxpr/ppermute | solution.py:12
  114.5 13.7 %all-to-all-start = ((bf16[16,16,1024]{2,1,0:T(8,128)(2,1)}), bf16[16,16,1024]{2,1,0:T(8,128)(2,1)S(1)}, u32[]{:S(2)}, u32[]{:S(2)}) async-start(bf16[16,16,1024]{2,1,0:T(8,128)(2,1)} %bitcast.63), calls=%async_computation | async-start | bytes 1048576 | tf_op jit(solution)/shard_map/while/body/eval_jaxpr/all_to_all | solution.py:131
  129.2 13.7 %all-to-all-start.1 = ((bf16[16,16,1024]{2,1,0:T(8,128)(2,1)}), bf16[16,16,1024]{2,1,0:T(8,128)(2,1)S(1)}, u32[]{:S(2)}, u32[]{:S(2)}) async-start(bf16[16,16,1024]{2,1,0:T(8,128)(2,1)} %broadcast_in_dim.149), calls=%async_computation.1 | async-start | bytes 1048576 | tf_op jit(solution)/shard_map/while/body/eval_jaxpr/all_to_all | solution.py:138
  142.9 10.5 %collective-permute-start = (bf16[256,1024]{1,0:T(8,128)(2,1)S(1)}, bf16[256,1024]{1,0:T(8,128)(2,1)S(1)}, u32[]{:S(2)}, u32[]{:S(2)}) collective-permute-start(bf16[256,1024]{1,0:T(8,128)(2,1)S(1)} %get-tuple-element.587), channel_id=1, source_target_pairs={{0,16},{16,32},{32,48},{48,64},{64,80},{80,96},{96,112},{112,128},... | collective-permute-start | bytes 1572872 | tf_op jit(solution)/shard_map/while/body/eval_jaxpr/ppermute | solution.py:12
  156.0 13.7 %all-to-all-start = ((bf16[16,16,1024]{2,1,0:T(8,128)(2,1)}), bf16[16,16,1024]{2,1,0:T(8,128)(2,1)S(1)}, u32[]{:S(2)}, u32[]{:S(2)}) async-start(bf16[16,16,1024]{2,1,0:T(8,128)(2,1)} %bitcast.63), calls=%async_computation | async-start | bytes 1048576 | tf_op jit(solution)/shard_map/while/body/eval_jaxpr/all_to_all | solution.py:131
  170.7 13.7 %all-to-all-start.1 = ((bf16[16,16,1024]{2,1,0:T(8,128)(2,1)}), bf16[16,16,1024]{2,1,0:T(8,128)(2,1)S(1)}, u32[]{:S(2)}, u32[]{:S(2)}) async-start(bf16[16,16,1024]{2,1,0:T(8,128)(2,1)} %broadcast_in_dim.149), calls=%async_computation.1 | async-start | bytes 1048576 | tf_op jit(solution)/shard_map/while/body/eval_jaxpr/all_to_all | solution.py:138
  184.4 10.5 %collective-permute-start = (bf16[256,1024]{1,0:T(8,128)(2,1)S(1)}, bf16[256,1024]{1,0:T(8,128)(2,1)S(1)}, u32[]{:S(2)}, u32[]{:S(2)}) collective-permute-start(bf16[256,1024]{1,0:T(8,128)(2,1)S(1)} %get-tuple-element.587), channel_id=1, source_target_pairs={{0,16},{16,32},{32,48},{48,64},{64,80},{80,96},{96,112},{112,128},... | collective-permute-start | bytes 1572872 | tf_op jit(solution)/shard_map/while/body/eval_jaxpr/ppermute | solution.py:12
  197.4 13.7 %all-to-all-start = ((bf16[16,16,1024]{2,1,0:T(8,128)(2,1)}), bf16[16,16,1024]{2,1,0:T(8,128)(2,1)S(1)}, u32[]{:S(2)}, u32[]{:S(2)}) async-start(bf16[16,16,1024]{2,1,0:T(8,128)(2,1)} %bitcast.63), calls=%async_computation | async-start | bytes 1048576 | tf_op jit(solution)/shard_map/while/body/eval_jaxpr/all_to_all | solution.py:131
  212.1 13.7 %all-to-all-start.1 = ((bf16[16,16,1024]{2,1,0:T(8,128)(2,1)}), bf16[16,16,1024]{2,1,0:T(8,128)(2,1)S(1)}, u32[]{:S(2)}, u32[]{:S(2)}) async-start(bf16[16,16,1024]{2,1,0:T(8,128)(2,1)} %broadcast_in_dim.149), calls=%async_computation.1 | async-start | bytes 1048576 | tf_op jit(solution)/shard_map/while/body/eval_jaxpr/all_to_all | solution.py:138
  225.8 10.5 %collective-permute-start = (bf16[256,1024]{1,0:T(8,128)(2,1)S(1)}, bf16[256,1024]{1,0:T(8,128)(2,1)S(1)}, u32[]{:S(2)}, u32[]{:S(2)}) collective-permute-start(bf16[256,1024]{1,0:T(8,128)(2,1)S(1)} %get-tuple-element.587), channel_id=1, source_target_pairs={{0,16},{16,32},{32,48},{48,64},{64,80},{80,96},{96,112},{112,128},... | collective-permute-start | bytes 1572872 | tf_op jit(solution)/shard_map/while/body/eval_jaxpr/ppermute | solution.py:12
  238.9 13.7 %all-to-all-start = ((bf16[16,16,1024]{2,1,0:T(8,128)(2,1)}), bf16[16,16,1024]{2,1,0:T(8,128)(2,1)S(1)}, u32[]{:S(2)}, u32[]{:S(2)}) async-start(bf16[16,16,1024]{2,1,0:T(8,128)(2,1)} %bitcast.63), calls=%async_computation | async-start | bytes 1048576 | tf_op jit(solution)/shard_map/while/body/eval_jaxpr/all_to_all | solution.py:131
  253.6 13.7 %all-to-all-start.1 = ((bf16[16,16,1024]{2,1,0:T(8,128)(2,1)}), bf16[16,16,1024]{2,1,0:T(8,128)(2,1)S(1)}, u32[]{:S(2)}, u32[]{:S(2)}) async-start(bf16[16,16,1024]{2,1,0:T(8,128)(2,1)} %broadcast_in_dim.149), calls=%async_computation.1 | async-start | bytes 1048576 | tf_op jit(solution)/shard_map/while/body/eval_jaxpr/all_to_all | solution.py:138
  267.3 10.5 %collective-permute-start = (bf16[256,1024]{1,0:T(8,128)(2,1)S(1)}, bf16[256,1024]{1,0:T(8,128)(2,1)S(1)}, u32[]{:S(2)}, u32[]{:S(2)}) collective-permute-start(bf16[256,1024]{1,0:T(8,128)(2,1)S(1)} %get-tuple-element.587), channel_id=1, source_target_pairs={{0,16},{16,32},{32,48},{48,64},{64,80},{80,96},{96,112},{112,128},... | collective-permute-start | bytes 1572872 | tf_op jit(solution)/shard_map/while/body/eval_jaxpr/ppermute | solution.py:12
  280.3 13.7 %all-to-all-start = ((bf16[16,16,1024]{2,1,0:T(8,128)(2,1)}), bf16[16,16,1024]{2,1,0:T(8,128)(2,1)S(1)}, u32[]{:S(2)}, u32[]{:S(2)}) async-start(bf16[16,16,1024]{2,1,0:T(8,128)(2,1)} %bitcast.63), calls=%async_computation | async-start | bytes 1048576 | tf_op jit(solution)/shard_map/while/body/eval_jaxpr/all_to_all | solution.py:131
  295.0 13.7 %all-to-all-start.1 = ((bf16[16,16,1024]{2,1,0:T(8,128)(2,1)}), bf16[16,16,1024]{2,1,0:T(8,128)(2,1)S(1)}, u32[]{:S(2)}, u32[]{:S(2)}) async-start(bf16[16,16,1024]{2,1,0:T(8,128)(2,1)} %broadcast_in_dim.149), calls=%async_computation.1 | async-start | bytes 1048576 | tf_op jit(solution)/shard_map/while/body/eval_jaxpr/all_to_all | solution.py:138
  308.7 10.5 %collective-permute-start = (bf16[256,1024]{1,0:T(8,128)(2,1)S(1)}, bf16[256,1024]{1,0:T(8,128)(2,1)S(1)}, u32[]{:S(2)}, u32[]{:S(2)}) collective-permute-start(bf16[256,1024]{1,0:T(8,128)(2,1)S(1)} %get-tuple-element.587), channel_id=1, source_target_pairs={{0,16},{16,32},{32,48},{48,64},{64,80},{80,96},{96,112},{112,128},... | collective-permute-start | bytes 1572872 | tf_op jit(solution)/shard_map/while/body/eval_jaxpr/ppermute | solution.py:12
  321.8 13.7 %all-to-all-start = ((bf16[16,16,1024]{2,1,0:T(8,128)(2,1)}), bf16[16,16,1024]{2,1,0:T(8,128)(2,1)S(1)}, u32[]{:S(2)}, u32[]{:S(2)}) async-start(bf16[16,16,1024]{2,1,0:T(8,128)(2,1)} %bitcast.63), calls=%async_computation | async-start | bytes 1048576 | tf_op jit(solution)/shard_map/while/body/eval_jaxpr/all_to_all | solution.py:131
  336.5 13.7 %all-to-all-start.1 = ((bf16[16,16,1024]{2,1,0:T(8,128)(2,1)}), bf16[16,16,1024]{2,1,0:T(8,128)(2,1)S(1)}, u32[]{:S(2)}, u32[]{:S(2)}) async-start(bf16[16,16,1024]{2,1,0:T(8,128)(2,1)} %broadcast_in_dim.149), calls=%async_computation.1 | async-start | bytes 1048576 | tf_op jit(solution)/shard_map/while/body/eval_jaxpr/all_to_all | solution.py:138
  350.2 10.5 %collective-permute-start = (bf16[256,1024]{1,0:T(8,128)(2,1)S(1)}, bf16[256,1024]{1,0:T(8,128)(2,1)S(1)}, u32[]{:S(2)}, u32[]{:S(2)}) collective-permute-start(bf16[256,1024]{1,0:T(8,128)(2,1)S(1)} %get-tuple-element.587), channel_id=1, source_target_pairs={{0,16},{16,32},{32,48},{48,64},{64,80},{80,96},{96,112},{112,128},... | collective-permute-start | bytes 1572872 | tf_op jit(solution)/shard_map/while/body/eval_jaxpr/ppermute | solution.py:12
  363.2 13.7 %all-to-all-start = ((bf16[16,16,1024]{2,1,0:T(8,128)(2,1)}), bf16[16,16,1024]{2,1,0:T(8,128)(2,1)S(1)}, u32[]{:S(2)}, u32[]{:S(2)}) async-start(bf16[16,16,1024]{2,1,0:T(8,128)(2,1)} %bitcast.63), calls=%async_computation | async-start | bytes 1048576 | tf_op jit(solution)/shard_map/while/body/eval_jaxpr/all_to_all | solution.py:131
  377.9 13.7 %all-to-all-start.1 = ((bf16[16,16,1024]{2,1,0:T(8,128)(2,1)}), bf16[16,16,1024]{2,1,0:T(8,128)(2,1)S(1)}, u32[]{:S(2)}, u32[]{:S(2)}) async-start(bf16[16,16,1024]{2,1,0:T(8,128)(2,1)} %broadcast_in_dim.149), calls=%async_computation.1 | async-start | bytes 1048576 | tf_op jit(solution)/shard_map/while/body/eval_jaxpr/all_to_all | solution.py:138
  391.6 10.5 %collective-permute-start = (bf16[256,1024]{1,0:T(8,128)(2,1)S(1)}, bf16[256,1024]{1,0:T(8,128)(2,1)S(1)}, u32[]{:S(2)}, u32[]{:S(2)}) collective-permute-start(bf16[256,1024]{1,0:T(8,128)(2,1)S(1)} %get-tuple-element.587), channel_id=1, source_target_pairs={{0,16},{16,32},{32,48},{48,64},{64,80},{80,96},{96,112},{112,128},... | collective-permute-start | bytes 1572872 | tf_op jit(solution)/shard_map/while/body/eval_jaxpr/ppermute | solution.py:12
  404.7 13.7 %all-to-all-start = ((bf16[16,16,1024]{2,1,0:T(8,128)(2,1)}), bf16[16,16,1024]{2,1,0:T(8,128)(2,1)S(1)}, u32[]{:S(2)}, u32[]{:S(2)}) async-start(bf16[16,16,1024]{2,1,0:T(8,128)(2,1)} %bitcast.63), calls=%async_computation | async-start | bytes 1048576 | tf_op jit(solution)/shard_map/while/body/eval_jaxpr/all_to_all | solution.py:131
  419.4 13.7 %all-to-all-start.1 = ((bf16[16,16,1024]{2,1,0:T(8,128)(2,1)}), bf16[16,16,1024]{2,1,0:T(8,128)(2,1)S(1)}, u32[]{:S(2)}, u32[]{:S(2)}) async-start(bf16[16,16,1024]{2,1,0:T(8,128)(2,1)} %broadcast_in_dim.149), calls=%async_computation.1 | async-start | bytes 1048576 | tf_op jit(solution)/shard_map/while/body/eval_jaxpr/all_to_all | solution.py:138
  433.1 10.5 %collective-permute-start = (bf16[256,1024]{1,0:T(8,128)(2,1)S(1)}, bf16[256,1024]{1,0:T(8,128)(2,1)S(1)}, u32[]{:S(2)}, u32[]{:S(2)}) collective-permute-start(bf16[256,1024]{1,0:T(8,128)(2,1)S(1)} %get-tuple-element.587), channel_id=1, source_target_pairs={{0,16},{16,32},{32,48},{48,64},{64,80},{80,96},{96,112},{112,128},... | collective-permute-start | bytes 1572872 | tf_op jit(solution)/shard_map/while/body/eval_jaxpr/ppermute | solution.py:12
  446.1 13.7 %all-to-all-start = ((bf16[16,16,1024]{2,1,0:T(8,128)(2,1)}), bf16[16,16,1024]{2,1,0:T(8,128)(2,1)S(1)}, u32[]{:S(2)}, u32[]{:S(2)}) async-start(bf16[16,16,1024]{2,1,0:T(8,128)(2,1)} %bitcast.63), calls=%async_computation | async-start | bytes 1048576 | tf_op jit(solution)/shard_map/while/body/eval_jaxpr/all_to_all | solution.py:131
  460.8 13.7 %all-to-all-start.1 = ((bf16[16,16,1024]{2,1,0:T(8,128)(2,1)}), bf16[16,16,1024]{2,1,0:T(8,128)(2,1)S(1)}, u32[]{:S(2)}, u32[]{:S(2)}) async-start(bf16[16,16,1024]{2,1,0:T(8,128)(2,1)} %broadcast_in_dim.149), calls=%async_computation.1 | async-start | bytes 1048576 | tf_op jit(solution)/shard_map/while/body/eval_jaxpr/all_to_all | solution.py:138
  474.5 10.5 %collective-permute-start = (bf16[256,1024]{1,0:T(8,128)(2,1)S(1)}, bf16[256,1024]{1,0:T(8,128)(2,1)S(1)}, u32[]{:S(2)}, u32[]{:S(2)}) collective-permute-start(bf16[256,1024]{1,0:T(8,128)(2,1)S(1)} %get-tuple-element.587), channel_id=1, source_target_pairs={{0,16},{16,32},{32,48},{48,64},{64,80},{80,96},{96,112},{112,128},... | collective-permute-start | bytes 1572872 | tf_op jit(solution)/shard_map/while/body/eval_jaxpr/ppermute | solution.py:12
  487.6 13.7 %all-to-all-start = ((bf16[16,16,1024]{2,1,0:T(8,128)(2,1)}), bf16[16,16,1024]{2,1,0:T(8,128)(2,1)S(1)}, u32[]{:S(2)}, u32[]{:S(2)}) async-start(bf16[16,16,1024]{2,1,0:T(8,128)(2,1)} %bitcast.63), calls=%async_computation | async-start | bytes 1048576 | tf_op jit(solution)/shard_map/while/body/eval_jaxpr/all_to_all | solution.py:131
  502.3 13.7 %all-to-all-start.1 = ((bf16[16,16,1024]{2,1,0:T(8,128)(2,1)}), bf16[16,16,1024]{2,1,0:T(8,128)(2,1)S(1)}, u32[]{:S(2)}, u32[]{:S(2)}) async-start(bf16[16,16,1024]{2,1,0:T(8,128)(2,1)} %broadcast_in_dim.149), calls=%async_computation.1 | async-start | bytes 1048576 | tf_op jit(solution)/shard_map/while/body/eval_jaxpr/all_to_all | solution.py:138
  529.0 13.7 %all-to-all-start = ((bf16[16,16,1024]{2,1,0:T(8,128)(2,1)}), bf16[16,16,1024]{2,1,0:T(8,128)(2,1)S(1)}, u32[]{:S(2)}, u32[]{:S(2)}) async-start(bf16[16,16,1024]{2,1,0:T(8,128)(2,1)} %bitcast.63), calls=%async_computation | async-start | bytes 1048576 | tf_op jit(solution)/shard_map/while/body/eval_jaxpr/all_to_all | solution.py:131
  543.7 13.7 %all-to-all-start.1 = ((bf16[16,16,1024]{2,1,0:T(8,128)(2,1)}), bf16[16,16,1024]{2,1,0:T(8,128)(2,1)S(1)}, u32[]{:S(2)}, u32[]{:S(2)}) async-start(bf16[16,16,1024]{2,1,0:T(8,128)(2,1)} %broadcast_in_dim.149), calls=%async_computation.1 | async-start | bytes 1048576 | tf_op jit(solution)/shard_map/while/body/eval_jaxpr/all_to_all | solution.py:138
  570.5 13.7 %all-to-all-start = ((bf16[16,16,1024]{2,1,0:T(8,128)(2,1)}), bf16[16,16,1024]{2,1,0:T(8,128)(2,1)S(1)}, u32[]{:S(2)}, u32[]{:S(2)}) async-start(bf16[16,16,1024]{2,1,0:T(8,128)(2,1)} %bitcast.63), calls=%async_computation | async-start | bytes 1048576 | tf_op jit(solution)/shard_map/while/body/eval_jaxpr/all_to_all | solution.py:131
  585.2 13.7 %all-to-all-start.1 = ((bf16[16,16,1024]{2,1,0:T(8,128)(2,1)}), bf16[16,16,1024]{2,1,0:T(8,128)(2,1)S(1)}, u32[]{:S(2)}, u32[]{:S(2)}) async-start(bf16[16,16,1024]{2,1,0:T(8,128)(2,1)} %broadcast_in_dim.149), calls=%async_computation.1 | async-start | bytes 1048576 | tf_op jit(solution)/shard_map/while/body/eval_jaxpr/all_to_all | solution.py:138
  611.9 13.7 %all-to-all-start = ((bf16[16,16,1024]{2,1,0:T(8,128)(2,1)}), bf16[16,16,1024]{2,1,0:T(8,128)(2,1)S(1)}, u32[]{:S(2)}, u32[]{:S(2)}) async-start(bf16[16,16,1024]{2,1,0:T(8,128)(2,1)} %bitcast.63), calls=%async_computation | async-start | bytes 1048576 | tf_op jit(solution)/shard_map/while/body/eval_jaxpr/all_to_all | solution.py:131
  626.6 13.7 %all-to-all-start.1 = ((bf16[16,16,1024]{2,1,0:T(8,128)(2,1)}), bf16[16,16,1024]{2,1,0:T(8,128)(2,1)S(1)}, u32[]{:S(2)}, u32[]{:S(2)}) async-start(bf16[16,16,1024]{2,1,0:T(8,128)(2,1)} %broadcast_in_dim.149), calls=%async_computation.1 | async-start | bytes 1048576 | tf_op jit(solution)/shard_map/while/body/eval_jaxpr/all_to_all | solution.py:138
  640.3 47.4 %collective-permute-start = (bf16[256,1024]{1,0:T(8,128)(2,1)S(1)}, bf16[256,1024]{1,0:T(8,128)(2,1)S(1)}, u32[]{:S(2)}, u32[]{:S(2)}) collective-permute-start(bf16[256,1024]{1,0:T(8,128)(2,1)S(1)} %get-tuple-element.587), channel_id=1, source_target_pairs={{0,16},{16,32},{32,48},{48,64},{64,80},{80,96},{96,112},{112,128},... | collective-permute-start | bytes 1572872 | tf_op jit(solution)/shard_map/while/body/eval_jaxpr/ppermute | solution.py:12
  697.8 13.7 %all-to-all-start = ((bf16[16,16,1024]{2,1,0:T(8,128)(2,1)}), bf16[16,16,1024]{2,1,0:T(8,128)(2,1)S(1)}, u32[]{:S(2)}, u32[]{:S(2)}) async-start(bf16[16,16,1024]{2,1,0:T(8,128)(2,1)} %bitcast.63), calls=%async_computation | async-start | bytes 1048576 | tf_op jit(solution)/shard_map/while/body/eval_jaxpr/all_to_all | solution.py:131
  712.5 13.7 %all-to-all-start.1 = ((bf16[16,16,1024]{2,1,0:T(8,128)(2,1)}), bf16[16,16,1024]{2,1,0:T(8,128)(2,1)S(1)}, u32[]{:S(2)}, u32[]{:S(2)}) async-start(bf16[16,16,1024]{2,1,0:T(8,128)(2,1)} %broadcast_in_dim.149), calls=%async_computation.1 | async-start | bytes 1048576 | tf_op jit(solution)/shard_map/while/body/eval_jaxpr/all_to_all | solution.py:138
  726.2 36.3 %collective-permute-start = (bf16[256,1024]{1,0:T(8,128)(2,1)S(1)}, bf16[256,1024]{1,0:T(8,128)(2,1)S(1)}, u32[]{:S(2)}, u32[]{:S(2)}) collective-permute-start(bf16[256,1024]{1,0:T(8,128)(2,1)S(1)} %get-tuple-element.587), channel_id=1, source_target_pairs={{0,16},{16,32},{32,48},{48,64},{64,80},{80,96},{96,112},{112,128},... | collective-permute-start | bytes 1572872 | tf_op jit(solution)/shard_map/while/body/eval_jaxpr/ppermute | solution.py:12
  772.6 13.7 %all-to-all-start = ((bf16[16,16,1024]{2,1,0:T(8,128)(2,1)}), bf16[16,16,1024]{2,1,0:T(8,128)(2,1)S(1)}, u32[]{:S(2)}, u32[]{:S(2)}) async-start(bf16[16,16,1024]{2,1,0:T(8,128)(2,1)} %bitcast.63), calls=%async_computation | async-start | bytes 1048576 | tf_op jit(solution)/shard_map/while/body/eval_jaxpr/all_to_all | solution.py:131
  787.4 13.7 %all-to-all-start.1 = ((bf16[16,16,1024]{2,1,0:T(8,128)(2,1)}), bf16[16,16,1024]{2,1,0:T(8,128)(2,1)S(1)}, u32[]{:S(2)}, u32[]{:S(2)}) async-start(bf16[16,16,1024]{2,1,0:T(8,128)(2,1)} %broadcast_in_dim.149), calls=%async_computation.1 | async-start | bytes 1048576 | tf_op jit(solution)/shard_map/while/body/eval_jaxpr/all_to_all | solution.py:138
  814.1 16.7 %all-to-all-start = ((bf16[16,16,1024]{2,1,0:T(8,128)(2,1)}), bf16[16,16,1024]{2,1,0:T(8,128)(2,1)S(1)}, u32[]{:S(2)}, u32[]{:S(2)}) async-start(bf16[16,16,1024]{2,1,0:T(8,128)(2,1)} %bitcast.63), calls=%async_computation | async-start | bytes 1048576 | tf_op jit(solution)/shard_map/while/body/eval_jaxpr/all_to_all | solution.py:131
  831.8 15.5 %all-to-all-start.1 = ((bf16[16,16,1024]{2,1,0:T(8,128)(2,1)}), bf16[16,16,1024]{2,1,0:T(8,128)(2,1)S(1)}, u32[]{:S(2)}, u32[]{:S(2)}) async-start(bf16[16,16,1024]{2,1,0:T(8,128)(2,1)} %broadcast_in_dim.149), calls=%async_computation.1 | async-start | bytes 1048576 | tf_op jit(solution)/shard_map/while/body/eval_jaxpr/all_to_all | solution.py:138
  (47 other events, 111.1 us)
Sparse Core Ops, SparseCore 0:
  9.8 48.1 all-gather.1

commit v2 on v1

v2 whole, which is shorter than its diff:
```python
import functools

import jax
import jax.numpy as jnp
from jax import lax
from jax.experimental import pallas as pl
from jax.experimental.pallas import tpu as pltpu
from jax.sharding import PartitionSpec as P

DH = 128
SIDE = 4
WINDOW = 128
STARTS = (0, 32, 96, 128)


def layer_kernel(flag_ref, hidden_ref, gain_ref, bias_ref, live_ref, *refs):
    weights, out_ref = refs[:16], refs[16]

    @pl.when(flag_ref[0] > 0)
    def _():
        wide = hidden_ref[...].astype(jnp.float32)
        mean_square = jnp.mean(wide * wide, axis=-1, keepdims=True)
        normed = (wide * lax.rsqrt(mean_square + 1e-06) * gain_ref[...]).astype(jnp.bfloat16)
        bias = bias_ref[...]
        heads = weights[0].shape[1] // DH

        def project(ref):
            return jnp.dot(
                normed, ref[...], preferred_element_type=jnp.float32
            ).astype(jnp.bfloat16)

        def attend(queries, keyed, values):
            parts = []
            for head in range(heads):
                cols = slice(head * DH, (head + 1) * DH)
                scores = lax.dot_general(
                    queries[:, cols], keyed[:, cols], (((1,), (1,)), ((), ())),
                    preferred_element_type=jnp.float32,
                ) * DH ** (-0.5) + bias
                expo = jnp.exp(scores - jnp.max(scores, axis=-1, keepdims=True))
                weight = (expo / jnp.sum(expo, axis=-1, keepdims=True)).astype(jnp.bfloat16)
                parts.append(
                    jnp.dot(weight, values[:, cols], preferred_element_type=jnp.float32)
                    .astype(jnp.bfloat16)
                )
            return jnp.concatenate(parts, axis=1)

        total = None
        for j in range(SIDE):
            context = attend(*[project(ref) for ref in weights[4 * j : 4 * j + 3]])
            term = jnp.dot(
                context, weights[4 * j + 3][...], preferred_element_type=jnp.float32
            )
            total = term if total is None else total + term
        out_ref[...] = jnp.where(live_ref[...] > 0.0, total, 0.0).astype(out_ref.dtype)


def run_layer(flag, hidden, gain, bias, live, weights):
    rows, model = hidden.shape
    width = weights[0].shape[1]
    vmem = pl.BlockSpec(memory_space=pltpu.VMEM)
    return pl.pallas_call(
        layer_kernel,
        out_shape=jax.ShapeDtypeStruct((rows, model), jnp.bfloat16),
        in_specs=[pl.BlockSpec(memory_space=pltpu.SMEM)] + [vmem] * 20,
        out_specs=vmem,
        compiler_params=pltpu.CompilerParams(vmem_limit_bytes=32 * 1024 * 1024),
        cost_estimate=pl.CostEstimate(
            flops=2 * rows * model * width * 16, bytes_accessed=16 * model * width * 2,
            transcendentals=rows * rows * 16,
        ),
    )(flag, hidden, gain, bias, live, *weights)


def group_bounds(segments):
    seq_len = segments.shape[0]
    quarter = seq_len // SIDE
    position = jnp.arange(seq_len, dtype=jnp.int32)
    before = jnp.concatenate([segments[:1] - 1, segments[:-1]])
    begins = segments != before
    bounds = [jnp.int32(0)]
    for g in range(1, SIDE):
        middle = g * quarter
        low = jnp.max(jnp.where(begins & (position <= middle), position, 0))
        high = jnp.min(jnp.where(begins & (position >= middle), position, seq_len))
        bounds.append(jnp.where(middle - low <= high - middle, low, high))
    return jnp.stack(bounds)


def window_masks(segments, prefixes, length, start):
    seq_len = segments.shape[0]
    count_seg = prefixes.shape[0]
    position = jnp.arange(seq_len, dtype=jnp.int32)
    member = segments[:, None] == jnp.arange(count_seg, dtype=jnp.int32)[None, :]
    seg_start = jnp.min(jnp.where(member, position[:, None], jnp.int32(seq_len)), axis=0)
    prefix_end = jnp.sum(jnp.where(member, (seg_start + prefixes)[None, :], jnp.int32(0)), axis=1)
    seg_w = lax.dynamic_slice_in_dim(segments, start, WINDOW, 0)
    end_w = lax.dynamic_slice_in_dim(prefix_end, start, WINDOW, 0)
    pos_w = start + jnp.arange(WINDOW, dtype=jnp.int32)
    key_ok = (pos_w[None, :] <= pos_w[:, None]) | (pos_w[None, :] < end_w[None, :])
    live_keys = (pos_w[None, :] < length) | (pos_w[None, :] == pos_w[:, None])
    visible = (seg_w[:, None] == seg_w[None, :]) & key_ok & live_keys
    bias = jnp.where(visible, jnp.float32(0.0), jnp.float32(-1e30))
    live = (pos_w < length).astype(jnp.float32)[:, None]
    return bias, live


def everywhere(sections, groups, move):
    pairs = []
    for section in sections:
        for y in range(SIDE):
            for x in range(SIDE):
                there = move(section, y, x)
                if there is not None:
                    to, ty, tx = there
                    pairs.append(
                        (section * groups + y * SIDE + x,
                         to * groups + (ty % SIDE) * SIDE + tx % SIDE)
                    )
    return pairs


AXES = ("section", "dp")


def shards(
    inputs, norm_gain, w_query, w_key, w_value, w_output, segment_ids, prefix_lengths, batch_lengths
):
    section = lax.axis_index("section")
    sections = lax.axis_size("section")
    groups = lax.axis_size("dp")
    place = lax.axis_index("dp")
    micro_count, row_count, model = inputs.shape
    seq_len = row_count * groups
    quarter = seq_len // SIDE
    y, x = place // SIDE, place % SIDE
    group = (y + x) % SIDE
    start = jnp.asarray(STARTS, jnp.int32)[group]

    def ring(step):
        return everywhere(
            range(sections), groups,
            lambda s, a, b: (s, a + step, b) if s % 2 == 0 else (s, a, b + step),
        )

    own = [w_query[0], w_key[0], w_value[0], w_output[0]]
    ahead, behind = ring(1), ring(-1)
    from_low = [lax.ppermute(w, AXES, ahead) for w in own]
    from_high = [lax.ppermute(w, AXES, behind) for w in own]
    opposite = [lax.ppermute(w, AXES, ahead) for w in from_low[:2]]
    opposite += [lax.ppermute(w, AXES, behind) for w in from_high[2:]]
    weights = own + from_low + from_high + opposite

    inputs_all = lax.all_gather(inputs, "dp", axis=1, tiled=True)
    window_in = lax.dynamic_slice_in_dim(inputs_all, start, WINDOW, 1)

    masks = [
        window_masks(segment_ids[m], prefix_lengths[m], batch_lengths[m], start)
        for m in range(micro_count)
    ]
    biases = jnp.stack([m[0] for m in masks])
    lives = jnp.stack([m[1] for m in masks])

    own_from = quarter * group + row_count * x - start
    side_group = jnp.where(x < SIDE // 2, group + 1, group - 1)
    side_from = jnp.clip(quarter * side_group + row_count * x - start, 0, WINDOW - row_count)

    kept = [jnp.zeros((2, row_count, model), jnp.bfloat16)] * micro_count
    hidden = window_in[0]
    for tick in range(sections + micro_count - 1):
        busy = [s for s in (tick, tick - 1) if 0 <= s < sections]
        micro = jnp.clip(tick - section, 0, micro_count - 1)
        active = (section <= tick) & (section > tick - micro_count)
        partial = run_layer(
            active.astype(jnp.int32)[None], hidden, norm_gain, biases[micro], lives[micro], weights
        )
        arrived = [
            lax.ppermute(
                partial, AXES,
                everywhere(busy, groups, lambda s, a, b, k=k: (s, a + k, b - k)),
            )
            for k in range(1, SIDE)
        ]
        total = partial.astype(jnp.float32)
        for piece in arrived:
            total = total + piece.astype(jnp.float32)
        layer_out = (hidden.astype(jnp.float32) + total).astype(jnp.bfloat16)
        rows = jnp.stack([
            lax.dynamic_slice_in_dim(layer_out, own_from, row_count, 0),
            lax.dynamic_slice_in_dim(layer_out, side_from, row_count, 0),
        ])
        kept = [
            jnp.where(section == tick - m, rows, kept[m]) if 0 <= tick - m < sections else kept[m]
            for m in range(micro_count)
        ]
        onward = [s for s in busy if s + 1 < sections]
        if onward:
            hidden = lax.ppermute(
                layer_out, AXES, everywhere(onward, groups, lambda s, a, b: (s + 1, a, b))
            )
            if tick + 1 < micro_count:
                hidden = jnp.where(section == 0, window_in[tick + 1], hidden)

    stacked = jnp.stack(kept, axis=1)
    mine = lax.ppermute(
        stacked[0], AXES,
        everywhere(range(sections), groups, lambda s, a, b: (s, (a + b) % SIDE, b)),
    )

    def to_side(s, a, b):
        owner = (a + b) % SIDE + (1 if b < SIDE // 2 else -1)
        return (s, owner, b) if 0 <= owner < SIDE else None

    other = lax.ppermute(stacked[1], AXES, everywhere(range(sections), groups, to_side))
    slots = place * row_count + jnp.arange(row_count, dtype=jnp.int32)
    picked = []
    for m in range(micro_count):
        bounds = group_bounds(segment_ids[m])
        holder = jnp.sum((slots[:, None] >= bounds[None, 1:]).astype(jnp.int32), axis=1)
        picked.append(jnp.where((holder == y)[:, None], mine[m], other[m]))
    return jnp.stack(picked)[None]


def solution(mesh):
    return jax.shard_map(
        shards,
        mesh=mesh,
        in_specs=(
            P(None, "dp", None),
            P("section", None),
            P("section", None, "dp"),
            P("section", None, "dp"),
            P("section", None, "dp"),
            P("section", "dp", None),
            P(),
            P(),
            P(),
        ),
        out_specs=P("section", None, "dp", None),
        check_vma=False,
    )
```

time: 860 us -> 1160 us (1.35); the launches traced: 855 us -> 1140 us
  starting transfers between devices: 155 us -> 845 us
  waiting for transfers between devices: 586 us -> 49.8 us
  Pallas kernels: 0 us -> 84.5 us
  local copies, waits for them, and re-layouts: 41.9 us -> 92.7 us
  between operations: 13.4 us -> 35.1 us
  matrix products: 13 us -> 0 us
  other arithmetic: 43.8 us -> 31.2 us
    ppermute x17 -> x81, starting transfers between devices: 32.5 us -> 845 us  [the longest x51 617 us: shards(): lax.ppermute(partial, AXES, everywhere(busy, groups, lambda s, a, b, k=k:...]
    all_to_all x34 -> x0, waiting for transfers between devices: 326 us -> none  [the longest x17 174 us: tick_whole(): lax.all_to_all(copies, 'dp', 0, 0).reshape(seq_len, model_width)]
    ppermute x17 -> x81, waiting for transfers between devices: 208 us -> 49.7 us  [the longest x51 13.5 us: shards(): lax.ppermute(partial, AXES, everywhere(busy, groups, lambda s, a, b, k=k:...]
    all_to_all x34 -> x0, starting transfers between devices: 123 us -> none  [the longest x17 62 us: tick_whole(): lax.all_to_all(terms.astype(jnp.bfloat16).reshape(groups, row_count, mode...]
    pallas_call x0 -> x17, Pallas kernels: none -> 84.5 us  [run_layer(): pl.pallas_call(layer_kernel, out_shape=jax.ShapeDtypeStruct((rows, model)...]
    unnamed x10 -> x148, local copies, waits for them, and re-layouts: 1.3 us -> 67.6 us
    all_gather x1, waiting for transfers between devices: 50.7 us -> 0.01 us  [shards(): inputs_all = lax.all_gather(inputs, 'dp', axis=1, tiled=True)]
    reduce_sum x36 -> x2, other arithmetic: 26.2 us -> 0.17 us  [the longest x1 0.09 us: window_masks(): jnp.sum(jnp.where(member, (seg_start + prefixes)[None, :], jnp.int32(0)),...]
  transfers between devices with their start and end apart: 52 -> 82, of which waited for: 52 -> 8; matrix products, arithmetic and copies ran while one was open for 3% -> 3% of each run, Pallas kernels for 0% -> 0%
where the time goes in v2:
time: 1160 us; the launch traced here: 1140 us
  starting transfers between devices  845 us (73%)
  local copies, waits for them, and re-layouts  92.7 us (8%)
  Pallas kernels  84.5 us (7%)
  waiting for transfers between devices  49.8 us (4%)
  between operations  35.1 us (3%)
  other arithmetic  31.2 us (3%)
    ppermute x51, starting transfers between devices, shards(): lax.ppermute(partial, AXES, everywhere(busy, groups, lambda s, a, b, k=k:...  617 us
    ppermute x16, starting transfers between devices, shards(): lax.ppermute(layer_out, AXES, everywhere(onward, groups, lambda s, a, b:...  141 us
    pallas_call x17, Pallas kernels, run_layer(): pl.pallas_call(layer_kernel, out_shape=jax.ShapeDtypeStruct((rows, model)...  84.5 us
    unnamed x148, local copies, waits for them, and re-layouts  67.6 us
    ppermute x1, starting transfers between devices, shards(): lax.ppermute(stacked[1], AXES, everywhere(range(sections), groups, to_side))  30 us
    ppermute x4, starting transfers between devices, shards(): from_high = [lax.ppermute(w, AXES, behind) for w in own]  26.6 us
  transfers between devices with their start and end apart: 82, of which 8 were waited for; matrix products, arithmetic and copies ran while one was open for 3% of the time, Pallas kernels for 0%

profile of v2, /device:TPU:224, one launch (start us, length us, event | category | flops | bytes accessed | tf_op | source)
XLA Modules:
  0.0 1138.4 jit_solution(11012132254936694736)
XLA Ops:
  11.4 9.9 collective-permute-start.2
  24.3 9.7 collective-permute-done.1.refs_5_
  34.0 10.2 collective-permute-start.7
  50.7 11.8 %collective-permute-start.5 = (bf16[1024,512]{1,0:T(8,128)(2,1)}, bf16[1024,512]{1,0:T(8,128)(2,1)}, u32[]{:S(2)}, u32[]{:S(2)}) collective-permute-start(bf16[1024,512]{1,0:T(8,128)(2,1)} %bitcast.222), channel_id=1, source_target_pairs={{0,12},{1,13},{2,14},{3,15},{4,0},{5,1},{6,2},{7,3},{8,4},{9,5},{1... | collective-permute-start | bytes 3145736 | tf_op jit(solution)/shard_map/ppermute | solution.py:149
  79.7 11.2 collective-permute-done.9.refs_13_
  90.9 9.9 collective-permute-done.11.refs_15_
  202.8 212.0 %collective-permute-start.42 = (bf16[128,1024]{1,0:T(8,128)(2,1)S(1)}, bf16[128,1024]{1,0:T(8,128)(2,1)S(1)}, u32[]{:S(2)}, u32[]{:S(2)}) collective-permute-start(bf16[128,1024]{1,0:T(8,128)(2,1)S(1)} %shard_map.107), channel_id=1, source_target_pairs={{112,125},{113,126},{114,127},{115,124},{116,113},{117,114},{118,1... | collective-permute-start | bytes 786440 | tf_op jit(solution)/shard_map/ppermute | solution.py:178
  414.8 12.5 %collective-permute-start.41 = (bf16[128,1024]{1,0:T(8,128)(2,1)S(1)}, bf16[128,1024]{1,0:T(8,128)(2,1)S(1)}, u32[]{:S(2)}, u32[]{:S(2)}) collective-permute-start(bf16[128,1024]{1,0:T(8,128)(2,1)S(1)} %shard_map.107), channel_id=1, source_target_pairs={{112,122},{113,123},{114,120},{115,121},{116,126},{117,127},{118,1... | collective-permute-start | bytes 786440 | tf_op jit(solution)/shard_map/ppermute | solution.py:178
  427.3 12.5 %collective-permute-start.40 = (bf16[128,1024]{1,0:T(8,128)(2,1)S(1)}, bf16[128,1024]{1,0:T(8,128)(2,1)S(1)}, u32[]{:S(2)}, u32[]{:S(2)}) collective-permute-start(bf16[128,1024]{1,0:T(8,128)(2,1)S(1)} %shard_map.107), channel_id=1, source_target_pairs={{112,119},{113,116},{114,117},{115,118},{116,123},{117,120},{118,1... | collective-permute-start | bytes 786440 | tf_op jit(solution)/shard_map/ppermute | solution.py:178
  440.7 18.5 %collective-permute-start.43 = (bf16[128,1024]{1,0:T(8,128)(2,1)}, bf16[128,1024]{1,0:T(8,128)(2,1)S(1)}, u32[]{:S(2)}, u32[]{:S(2)}) collective-permute-start(bf16[128,1024]{1,0:T(8,128)(2,1)} %add_convert_fusion.9), channel_id=1, source_target_pairs={{112,128},{113,129},{114,130},{115,131},{116,132},{117,133},{118,1... | collective-permute-start | bytes 786440 | tf_op jit(solution)/shard_map/ppermute | solution.py:198
  468.9 23.4 %collective-permute-start.46 = (bf16[128,1024]{1,0:T(8,128)(2,1)S(1)}, bf16[128,1024]{1,0:T(8,128)(2,1)S(1)}, u32[]{:S(2)}, u32[]{:S(2)}) collective-permute-start(bf16[128,1024]{1,0:T(8,128)(2,1)S(1)} %shard_map.108), channel_id=1, source_target_pairs={{128,141},{129,142},{130,143},{131,140},{132,129},{133,130},{134,1... | collective-permute-start | bytes 786440 | tf_op jit(solution)/shard_map/ppermute | solution.py:178
  492.3 13.1 %collective-permute-start.45 = (bf16[128,1024]{1,0:T(8,128)(2,1)S(1)}, bf16[128,1024]{1,0:T(8,128)(2,1)S(1)}, u32[]{:S(2)}, u32[]{:S(2)}) collective-permute-start(bf16[128,1024]{1,0:T(8,128)(2,1)S(1)} %shard_map.108), channel_id=1, source_target_pairs={{128,138},{129,139},{130,136},{131,137},{132,142},{133,143},{134,1... | collective-permute-start | bytes 786440 | tf_op jit(solution)/shard_map/ppermute | solution.py:178
  505.5 13.1 %collective-permute-start.44 = (bf16[128,1024]{1,0:T(8,128)(2,1)S(1)}, bf16[128,1024]{1,0:T(8,128)(2,1)S(1)}, u32[]{:S(2)}, u32[]{:S(2)}) collective-permute-start(bf16[128,1024]{1,0:T(8,128)(2,1)S(1)} %shard_map.108), channel_id=1, source_target_pairs={{128,135},{129,132},{130,133},{131,134},{132,139},{133,136},{134,1... | collective-permute-start | bytes 786440 | tf_op jit(solution)/shard_map/ppermute | solution.py:178
  519.6 18.6 %collective-permute-start.47 = (bf16[128,1024]{1,0:T(8,128)(2,1)}, bf16[128,1024]{1,0:T(8,128)(2,1)S(1)}, u32[]{:S(2)}, u32[]{:S(2)}) collective-permute-start(bf16[128,1024]{1,0:T(8,128)(2,1)} %add_convert_fusion.8), channel_id=1, source_target_pairs={{128,144},{129,145},{130,146},{131,147},{132,148},{133,149},{134,1... | collective-permute-start | bytes 786440 | tf_op jit(solution)/shard_map/ppermute | solution.py:198
  546.6 23.5 %collective-permute-start.50 = (bf16[128,1024]{1,0:T(8,128)(2,1)S(1)}, bf16[128,1024]{1,0:T(8,128)(2,1)S(1)}, u32[]{:S(2)}, u32[]{:S(2)}) collective-permute-start(bf16[128,1024]{1,0:T(8,128)(2,1)S(1)} %shard_map.109), channel_id=1, source_target_pairs={{144,157},{145,158},{146,159},{147,156},{148,145},{149,146},{150,1... | collective-permute-start | bytes 786440 | tf_op jit(solution)/shard_map/ppermute | solution.py:178
  570.0 13.1 %collective-permute-start.49 = (bf16[128,1024]{1,0:T(8,128)(2,1)S(1)}, bf16[128,1024]{1,0:T(8,128)(2,1)S(1)}, u32[]{:S(2)}, u32[]{:S(2)}) collective-permute-start(bf16[128,1024]{1,0:T(8,128)(2,1)S(1)} %shard_map.109), channel_id=1, source_target_pairs={{144,154},{145,155},{146,152},{147,153},{148,158},{149,159},{150,1... | collective-permute-start | bytes 786440 | tf_op jit(solution)/shard_map/ppermute | solution.py:178
  583.2 13.1 %collective-permute-start.48 = (bf16[128,1024]{1,0:T(8,128)(2,1)S(1)}, bf16[128,1024]{1,0:T(8,128)(2,1)S(1)}, u32[]{:S(2)}, u32[]{:S(2)}) collective-permute-start(bf16[128,1024]{1,0:T(8,128)(2,1)S(1)} %shard_map.109), channel_id=1, source_target_pairs={{144,151},{145,148},{146,149},{147,150},{148,155},{149,152},{150,1... | collective-permute-start | bytes 786440 | tf_op jit(solution)/shard_map/ppermute | solution.py:178
  597.3 20.9 %collective-permute-start.51 = (bf16[128,1024]{1,0:T(8,128)(2,1)}, bf16[128,1024]{1,0:T(8,128)(2,1)S(1)}, u32[]{:S(2)}, u32[]{:S(2)}) collective-permute-start(bf16[128,1024]{1,0:T(8,128)(2,1)} %add_convert_fusion.7), channel_id=1, source_target_pairs={{144,160},{145,161},{146,162},{147,163},{148,164},{149,165},{150,1... | collective-permute-start | bytes 786440 | tf_op jit(solution)/shard_map/ppermute | solution.py:198
  628.5 21.9 %collective-permute-start.54 = (bf16[128,1024]{1,0:T(8,128)(2,1)S(1)}, bf16[128,1024]{1,0:T(8,128)(2,1)S(1)}, u32[]{:S(2)}, u32[]{:S(2)}) collective-permute-start(bf16[128,1024]{1,0:T(8,128)(2,1)S(1)} %shard_map.110), channel_id=1, source_target_pairs={{160,173},{161,174},{162,175},{163,172},{164,161},{165,162},{166,1... | collective-permute-start | bytes 786440 | tf_op jit(solution)/shard_map/ppermute | solution.py:178
  650.4 12.9 %collective-permute-start.53 = (bf16[128,1024]{1,0:T(8,128)(2,1)S(1)}, bf16[128,1024]{1,0:T(8,128)(2,1)S(1)}, u32[]{:S(2)}, u32[]{:S(2)}) collective-permute-start(bf16[128,1024]{1,0:T(8,128)(2,1)S(1)} %shard_map.110), channel_id=1, source_target_pairs={{160,170},{161,171},{162,168},{163,169},{164,174},{165,175},{166,1... | collective-permute-start | bytes 786440 | tf_op jit(solution)/shard_map/ppermute | solution.py:178
  663.3 12.9 %collective-permute-start.52 = (bf16[128,1024]{1,0:T(8,128)(2,1)S(1)}, bf16[128,1024]{1,0:T(8,128)(2,1)S(1)}, u32[]{:S(2)}, u32[]{:S(2)}) collective-permute-start(bf16[128,1024]{1,0:T(8,128)(2,1)S(1)} %shard_map.110), channel_id=1, source_target_pairs={{160,167},{161,164},{162,165},{163,166},{164,171},{165,168},{166,1... | collective-permute-start | bytes 786440 | tf_op jit(solution)/shard_map/ppermute | solution.py:178
  677.1 18.0 %collective-permute-start.55 = (bf16[128,1024]{1,0:T(8,128)(2,1)}, bf16[128,1024]{1,0:T(8,128)(2,1)S(1)}, u32[]{:S(2)}, u32[]{:S(2)}) collective-permute-start(bf16[128,1024]{1,0:T(8,128)(2,1)} %add_convert_fusion.6), channel_id=1, source_target_pairs={{160,176},{161,177},{162,178},{163,179},{164,180},{165,181},{166,1... | collective-permute-start | bytes 786440 | tf_op jit(solution)/shard_map/ppermute | solution.py:198
  703.8 24.4 %collective-permute-start.58 = (bf16[128,1024]{1,0:T(8,128)(2,1)S(1)}, bf16[128,1024]{1,0:T(8,128)(2,1)S(1)}, u32[]{:S(2)}, u32[]{:S(2)}) collective-permute-start(bf16[128,1024]{1,0:T(8,128)(2,1)S(1)} %shard_map.111), channel_id=1, source_target_pairs={{176,189},{177,190},{178,191},{179,188},{180,177},{181,178},{182,1... | collective-permute-start | bytes 786440 | tf_op jit(solution)/shard_map/ppermute | solution.py:178
  728.1 12.5 %collective-permute-start.57 = (bf16[128,1024]{1,0:T(8,128)(2,1)S(1)}, bf16[128,1024]{1,0:T(8,128)(2,1)S(1)}, u32[]{:S(2)}, u32[]{:S(2)}) collective-permute-start(bf16[128,1024]{1,0:T(8,128)(2,1)S(1)} %shard_map.111), channel_id=1, source_target_pairs={{176,186},{177,187},{178,184},{179,185},{180,190},{181,191},{182,1... | collective-permute-start | bytes 786440 | tf_op jit(solution)/shard_map/ppermute | solution.py:178
  740.6 12.5 %collective-permute-start.56 = (bf16[128,1024]{1,0:T(8,128)(2,1)S(1)}, bf16[128,1024]{1,0:T(8,128)(2,1)S(1)}, u32[]{:S(2)}, u32[]{:S(2)}) collective-permute-start(bf16[128,1024]{1,0:T(8,128)(2,1)S(1)} %shard_map.111), channel_id=1, source_target_pairs={{176,183},{177,180},{178,181},{179,182},{180,187},{181,184},{182,1... | collective-permute-start | bytes 786440 | tf_op jit(solution)/shard_map/ppermute | solution.py:178
  754.1 20.2 %collective-permute-start.59 = (bf16[128,1024]{1,0:T(8,128)(2,1)}, bf16[128,1024]{1,0:T(8,128)(2,1)S(1)}, u32[]{:S(2)}, u32[]{:S(2)}) collective-permute-start(bf16[128,1024]{1,0:T(8,128)(2,1)} %add_convert_fusion.5), channel_id=1, source_target_pairs={{176,192},{177,193},{178,194},{179,195},{180,196},{181,197},{182,1... | collective-permute-start | bytes 786440 | tf_op jit(solution)/shard_map/ppermute | solution.py:198
  783.8 23.1 %collective-permute-start.62 = (bf16[128,1024]{1,0:T(8,128)(2,1)S(1)}, bf16[128,1024]{1,0:T(8,128)(2,1)S(1)}, u32[]{:S(2)}, u32[]{:S(2)}) collective-permute-start(bf16[128,1024]{1,0:T(8,128)(2,1)S(1)} %shard_map.112), channel_id=1, source_target_pairs={{192,205},{193,206},{194,207},{195,204},{196,193},{197,194},{198,1... | collective-permute-start | bytes 786440 | tf_op jit(solution)/shard_map/ppermute | solution.py:178
  806.9 12.5 %collective-permute-start.61 = (bf16[128,1024]{1,0:T(8,128)(2,1)S(1)}, bf16[128,1024]{1,0:T(8,128)(2,1)S(1)}, u32[]{:S(2)}, u32[]{:S(2)}) collective-permute-start(bf16[128,1024]{1,0:T(8,128)(2,1)S(1)} %shard_map.112), channel_id=1, source_target_pairs={{192,202},{193,203},{194,200},{195,201},{196,206},{197,207},{198,2... | collective-permute-start | bytes 786440 | tf_op jit(solution)/shard_map/ppermute | solution.py:178
  819.4 12.5 %collective-permute-start.60 = (bf16[128,1024]{1,0:T(8,128)(2,1)S(1)}, bf16[128,1024]{1,0:T(8,128)(2,1)S(1)}, u32[]{:S(2)}, u32[]{:S(2)}) collective-permute-start(bf16[128,1024]{1,0:T(8,128)(2,1)S(1)} %shard_map.112), channel_id=1, source_target_pairs={{192,199},{193,196},{194,197},{195,198},{196,203},{197,200},{198,2... | collective-permute-start | bytes 786440 | tf_op jit(solution)/shard_map/ppermute | solution.py:178
  833.4 16.8 %collective-permute-start.63 = (bf16[128,1024]{1,0:T(8,128)(2,1)}, bf16[128,1024]{1,0:T(8,128)(2,1)S(1)}, u32[]{:S(2)}, u32[]{:S(2)}) collective-permute-start(bf16[128,1024]{1,0:T(8,128)(2,1)} %add_convert_fusion.4), channel_id=1, source_target_pairs={{192,208},{193,209},{194,210},{195,211},{196,212},{197,213},{198,2... | collective-permute-start | bytes 786440 | tf_op jit(solution)/shard_map/ppermute | solution.py:198
  865.8 4.7 shard_map.113
  870.5 19.3 %collective-permute-start.66 = (bf16[128,1024]{1,0:T(8,128)(2,1)}, bf16[128,1024]{1,0:T(8,128)(2,1)}, u32[]{:S(2)}, u32[]{:S(2)}) collective-permute-start(bf16[128,1024]{1,0:T(8,128)(2,1)} %shard_map.113), channel_id=1, source_target_pairs={{208,221},{209,222},{210,223},{211,220},{212,209},{213,210},{214,2... | collective-permute-start | bytes 786440 | tf_op jit(solution)/shard_map/ppermute | solution.py:178
  889.9 13.2 %collective-permute-start.65 = (bf16[128,1024]{1,0:T(8,128)(2,1)}, bf16[128,1024]{1,0:T(8,128)(2,1)}, u32[]{:S(2)}, u32[]{:S(2)}) collective-permute-start(bf16[128,1024]{1,0:T(8,128)(2,1)} %shard_map.113), channel_id=1, source_target_pairs={{208,218},{209,219},{210,216},{211,217},{212,222},{213,223},{214,2... | collective-permute-start | bytes 786440 | tf_op jit(solution)/shard_map/ppermute | solution.py:178
  903.1 13.2 %collective-permute-start.64 = (bf16[128,1024]{1,0:T(8,128)(2,1)}, bf16[128,1024]{1,0:T(8,128)(2,1)}, u32[]{:S(2)}, u32[]{:S(2)}) collective-permute-start(bf16[128,1024]{1,0:T(8,128)(2,1)} %shard_map.113), channel_id=1, source_target_pairs={{208,215},{209,212},{210,213},{211,214},{212,219},{213,216},{214,2... | collective-permute-start | bytes 786440 | tf_op jit(solution)/shard_map/ppermute | solution.py:178
  926.7 12.5 %collective-permute-start.67 = (bf16[128,1024]{1,0:T(8,128)(2,1)}, bf16[128,1024]{1,0:T(8,128)(2,1)S(1)}, u32[]{:S(2)}, u32[]{:S(2)}) collective-permute-start(bf16[128,1024]{1,0:T(8,128)(2,1)} %add_convert_fusion.3), channel_id=1, source_target_pairs={{208,224},{209,225},{210,226},{211,227},{212,228},{213,229},{214,2... | collective-permute-start | bytes 786440 | tf_op jit(solution)/shard_map/ppermute | solution.py:198
  949.0 11.0 shard_map.114
  960.0 12.3 %collective-permute-start.70 = (bf16[128,1024]{1,0:T(8,128)(2,1)S(1)}, bf16[128,1024]{1,0:T(8,128)(2,1)S(1)}, u32[]{:S(2)}, u32[]{:S(2)}) collective-permute-start(bf16[128,1024]{1,0:T(8,128)(2,1)S(1)} %shard_map.114), channel_id=1, source_target_pairs={{224,237},{225,238},{226,239},{227,236},{228,225},{229,226},{230,2... | collective-permute-start | bytes 786440 | tf_op jit(solution)/shard_map/ppermute | solution.py:178
  972.3 12.5 %collective-permute-start.69 = (bf16[128,1024]{1,0:T(8,128)(2,1)S(1)}, bf16[128,1024]{1,0:T(8,128)(2,1)S(1)}, u32[]{:S(2)}, u32[]{:S(2)}) collective-permute-start(bf16[128,1024]{1,0:T(8,128)(2,1)S(1)} %shard_map.114), channel_id=1, source_target_pairs={{224,234},{225,235},{226,232},{227,233},{228,238},{229,239},{230,2... | collective-permute-start | bytes 786440 | tf_op jit(solution)/shard_map/ppermute | solution.py:178
  984.8 12.5 %collective-permute-start.68 = (bf16[128,1024]{1,0:T(8,128)(2,1)S(1)}, bf16[128,1024]{1,0:T(8,128)(2,1)S(1)}, u32[]{:S(2)}, u32[]{:S(2)}) collective-permute-start(bf16[128,1024]{1,0:T(8,128)(2,1)S(1)} %shard_map.114), channel_id=1, source_target_pairs={{224,231},{225,228},{226,229},{227,230},{228,235},{229,232},{230,2... | collective-permute-start | bytes 786440 | tf_op jit(solution)/shard_map/ppermute | solution.py:178
  999.9 5.6 collective-permute-done.68
  1005.6 8.6 collective-permute-start.71
  1019.3 10.8 shard_map.115
  1030.1 11.2 collective-permute-start.74
  1041.3 12.5 %collective-permute-start.73 = (bf16[128,1024]{1,0:T(8,128)(2,1)S(1)}, bf16[128,1024]{1,0:T(8,128)(2,1)S(1)}, u32[]{:S(2)}, u32[]{:S(2)}) collective-permute-start(bf16[128,1024]{1,0:T(8,128)(2,1)S(1)} %shard_map.115), channel_id=1, source_target_pairs={{240,250},{241,251},{242,248},{243,249},{244,254},{245,255},{246,2... | collective-permute-start | bytes 786440 | tf_op jit(solution)/shard_map/ppermute | solution.py:178
  1053.8 12.5 %collective-permute-start.72 = (bf16[128,1024]{1,0:T(8,128)(2,1)S(1)}, bf16[128,1024]{1,0:T(8,128)(2,1)S(1)}, u32[]{:S(2)}, u32[]{:S(2)}) collective-permute-start(bf16[128,1024]{1,0:T(8,128)(2,1)S(1)} %shard_map.115), channel_id=1, source_target_pairs={{240,247},{241,244},{242,245},{243,246},{244,251},{245,248},{246,2... | collective-permute-start | bytes 786440 | tf_op jit(solution)/shard_map/ppermute | solution.py:178
  1068.9 7.8 collective-permute-done.72
  1088.1 30.0 %collective-permute-start.80 = (bf16[2,16,1024]{2,1,0:T(8,128)(2,1)S(1)}, bf16[2,16,1024]{2,1,0:T(8,128)(2,1)S(1)}, u32[]{:S(2)}, u32[]{:S(2)}) collective-permute-start(bf16[2,16,1024]{2,1,0:T(8,128)(2,1)S(1)} %get-tuple-element.56), channel_id=1, source_target_pairs={{0,4},{1,9},{2,6},{3,11},{4,8},{5,13},{6,10},{8,12},{11,3},{13,5},... | collective-permute-start | bytes 196616 | tf_op jit(solution)/shard_map/ppermute | solution.py:214
  1118.1 12.3 %collective-permute-start.79 = (bf16[2,16,1024]{2,1,0:T(8,128)(2,1)S(1)}, bf16[2,16,1024]{2,1,0:T(8,128)(2,1)S(1)}, u32[]{:S(2)}, u32[]{:S(2)}) collective-permute-start(bf16[2,16,1024]{2,1,0:T(8,128)(2,1)S(1)} %get-tuple-element.55), channel_id=1, source_target_pairs={{0,0},{1,5},{2,10},{3,15},{4,4},{5,9},{6,14},{7,3},{8,8},{9,13},{1... | collective-permute-start | bytes 196616 | tf_op jit(solution)/shard_map/ppermute | solution.py:205
  (368 shorter events, 223.6 us)
Async XLA Ops:
  6.5 69.3 %all-gather.2.cloned.1.call-start = ((), (), s32[]{:S(2)}) async-start(), calls=%async_computation | async-start | bytes 1114112 | tf_op jit(solution)/shard_map/all_gather | solution.py:154
  6.5 17.6 %collective-permute-start = (bf16[1024,512]{1,0:T(8,128)(2,1)}, bf16[1024,512]{1,0:T(8,128)(2,1)S(1)}, u32[]{:S(2)}, u32[]{:S(2)}) collective-permute-start(bf16[1024,512]{1,0:T(8,128)(2,1)} %bitcast.202), channel_id=1, source_target_pairs={{0,4},{1,5},{2,6},{3,7},{4,8},{5,9},{6,10},{7,11},{8,12},{9,13},{1... | collective-permute-start | bytes 3145736 | tf_op jit(solution)/shard_map/ppermute | solution.py:148
  8.1 25.9 %collective-permute-start.1 = (bf16[1024,512]{1,0:T(8,128)(2,1)}, bf16[1024,512]{1,0:T(8,128)(2,1)S(1)}, u32[]{:S(2)}, u32[]{:S(2)}) collective-permute-start(bf16[1024,512]{1,0:T(8,128)(2,1)} %bitcast.221), channel_id=1, source_target_pairs={{0,4},{1,5},{2,6},{3,7},{4,8},{5,9},{6,10},{7,11},{8,12},{9,13},{1... | collective-permute-start | bytes 3145736 | tf_op jit(solution)/shard_map/ppermute | solution.py:148
  9.7 54.4 %collective-permute-start.4 = (bf16[1024,512]{1,0:T(8,128)(2,1)}, bf16[1024,512]{1,0:T(8,128)(2,1)}, u32[]{:S(2)}, u32[]{:S(2)}) collective-permute-start(bf16[1024,512]{1,0:T(8,128)(2,1)} %bitcast.203), channel_id=1, source_target_pairs={{0,12},{1,13},{2,14},{3,15},{4,0},{5,1},{6,2},{7,3},{8,4},{9,5},{1... | collective-permute-start | bytes 3145736 | tf_op jit(solution)/shard_map/ppermute | solution.py:149
  11.4 39.3 %collective-permute-start.2 = (bf16[1024,512]{1,0:T(8,128)(2,1)}, bf16[1024,512]{1,0:T(8,128)(2,1)}, u32[]{:S(2)}, u32[]{:S(2)}) collective-permute-start(bf16[1024,512]{1,0:T(8,128)(2,1)} %bitcast.240), channel_id=1, source_target_pairs={{0,4},{1,5},{2,6},{3,7},{4,8},{5,9},{6,10},{7,11},{8,12},{9,13},{1... | collective-permute-start | bytes 3145736 | tf_op jit(solution)/shard_map/ppermute | solution.py:148
  21.2 44.3 %collective-permute-start.6 = (bf16[1024,512]{1,0:T(8,128)(2,1)}, bf16[1024,512]{1,0:T(8,128)(2,1)}, u32[]{:S(2)}, u32[]{:S(2)}) collective-permute-start(bf16[1024,512]{1,0:T(8,128)(2,1)} %bitcast.241), channel_id=1, source_target_pairs={{0,12},{1,13},{2,14},{3,15},{4,0},{5,1},{6,2},{7,3},{8,4},{9,5},{1... | collective-permute-start | bytes 3145736 | tf_op jit(solution)/shard_map/ppermute | solution.py:149
  24.2 38.4 %collective-permute-start.3 = (bf16[512,1024]{1,0:T(8,128)(2,1)}, bf16[512,1024]{1,0:T(8,128)(2,1)}, u32[]{:S(2)}, u32[]{:S(2)}) collective-permute-start(bf16[512,1024]{1,0:T(8,128)(2,1)} %bitcast.259), channel_id=1, source_target_pairs={{0,4},{1,5},{2,6},{3,7},{4,8},{5,9},{6,10},{7,11},{8,12},{9,13},{1... | collective-permute-start | bytes 3145736 | tf_op jit(solution)/shard_map/ppermute | solution.py:148
  34.0 33.3 %collective-permute-start.7 = (bf16[512,1024]{1,0:T(8,128)(2,1)}, bf16[512,1024]{1,0:T(8,128)(2,1)}, u32[]{:S(2)}, u32[]{:S(2)}) collective-permute-start(bf16[512,1024]{1,0:T(8,128)(2,1)} %bitcast.260), channel_id=1, source_target_pairs={{0,12},{1,13},{2,14},{3,15},{4,0},{5,1},{6,2},{7,3},{8,4},{9,5},{1... | collective-permute-start | bytes 3145736 | tf_op jit(solution)/shard_map/ppermute | solution.py:149
  50.7 27.7 %collective-permute-start.5 = (bf16[1024,512]{1,0:T(8,128)(2,1)}, bf16[1024,512]{1,0:T(8,128)(2,1)}, u32[]{:S(2)}, u32[]{:S(2)}) collective-permute-start(bf16[1024,512]{1,0:T(8,128)(2,1)} %bitcast.222), channel_id=1, source_target_pairs={{0,12},{1,13},{2,14},{3,15},{4,0},{5,1},{6,2},{7,3},{8,4},{9,5},{1... | collective-permute-start | bytes 3145736 | tf_op jit(solution)/shard_map/ppermute | solution.py:149
  62.5 17.2 %collective-permute-start.8 = (bf16[1024,512]{1,0:T(8,128)(2,1)S(1)}, bf16[1024,512]{1,0:T(8,128)(2,1)}, u32[]{:S(2)}, u32[]{:S(2)}) collective-permute-start(bf16[1024,512]{1,0:T(8,128)(2,1)S(1)} %collective-permute-done.refs_4_), channel_id=1, source_target_pairs={{0,4},{1,5},{2,6},{3,7},{4,8},{5,9},{6,10},{7,11},{8,12},{9,13},{1... | collective-permute-start | bytes 3145736 | tf_op jit(solution)/shard_map/ppermute | solution.py:150
  64.1 26.9 %collective-permute-start.9 = (bf16[1024,512]{1,0:T(8,128)(2,1)S(1)}, bf16[1024,512]{1,0:T(8,128)(2,1)}, u32[]{:S(2)}, u32[]{:S(2)}) collective-permute-start(bf16[1024,512]{1,0:T(8,128)(2,1)S(1)} %collective-permute-done.1.refs_5_), channel_id=1, source_target_pairs={{0,4},{1,5},{2,6},{3,7},{4,8},{5,9},{6,10},{7,11},{8,12},{9,13},{1... | collective-permute-start | bytes 3145736 | tf_op jit(solution)/shard_map/ppermute | solution.py:150
  65.6 25.3 %collective-permute-start.10 = (bf16[1024,512]{1,0:T(8,128)(2,1)}, bf16[1024,512]{1,0:T(8,128)(2,1)}, u32[]{:S(2)}, u32[]{:S(2)}) collective-permute-start(bf16[1024,512]{1,0:T(8,128)(2,1)} %collective-permute-done.6.refs_10_), channel_id=1, source_target_pairs={{0,12},{1,13},{2,14},{3,15},{4,0},{5,1},{6,2},{7,3},{8,4},{9,5},{1... | collective-permute-start | bytes 3145736 | tf_op jit(solution)/shard_map/ppermute | solution.py:151
  67.3 33.5 %collective-permute-start.11 = (bf16[512,1024]{1,0:T(8,128)(2,1)}, bf16[512,1024]{1,0:T(8,128)(2,1)}, u32[]{:S(2)}, u32[]{:S(2)}) collective-permute-start(bf16[512,1024]{1,0:T(8,128)(2,1)} %collective-permute-done.7.refs_11_), channel_id=1, source_target_pairs={{0,12},{1,13},{2,14},{3,15},{4,0},{5,1},{6,2},{7,3},{8,4},{9,5},{1... | collective-permute-start | bytes 3145736 | tf_op jit(solution)/shard_map/ppermute | solution.py:151
  202.8 237.0 %collective-permute-start.42 = (bf16[128,1024]{1,0:T(8,128)(2,1)S(1)}, bf16[128,1024]{1,0:T(8,128)(2,1)S(1)}, u32[]{:S(2)}, u32[]{:S(2)}) collective-permute-start(bf16[128,1024]{1,0:T(8,128)(2,1)S(1)} %shard_map.107), channel_id=1, source_target_pairs={{112,125},{113,126},{114,127},{115,124},{116,113},{117,114},{118,1... | collective-permute-start | bytes 786440 | tf_op jit(solution)/shard_map/ppermute | solution.py:178
  414.8 25.0 %collective-permute-start.41 = (bf16[128,1024]{1,0:T(8,128)(2,1)S(1)}, bf16[128,1024]{1,0:T(8,128)(2,1)S(1)}, u32[]{:S(2)}, u32[]{:S(2)}) collective-permute-start(bf16[128,1024]{1,0:T(8,128)(2,1)S(1)} %shard_map.107), channel_id=1, source_target_pairs={{112,122},{113,123},{114,120},{115,121},{116,126},{117,127},{118,1... | collective-permute-start | bytes 786440 | tf_op jit(solution)/shard_map/ppermute | solution.py:178
  427.3 12.5 %collective-permute-start.40 = (bf16[128,1024]{1,0:T(8,128)(2,1)S(1)}, bf16[128,1024]{1,0:T(8,128)(2,1)S(1)}, u32[]{:S(2)}, u32[]{:S(2)}) collective-permute-start(bf16[128,1024]{1,0:T(8,128)(2,1)S(1)} %shard_map.107), channel_id=1, source_target_pairs={{112,119},{113,116},{114,117},{115,118},{116,123},{117,120},{118,1... | collective-permute-start | bytes 786440 | tf_op jit(solution)/shard_map/ppermute | solution.py:178
  440.7 19.3 %collective-permute-start.43 = (bf16[128,1024]{1,0:T(8,128)(2,1)}, bf16[128,1024]{1,0:T(8,128)(2,1)S(1)}, u32[]{:S(2)}, u32[]{:S(2)}) collective-permute-start(bf16[128,1024]{1,0:T(8,128)(2,1)} %add_convert_fusion.9), channel_id=1, source_target_pairs={{112,128},{113,129},{114,130},{115,131},{116,132},{117,133},{118,1... | collective-permute-start | bytes 786440 | tf_op jit(solution)/shard_map/ppermute | solution.py:198
  468.9 49.7 %collective-permute-start.46 = (bf16[128,1024]{1,0:T(8,128)(2,1)S(1)}, bf16[128,1024]{1,0:T(8,128)(2,1)S(1)}, u32[]{:S(2)}, u32[]{:S(2)}) collective-permute-start(bf16[128,1024]{1,0:T(8,128)(2,1)S(1)} %shard_map.108), channel_id=1, source_target_pairs={{128,141},{129,142},{130,143},{131,140},{132,129},{133,130},{134,1... | collective-permute-start | bytes 786440 | tf_op jit(solution)/shard_map/ppermute | solution.py:178
  492.3 26.3 %collective-permute-start.45 = (bf16[128,1024]{1,0:T(8,128)(2,1)S(1)}, bf16[128,1024]{1,0:T(8,128)(2,1)S(1)}, u32[]{:S(2)}, u32[]{:S(2)}) collective-permute-start(bf16[128,1024]{1,0:T(8,128)(2,1)S(1)} %shard_map.108), channel_id=1, source_target_pairs={{128,138},{129,139},{130,136},{131,137},{132,142},{133,143},{134,1... | collective-permute-start | bytes 786440 | tf_op jit(solution)/shard_map/ppermute | solution.py:178
  505.5 13.2 %collective-permute-start.44 = (bf16[128,1024]{1,0:T(8,128)(2,1)S(1)}, bf16[128,1024]{1,0:T(8,128)(2,1)S(1)}, u32[]{:S(2)}, u32[]{:S(2)}) collective-permute-start(bf16[128,1024]{1,0:T(8,128)(2,1)S(1)} %shard_map.108), channel_id=1, source_target_pairs={{128,135},{129,132},{130,133},{131,134},{132,139},{133,136},{134,1... | collective-permute-start | bytes 786440 | tf_op jit(solution)/shard_map/ppermute | solution.py:178
  519.6 19.3 %collective-permute-start.47 = (bf16[128,1024]{1,0:T(8,128)(2,1)}, bf16[128,1024]{1,0:T(8,128)(2,1)S(1)}, u32[]{:S(2)}, u32[]{:S(2)}) collective-permute-start(bf16[128,1024]{1,0:T(8,128)(2,1)} %add_convert_fusion.8), channel_id=1, source_target_pairs={{128,144},{129,145},{130,146},{131,147},{132,148},{133,149},{134,1... | collective-permute-start | bytes 786440 | tf_op jit(solution)/shard_map/ppermute | solution.py:198
  546.6 49.7 %collective-permute-start.50 = (bf16[128,1024]{1,0:T(8,128)(2,1)S(1)}, bf16[128,1024]{1,0:T(8,128)(2,1)S(1)}, u32[]{:S(2)}, u32[]{:S(2)}) collective-permute-start(bf16[128,1024]{1,0:T(8,128)(2,1)S(1)} %shard_map.109), channel_id=1, source_target_pairs={{144,157},{145,158},{146,159},{147,156},{148,145},{149,146},{150,1... | collective-permute-start | bytes 786440 | tf_op jit(solution)/shard_map/ppermute | solution.py:178
  570.0 26.3 %collective-permute-start.49 = (bf16[128,1024]{1,0:T(8,128)(2,1)S(1)}, bf16[128,1024]{1,0:T(8,128)(2,1)S(1)}, u32[]{:S(2)}, u32[]{:S(2)}) collective-permute-start(bf16[128,1024]{1,0:T(8,128)(2,1)S(1)} %shard_map.109), channel_id=1, source_target_pairs={{144,154},{145,155},{146,152},{147,153},{148,158},{149,159},{150,1... | collective-permute-start | bytes 786440 | tf_op jit(solution)/shard_map/ppermute | solution.py:178
  583.2 13.2 %collective-permute-start.48 = (bf16[128,1024]{1,0:T(8,128)(2,1)S(1)}, bf16[128,1024]{1,0:T(8,128)(2,1)S(1)}, u32[]{:S(2)}, u32[]{:S(2)}) collective-permute-start(bf16[128,1024]{1,0:T(8,128)(2,1)S(1)} %shard_map.109), channel_id=1, source_target_pairs={{144,151},{145,148},{146,149},{147,150},{148,155},{149,152},{150,1... | collective-permute-start | bytes 786440 | tf_op jit(solution)/shard_map/ppermute | solution.py:178
  597.3 23.4 %collective-permute-start.51 = (bf16[128,1024]{1,0:T(8,128)(2,1)}, bf16[128,1024]{1,0:T(8,128)(2,1)S(1)}, u32[]{:S(2)}, u32[]{:S(2)}) collective-permute-start(bf16[128,1024]{1,0:T(8,128)(2,1)} %add_convert_fusion.7), channel_id=1, source_target_pairs={{144,160},{145,161},{146,162},{147,163},{148,164},{149,165},{150,1... | collective-permute-start | bytes 786440 | tf_op jit(solution)/shard_map/ppermute | solution.py:198
  628.5 47.7 %collective-permute-start.54 = (bf16[128,1024]{1,0:T(8,128)(2,1)S(1)}, bf16[128,1024]{1,0:T(8,128)(2,1)S(1)}, u32[]{:S(2)}, u32[]{:S(2)}) collective-permute-start(bf16[128,1024]{1,0:T(8,128)(2,1)S(1)} %shard_map.110), channel_id=1, source_target_pairs={{160,173},{161,174},{162,175},{163,172},{164,161},{165,162},{166,1... | collective-permute-start | bytes 786440 | tf_op jit(solution)/shard_map/ppermute | solution.py:178
  650.4 25.8 %collective-permute-start.53 = (bf16[128,1024]{1,0:T(8,128)(2,1)S(1)}, bf16[128,1024]{1,0:T(8,128)(2,1)S(1)}, u32[]{:S(2)}, u32[]{:S(2)}) collective-permute-start(bf16[128,1024]{1,0:T(8,128)(2,1)S(1)} %shard_map.110), channel_id=1, source_target_pairs={{160,170},{161,171},{162,168},{163,169},{164,174},{165,175},{166,1... | collective-permute-start | bytes 786440 | tf_op jit(solution)/shard_map/ppermute | solution.py:178
  663.3 12.9 %collective-permute-start.52 = (bf16[128,1024]{1,0:T(8,128)(2,1)S(1)}, bf16[128,1024]{1,0:T(8,128)(2,1)S(1)}, u32[]{:S(2)}, u32[]{:S(2)}) collective-permute-start(bf16[128,1024]{1,0:T(8,128)(2,1)S(1)} %shard_map.110), channel_id=1, source_target_pairs={{160,167},{161,164},{162,165},{163,166},{164,171},{165,168},{166,1... | collective-permute-start | bytes 786440 | tf_op jit(solution)/shard_map/ppermute | solution.py:178
  677.1 18.1 %collective-permute-start.55 = (bf16[128,1024]{1,0:T(8,128)(2,1)}, bf16[128,1024]{1,0:T(8,128)(2,1)S(1)}, u32[]{:S(2)}, u32[]{:S(2)}) collective-permute-start(bf16[128,1024]{1,0:T(8,128)(2,1)} %add_convert_fusion.6), channel_id=1, source_target_pairs={{160,176},{161,177},{162,178},{163,179},{164,180},{165,181},{166,1... | collective-permute-start | bytes 786440 | tf_op jit(solution)/shard_map/ppermute | solution.py:198
  703.8 49.4 %collective-permute-start.58 = (bf16[128,1024]{1,0:T(8,128)(2,1)S(1)}, bf16[128,1024]{1,0:T(8,128)(2,1)S(1)}, u32[]{:S(2)}, u32[]{:S(2)}) collective-permute-start(bf16[128,1024]{1,0:T(8,128)(2,1)S(1)} %shard_map.111), channel_id=1, source_target_pairs={{176,189},{177,190},{178,191},{179,188},{180,177},{181,178},{182,1... | collective-permute-start | bytes 786440 | tf_op jit(solution)/shard_map/ppermute | solution.py:178
  728.1 25.0 %collective-permute-start.57 = (bf16[128,1024]{1,0:T(8,128)(2,1)S(1)}, bf16[128,1024]{1,0:T(8,128)(2,1)S(1)}, u32[]{:S(2)}, u32[]{:S(2)}) collective-permute-start(bf16[128,1024]{1,0:T(8,128)(2,1)S(1)} %shard_map.111), channel_id=1, source_target_pairs={{176,186},{177,187},{178,184},{179,185},{180,190},{181,191},{182,1... | collective-permute-start | bytes 786440 | tf_op jit(solution)/shard_map/ppermute | solution.py:178
  754.1 21.0 %collective-permute-start.59 = (bf16[128,1024]{1,0:T(8,128)(2,1)}, bf16[128,1024]{1,0:T(8,128)(2,1)S(1)}, u32[]{:S(2)}, u32[]{:S(2)}) collective-permute-start(bf16[128,1024]{1,0:T(8,128)(2,1)} %add_convert_fusion.5), channel_id=1, source_target_pairs={{176,192},{177,193},{178,194},{179,195},{180,196},{181,197},{182,1... | collective-permute-start | bytes 786440 | tf_op jit(solution)/shard_map/ppermute | solution.py:198
  783.8 48.7 %collective-permute-start.62 = (bf16[128,1024]{1,0:T(8,128)(2,1)S(1)}, bf16[128,1024]{1,0:T(8,128)(2,1)S(1)}, u32[]{:S(2)}, u32[]{:S(2)}) collective-permute-start(bf16[128,1024]{1,0:T(8,128)(2,1)S(1)} %shard_map.112), channel_id=1, source_target_pairs={{192,205},{193,206},{194,207},{195,204},{196,193},{197,194},{198,1... | collective-permute-start | bytes 786440 | tf_op jit(solution)/shard_map/ppermute | solution.py:178
  806.9 25.6 %collective-permute-start.61 = (bf16[128,1024]{1,0:T(8,128)(2,1)S(1)}, bf16[128,1024]{1,0:T(8,128)(2,1)S(1)}, u32[]{:S(2)}, u32[]{:S(2)}) collective-permute-start(bf16[128,1024]{1,0:T(8,128)(2,1)S(1)} %shard_map.112), channel_id=1, source_target_pairs={{192,202},{193,203},{194,200},{195,201},{196,206},{197,207},{198,2... | collective-permute-start | bytes 786440 | tf_op jit(solution)/shard_map/ppermute | solution.py:178
  819.4 13.1 %collective-permute-start.60 = (bf16[128,1024]{1,0:T(8,128)(2,1)S(1)}, bf16[128,1024]{1,0:T(8,128)(2,1)S(1)}, u32[]{:S(2)}, u32[]{:S(2)}) collective-permute-start(bf16[128,1024]{1,0:T(8,128)(2,1)S(1)} %shard_map.112), channel_id=1, source_target_pairs={{192,199},{193,196},{194,197},{195,198},{196,203},{197,200},{198,2... | collective-permute-start | bytes 786440 | tf_op jit(solution)/shard_map/ppermute | solution.py:178
  833.4 28.7 %collective-permute-start.63 = (bf16[128,1024]{1,0:T(8,128)(2,1)}, bf16[128,1024]{1,0:T(8,128)(2,1)S(1)}, u32[]{:S(2)}, u32[]{:S(2)}) collective-permute-start(bf16[128,1024]{1,0:T(8,128)(2,1)} %add_convert_fusion.4), channel_id=1, source_target_pairs={{192,208},{193,209},{194,210},{195,211},{196,212},{197,213},{198,2... | collective-permute-start | bytes 786440 | tf_op jit(solution)/shard_map/ppermute | solution.py:198
  870.5 54.0 %collective-permute-start.66 = (bf16[128,1024]{1,0:T(8,128)(2,1)}, bf16[128,1024]{1,0:T(8,128)(2,1)}, u32[]{:S(2)}, u32[]{:S(2)}) collective-permute-start(bf16[128,1024]{1,0:T(8,128)(2,1)} %shard_map.113), channel_id=1, source_target_pairs={{208,221},{209,222},{210,223},{211,220},{212,209},{213,210},{214,2... | collective-permute-start | bytes 786440 | tf_op jit(solution)/shard_map/ppermute | solution.py:178
  889.9 34.7 %collective-permute-start.65 = (bf16[128,1024]{1,0:T(8,128)(2,1)}, bf16[128,1024]{1,0:T(8,128)(2,1)}, u32[]{:S(2)}, u32[]{:S(2)}) collective-permute-start(bf16[128,1024]{1,0:T(8,128)(2,1)} %shard_map.113), channel_id=1, source_target_pairs={{208,218},{209,219},{210,216},{211,217},{212,222},{213,223},{214,2... | collective-permute-start | bytes 786440 | tf_op jit(solution)/shard_map/ppermute | solution.py:178
  903.1 21.5 %collective-permute-start.64 = (bf16[128,1024]{1,0:T(8,128)(2,1)}, bf16[128,1024]{1,0:T(8,128)(2,1)}, u32[]{:S(2)}, u32[]{:S(2)}) collective-permute-start(bf16[128,1024]{1,0:T(8,128)(2,1)} %shard_map.113), channel_id=1, source_target_pairs={{208,215},{209,212},{210,213},{211,214},{212,219},{213,216},{214,2... | collective-permute-start | bytes 786440 | tf_op jit(solution)/shard_map/ppermute | solution.py:178
  926.7 18.6 %collective-permute-start.67 = (bf16[128,1024]{1,0:T(8,128)(2,1)}, bf16[128,1024]{1,0:T(8,128)(2,1)S(1)}, u32[]{:S(2)}, u32[]{:S(2)}) collective-permute-start(bf16[128,1024]{1,0:T(8,128)(2,1)} %add_convert_fusion.3), channel_id=1, source_target_pairs={{208,224},{209,225},{210,226},{211,227},{212,228},{213,229},{214,2... | collective-permute-start | bytes 786440 | tf_op jit(solution)/shard_map/ppermute | solution.py:198
  960.0 39.8 %collective-permute-start.70 = (bf16[128,1024]{1,0:T(8,128)(2,1)S(1)}, bf16[128,1024]{1,0:T(8,128)(2,1)S(1)}, u32[]{:S(2)}, u32[]{:S(2)}) collective-permute-start(bf16[128,1024]{1,0:T(8,128)(2,1)S(1)} %shard_map.114), channel_id=1, source_target_pairs={{224,237},{225,238},{226,239},{227,236},{228,225},{229,226},{230,2... | collective-permute-start | bytes 786440 | tf_op jit(solution)/shard_map/ppermute | solution.py:178
  972.3 27.5 %collective-permute-start.69 = (bf16[128,1024]{1,0:T(8,128)(2,1)S(1)}, bf16[128,1024]{1,0:T(8,128)(2,1)S(1)}, u32[]{:S(2)}, u32[]{:S(2)}) collective-permute-start(bf16[128,1024]{1,0:T(8,128)(2,1)S(1)} %shard_map.114), channel_id=1, source_target_pairs={{224,234},{225,235},{226,232},{227,233},{228,238},{229,239},{230,2... | collective-permute-start | bytes 786440 | tf_op jit(solution)/shard_map/ppermute | solution.py:178
  984.8 20.6 %collective-permute-start.68 = (bf16[128,1024]{1,0:T(8,128)(2,1)S(1)}, bf16[128,1024]{1,0:T(8,128)(2,1)S(1)}, u32[]{:S(2)}, u32[]{:S(2)}) collective-permute-start(bf16[128,1024]{1,0:T(8,128)(2,1)S(1)} %shard_map.114), channel_id=1, source_target_pairs={{224,231},{225,228},{226,229},{227,230},{228,235},{229,232},{230,2... | collective-permute-start | bytes 786440 | tf_op jit(solution)/shard_map/ppermute | solution.py:178
  1005.6 13.6 %collective-permute-start.71 = (bf16[128,1024]{1,0:T(8,128)(2,1)S(1)}, bf16[128,1024]{1,0:T(8,128)(2,1)S(1)}, u32[]{:S(2)}, u32[]{:S(2)}) collective-permute-start(bf16[128,1024]{1,0:T(8,128)(2,1)S(1)} %add_convert_fusion.2), channel_id=1, source_target_pairs={{224,240},{225,241},{226,242},{227,243},{228,244},{229,245},{230,2... | collective-permute-start | bytes 786440 | tf_op jit(solution)/shard_map/ppermute | solution.py:198
  1030.1 38.8 %collective-permute-start.74 = (bf16[128,1024]{1,0:T(8,128)(2,1)S(1)}, bf16[128,1024]{1,0:T(8,128)(2,1)S(1)}, u32[]{:S(2)}, u32[]{:S(2)}) collective-permute-start(bf16[128,1024]{1,0:T(8,128)(2,1)S(1)} %shard_map.115), channel_id=1, source_target_pairs={{240,253},{241,254},{242,255},{243,252},{244,241},{245,242},{246,2... | collective-permute-start | bytes 786440 | tf_op jit(solution)/shard_map/ppermute | solution.py:178
  1041.3 27.5 %collective-permute-start.73 = (bf16[128,1024]{1,0:T(8,128)(2,1)S(1)}, bf16[128,1024]{1,0:T(8,128)(2,1)S(1)}, u32[]{:S(2)}, u32[]{:S(2)}) collective-permute-start(bf16[128,1024]{1,0:T(8,128)(2,1)S(1)} %shard_map.115), channel_id=1, source_target_pairs={{240,250},{241,251},{242,248},{243,249},{244,254},{245,255},{246,2... | collective-permute-start | bytes 786440 | tf_op jit(solution)/shard_map/ppermute | solution.py:178
  1053.8 22.9 %collective-permute-start.72 = (bf16[128,1024]{1,0:T(8,128)(2,1)S(1)}, bf16[128,1024]{1,0:T(8,128)(2,1)S(1)}, u32[]{:S(2)}, u32[]{:S(2)}) collective-permute-start(bf16[128,1024]{1,0:T(8,128)(2,1)S(1)} %shard_map.115), channel_id=1, source_target_pairs={{240,247},{241,244},{242,245},{243,246},{244,251},{245,248},{246,2... | collective-permute-start | bytes 786440 | tf_op jit(solution)/shard_map/ppermute | solution.py:178
  1088.1 42.3 %collective-permute-start.80 = (bf16[2,16,1024]{2,1,0:T(8,128)(2,1)S(1)}, bf16[2,16,1024]{2,1,0:T(8,128)(2,1)S(1)}, u32[]{:S(2)}, u32[]{:S(2)}) collective-permute-start(bf16[2,16,1024]{2,1,0:T(8,128)(2,1)S(1)} %get-tuple-element.56), channel_id=1, source_target_pairs={{0,4},{1,9},{2,6},{3,11},{4,8},{5,13},{6,10},{8,12},{11,3},{13,5},... | collective-permute-start | bytes 196616 | tf_op jit(solution)/shard_map/ppermute | solution.py:214
  (108 other events, 449.9 us)
Sparse Core Ops, SparseCore 0:
  24.3 46.8 all-gather.1

commit v3 on v2

v3 whole, which is shorter than its diff:
```python
import jax
import jax.numpy as jnp
from jax import lax
from jax.experimental import pallas as pl
from jax.experimental.pallas import tpu as pltpu
from jax.sharding import PartitionSpec as P

DH = 128
SIDE = 4
WINDOW = 128
HALF = WINDOW // 2
STARTS = (0, 32, 96, 128)
AXES = ("section", "dp")


def layer_kernel(state_ref, mine_ref, other_ref, gain_ref, bias_ref, live_ref, *refs):
    own, from_x, from_y, top, bottom = refs[:5]
    keep_ref, send_ref, buf_in, buf_out, sem_in, sem_out = refs[5:]
    model, width = buf_in.shape[2:]

    def piece(j, n, row, rows):
        if j < 3:
            return (own, from_x, from_y)[j].at[pl.ds(n * model + row, rows)]
        source = top if n < 2 else bottom
        return source.at[pl.ds((n % 2) * model + row, rows)]

    def load_in(j, n):
        return pltpu.make_async_copy(piece(j, n, 0, model), buf_in.at[j, n], sem_in.at[j, n])

    def load_out(j, b):
        return pltpu.make_async_copy(
            piece(j, 3, b * width, width), buf_out.at[b, pl.ds(j * width, width)], sem_out.at[j, b]
        )

    @pl.when(state_ref[0] > 0)
    def _():
        for j in range(4):
            for n in range(3):
                load_in(j, n).start()
        for j in range(4):
            for b in range(4):
                load_out(j, b).start()

        wide = jnp.concatenate([mine_ref[...], other_ref[...]], axis=0).astype(jnp.float32)
        mean_square = jnp.mean(wide * wide, axis=-1, keepdims=True)
        normed = (wide * lax.rsqrt(mean_square + 1e-06) * gain_ref[...]).astype(jnp.bfloat16)
        bias = bias_ref[state_ref[1]]

        def project(j, n):
            load_in(j, n).wait()
            return jnp.dot(
                normed, buf_in[j, n], preferred_element_type=jnp.float32
            ).astype(jnp.bfloat16)

        context = []
        for j in range(4):
            queries, keyed, values = project(j, 0), project(j, 1), project(j, 2)
            for head in range(width // DH):
                cols = slice(head * DH, (head + 1) * DH)
                scores = lax.dot_general(
                    queries[:, cols], keyed[:, cols], (((1,), (1,)), ((), ())),
                    preferred_element_type=jnp.float32,
                ) * DH ** (-0.5) + bias
                expo = jnp.exp(scores - jnp.max(scores, axis=-1, keepdims=True))
                weight = (expo / jnp.sum(expo, axis=-1, keepdims=True)).astype(jnp.bfloat16)
                context.append(
                    jnp.dot(weight, values[:, cols], preferred_element_type=jnp.float32)
                    .astype(jnp.bfloat16)
                )
        context = jnp.concatenate(context, axis=1)
        live = live_ref[state_ref[1]] > 0.0
        for j in range(4):
            for b in range(4):
                load_out(j, b).wait()
        for b in range(4):
            term = jnp.dot(context, buf_out[b], preferred_element_type=jnp.float32)
            term = jnp.where(live, term, 0.0).astype(keep_ref.dtype)
            cols = slice(b * width, (b + 1) * width)
            keep_ref[:, cols] = term[:HALF]
            send_ref[:, cols] = term[HALF:]


def run_layer(state, mine, other, gain, biases, lives, weights):
    rows, model = mine.shape
    width = weights[0].shape[1]
    vmem = pl.BlockSpec(memory_space=pltpu.VMEM)
    anywhere = pl.BlockSpec(memory_space=pl.ANY)
    half = jax.ShapeDtypeStruct((rows, model), jnp.bfloat16)
    return pl.pallas_call(
        layer_kernel,
        out_shape=(half, half),
        in_specs=[pl.BlockSpec(memory_space=pltpu.SMEM)] + [vmem] * 5 + [anywhere] * 5,
        out_specs=(vmem, vmem),
        scratch_shapes=[
            pltpu.VMEM((4, 3, model, width), jnp.bfloat16),
            pltpu.VMEM((4, 4 * width, width), jnp.bfloat16),
            pltpu.SemaphoreType.DMA((4, 3)),
            pltpu.SemaphoreType.DMA((4, 4)),
        ],
        compiler_params=pltpu.CompilerParams(vmem_limit_bytes=56 * 1024 * 1024),
        cost_estimate=pl.CostEstimate(
            flops=2 * WINDOW * model * width * 16, bytes_accessed=16 * model * width * 2,
            transcendentals=WINDOW * WINDOW * 8,
        ),
    )(state, mine, other, gain, biases, lives, *weights)


def group_bounds(segments):
    seq_len = segments.shape[0]
    quarter = seq_len // SIDE
    position = jnp.arange(seq_len, dtype=jnp.int32)
    before = jnp.concatenate([segments[:1] - 1, segments[:-1]])
    begins = segments != before
    bounds = [jnp.int32(0)]
    for g in range(1, SIDE):
        middle = g * quarter
        low = jnp.max(jnp.where(begins & (position <= middle), position, 0))
        high = jnp.min(jnp.where(begins & (position >= middle), position, seq_len))
        bounds.append(jnp.where(middle - low <= high - middle, low, high))
    return jnp.stack(bounds)


def window_masks(segments, prefixes, length, start, core):
    seq_len = segments.shape[0]
    count_seg = prefixes.shape[0]
    position = jnp.arange(seq_len, dtype=jnp.int32)
    member = segments[:, None] == jnp.arange(count_seg, dtype=jnp.int32)[None, :]
    seg_start = jnp.min(jnp.where(member, position[:, None], jnp.int32(seq_len)), axis=0)
    prefix_end = jnp.sum(jnp.where(member, (seg_start + prefixes)[None, :], jnp.int32(0)), axis=1)

    def halves_of(array):
        return jnp.concatenate([
            lax.dynamic_slice_in_dim(array, start + HALF * core, HALF, 0),
            lax.dynamic_slice_in_dim(array, start + HALF * (1 - core), HALF, 0),
        ])

    seg_w, end_w, pos_w = halves_of(segments), halves_of(prefix_end), halves_of(position)
    key_ok = (pos_w[None, :] <= pos_w[:, None]) | (pos_w[None, :] < end_w[None, :])
    live_keys = (pos_w[None, :] < length) | (pos_w[None, :] == pos_w[:, None])
    visible = (seg_w[:, None] == seg_w[None, :]) & key_ok & live_keys
    bias = jnp.where(visible, jnp.float32(0.0), jnp.float32(-1e30))
    live = (pos_w < length).astype(jnp.float32)[:, None]
    return bias, live


def shards(
    inputs, norm_gain, w_query, w_key, w_value, w_output, segment_ids, prefix_lengths, batch_lengths
):
    section = lax.axis_index("section")
    sections = lax.axis_size("section")
    groups = lax.axis_size("dp")
    place = lax.axis_index("dp")
    micro_count, row_count, model = inputs.shape
    seq_len = row_count * groups
    quarter = seq_len // SIDE
    planes = sections // 2
    plane, core = section // 2, section % 2
    y, x = place // SIDE, place % SIDE
    group, member = (y // 2) * 2 + x // 2, (y % 2) * 2 + x % 2
    start = jnp.asarray(STARTS, jnp.int32)[group]

    def move(value, where):
        pairs = []
        for s in range(sections):
            for a in range(SIDE):
                for b in range(SIDE):
                    to, ta, tb = where(s, a, b)
                    pairs.append((
                        s * groups + a * SIDE + b,
                        (to % sections) * groups + (ta % SIDE) * SIDE + tb % SIDE,
                    ))
        return lax.ppermute(value, AXES, pairs)

    def swap_cores(value):
        return move(value, lambda s, a, b: (s ^ 1, a, b))

    def pack(h):
        width = w_query.shape[2] // 2
        cols = slice(h * width, (h + 1) * width)
        rows = w_output[0, cols]
        blocks = [rows[:, b * width : (b + 1) * width] for b in range(model // width)]
        return jnp.concatenate(
            [w_query[0, :, cols], w_key[0, :, cols], w_value[0, :, cols]] + blocks, axis=0
        )

    first = core == 0
    low, high = pack(0), pack(1)
    kept = jnp.where(first, low, high)
    got = swap_cores(jnp.where(first, high, low))
    got_gain = swap_cores(norm_gain)
    gain_a, gain_b = jnp.where(first, norm_gain, got_gain), jnp.where(first, got_gain, norm_gain)

    def gather(weights):
        def over_x(value):
            return move(value, lambda s, a, b: (s, a, b ^ 3))

        def over_y(value):
            return move(value, lambda s, a, b: (s, a ^ 3, b))

        cut = weights.shape[0] // 2
        from_x, from_y = over_x(weights), over_y(weights)
        return [weights, from_x, from_y, over_y(from_x[:cut]), over_x(from_y[cut:])]

    weights_a = gather(jnp.where(first, kept, got))
    before_b = jnp.where(first, got, kept)
    before_b, weights_a[3], weights_a[4] = lax.optimization_barrier(
        (before_b, weights_a[3], weights_a[4])
    )
    weights_b = gather(before_b)

    inputs_all = lax.all_gather(inputs, "dp", axis=1, tiled=True)
    window_mine = lax.dynamic_slice_in_dim(inputs_all, start + HALF * core, HALF, 1)
    window_other = lax.dynamic_slice_in_dim(inputs_all, start + HALF * (1 - core), HALF, 1)

    masks = [
        window_masks(segment_ids[m], prefix_lengths[m], batch_lengths[m], start, core)
        for m in range(micro_count)
    ]
    biases = jnp.stack([m[0] for m in masks])
    lives = jnp.stack([m[1] for m in masks])

    def one_layer(state, mine, other, gain, weights):
        keep, send = run_layer(state, mine, other, gain, biases, lives, weights)
        chip = (
            keep.astype(jnp.float32) + swap_cores(send).astype(jnp.float32)
        ).astype(jnp.bfloat16)
        total = mine.astype(jnp.float32) + chip.astype(jnp.float32)
        for piece in (
            move(chip, lambda s, a, b: (s, a ^ 1, b ^ 1)),
            move(chip, lambda s, a, b: (s, a ^ 1, b)),
            move(chip, lambda s, a, b: (s, a, b ^ 1)),
        ):
            total = total + piece.astype(jnp.float32)
        return total.astype(jnp.bfloat16)

    def one_round(turn, carry, last=False):
        mine, other, stash = carry
        micro = turn - plane
        active = (micro >= 0) & (micro < micro_count)
        micro = jnp.clip(micro, 0, micro_count - 1)
        state = jnp.stack([active.astype(jnp.int32), micro.astype(jnp.int32)])
        out_a = one_layer(state, mine, other, gain_a, weights_a)
        out_b = one_layer(state, out_a, swap_cores(out_a), gain_b, weights_b)
        stash = [
            [jnp.where(active & (micro == m), new, stash[n][m]) for m in range(micro_count)]
            for n, new in enumerate((out_a, out_b))
        ]
        if not last:
            onward = jnp.where(plane == planes - 1, window_mine[1], out_b)
            mine = move(onward, lambda s, a, b: (s + 2, a, b))
            other = swap_cores(mine)
        return mine, other, stash

    blank = jnp.zeros((HALF, model), jnp.bfloat16)
    carry = (window_mine[0], window_other[0], [[blank] * micro_count] * 2)
    carry = one_round(jnp.int32(0), carry)
    turns = planes + micro_count - 1
    carry = lax.fori_loop(1, turns - 1, one_round, carry)
    _, _, stash = one_round(jnp.int32(turns - 1), carry, last=True)

    stash_a, stash_b = jnp.stack(stash[0]), jnp.stack(stash[1])
    whole = jnp.concatenate(
        [jnp.where(first, stash_a, stash_b), swap_cores(jnp.where(first, stash_b, stash_a))], axis=1
    )

    def block_at(slot):
        local = (slot - start + HALF * core) % WINDOW
        return lax.dynamic_slice_in_dim(whole, local, row_count, 1)

    def owner(s, a, b, shift):
        g, t = (a // 2) * 2 + b // 2, (a % 2) * 2 + b % 2
        return (s, g + (0 if not shift else 1 if t < SIDE // 2 else -1), t)

    side = jnp.where(member < SIDE // 2, group + 1, group - 1)
    mine = move(block_at(quarter * group + row_count * member),
                lambda s, a, b: owner(s, a, b, False))
    other = move(block_at(quarter * side + row_count * member),
                 lambda s, a, b: owner(s, a, b, True))
    slots = place * row_count + jnp.arange(row_count, dtype=jnp.int32)
    picked = []
    for m in range(micro_count):
        bounds = group_bounds(segment_ids[m])
        holder = jnp.sum((slots[:, None] >= bounds[None, 1:]).astype(jnp.int32), axis=1)
        picked.append(jnp.where((holder == y)[:, None], mine[m], other[m]))
    return jnp.stack(picked)[None]


def solution(mesh):
    return jax.shard_map(
        shards,
        mesh=mesh,
        in_specs=(
            P(None, "dp", None),
            P("section", None),
            P("section", None, "dp"),
            P("section", None, "dp"),
            P("section", None, "dp"),
            P("section", "dp", None),
            P(),
            P(),
            P(),
        ),
        out_specs=P("section", None, "dp", None),
        check_vma=False,
    )
```

time: 1160 us -> 684 us (0.59); the launches traced: 1140 us -> 674 us
  starting transfers between devices: 845 us -> 156 us
  waiting for transfers between devices: 49.8 us -> 322 us
  local copies, waits for them, and re-layouts: 92.7 us -> 23.2 us
  other arithmetic: 31.2 us -> 76.6 us
  Pallas kernels: 84.5 us -> 61.9 us
    ppermute x81 -> x110, starting transfers between devices: 845 us -> 156 us  [move(): return lax.ppermute(value, AXES, pairs)]
    ppermute x81 -> x110, waiting for transfers between devices: 49.7 us -> 322 us  [move(): return lax.ppermute(value, AXES, pairs)]
    unnamed x148 -> x48, local copies, waits for them, and re-layouts: 67.6 us -> 4.13 us
    select_n x3 -> x28, other arithmetic: 1.39 us -> 46.5 us  [the longest x24 45.8 us: one_round(): jnp.where(active & (micro == m), new, stash[n][m])]
    pallas_call x17 -> x18, Pallas kernels: 84.5 us -> 61.9 us  [run_layer(): pl.pallas_call(layer_kernel, out_shape=(half, half), in_specs=[pl.BlockSp...]
    another operation x17 -> x0, local copies, waits for them, and re-layouts: 11.9 us -> none  [shards(): jnp.stack([lax.dynamic_slice_in_dim(layer_out, own_from, row_count, 0), l...]
  transfers between devices with their start and end apart: 82 -> 111, of which waited for: 8 -> 84; matrix products, arithmetic and copies ran while one was open for 3% -> 3% of each run, Pallas kernels for 0% -> 0%
where the time goes in v3:
time: 684 us; the launch traced here: 674 us
  waiting for transfers between devices  322 us (47%)
  starting transfers between devices  156 us (23%)
  other arithmetic  76.6 us (11%)
  Pallas kernels  61.9 us (9%)
  between operations  33.4 us (5%)
  local copies, waits for them, and re-layouts  23.2 us (3%)
    ppermute x110, waiting for transfers between devices, move(): return lax.ppermute(value, AXES, pairs)  322 us
    ppermute x110, starting transfers between devices, move(): return lax.ppermute(value, AXES, pairs)  156 us
    pallas_call x18, Pallas kernels, run_layer(): pl.pallas_call(layer_kernel, out_shape=(half, half), in_specs=[pl.BlockSp...  61.9 us
    select_n x24, other arithmetic, one_round(): jnp.where(active & (micro == m), new, stash[n][m])  45.8 us
    convert_element_type x18, other arithmetic, one_layer(): chip = (keep.astype(jnp.float32) + swap_cores(send).astype(jnp.float32))....  16.9 us
  transfers between devices with their start and end apart: 111, of which 84 were waited for; matrix products, arithmetic and copies ran while one was open for 3% of the time, Pallas kernels for 0%

profile of v3, /device:TPU:224, one launch (start us, length us, event | category | flops | bytes accessed | tf_op | source)
XLA Modules:
  0.0 674.2 jit_solution(14274571372220974163)
XLA Ops:
  10.0 4.1 collective-permute-done.12
  14.6 2.8 collective-permute-start.13
  17.4 3.0 collective-permute-start.14
  20.4 43.1 %collective-permute-done.13.refs_1_ = bf16[4096,256]{1,0:T(8,128)(2,1)S(1)} collective-permute-done((bf16[4096,256]{1,0:T(8,128)(2,1)S(1)}, bf16[4096,256]{1,0:T(8,128)(2,1)S(1)}, u32[]{:S(2)}, u32[]{:S(2)}) %collective-permute-start.13) | collective-permute-done | bytes 2097184 | tf_op jit(solution)/shard_map/ppermute | solution.py:172
  64.7 3.0 collective-permute-start.15
  69.3 2.8 collective-permute-start.16
  76.2 15.1 %collective-permute-done.15.refs_3_ = bf16[2048,256]{1,0:T(8,128)(2,1)S(1)} collective-permute-done((bf16[2048,256]{1,0:T(8,128)(2,1)}, bf16[2048,256]{1,0:T(8,128)(2,1)S(1)}, u32[]{:S(2)}, u32[]{:S(2)}) %collective-permute-start.15) | collective-permute-done | bytes 1048608 | tf_op jit(solution)/shard_map/ppermute | solution.py:172
  91.3 4.7 collective-permute-done.16.refs_4_
  96.0 2.8 collective-permute-start.22
  102.8 44.4 %collective-permute-done.22.refs_1_ = bf16[4096,256]{1,0:T(8,128)(2,1)} collective-permute-done((bf16[4096,256]{1,0:T(8,128)(2,1)S(1)}, bf16[4096,256]{1,0:T(8,128)(2,1)}, u32[]{:S(2)}, u32[]{:S(2)}) %collective-permute-start.22) | collective-permute-done | bytes 2097184 | tf_op jit(solution)/shard_map/ppermute | solution.py:172
  152.9 2.7 collective-permute-start.25
  162.4 3.3 collective-permute-start.20
  165.7 3.6 collective-permute-done.18
  181.4 3.2 collective-permute-start.29
  184.6 3.9 collective-permute-done.27
  193.4 9.7 %collective-permute-start.30 = (bf16[64,1024]{1,0:T(8,128)(2,1)}, bf16[64,1024]{1,0:T(8,128)(2,1)S(1)}, u32[]{:S(2)}, u32[]{:S(2)}) collective-permute-start(bf16[64,1024]{1,0:T(8,128)(2,1)} %get-tuple-element.568), channel_id=1, source_target_pairs={{0,32},{1,33},{2,34},{3,35},{4,36},{5,37},{6,38},{7,39},{8,40},{9,... | collective-permute-start | bytes 393224 | tf_op jit(solution)/shard_map/ppermute | solution.py:172
  203.1 2.9 collective-permute-done.30
  208.2 389.0 %while.24 = (s32[]{:T(128)}, bf16[64,1024]{1,0:T(8,128)(2,1)S(1)}, bf16[64,1024]{1,0:T(8,128)(2,1)}, bf16[64,1024]{1,0:T(8,128)(2,1)}, bf16[64,1024]{1,0:T(8,128...) while((s32[]{:T(128)}, bf16[64,1024]{1,0:T(8,128)(2,1)S(1)}, ...), condition=%wide.region_12.13_spmd, body=%wide.region_11.12_spmd.sunk | while | flops 2149646336 | bytes 28443520 | solution.py:258
  217.4 2.9 collective-permute-done.1
  237.7 3.5 collective-permute-done.7
  245.0 17.2 %collective-permute-start.9 = (bf16[64,1024]{1,0:T(8,128)(2,1)S(1)}, bf16[64,1024]{1,0:T(8,128)(2,1)S(1)}, u32[]{:S(2)}, u32[]{:S(2)}) collective-permute-start(bf16[64,1024]{1,0:T(8,128)(2,1)S(1)} %get-tuple-element.771), channel_id=1, source_target_pairs={{0,32},{1,33},{2,34},{3,35},{4,36},{5,37},{6,38},{7,39},{8,40},{9,... | collective-permute-start | bytes 393224 | tf_op jit(solution)/shard_map/while/body/eval_jaxpr/ppermute | solution.py:172
  274.9 3.0 collective-permute-done.1
  292.3 2.6 collective-permute-done.6
  294.9 3.5 collective-permute-done.7
  302.2 3.7 collective-permute-start.9
  318.5 3.0 collective-permute-done.1
  338.6 3.5 collective-permute-done.7
  345.8 12.4 %collective-permute-start.9 = (bf16[64,1024]{1,0:T(8,128)(2,1)S(1)}, bf16[64,1024]{1,0:T(8,128)(2,1)S(1)}, u32[]{:S(2)}, u32[]{:S(2)}) collective-permute-start(bf16[64,1024]{1,0:T(8,128)(2,1)S(1)} %get-tuple-element.771), channel_id=1, source_target_pairs={{0,32},{1,33},{2,34},{3,35},{4,36},{5,37},{6,38},{7,39},{8,40},{9,... | collective-permute-start | bytes 393224 | tf_op jit(solution)/shard_map/while/body/eval_jaxpr/ppermute | solution.py:172
  370.9 3.0 collective-permute-done.1
  391.0 3.5 collective-permute-done.7
  398.2 3.7 collective-permute-start.9
  414.5 3.0 collective-permute-done.1
  432.0 2.6 collective-permute-done.6
  434.6 3.5 collective-permute-done.7
  441.9 12.4 %collective-permute-start.9 = (bf16[64,1024]{1,0:T(8,128)(2,1)S(1)}, bf16[64,1024]{1,0:T(8,128)(2,1)S(1)}, u32[]{:S(2)}, u32[]{:S(2)}) collective-permute-start(bf16[64,1024]{1,0:T(8,128)(2,1)S(1)} %get-tuple-element.771), channel_id=1, source_target_pairs={{0,32},{1,33},{2,34},{3,35},{4,36},{5,37},{6,38},{7,39},{8,40},{9,... | collective-permute-start | bytes 393224 | tf_op jit(solution)/shard_map/while/body/eval_jaxpr/ppermute | solution.py:172
  467.0 3.0 collective-permute-done.1
  487.0 3.5 collective-permute-done.7
  494.3 3.7 collective-permute-start.9
  497.9 40.4 %collective-permute-done.9 = bf16[64,1024]{1,0:T(8,128)(2,1)S(1)} collective-permute-done((bf16[64,1024]{1,0:T(8,128)(2,1)S(1)}, bf16[64,1024]{1,0:T(8,128)(2,1)S(1)}, u32[]{:S(2)}, u32[]{:S(2)}) %collective-permute-start.9) | collective-permute-done | bytes 131104 | tf_op jit(solution)/shard_map/while/body/eval_jaxpr/ppermute | solution.py:172
  540.4 8.8 %eval_jaxpr.12 = (bf16[64,1024]{1,0:T(8,128)(2,1)}, bf16[64,1024]{1,0:T(8,128)(2,1)}) custom-call(s32[2]{0:T(128)} %pad_add_fusion.11.state_ref, bf16[64,1024]{1,0:T(8,128)(2,1)S(1)} %get-tuple-element.804.mine_ref, bf16[64,1024]{1,0:T(8,128)(2,1)} %get-tuple-element.805.other_ref, f32[1,1024]{1,0:T(1,128)S(1)} %get-tuple-element.840.gain_ref, ...), custom_call_target="tpu_custom_call" | custom-call | flops 1073741824 | bytes 8388608 | tf_op jit(solution)/shard_map/while/body/eval_jaxpr/pallas_call | solution.py:89
  555.3 3.0 collective-permute-done.1
  564.7 8.8 %eval_jaxpr.13 = (bf16[64,1024]{1,0:T(8,128)(2,1)}, bf16[64,1024]{1,0:T(8,128)(2,1)}) custom-call(s32[2]{0:T(128)} %pad_add_fusion.11.state_ref, bf16[64,1024]{1,0:T(8,128)(2,1)} %copy-done.3, bf16[64,1024]{1,0:T(8,128)(2,1)} %copy-done.9, f32[1,1024]{1,0:T(1,128)S(1)} %get-tuple-element.848.gain_ref, f32[2,128,128]{2,1,0:T(8,128)S(1)} %get-tuple-element.841.bias_ref, ...), custom_call_target="tpu_custom_call" | custom-call | flops 1073741824 | bytes 8388608 | tf_op jit(solution)/shard_map/while/body/eval_jaxpr/pallas_call | solution.py:89
  582.2 3.5 collective-permute-done.7
  589.4 6.3 collective-permute-done.9
  597.3 8.8 %shard_map.102 = (bf16[64,1024]{1,0:T(8,128)(2,1)}, bf16[64,1024]{1,0:T(8,128)(2,1)}) custom-call(s32[2]{0:T(128)} %pad_add_fusion.7.state_ref, bf16[64,1024]{1,0:T(8,128)(2,1)S(1)} %get-tuple-element.459.mine_ref, bf16[64,1024]{1,0:T(8,128)(2,1)} %get-tuple-element.460.other_ref, f32[1,1024]{1,0:T(1,128)S(1)} %get-tuple-element.905, ...), custom_call_target="tpu_custom_call" | custom-call | flops 1073741824 | bytes 8388608 | tf_op jit(solution)/shard_map/pallas_call | solution.py:89
  621.7 8.7 %shard_map.103 = (bf16[64,1024]{1,0:T(8,128)(2,1)}, bf16[64,1024]{1,0:T(8,128)(2,1)}) custom-call(s32[2]{0:T(128)} %pad_add_fusion.7.state_ref, bf16[64,1024]{1,0:T(8,128)(2,1)} %copy-done.11, bf16[64,1024]{1,0:T(8,128)(2,1)} %copy-done.17, f32[1,1024]{1,0:T(1,128)S(1)} %get-tuple-element.904, f32[2,128,128]{2,1,0:T(8,128)S(1)} %get-tuple-element.870, ...), custom_call_target="tpu_custom_call" | custom-call | flops 1073741824 | bytes 8388608 | tf_op jit(solution)/shard_map/pallas_call | solution.py:89
  655.4 4.0 collective-permute-start.43
  659.4 7.0 %collective-permute-done.43 = bf16[2,16,1024]{2,1,0:T(8,128)(2,1)S(1)} collective-permute-done((bf16[2,16,1024]{2,1,0:T(8,128)(2,1)S(1)}, bf16[2,16,1024]{2,1,0:T(8,128)(2,1)S(1)}, u32[]{:S(2)}, u32[]{:S(2)}) %collective-permute-start.43) | collective-permute-done | bytes 65568 | tf_op jit(solution)/shard_map/ppermute | solution.py:172
  (403 shorter events, 288.6 us)
Async XLA Ops:
  6.5 149.1 %all-gather.2.cloned.1.call-start = ((), (), s32[]{:S(2)}) async-start(), calls=%async_computation | async-start | bytes 1114112 | tf_op jit(solution)/shard_map/all_gather | solution.py:211
  14.6 49.0 %collective-permute-start.13 = (bf16[4096,256]{1,0:T(8,128)(2,1)S(1)}, bf16[4096,256]{1,0:T(8,128)(2,1)S(1)}, u32[]{:S(2)}, u32[]{:S(2)}) collective-permute-start(bf16[4096,256]{1,0:T(8,128)(2,1)S(1)} %get-tuple-element.789.refs_0_), channel_id=1, source_target_pairs={{0,3},{1,2},{2,1},{3,0},{4,7},{5,6},{6,5},{7,4},{8,11},{9,10},{10,... | collective-permute-start | bytes 6291464 | tf_op jit(solution)/shard_map/ppermute | solution.py:172
  17.4 50.3 %collective-permute-start.14 = (bf16[4096,256]{1,0:T(8,128)(2,1)S(1)}, bf16[4096,256]{1,0:T(8,128)(2,1)S(1)}, u32[]{:S(2)}, u32[]{:S(2)}) collective-permute-start(bf16[4096,256]{1,0:T(8,128)(2,1)S(1)} %get-tuple-element.789.refs_0_), channel_id=1, source_target_pairs={{0,12},{1,13},{2,14},{3,15},{4,8},{5,9},{6,10},{7,11},{8,4},{9,5},... | collective-permute-start | bytes 6291464 | tf_op jit(solution)/shard_map/ppermute | solution.py:172
  64.7 26.6 %collective-permute-start.15 = (bf16[2048,256]{1,0:T(8,128)(2,1)}, bf16[2048,256]{1,0:T(8,128)(2,1)S(1)}, u32[]{:S(2)}, u32[]{:S(2)}) collective-permute-start(bf16[2048,256]{1,0:T(8,128)(2,1)} %slice.180), channel_id=1, source_target_pairs={{0,12},{1,13},{2,14},{3,15},{4,8},{5,9},{6,10},{7,11},{8,4},{9,5},... | collective-permute-start | bytes 3145736 | tf_op jit(solution)/shard_map/ppermute | solution.py:172
  69.3 26.7 %collective-permute-start.16 = (bf16[2048,256]{1,0:T(8,128)(2,1)}, bf16[2048,256]{1,0:T(8,128)(2,1)}, u32[]{:S(2)}, u32[]{:S(2)}) collective-permute-start(bf16[2048,256]{1,0:T(8,128)(2,1)} %slice.181), channel_id=1, source_target_pairs={{0,3},{1,2},{2,1},{3,0},{4,7},{5,6},{6,5},{7,4},{8,11},{9,10},{10,... | collective-permute-start | bytes 3145736 | tf_op jit(solution)/shard_map/ppermute | solution.py:172
  72.1 30.6 %collective-permute-start.11 = (f32[1,1024]{1,0:T(1,128)S(1)}, f32[1,1024]{1,0:T(1,128)S(1)}, u32[]{:S(2)}, u32[]{:S(2)}) collective-permute-start(f32[1,1024]{1,0:T(1,128)S(1)} %copy-done.20), channel_id=1, source_target_pairs={{0,16},{1,17},{2,18},{3,19},{4,20},{5,21},{6,22},{7,23},{8,24},{9,... | collective-permute-start | bytes 12296 | tf_op jit(solution)/shard_map/ppermute | solution.py:172
  96.0 51.2 %collective-permute-start.22 = (bf16[4096,256]{1,0:T(8,128)(2,1)S(1)}, bf16[4096,256]{1,0:T(8,128)(2,1)}, u32[]{:S(2)}, u32[]{:S(2)}) collective-permute-start(bf16[4096,256]{1,0:T(8,128)(2,1)S(1)} %get-tuple-element.795.refs_0_), channel_id=1, source_target_pairs={{0,3},{1,2},{2,1},{3,0},{4,7},{5,6},{6,5},{7,4},{8,11},{9,10},{10,... | collective-permute-start | bytes 6291464 | tf_op jit(solution)/shard_map/ppermute | solution.py:172
  98.8 51.9 %collective-permute-start.23 = (bf16[4096,256]{1,0:T(8,128)(2,1)S(1)}, bf16[4096,256]{1,0:T(8,128)(2,1)}, u32[]{:S(2)}, u32[]{:S(2)}) collective-permute-start(bf16[4096,256]{1,0:T(8,128)(2,1)S(1)} %get-tuple-element.795.refs_0_), channel_id=1, source_target_pairs={{0,12},{1,13},{2,14},{3,15},{4,8},{5,9},{6,10},{7,11},{8,4},{9,5},... | collective-permute-start | bytes 6291464 | tf_op jit(solution)/shard_map/ppermute | solution.py:172
  149.5 24.6 %collective-permute-start.24 = (bf16[2048,256]{1,0:T(8,128)(2,1)}, bf16[2048,256]{1,0:T(8,128)(2,1)}, u32[]{:S(2)}, u32[]{:S(2)}) collective-permute-start(bf16[2048,256]{1,0:T(8,128)(2,1)} %slice.182), channel_id=1, source_target_pairs={{0,12},{1,13},{2,14},{3,15},{4,8},{5,9},{6,10},{7,11},{8,4},{9,5},... | collective-permute-start | bytes 3145736 | tf_op jit(solution)/shard_map/ppermute | solution.py:172
  152.9 23.6 %collective-permute-start.25 = (bf16[2048,256]{1,0:T(8,128)(2,1)}, bf16[2048,256]{1,0:T(8,128)(2,1)}, u32[]{:S(2)}, u32[]{:S(2)}) collective-permute-start(bf16[2048,256]{1,0:T(8,128)(2,1)} %slice.183), channel_id=1, source_target_pairs={{0,3},{1,2},{2,1},{3,0},{4,7},{5,6},{6,5},{7,4},{8,11},{9,10},{10,... | collective-permute-start | bytes 3145736 | tf_op jit(solution)/shard_map/ppermute | solution.py:172
  161.9 7.5 %collective-permute-start.18 = (bf16[64,1024]{1,0:T(8,128)(2,1)S(1)}, bf16[64,1024]{1,0:T(8,128)(2,1)}, u32[]{:S(2)}, u32[]{:S(2)}) collective-permute-start(bf16[64,1024]{1,0:T(8,128)(2,1)S(1)} %add_convert_fusion.11), channel_id=1, source_target_pairs={{0,5},{1,4},{2,7},{3,6},{4,1},{5,0},{6,3},{7,2},{8,13},{9,12},{10,... | collective-permute-start | bytes 393224 | tf_op jit(solution)/shard_map/ppermute | solution.py:172
  162.0 8.8 %collective-permute-start.19 = (bf16[64,1024]{1,0:T(8,128)(2,1)S(1)}, bf16[64,1024]{1,0:T(8,128)(2,1)}, u32[]{:S(2)}, u32[]{:S(2)}) collective-permute-start(bf16[64,1024]{1,0:T(8,128)(2,1)S(1)} %add_convert_fusion.11), channel_id=1, source_target_pairs={{0,4},{1,5},{2,6},{3,7},{4,0},{5,1},{6,2},{7,3},{8,12},{9,13},{10,... | collective-permute-start | bytes 393224 | tf_op jit(solution)/shard_map/ppermute | solution.py:172
  162.4 8.3 %collective-permute-start.20 = (bf16[64,1024]{1,0:T(8,128)(2,1)S(1)}, bf16[64,1024]{1,0:T(8,128)(2,1)}, u32[]{:S(2)}, u32[]{:S(2)}) collective-permute-start(bf16[64,1024]{1,0:T(8,128)(2,1)S(1)} %add_convert_fusion.11), channel_id=1, source_target_pairs={{0,1},{1,0},{2,3},{3,2},{4,5},{5,4},{6,7},{7,6},{8,9},{9,8},{10,11... | collective-permute-start | bytes 393224 | tf_op jit(solution)/shard_map/ppermute | solution.py:172
  181.0 7.5 %collective-permute-start.27 = (bf16[64,1024]{1,0:T(8,128)(2,1)S(1)}, bf16[64,1024]{1,0:T(8,128)(2,1)}, u32[]{:S(2)}, u32[]{:S(2)}) collective-permute-start(bf16[64,1024]{1,0:T(8,128)(2,1)S(1)} %add_convert_fusion.9), channel_id=1, source_target_pairs={{0,5},{1,4},{2,7},{3,6},{4,1},{5,0},{6,3},{7,2},{8,13},{9,12},{10,... | collective-permute-start | bytes 393224 | tf_op jit(solution)/shard_map/ppermute | solution.py:172
  181.1 8.6 %collective-permute-start.28 = (bf16[64,1024]{1,0:T(8,128)(2,1)S(1)}, bf16[64,1024]{1,0:T(8,128)(2,1)}, u32[]{:S(2)}, u32[]{:S(2)}) collective-permute-start(bf16[64,1024]{1,0:T(8,128)(2,1)S(1)} %add_convert_fusion.9), channel_id=1, source_target_pairs={{0,4},{1,5},{2,6},{3,7},{4,0},{5,1},{6,2},{7,3},{8,12},{9,13},{10,... | collective-permute-start | bytes 393224 | tf_op jit(solution)/shard_map/ppermute | solution.py:172
  181.4 8.3 %collective-permute-start.29 = (bf16[64,1024]{1,0:T(8,128)(2,1)S(1)}, bf16[64,1024]{1,0:T(8,128)(2,1)}, u32[]{:S(2)}, u32[]{:S(2)}) collective-permute-start(bf16[64,1024]{1,0:T(8,128)(2,1)S(1)} %add_convert_fusion.9), channel_id=1, source_target_pairs={{0,1},{1,0},{2,3},{3,2},{4,5},{5,4},{6,7},{7,6},{8,9},{9,8},{10,11... | collective-permute-start | bytes 393224 | tf_op jit(solution)/shard_map/ppermute | solution.py:172
  193.4 12.6 %collective-permute-start.30 = (bf16[64,1024]{1,0:T(8,128)(2,1)}, bf16[64,1024]{1,0:T(8,128)(2,1)S(1)}, u32[]{:S(2)}, u32[]{:S(2)}) collective-permute-start(bf16[64,1024]{1,0:T(8,128)(2,1)} %get-tuple-element.568), channel_id=1, source_target_pairs={{0,32},{1,33},{2,34},{3,35},{4,36},{5,37},{6,38},{7,39},{8,40},{9,... | collective-permute-start | bytes 393224 | tf_op jit(solution)/shard_map/ppermute | solution.py:172
  233.0 8.2 %collective-permute-start.7 = (bf16[64,1024]{1,0:T(8,128)(2,1)S(1)}, bf16[64,1024]{1,0:T(8,128)(2,1)}, u32[]{:S(2)}, u32[]{:S(2)}) collective-permute-start(bf16[64,1024]{1,0:T(8,128)(2,1)S(1)} %add_convert_fusion.22), channel_id=1, source_target_pairs={{0,4},{1,5},{2,6},{3,7},{4,0},{5,1},{6,2},{7,3},{8,12},{9,13},{10,... | collective-permute-start | bytes 393224 | tf_op jit(solution)/shard_map/while/body/eval_jaxpr/ppermute | solution.py:172
  233.8 7.4 %collective-permute-start.8 = (bf16[64,1024]{1,0:T(8,128)(2,1)S(1)}, bf16[64,1024]{1,0:T(8,128)(2,1)}, u32[]{:S(2)}, u32[]{:S(2)}) collective-permute-start(bf16[64,1024]{1,0:T(8,128)(2,1)S(1)} %add_convert_fusion.22), channel_id=1, source_target_pairs={{0,5},{1,4},{2,7},{3,6},{4,1},{5,0},{6,3},{7,2},{8,13},{9,12},{10,... | collective-permute-start | bytes 393224 | tf_op jit(solution)/shard_map/while/body/eval_jaxpr/ppermute | solution.py:172
  245.0 19.8 %collective-permute-start.9 = (bf16[64,1024]{1,0:T(8,128)(2,1)S(1)}, bf16[64,1024]{1,0:T(8,128)(2,1)S(1)}, u32[]{:S(2)}, u32[]{:S(2)}) collective-permute-start(bf16[64,1024]{1,0:T(8,128)(2,1)S(1)} %get-tuple-element.771), channel_id=1, source_target_pairs={{0,32},{1,33},{2,34},{3,35},{4,36},{5,37},{6,38},{7,39},{8,40},{9,... | collective-permute-start | bytes 393224 | tf_op jit(solution)/shard_map/while/body/eval_jaxpr/ppermute | solution.py:172
  272.0 8.2 %collective-permute-start.2 = (bf16[64,1024]{1,0:T(8,128)(2,1)S(1)}, bf16[64,1024]{1,0:T(8,128)(2,1)}, u32[]{:S(2)}, u32[]{:S(2)}) collective-permute-start(bf16[64,1024]{1,0:T(8,128)(2,1)S(1)} %add_convert_fusion.21), channel_id=1, source_target_pairs={{0,4},{1,5},{2,6},{3,7},{4,0},{5,1},{6,2},{7,3},{8,12},{9,13},{10,... | collective-permute-start | bytes 393224 | tf_op jit(solution)/shard_map/while/body/eval_jaxpr/ppermute | solution.py:172
  290.2 8.2 %collective-permute-start.7 = (bf16[64,1024]{1,0:T(8,128)(2,1)S(1)}, bf16[64,1024]{1,0:T(8,128)(2,1)}, u32[]{:S(2)}, u32[]{:S(2)}) collective-permute-start(bf16[64,1024]{1,0:T(8,128)(2,1)S(1)} %add_convert_fusion.22), channel_id=1, source_target_pairs={{0,4},{1,5},{2,6},{3,7},{4,0},{5,1},{6,2},{7,3},{8,12},{9,13},{10,... | collective-permute-start | bytes 393224 | tf_op jit(solution)/shard_map/while/body/eval_jaxpr/ppermute | solution.py:172
  291.0 7.4 %collective-permute-start.8 = (bf16[64,1024]{1,0:T(8,128)(2,1)S(1)}, bf16[64,1024]{1,0:T(8,128)(2,1)}, u32[]{:S(2)}, u32[]{:S(2)}) collective-permute-start(bf16[64,1024]{1,0:T(8,128)(2,1)S(1)} %add_convert_fusion.22), channel_id=1, source_target_pairs={{0,5},{1,4},{2,7},{3,6},{4,1},{5,0},{6,3},{7,2},{8,13},{9,12},{10,... | collective-permute-start | bytes 393224 | tf_op jit(solution)/shard_map/while/body/eval_jaxpr/ppermute | solution.py:172
  315.6 8.2 %collective-permute-start.2 = (bf16[64,1024]{1,0:T(8,128)(2,1)S(1)}, bf16[64,1024]{1,0:T(8,128)(2,1)}, u32[]{:S(2)}, u32[]{:S(2)}) collective-permute-start(bf16[64,1024]{1,0:T(8,128)(2,1)S(1)} %add_convert_fusion.21), channel_id=1, source_target_pairs={{0,4},{1,5},{2,6},{3,7},{4,0},{5,1},{6,2},{7,3},{8,12},{9,13},{10,... | collective-permute-start | bytes 393224 | tf_op jit(solution)/shard_map/while/body/eval_jaxpr/ppermute | solution.py:172
  333.9 8.2 %collective-permute-start.7 = (bf16[64,1024]{1,0:T(8,128)(2,1)S(1)}, bf16[64,1024]{1,0:T(8,128)(2,1)}, u32[]{:S(2)}, u32[]{:S(2)}) collective-permute-start(bf16[64,1024]{1,0:T(8,128)(2,1)S(1)} %add_convert_fusion.22), channel_id=1, source_target_pairs={{0,4},{1,5},{2,6},{3,7},{4,0},{5,1},{6,2},{7,3},{8,12},{9,13},{10,... | collective-permute-start | bytes 393224 | tf_op jit(solution)/shard_map/while/body/eval_jaxpr/ppermute | solution.py:172
  334.6 7.4 %collective-permute-start.8 = (bf16[64,1024]{1,0:T(8,128)(2,1)S(1)}, bf16[64,1024]{1,0:T(8,128)(2,1)}, u32[]{:S(2)}, u32[]{:S(2)}) collective-permute-start(bf16[64,1024]{1,0:T(8,128)(2,1)S(1)} %add_convert_fusion.22), channel_id=1, source_target_pairs={{0,5},{1,4},{2,7},{3,6},{4,1},{5,0},{6,3},{7,2},{8,13},{9,12},{10,... | collective-permute-start | bytes 393224 | tf_op jit(solution)/shard_map/while/body/eval_jaxpr/ppermute | solution.py:172
  345.8 15.0 %collective-permute-start.9 = (bf16[64,1024]{1,0:T(8,128)(2,1)S(1)}, bf16[64,1024]{1,0:T(8,128)(2,1)S(1)}, u32[]{:S(2)}, u32[]{:S(2)}) collective-permute-start(bf16[64,1024]{1,0:T(8,128)(2,1)S(1)} %get-tuple-element.771), channel_id=1, source_target_pairs={{0,32},{1,33},{2,34},{3,35},{4,36},{5,37},{6,38},{7,39},{8,40},{9,... | collective-permute-start | bytes 393224 | tf_op jit(solution)/shard_map/while/body/eval_jaxpr/ppermute | solution.py:172
  368.1 8.2 %collective-permute-start.2 = (bf16[64,1024]{1,0:T(8,128)(2,1)S(1)}, bf16[64,1024]{1,0:T(8,128)(2,1)}, u32[]{:S(2)}, u32[]{:S(2)}) collective-permute-start(bf16[64,1024]{1,0:T(8,128)(2,1)S(1)} %add_convert_fusion.21), channel_id=1, source_target_pairs={{0,4},{1,5},{2,6},{3,7},{4,0},{5,1},{6,2},{7,3},{8,12},{9,13},{10,... | collective-permute-start | bytes 393224 | tf_op jit(solution)/shard_map/while/body/eval_jaxpr/ppermute | solution.py:172
  386.3 8.2 %collective-permute-start.7 = (bf16[64,1024]{1,0:T(8,128)(2,1)S(1)}, bf16[64,1024]{1,0:T(8,128)(2,1)}, u32[]{:S(2)}, u32[]{:S(2)}) collective-permute-start(bf16[64,1024]{1,0:T(8,128)(2,1)S(1)} %add_convert_fusion.22), channel_id=1, source_target_pairs={{0,4},{1,5},{2,6},{3,7},{4,0},{5,1},{6,2},{7,3},{8,12},{9,13},{10,... | collective-permute-start | bytes 393224 | tf_op jit(solution)/shard_map/while/body/eval_jaxpr/ppermute | solution.py:172
  387.1 7.4 %collective-permute-start.8 = (bf16[64,1024]{1,0:T(8,128)(2,1)S(1)}, bf16[64,1024]{1,0:T(8,128)(2,1)}, u32[]{:S(2)}, u32[]{:S(2)}) collective-permute-start(bf16[64,1024]{1,0:T(8,128)(2,1)S(1)} %add_convert_fusion.22), channel_id=1, source_target_pairs={{0,5},{1,4},{2,7},{3,6},{4,1},{5,0},{6,3},{7,2},{8,13},{9,12},{10,... | collective-permute-start | bytes 393224 | tf_op jit(solution)/shard_map/while/body/eval_jaxpr/ppermute | solution.py:172
  411.7 8.2 %collective-permute-start.2 = (bf16[64,1024]{1,0:T(8,128)(2,1)S(1)}, bf16[64,1024]{1,0:T(8,128)(2,1)}, u32[]{:S(2)}, u32[]{:S(2)}) collective-permute-start(bf16[64,1024]{1,0:T(8,128)(2,1)S(1)} %add_convert_fusion.21), channel_id=1, source_target_pairs={{0,4},{1,5},{2,6},{3,7},{4,0},{5,1},{6,2},{7,3},{8,12},{9,13},{10,... | collective-permute-start | bytes 393224 | tf_op jit(solution)/shard_map/while/body/eval_jaxpr/ppermute | solution.py:172
  429.9 8.2 %collective-permute-start.7 = (bf16[64,1024]{1,0:T(8,128)(2,1)S(1)}, bf16[64,1024]{1,0:T(8,128)(2,1)}, u32[]{:S(2)}, u32[]{:S(2)}) collective-permute-start(bf16[64,1024]{1,0:T(8,128)(2,1)S(1)} %add_convert_fusion.22), channel_id=1, source_target_pairs={{0,4},{1,5},{2,6},{3,7},{4,0},{5,1},{6,2},{7,3},{8,12},{9,13},{10,... | collective-permute-start | bytes 393224 | tf_op jit(solution)/shard_map/while/body/eval_jaxpr/ppermute | solution.py:172
  430.7 7.4 %collective-permute-start.8 = (bf16[64,1024]{1,0:T(8,128)(2,1)S(1)}, bf16[64,1024]{1,0:T(8,128)(2,1)}, u32[]{:S(2)}, u32[]{:S(2)}) collective-permute-start(bf16[64,1024]{1,0:T(8,128)(2,1)S(1)} %add_convert_fusion.22), channel_id=1, source_target_pairs={{0,5},{1,4},{2,7},{3,6},{4,1},{5,0},{6,3},{7,2},{8,13},{9,12},{10,... | collective-permute-start | bytes 393224 | tf_op jit(solution)/shard_map/while/body/eval_jaxpr/ppermute | solution.py:172
  441.9 15.0 %collective-permute-start.9 = (bf16[64,1024]{1,0:T(8,128)(2,1)S(1)}, bf16[64,1024]{1,0:T(8,128)(2,1)S(1)}, u32[]{:S(2)}, u32[]{:S(2)}) collective-permute-start(bf16[64,1024]{1,0:T(8,128)(2,1)S(1)} %get-tuple-element.771), channel_id=1, source_target_pairs={{0,32},{1,33},{2,34},{3,35},{4,36},{5,37},{6,38},{7,39},{8,40},{9,... | collective-permute-start | bytes 393224 | tf_op jit(solution)/shard_map/while/body/eval_jaxpr/ppermute | solution.py:172
  464.1 8.2 %collective-permute-start.2 = (bf16[64,1024]{1,0:T(8,128)(2,1)S(1)}, bf16[64,1024]{1,0:T(8,128)(2,1)}, u32[]{:S(2)}, u32[]{:S(2)}) collective-permute-start(bf16[64,1024]{1,0:T(8,128)(2,1)S(1)} %add_convert_fusion.21), channel_id=1, source_target_pairs={{0,4},{1,5},{2,6},{3,7},{4,0},{5,1},{6,2},{7,3},{8,12},{9,13},{10,... | collective-permute-start | bytes 393224 | tf_op jit(solution)/shard_map/while/body/eval_jaxpr/ppermute | solution.py:172
  482.3 8.2 %collective-permute-start.7 = (bf16[64,1024]{1,0:T(8,128)(2,1)S(1)}, bf16[64,1024]{1,0:T(8,128)(2,1)}, u32[]{:S(2)}, u32[]{:S(2)}) collective-permute-start(bf16[64,1024]{1,0:T(8,128)(2,1)S(1)} %add_convert_fusion.22), channel_id=1, source_target_pairs={{0,4},{1,5},{2,6},{3,7},{4,0},{5,1},{6,2},{7,3},{8,12},{9,13},{10,... | collective-permute-start | bytes 393224 | tf_op jit(solution)/shard_map/while/body/eval_jaxpr/ppermute | solution.py:172
  483.1 7.4 %collective-permute-start.8 = (bf16[64,1024]{1,0:T(8,128)(2,1)S(1)}, bf16[64,1024]{1,0:T(8,128)(2,1)}, u32[]{:S(2)}, u32[]{:S(2)}) collective-permute-start(bf16[64,1024]{1,0:T(8,128)(2,1)S(1)} %add_convert_fusion.22), channel_id=1, source_target_pairs={{0,5},{1,4},{2,7},{3,6},{4,1},{5,0},{6,3},{7,2},{8,13},{9,12},{10,... | collective-permute-start | bytes 393224 | tf_op jit(solution)/shard_map/while/body/eval_jaxpr/ppermute | solution.py:172
  494.3 44.0 %collective-permute-start.9 = (bf16[64,1024]{1,0:T(8,128)(2,1)S(1)}, bf16[64,1024]{1,0:T(8,128)(2,1)S(1)}, u32[]{:S(2)}, u32[]{:S(2)}) collective-permute-start(bf16[64,1024]{1,0:T(8,128)(2,1)S(1)} %get-tuple-element.771), channel_id=1, source_target_pairs={{0,32},{1,33},{2,34},{3,35},{4,36},{5,37},{6,38},{7,39},{8,40},{9,... | collective-permute-start | bytes 393224 | tf_op jit(solution)/shard_map/while/body/eval_jaxpr/ppermute | solution.py:172
  552.5 8.2 %collective-permute-start.2 = (bf16[64,1024]{1,0:T(8,128)(2,1)S(1)}, bf16[64,1024]{1,0:T(8,128)(2,1)}, u32[]{:S(2)}, u32[]{:S(2)}) collective-permute-start(bf16[64,1024]{1,0:T(8,128)(2,1)S(1)} %add_convert_fusion.21), channel_id=1, source_target_pairs={{0,4},{1,5},{2,6},{3,7},{4,0},{5,1},{6,2},{7,3},{8,12},{9,13},{10,... | collective-permute-start | bytes 393224 | tf_op jit(solution)/shard_map/while/body/eval_jaxpr/ppermute | solution.py:172
  577.5 8.2 %collective-permute-start.7 = (bf16[64,1024]{1,0:T(8,128)(2,1)S(1)}, bf16[64,1024]{1,0:T(8,128)(2,1)}, u32[]{:S(2)}, u32[]{:S(2)}) collective-permute-start(bf16[64,1024]{1,0:T(8,128)(2,1)S(1)} %add_convert_fusion.22), channel_id=1, source_target_pairs={{0,4},{1,5},{2,6},{3,7},{4,0},{5,1},{6,2},{7,3},{8,12},{9,13},{10,... | collective-permute-start | bytes 393224 | tf_op jit(solution)/shard_map/while/body/eval_jaxpr/ppermute | solution.py:172
  578.0 7.6 %collective-permute-start.8 = (bf16[64,1024]{1,0:T(8,128)(2,1)S(1)}, bf16[64,1024]{1,0:T(8,128)(2,1)}, u32[]{:S(2)}, u32[]{:S(2)}) collective-permute-start(bf16[64,1024]{1,0:T(8,128)(2,1)S(1)} %add_convert_fusion.22), channel_id=1, source_target_pairs={{0,5},{1,4},{2,7},{3,6},{4,1},{5,0},{6,3},{7,2},{8,13},{9,12},{10,... | collective-permute-start | bytes 393224 | tf_op jit(solution)/shard_map/while/body/eval_jaxpr/ppermute | solution.py:172
  608.6 7.3 %collective-permute-start.33 = (bf16[64,1024]{1,0:T(8,128)(2,1)S(1)}, bf16[64,1024]{1,0:T(8,128)(2,1)S(1)}, u32[]{:S(2)}, u32[]{:S(2)}) collective-permute-start(bf16[64,1024]{1,0:T(8,128)(2,1)S(1)} %add_convert_fusion.7), channel_id=1, source_target_pairs={{0,5},{1,4},{2,7},{3,6},{4,1},{5,0},{6,3},{7,2},{8,13},{9,12},{10,... | collective-permute-start | bytes 393224 | tf_op jit(solution)/shard_map/ppermute | solution.py:172
  610.2 7.8 %collective-permute-start.34 = (bf16[64,1024]{1,0:T(8,128)(2,1)S(1)}, bf16[64,1024]{1,0:T(8,128)(2,1)S(1)}, u32[]{:S(2)}, u32[]{:S(2)}) collective-permute-start(bf16[64,1024]{1,0:T(8,128)(2,1)S(1)} %add_convert_fusion.7), channel_id=1, source_target_pairs={{0,4},{1,5},{2,6},{3,7},{4,0},{5,1},{6,2},{7,3},{8,12},{9,13},{10,... | collective-permute-start | bytes 393224 | tf_op jit(solution)/shard_map/ppermute | solution.py:172
  630.4 9.0 %collective-permute-start.37 = (bf16[64,1024]{1,0:T(8,128)(2,1)}, bf16[64,1024]{1,0:T(8,128)(2,1)S(1)}, u32[]{:S(2)}, u32[]{:S(2)}) collective-permute-start(bf16[64,1024]{1,0:T(8,128)(2,1)} %get-tuple-element.466), channel_id=1, source_target_pairs={{0,16},{1,17},{2,18},{3,19},{4,20},{5,21},{6,22},{7,23},{8,24},{9,... | collective-permute-start | bytes 393224 | tf_op jit(solution)/shard_map/ppermute | solution.py:172
  640.4 11.2 %collective-permute-start.38 = (bf16[64,1024]{1,0:T(8,128)(2,1)S(1)}, bf16[64,1024]{1,0:T(8,128)(2,1)S(1)}, u32[]{:S(2)}, u32[]{:S(2)}) collective-permute-start(bf16[64,1024]{1,0:T(8,128)(2,1)S(1)} %add_convert_fusion.5), channel_id=1, source_target_pairs={{0,5},{1,4},{2,7},{3,6},{4,1},{5,0},{6,3},{7,2},{8,13},{9,12},{10,... | collective-permute-start | bytes 393224 | tf_op jit(solution)/shard_map/ppermute | solution.py:172
  642.0 9.6 %collective-permute-start.39 = (bf16[64,1024]{1,0:T(8,128)(2,1)S(1)}, bf16[64,1024]{1,0:T(8,128)(2,1)S(1)}, u32[]{:S(2)}, u32[]{:S(2)}) collective-permute-start(bf16[64,1024]{1,0:T(8,128)(2,1)S(1)} %add_convert_fusion.5), channel_id=1, source_target_pairs={{0,4},{1,5},{2,6},{3,7},{4,0},{5,1},{6,2},{7,3},{8,12},{9,13},{10,... | collective-permute-start | bytes 393224 | tf_op jit(solution)/shard_map/ppermute | solution.py:172
  642.6 9.0 %collective-permute-start.40 = (bf16[64,1024]{1,0:T(8,128)(2,1)S(1)}, bf16[64,1024]{1,0:T(8,128)(2,1)S(1)}, u32[]{:S(2)}, u32[]{:S(2)}) collective-permute-start(bf16[64,1024]{1,0:T(8,128)(2,1)S(1)} %add_convert_fusion.5), channel_id=1, source_target_pairs={{0,1},{1,0},{2,3},{3,2},{4,5},{5,4},{6,7},{7,6},{8,9},{9,8},{10,11... | collective-permute-start | bytes 393224 | tf_op jit(solution)/shard_map/ppermute | solution.py:172
  655.4 11.1 %collective-permute-start.43 = (bf16[2,16,1024]{2,1,0:T(8,128)(2,1)S(1)}, bf16[2,16,1024]{2,1,0:T(8,128)(2,1)S(1)}, u32[]{:S(2)}, u32[]{:S(2)}) collective-permute-start(bf16[2,16,1024]{2,1,0:T(8,128)(2,1)S(1)} %get-tuple-element.561), channel_id=1, source_target_pairs={{0,4},{1,5},{2,8},{3,9},{4,14},{5,15},{6,2},{7,3},{8,12},{9,13},{1... | collective-permute-start | bytes 196616 | tf_op jit(solution)/shard_map/ppermute | solution.py:172
  (111 other events, 856.0 us)
Sparse Core Ops, SparseCore 0:
  72.2 45.9 all-gather.1

commit v4 on v3

v4 whole, which is shorter than its diff:
```python
import functools

import jax
import jax.numpy as jnp
from jax import lax
from jax.experimental import pallas as pl
from jax.experimental.pallas import tpu as pltpu
from jax.sharding import PartitionSpec as P

DH = 128
SIDE = 4
WINDOW = 128
HALF = WINDOW // 2
STARTS = (0, 32, 96, 128)
AXES = ("section", "dp")


def layer_kernel(turn, place_ref, mine_ref, other_ref, gain_ref, bias_ref, *refs):
    own, from_x, from_y, top, bottom = refs[:5]
    keep_ref, send_ref = refs[5:]
    model, width = mine_ref.shape[1], own.shape[1]
    plane, core, start = place_ref[0], place_ref[1], place_ref[2]
    micro = turn - plane

    def weight(j, n, row, rows):
        if j < 3:
            return (own, from_x, from_y)[j][pl.ds(n * model + row, rows)]
        return (top if n < 2 else bottom)[pl.ds((n % 2) * model + row, rows)]

    @pl.when((micro >= 0) & (micro < bias_ref.shape[0]))
    def _():
        wide = jnp.concatenate([mine_ref[...], other_ref[...]], axis=0).astype(jnp.float32)
        mean_square = jnp.mean(wide * wide, axis=-1, keepdims=True)
        normed = (wide * lax.rsqrt(mean_square + 1e-06) * gain_ref[...]).astype(jnp.bfloat16)
        bias = bias_ref[micro]
        context = []
        for j in range(4):
            queries, keyed, values = [
                jnp.dot(
                    normed, weight(j, n, 0, model), preferred_element_type=jnp.float32
                ).astype(jnp.bfloat16)
                for n in range(3)
            ]
            for head in range(width // DH):
                cols = slice(head * DH, (head + 1) * DH)
                scores = lax.dot_general(
                    queries[:, cols], keyed[:, cols], (((1,), (1,)), ((), ())),
                    preferred_element_type=jnp.float32,
                ) * DH ** (-0.5) + bias
                expo = jnp.exp(scores - jnp.max(scores, axis=-1, keepdims=True))
                share = (expo / jnp.sum(expo, axis=-1, keepdims=True)).astype(jnp.bfloat16)
                context.append(
                    jnp.dot(share, values[:, cols], preferred_element_type=jnp.float32)
                    .astype(jnp.bfloat16)
                )
        heads = width // DH
        context = [
            jnp.concatenate(context[j * heads : (j + 1) * heads], axis=1) for j in range(4)
        ]
        row = lax.broadcasted_iota(jnp.int32, (WINDOW, width), 0)
        slot = start + (row + HALF * core) % WINDOW
        live = slot < place_ref[3 + micro]
        for b in range(model // width):
            term = sum(
                jnp.dot(
                    context[j], weight(j, 3, b * width, width), preferred_element_type=jnp.float32
                )
                for j in range(4)
            )
            term = jnp.where(live, term, 0.0).astype(keep_ref.dtype)
            cols = slice(b * width, (b + 1) * width)
            keep_ref[:, cols] = term[:HALF]
            send_ref[:, cols] = term[HALF:]


def run_layer(turn, place, mine, other, gain, biases, weights):
    rows, model = mine.shape
    width = weights[0].shape[1]
    vmem = pl.BlockSpec(memory_space=pltpu.VMEM)
    half = jax.ShapeDtypeStruct((rows, model), jnp.bfloat16)
    resident = [pltpu.with_memory_space_constraint(v, pltpu.VMEM) for v in [biases] + weights]
    return pl.pallas_call(
        functools.partial(layer_kernel, turn),
        out_shape=(half, half),
        in_specs=[pl.BlockSpec(memory_space=pltpu.SMEM)] + [vmem] * 9,
        out_specs=(vmem, vmem),
        compiler_params=pltpu.CompilerParams(vmem_limit_bytes=16 * 1024 * 1024),
        cost_estimate=pl.CostEstimate(
            flops=2 * WINDOW * model * width * 16, bytes_accessed=16 * model * width * 2,
            transcendentals=WINDOW * WINDOW * 8,
        ),
    )(place, mine, other, gain, *resident)


def group_bounds(segments):
    seq_len = segments.shape[0]
    quarter = seq_len // SIDE
    position = jnp.arange(seq_len, dtype=jnp.int32)
    before = jnp.concatenate([segments[:1] - 1, segments[:-1]])
    begins = segments != before
    bounds = [jnp.int32(0)]
    for g in range(1, SIDE):
        middle = g * quarter
        low = jnp.max(jnp.where(begins & (position <= middle), position, 0))
        high = jnp.min(jnp.where(begins & (position >= middle), position, seq_len))
        bounds.append(jnp.where(middle - low <= high - middle, low, high))
    return jnp.stack(bounds)


def window_masks(segments, prefixes, length, start, core):
    seq_len = segments.shape[0]
    count_seg = prefixes.shape[0]
    position = jnp.arange(seq_len, dtype=jnp.int32)
    member = segments[:, None] == jnp.arange(count_seg, dtype=jnp.int32)[None, :]
    seg_start = jnp.min(jnp.where(member, position[:, None], jnp.int32(seq_len)), axis=0)
    prefix_end = jnp.sum(jnp.where(member, (seg_start + prefixes)[None, :], jnp.int32(0)), axis=1)

    def halves_of(array):
        return jnp.concatenate([
            lax.dynamic_slice_in_dim(array, start + HALF * core, HALF, 0),
            lax.dynamic_slice_in_dim(array, start + HALF * (1 - core), HALF, 0),
        ])

    seg_w, end_w, pos_w = halves_of(segments), halves_of(prefix_end), halves_of(position)
    key_ok = (pos_w[None, :] <= pos_w[:, None]) | (pos_w[None, :] < end_w[None, :])
    live_keys = (pos_w[None, :] < length) | (pos_w[None, :] == pos_w[:, None])
    visible = (seg_w[:, None] == seg_w[None, :]) & key_ok & live_keys
    return jnp.where(visible, jnp.float32(0.0), jnp.float32(-1e30))


def shards(
    inputs, norm_gain, w_query, w_key, w_value, w_output, segment_ids, prefix_lengths, batch_lengths
):
    section = lax.axis_index("section")
    sections = lax.axis_size("section")
    groups = lax.axis_size("dp")
    place = lax.axis_index("dp")
    micro_count, row_count, model = inputs.shape
    seq_len = row_count * groups
    quarter = seq_len // SIDE
    planes = sections // 2
    plane, core = section // 2, section % 2
    y, x = place // SIDE, place % SIDE
    group, member = (y // 2) * 2 + x // 2, (y % 2) * 2 + x % 2
    start = jnp.asarray(STARTS, jnp.int32)[group]

    def move(value, where):
        pairs = []
        for s in range(sections):
            for a in range(SIDE):
                for b in range(SIDE):
                    to, ta, tb = where(s, a, b)
                    pairs.append((
                        s * groups + a * SIDE + b,
                        (to % sections) * groups + (ta % SIDE) * SIDE + tb % SIDE,
                    ))
        return lax.ppermute(value, AXES, pairs)

    def swap_cores(value):
        return move(value, lambda s, a, b: (s ^ 1, a, b))

    def pack(h):
        width = w_query.shape[2] // 2
        cols = slice(h * width, (h + 1) * width)
        rows = w_output[0, cols]
        blocks = [rows[:, b * width : (b + 1) * width] for b in range(model // width)]
        return jnp.concatenate(
            [w_query[0, :, cols], w_key[0, :, cols], w_value[0, :, cols]] + blocks, axis=0
        )

    first = core == 0
    low, high = pack(0), pack(1)
    kept = jnp.where(first, low, high)
    got = swap_cores(jnp.where(first, high, low))
    got_gain = swap_cores(norm_gain)
    gain_a, gain_b = jnp.where(first, norm_gain, got_gain), jnp.where(first, got_gain, norm_gain)

    def over_x(value):
        return move(value, lambda s, a, b: (s, a, b ^ 3))

    def over_y(value):
        return move(value, lambda s, a, b: (s, a ^ 3, b))

    cut = low.shape[0] // 2
    own_a, own_b = jnp.where(first, kept, got), jnp.where(first, got, kept)
    x_a, y_a = over_x(own_a), over_y(own_a)
    weights_a = [own_a, x_a, y_a, over_y(x_a[:cut]), over_x(y_a[cut:])]
    own_b, weights_a[3], weights_a[4] = lax.optimization_barrier(
        (own_b, weights_a[3], weights_a[4])
    )
    x_b, y_b = over_x(own_b), over_y(own_b)

    inputs_all = lax.all_gather(inputs, "dp", axis=1, tiled=True)
    window_mine = lax.dynamic_slice_in_dim(inputs_all, start + HALF * core, HALF, 1)
    window_other = lax.dynamic_slice_in_dim(inputs_all, start + HALF * (1 - core), HALF, 1)

    biases = jnp.stack([
        window_masks(segment_ids[m], prefix_lengths[m], batch_lengths[m], start, core)
        for m in range(micro_count)
    ])
    where_am_i = jnp.concatenate([
        jnp.stack([plane, core, start]).astype(jnp.int32), batch_lengths.astype(jnp.int32)
    ])

    def one_layer(turn, mine, other, gain, weights):
        keep, send = run_layer(turn, where_am_i, mine, other, gain, biases, weights)
        chip = (
            keep.astype(jnp.float32) + swap_cores(send).astype(jnp.float32)
        ).astype(jnp.bfloat16)
        total = mine.astype(jnp.float32) + chip.astype(jnp.float32)
        for piece in (
            move(chip, lambda s, a, b: (s, a ^ 1, b ^ 1)),
            move(chip, lambda s, a, b: (s, a ^ 1, b)),
            move(chip, lambda s, a, b: (s, a, b ^ 1)),
        ):
            total = total + piece.astype(jnp.float32)
        return total.astype(jnp.bfloat16)

    side = jnp.where(member < SIDE // 2, group + 1, group - 1)
    own_at = (quarter * group + row_count * member - start) % WINDOW
    side_at = (quarter * side + row_count * member - start) % WINDOW

    def blocks(rows):
        return jnp.stack([
            lax.dynamic_slice_in_dim(rows, at % HALF, row_count, 0) for at in (own_at, side_at)
        ])

    blank = jnp.zeros((2, row_count, model), jnp.bfloat16)
    stash = [[blank] * micro_count, [blank] * micro_count]

    def keep_blocks(layer, turn, rows):
        found = blocks(rows)
        for m in range(micro_count):
            if 0 <= turn - m < planes:
                stash[layer][m] = jnp.where(plane == turn - m, found, stash[layer][m])

    mine, other = window_mine[0], window_other[0]
    weights_b = None
    turns = planes + micro_count - 1
    for turn in range(turns):
        out_a = one_layer(turn, mine, other, gain_a, weights_a)
        if weights_b is None:
            x_b, y_b, out_a = lax.optimization_barrier((x_b, y_b, out_a))
            weights_b = [own_b, x_b, y_b, over_y(x_b[:cut]), over_x(y_b[cut:])]
        out_b = one_layer(turn, out_a, swap_cores(out_a), gain_b, weights_b)
        if turn < turns - 1:
            onward = (
                jnp.where(plane == planes - 1, window_mine[1], out_b) if turn == 0 else out_b
            )
            mine = move(onward, lambda s, a, b: (s + 2, a, b))
            other = swap_cores(mine)
        keep_blocks(0, turn, out_a)
        keep_blocks(1, turn, out_b)

    stash_a, stash_b = [jnp.stack(rows, axis=1) for rows in stash]
    here = jnp.where(first, stash_a, stash_b)
    there = swap_cores(jnp.where(first, stash_b, stash_a))

    def owner(s, a, b, shift):
        g, t = (a // 2) * 2 + b // 2, (a % 2) * 2 + b % 2
        return (s, g + (0 if not shift else 1 if t < SIDE // 2 else -1), t)

    mine = move(jnp.where(own_at // HALF == core, here[0], there[0]),
                lambda s, a, b: owner(s, a, b, False))
    other = move(jnp.where(side_at // HALF == core, here[1], there[1]),
                 lambda s, a, b: owner(s, a, b, True))
    slots = place * row_count + jnp.arange(row_count, dtype=jnp.int32)
    picked = []
    for m in range(micro_count):
        bounds = group_bounds(segment_ids[m])
        holder = jnp.sum((slots[:, None] >= bounds[None, 1:]).astype(jnp.int32), axis=1)
        picked.append(jnp.where((holder == y)[:, None], mine[m], other[m]))
    return jnp.stack(picked)[None]


def solution(mesh):
    return jax.shard_map(
        shards,
        mesh=mesh,
        in_specs=(
            P(None, "dp", None),
            P("section", None),
            P("section", None, "dp"),
            P("section", None, "dp"),
            P("section", None, "dp"),
            P("section", "dp", None),
            P(),
            P(),
            P(),
        ),
        out_specs=P("section", None, "dp", None),
        check_vma=False,
    )
```

time: 684 us -> 596 us (0.87)
  other arithmetic: 76.6 us -> 16 us
  starting transfers between devices: 156 us -> 129 us
    select_n x27 -> x9, other arithmetic: 46.4 us -> 3.94 us  [the longest x1 1.86 us: shards(): jnp.where(plane == planes - 1, window_mine[1], out_b)]
    ppermute x110, starting transfers between devices: 156 us -> 129 us  [move(): return lax.ppermute(value, AXES, pairs)]
    convert_element_type x18, other arithmetic: 16.9 us -> 2.28 us  [one_layer(): chip = (keep.astype(jnp.float32) + swap_cores(send).astype(jnp.float32))....]
    another operation x14 -> x1, other arithmetic: 8.15 us -> 0.01 us  [shards(): jnp.stack([window_masks(segment_ids[m], prefix_lengths[m], batch_lengths[...]
  transfers between devices with their start and end apart: 111 -> 111, of which waited for: 84 -> 89; matrix products, arithmetic and copies ran while one was open for 3% -> 3% of each run, Pallas kernels for 0% -> 1%
where the time goes in v4:
time: 596 us; the launch traced here: 587 us
  waiting for transfers between devices  321 us (54%)
  starting transfers between devices  129 us (22%)
  Pallas kernels  67.5 us (11%)
  between operations  34 us (6%)
  local copies, waits for them, and re-layouts  19.2 us (3%)
  other arithmetic  16 us (3%)
    ppermute x110, waiting for transfers between devices, move(): return lax.ppermute(value, AXES, pairs)  321 us
    ppermute x110, starting transfers between devices, move(): return lax.ppermute(value, AXES, pairs)  129 us
    pallas_call x18, Pallas kernels, run_layer(): pl.pallas_call(functools.partial(layer_kernel, turn), out_shape=(half, ha...  67.5 us
  transfers between devices with their start and end apart: 111, of which 89 were waited for; matrix products, arithmetic and copies ran while one was open for 3% of the time, Pallas kernels for 1%

profile of v4, /device:TPU:224, one launch (start us, length us, event | category | flops | bytes accessed | tf_op | source)
XLA Modules:
  0.0 587.0 jit_solution(15702700220794737732)
XLA Ops:
  10.0 4.1 collective-permute-done
  18.6 3.0 collective-permute-start.3
  21.8 48.5 %collective-permute-done.1.refs_1_ = bf16[4096,256]{1,0:T(8,128)(2,1)} collective-permute-done((bf16[4096,256]{1,0:T(8,128)(2,1)}, bf16[4096,256]{1,0:T(8,128)(2,1)}, u32[]{:S(2)}, u32[]{:S(2)}) %collective-permute-start.1) | collective-permute-done | bytes 2097184 | tf_op jit(solution)/shard_map/ppermute | solution.py:157
  72.6 3.0 collective-permute-start.2
  83.4 15.0 %collective-permute-done.2.refs_3_ = bf16[2048,256]{1,0:T(8,128)(2,1)S(1)} collective-permute-done((bf16[2048,256]{1,0:T(8,128)(2,1)}, bf16[2048,256]{1,0:T(8,128)(2,1)S(1)}, u32[]{:S(2)}, u32[]{:S(2)}) %collective-permute-start.2) | collective-permute-done | bytes 1048608 | tf_op jit(solution)/shard_map/ppermute | solution.py:157
  98.4 5.1 collective-permute-done.4.refs_4_
  110.5 3.1 shard_map.100
  115.5 3.2 collective-permute-start.9
  124.8 25.6 %collective-permute-done.5.refs_1_ = bf16[4096,256]{1,0:T(8,128)(2,1)} collective-permute-done((bf16[4096,256]{1,0:T(8,128)(2,1)S(1)}, bf16[4096,256]{1,0:T(8,128)(2,1)}, u32[]{:S(2)}, u32[]{:S(2)}) %collective-permute-start.5) | collective-permute-done | bytes 2097184 | tf_op jit(solution)/shard_map/ppermute | solution.py:157
  158.0 19.5 %collective-permute-done.13.refs_3_ = bf16[2048,256]{1,0:T(8,128)(2,1)S(1)} collective-permute-done((bf16[2048,256]{1,0:T(8,128)(2,1)S(1)}, bf16[2048,256]{1,0:T(8,128)(2,1)S(1)}, u32[]{:S(2)}, u32[]{:S(2)}) %collective-permute-start.13) | collective-permute-done | bytes 1048608 | tf_op jit(solution)/shard_map/ppermute | solution.py:157
  183.5 3.4 collective-permute-start.18
  186.9 3.9 collective-permute-done.16
  195.2 3.5 collective-permute-done.19.mine_ref
  200.1 3.1 shard_map.102
  208.3 3.8 collective-permute-done.22
  223.1 3.8 collective-permute-done.27
  229.0 10.8 %collective-permute-start.30 = (bf16[64,1024]{1,0:T(8,128)(2,1)S(1)}, bf16[64,1024]{1,0:T(8,128)(2,1)S(1)}, u32[]{:S(2)}, u32[]{:S(2)}) collective-permute-start(bf16[64,1024]{1,0:T(8,128)(2,1)S(1)} %add_convert_fusion.28), channel_id=1, source_target_pairs={{0,32},{1,33},{2,34},{3,35},{4,36},{5,37},{6,38},{7,39},{8,40},{9,... | collective-permute-start | bytes 393224 | tf_op jit(solution)/shard_map/ppermute | solution.py:157
  239.8 2.9 collective-permute-done.30.mine_ref
  244.1 3.1 shard_map.104
  252.2 3.8 collective-permute-done.33
  267.3 3.8 collective-permute-done.38
  273.1 3.8 collective-permute-start.41
  281.2 3.1 shard_map.106
  289.4 3.8 collective-permute-done.44
  304.2 3.8 collective-permute-done.49
  310.0 7.2 %collective-permute-start.52 = (bf16[64,1024]{1,0:T(8,128)(2,1)S(1)}, bf16[64,1024]{1,0:T(8,128)(2,1)S(1)}, u32[]{:S(2)}, u32[]{:S(2)}) collective-permute-start(bf16[64,1024]{1,0:T(8,128)(2,1)S(1)} %add_convert_fusion.20), channel_id=1, source_target_pairs={{0,32},{1,33},{2,34},{3,35},{4,36},{5,37},{6,38},{7,39},{8,40},{9,... | collective-permute-start | bytes 393224 | tf_op jit(solution)/shard_map/ppermute | solution.py:157
  321.5 3.1 shard_map.108
  329.7 3.8 collective-permute-done.55
  344.5 3.8 collective-permute-done.60
  350.4 3.8 collective-permute-start.63
  358.5 3.1 shard_map.110
  366.7 3.8 collective-permute-done.66
  381.7 3.8 collective-permute-done.71
  387.6 7.2 %collective-permute-start.74 = (bf16[64,1024]{1,0:T(8,128)(2,1)S(1)}, bf16[64,1024]{1,0:T(8,128)(2,1)S(1)}, u32[]{:S(2)}, u32[]{:S(2)}) collective-permute-start(bf16[64,1024]{1,0:T(8,128)(2,1)S(1)} %add_convert_fusion.12), channel_id=1, source_target_pairs={{0,32},{1,33},{2,34},{3,35},{4,36},{5,37},{6,38},{7,39},{8,40},{9,... | collective-permute-start | bytes 393224 | tf_op jit(solution)/shard_map/ppermute | solution.py:157
  399.1 3.1 shard_map.112
  407.2 3.8 collective-permute-done.77
  422.0 3.8 collective-permute-done.82
  428.5 3.7 collective-permute-start.85
  432.8 24.8 %collective-permute-done.85.mine_ref = bf16[64,1024]{1,0:T(8,128)(2,1)} collective-permute-done((bf16[64,1024]{1,0:T(8,128)(2,1)S(1)}, bf16[64,1024]{1,0:T(8,128)(2,1)}, u32[]{:S(2)}, u32[]{:S(2)}) %collective-permute-start.85) | collective-permute-done | bytes 131104 | tf_op jit(solution)/shard_map/ppermute | solution.py:157
  461.0 7.9 %shard_map.114 = (bf16[64,1024]{1,0:T(8,128)(2,1)S(1)}, bf16[64,1024]{1,0:T(8,128)(2,1)}) custom-call(s32[5]{0:T(128)S(1)} %pad_add_fusion.1.place_ref, bf16[64,1024]{1,0:T(8,128)(2,1)} %collective-permute-done.85.mine_ref, bf16[64,1024]{1,0:T(8,128)(2,1)} %collective-permute-done.86.other_ref, f32[1,1024]{1,0:T(1,128)S(1)} %get-tuple-element.162.gain_ref, ...), custom_call_target="tpu_custom_call" | custom-call | flops 1073741824 | bytes 8388608 | tf_op jit(solution)/shard_map/pallas_call | solution.py:82
  502.1 6.6 %shard_map.115 = (bf16[64,1024]{1,0:T(8,128)(2,1)S(1)}, bf16[64,1024]{1,0:T(8,128)(2,1)S(1)}) custom-call(s32[5]{0:T(128)S(1)} %pad_add_fusion.1.place_ref, bf16[64,1024]{1,0:T(8,128)(2,1)S(1)} %add_convert_fusion.6.mine_ref, bf16[64,1024]{1,0:T(8,128)(2,1)S(1)} %collective-permute-done.91.other_ref, f32[1,1024]{1,0:T(1,128)S(1)} %get-tuple-element.161.gain_ref, ...), custom_call_target="tpu_custom_call" | custom-call | flops 1073741824 | bytes 8388608 | tf_op jit(solution)/shard_map/pallas_call | solution.py:82
  513.8 3.7 collective-permute-done.93
  519.8 6.8 %collective-permute-done.96.mine_ref = bf16[64,1024]{1,0:T(8,128)(2,1)S(1)} collective-permute-done((bf16[64,1024]{1,0:T(8,128)(2,1)S(1)}, bf16[64,1024]{1,0:T(8,128)(2,1)S(1)}, u32[]{:S(2)}, u32[]{:S(2)}) %collective-permute-start.96) | collective-permute-done | bytes 131104 | tf_op jit(solution)/shard_map/ppermute | solution.py:157
  527.9 7.1 %shard_map.116 = (bf16[64,1024]{1,0:T(8,128)(2,1)S(1)}, bf16[64,1024]{1,0:T(8,128)(2,1)S(1)}) custom-call(s32[5]{0:T(128)S(1)} %pad_add_fusion.1.place_ref, bf16[64,1024]{1,0:T(8,128)(2,1)S(1)} %collective-permute-done.96.mine_ref, bf16[64,1024]{1,0:T(8,128)(2,1)S(1)} %collective-permute-done.97.other_ref, f32[1,1024]{1,0:T(1,128)S(1)} %get-tuple-element.162.gain_ref, ...), custom_call_target="tpu_custom_call" | custom-call | flops 1073741824 | bytes 8388608 | tf_op jit(solution)/shard_map/pallas_call | solution.py:82
  547.7 6.5 %shard_map.117 = (bf16[64,1024]{1,0:T(8,128)(2,1)S(1)}, bf16[64,1024]{1,0:T(8,128)(2,1)S(1)}) custom-call(s32[5]{0:T(128)S(1)} %pad_add_fusion.1.place_ref, bf16[64,1024]{1,0:T(8,128)(2,1)S(1)} %add_convert_fusion.2.mine_ref, bf16[64,1024]{1,0:T(8,128)(2,1)S(1)} %collective-permute-done.102.other_ref, f32[1,1024]{1,0:T(1,128)S(1)} %get-tuple-element.161.gain_ref, ...), custom_call_target="tpu_custom_call" | custom-call | flops 1073741824 | bytes 8388608 | tf_op jit(solution)/shard_map/pallas_call | solution.py:82
  559.4 3.7 collective-permute-done.104
  567.4 4.9 collective-permute-start.109
  572.4 6.6 %collective-permute-done.109 = bf16[2,16,1024]{2,1,0:T(8,128)(2,1)S(1)} collective-permute-done((bf16[2,16,1024]{2,1,0:T(8,128)(2,1)S(1)}, bf16[2,16,1024]{2,1,0:T(8,128)(2,1)S(1)}, u32[]{:S(2)}, u32[]{:S(2)}) %collective-permute-start.109) | collective-permute-done | bytes 65568 | tf_op jit(solution)/shard_map/ppermute | solution.py:157
  (384 shorter events, 230.1 us)
Async XLA Ops:
  6.5 103.0 %all-gather.2.cloned.1.call-start = ((), (), s32[]{:S(2)}) async-start(), calls=%async_computation | async-start | bytes 1114112 | tf_op jit(solution)/shard_map/all_gather | solution.py:193
  15.8 54.5 %collective-permute-start.1 = (bf16[4096,256]{1,0:T(8,128)(2,1)}, bf16[4096,256]{1,0:T(8,128)(2,1)}, u32[]{:S(2)}, u32[]{:S(2)}) collective-permute-start(bf16[4096,256]{1,0:T(8,128)(2,1)} %get-tuple-element.107.refs_0_), channel_id=1, source_target_pairs={{0,3},{1,2},{2,1},{3,0},{4,7},{5,6},{6,5},{7,4},{8,11},{9,10},{10,... | collective-permute-start | bytes 6291464 | tf_op jit(solution)/shard_map/ppermute | solution.py:157
  18.6 57.0 %collective-permute-start.3 = (bf16[4096,256]{1,0:T(8,128)(2,1)}, bf16[4096,256]{1,0:T(8,128)(2,1)}, u32[]{:S(2)}, u32[]{:S(2)}) collective-permute-start(bf16[4096,256]{1,0:T(8,128)(2,1)} %get-tuple-element.107.refs_0_), channel_id=1, source_target_pairs={{0,12},{1,13},{2,14},{3,15},{4,8},{5,9},{6,10},{7,11},{8,4},{9,5},... | collective-permute-start | bytes 6291464 | tf_op jit(solution)/shard_map/ppermute | solution.py:157
  21.7 87.8 %collective-permute-start.7 = (f32[1,1024]{1,0:T(1,128)S(1)}, f32[1,1024]{1,0:T(1,128)S(1)}, u32[]{:S(2)}, u32[]{:S(2)}) collective-permute-start(f32[1,1024]{1,0:T(1,128)S(1)} %copy-done.37), channel_id=1, source_target_pairs={{0,16},{1,17},{2,18},{3,19},{4,20},{5,21},{6,22},{7,23},{8,24},{9,... | collective-permute-start | bytes 12296 | tf_op jit(solution)/shard_map/ppermute | solution.py:157
  72.6 25.9 %collective-permute-start.2 = (bf16[2048,256]{1,0:T(8,128)(2,1)}, bf16[2048,256]{1,0:T(8,128)(2,1)S(1)}, u32[]{:S(2)}, u32[]{:S(2)}) collective-permute-start(bf16[2048,256]{1,0:T(8,128)(2,1)} %slice.188), channel_id=1, source_target_pairs={{0,12},{1,13},{2,14},{3,15},{4,8},{5,9},{6,10},{7,11},{8,4},{9,5},... | collective-permute-start | bytes 3145736 | tf_op jit(solution)/shard_map/ppermute | solution.py:157
  77.9 25.6 %collective-permute-start.4 = (bf16[2048,256]{1,0:T(8,128)(2,1)}, bf16[2048,256]{1,0:T(8,128)(2,1)}, u32[]{:S(2)}, u32[]{:S(2)}) collective-permute-start(bf16[2048,256]{1,0:T(8,128)(2,1)} %slice.189), channel_id=1, source_target_pairs={{0,3},{1,2},{2,1},{3,0},{4,7},{5,6},{6,5},{7,4},{8,11},{9,10},{10,... | collective-permute-start | bytes 3145736 | tf_op jit(solution)/shard_map/ppermute | solution.py:157
  103.5 47.0 %collective-permute-start.5 = (bf16[4096,256]{1,0:T(8,128)(2,1)S(1)}, bf16[4096,256]{1,0:T(8,128)(2,1)}, u32[]{:S(2)}, u32[]{:S(2)}) collective-permute-start(bf16[4096,256]{1,0:T(8,128)(2,1)S(1)} %get-tuple-element.47.refs_0_), channel_id=1, source_target_pairs={{0,3},{1,2},{2,1},{3,0},{4,7},{5,6},{6,5},{7,4},{8,11},{9,10},{10,... | collective-permute-start | bytes 6291464 | tf_op jit(solution)/shard_map/ppermute | solution.py:157
  106.2 46.7 %collective-permute-start.6 = (bf16[4096,256]{1,0:T(8,128)(2,1)S(1)}, bf16[4096,256]{1,0:T(8,128)(2,1)}, u32[]{:S(2)}, u32[]{:S(2)}) collective-permute-start(bf16[4096,256]{1,0:T(8,128)(2,1)S(1)} %get-tuple-element.47.refs_0_), channel_id=1, source_target_pairs={{0,12},{1,13},{2,14},{3,15},{4,8},{5,9},{6,10},{7,11},{8,4},{9,5},... | collective-permute-start | bytes 6291464 | tf_op jit(solution)/shard_map/ppermute | solution.py:157
  115.5 9.2 %collective-permute-start.9 = (bf16[64,1024]{1,0:T(8,128)(2,1)S(1)}, bf16[64,1024]{1,0:T(8,128)(2,1)S(1)}, u32[]{:S(2)}, u32[]{:S(2)}) collective-permute-start(bf16[64,1024]{1,0:T(8,128)(2,1)S(1)} %add_convert_fusion.35), channel_id=1, source_target_pairs={{0,5},{1,4},{2,7},{3,6},{4,1},{5,0},{6,3},{7,2},{8,13},{9,12},{10,... | collective-permute-start | bytes 393224 | tf_op jit(solution)/shard_map/ppermute | solution.py:157
  154.2 23.3 %collective-permute-start.13 = (bf16[2048,256]{1,0:T(8,128)(2,1)S(1)}, bf16[2048,256]{1,0:T(8,128)(2,1)S(1)}, u32[]{:S(2)}, u32[]{:S(2)}) collective-permute-start(bf16[2048,256]{1,0:T(8,128)(2,1)S(1)} %slice.167), channel_id=1, source_target_pairs={{0,12},{1,13},{2,14},{3,15},{4,8},{5,9},{6,10},{7,11},{8,4},{9,5},... | collective-permute-start | bytes 3145736 | tf_op jit(solution)/shard_map/ppermute | solution.py:157
  155.9 23.2 %collective-permute-start.14 = (bf16[2048,256]{1,0:T(8,128)(2,1)S(1)}, bf16[2048,256]{1,0:T(8,128)(2,1)S(1)}, u32[]{:S(2)}, u32[]{:S(2)}) collective-permute-start(bf16[2048,256]{1,0:T(8,128)(2,1)S(1)} %slice.168), channel_id=1, source_target_pairs={{0,3},{1,2},{2,1},{3,0},{4,7},{5,6},{6,5},{7,4},{8,11},{9,10},{10,... | collective-permute-start | bytes 3145736 | tf_op jit(solution)/shard_map/ppermute | solution.py:157
  183.3 7.5 %collective-permute-start.16 = (bf16[64,1024]{1,0:T(8,128)(2,1)S(1)}, bf16[64,1024]{1,0:T(8,128)(2,1)}, u32[]{:S(2)}, u32[]{:S(2)}) collective-permute-start(bf16[64,1024]{1,0:T(8,128)(2,1)S(1)} %add_convert_fusion.33), channel_id=1, source_target_pairs={{0,5},{1,4},{2,7},{3,6},{4,1},{5,0},{6,3},{7,2},{8,13},{9,12},{10,... | collective-permute-start | bytes 393224 | tf_op jit(solution)/shard_map/ppermute | solution.py:157
  183.4 8.6 %collective-permute-start.17 = (bf16[64,1024]{1,0:T(8,128)(2,1)S(1)}, bf16[64,1024]{1,0:T(8,128)(2,1)}, u32[]{:S(2)}, u32[]{:S(2)}) collective-permute-start(bf16[64,1024]{1,0:T(8,128)(2,1)S(1)} %add_convert_fusion.33), channel_id=1, source_target_pairs={{0,4},{1,5},{2,6},{3,7},{4,0},{5,1},{6,2},{7,3},{8,12},{9,13},{10,... | collective-permute-start | bytes 393224 | tf_op jit(solution)/shard_map/ppermute | solution.py:157
  183.5 8.5 %collective-permute-start.18 = (bf16[64,1024]{1,0:T(8,128)(2,1)S(1)}, bf16[64,1024]{1,0:T(8,128)(2,1)}, u32[]{:S(2)}, u32[]{:S(2)}) collective-permute-start(bf16[64,1024]{1,0:T(8,128)(2,1)S(1)} %add_convert_fusion.33), channel_id=1, source_target_pairs={{0,1},{1,0},{2,3},{3,2},{4,5},{5,4},{6,7},{7,6},{8,9},{9,8},{10,11... | collective-permute-start | bytes 393224 | tf_op jit(solution)/shard_map/ppermute | solution.py:157
  204.7 7.3 %collective-permute-start.22 = (bf16[64,1024]{1,0:T(8,128)(2,1)S(1)}, bf16[64,1024]{1,0:T(8,128)(2,1)S(1)}, u32[]{:S(2)}, u32[]{:S(2)}) collective-permute-start(bf16[64,1024]{1,0:T(8,128)(2,1)S(1)} %add_convert_fusion.31), channel_id=1, source_target_pairs={{0,5},{1,4},{2,7},{3,6},{4,1},{5,0},{6,3},{7,2},{8,13},{9,12},{10,... | collective-permute-start | bytes 393224 | tf_op jit(solution)/shard_map/ppermute | solution.py:157
  206.3 7.7 %collective-permute-start.23 = (bf16[64,1024]{1,0:T(8,128)(2,1)S(1)}, bf16[64,1024]{1,0:T(8,128)(2,1)S(1)}, u32[]{:S(2)}, u32[]{:S(2)}) collective-permute-start(bf16[64,1024]{1,0:T(8,128)(2,1)S(1)} %add_convert_fusion.31), channel_id=1, source_target_pairs={{0,4},{1,5},{2,6},{3,7},{4,0},{5,1},{6,2},{7,3},{8,12},{9,13},{10,... | collective-permute-start | bytes 393224 | tf_op jit(solution)/shard_map/ppermute | solution.py:157
  206.4 7.6 %collective-permute-start.24 = (bf16[64,1024]{1,0:T(8,128)(2,1)S(1)}, bf16[64,1024]{1,0:T(8,128)(2,1)S(1)}, u32[]{:S(2)}, u32[]{:S(2)}) collective-permute-start(bf16[64,1024]{1,0:T(8,128)(2,1)S(1)} %add_convert_fusion.31), channel_id=1, source_target_pairs={{0,1},{1,0},{2,3},{3,2},{4,5},{5,4},{6,7},{7,6},{8,9},{9,8},{10,11... | collective-permute-start | bytes 393224 | tf_op jit(solution)/shard_map/ppermute | solution.py:157
  219.5 7.3 %collective-permute-start.27 = (bf16[64,1024]{1,0:T(8,128)(2,1)S(1)}, bf16[64,1024]{1,0:T(8,128)(2,1)S(1)}, u32[]{:S(2)}, u32[]{:S(2)}) collective-permute-start(bf16[64,1024]{1,0:T(8,128)(2,1)S(1)} %add_convert_fusion.29), channel_id=1, source_target_pairs={{0,5},{1,4},{2,7},{3,6},{4,1},{5,0},{6,3},{7,2},{8,13},{9,12},{10,... | collective-permute-start | bytes 393224 | tf_op jit(solution)/shard_map/ppermute | solution.py:157
  221.2 7.7 %collective-permute-start.28 = (bf16[64,1024]{1,0:T(8,128)(2,1)S(1)}, bf16[64,1024]{1,0:T(8,128)(2,1)S(1)}, u32[]{:S(2)}, u32[]{:S(2)}) collective-permute-start(bf16[64,1024]{1,0:T(8,128)(2,1)S(1)} %add_convert_fusion.29), channel_id=1, source_target_pairs={{0,4},{1,5},{2,6},{3,7},{4,0},{5,1},{6,2},{7,3},{8,12},{9,13},{10,... | collective-permute-start | bytes 393224 | tf_op jit(solution)/shard_map/ppermute | solution.py:157
  229.0 13.7 %collective-permute-start.30 = (bf16[64,1024]{1,0:T(8,128)(2,1)S(1)}, bf16[64,1024]{1,0:T(8,128)(2,1)S(1)}, u32[]{:S(2)}, u32[]{:S(2)}) collective-permute-start(bf16[64,1024]{1,0:T(8,128)(2,1)S(1)} %add_convert_fusion.28), channel_id=1, source_target_pairs={{0,32},{1,33},{2,34},{3,35},{4,36},{5,37},{6,38},{7,39},{8,40},{9,... | collective-permute-start | bytes 393224 | tf_op jit(solution)/shard_map/ppermute | solution.py:157
  248.7 7.3 %collective-permute-start.33 = (bf16[64,1024]{1,0:T(8,128)(2,1)S(1)}, bf16[64,1024]{1,0:T(8,128)(2,1)S(1)}, u32[]{:S(2)}, u32[]{:S(2)}) collective-permute-start(bf16[64,1024]{1,0:T(8,128)(2,1)S(1)} %add_convert_fusion.27), channel_id=1, source_target_pairs={{0,5},{1,4},{2,7},{3,6},{4,1},{5,0},{6,3},{7,2},{8,13},{9,12},{10,... | collective-permute-start | bytes 393224 | tf_op jit(solution)/shard_map/ppermute | solution.py:157
  250.3 7.7 %collective-permute-start.34 = (bf16[64,1024]{1,0:T(8,128)(2,1)S(1)}, bf16[64,1024]{1,0:T(8,128)(2,1)S(1)}, u32[]{:S(2)}, u32[]{:S(2)}) collective-permute-start(bf16[64,1024]{1,0:T(8,128)(2,1)S(1)} %add_convert_fusion.27), channel_id=1, source_target_pairs={{0,4},{1,5},{2,6},{3,7},{4,0},{5,1},{6,2},{7,3},{8,12},{9,13},{10,... | collective-permute-start | bytes 393224 | tf_op jit(solution)/shard_map/ppermute | solution.py:157
  263.7 7.3 %collective-permute-start.38 = (bf16[64,1024]{1,0:T(8,128)(2,1)S(1)}, bf16[64,1024]{1,0:T(8,128)(2,1)S(1)}, u32[]{:S(2)}, u32[]{:S(2)}) collective-permute-start(bf16[64,1024]{1,0:T(8,128)(2,1)S(1)} %add_convert_fusion.25), channel_id=1, source_target_pairs={{0,5},{1,4},{2,7},{3,6},{4,1},{5,0},{6,3},{7,2},{8,13},{9,12},{10,... | collective-permute-start | bytes 393224 | tf_op jit(solution)/shard_map/ppermute | solution.py:157
  265.3 7.7 %collective-permute-start.39 = (bf16[64,1024]{1,0:T(8,128)(2,1)S(1)}, bf16[64,1024]{1,0:T(8,128)(2,1)S(1)}, u32[]{:S(2)}, u32[]{:S(2)}) collective-permute-start(bf16[64,1024]{1,0:T(8,128)(2,1)S(1)} %add_convert_fusion.25), channel_id=1, source_target_pairs={{0,4},{1,5},{2,6},{3,7},{4,0},{5,1},{6,2},{7,3},{8,12},{9,13},{10,... | collective-permute-start | bytes 393224 | tf_op jit(solution)/shard_map/ppermute | solution.py:157
  285.8 7.3 %collective-permute-start.44 = (bf16[64,1024]{1,0:T(8,128)(2,1)S(1)}, bf16[64,1024]{1,0:T(8,128)(2,1)S(1)}, u32[]{:S(2)}, u32[]{:S(2)}) collective-permute-start(bf16[64,1024]{1,0:T(8,128)(2,1)S(1)} %add_convert_fusion.23), channel_id=1, source_target_pairs={{0,5},{1,4},{2,7},{3,6},{4,1},{5,0},{6,3},{7,2},{8,13},{9,12},{10,... | collective-permute-start | bytes 393224 | tf_op jit(solution)/shard_map/ppermute | solution.py:157
  287.4 7.7 %collective-permute-start.45 = (bf16[64,1024]{1,0:T(8,128)(2,1)S(1)}, bf16[64,1024]{1,0:T(8,128)(2,1)S(1)}, u32[]{:S(2)}, u32[]{:S(2)}) collective-permute-start(bf16[64,1024]{1,0:T(8,128)(2,1)S(1)} %add_convert_fusion.23), channel_id=1, source_target_pairs={{0,4},{1,5},{2,6},{3,7},{4,0},{5,1},{6,2},{7,3},{8,12},{9,13},{10,... | collective-permute-start | bytes 393224 | tf_op jit(solution)/shard_map/ppermute | solution.py:157
  300.6 7.3 %collective-permute-start.49 = (bf16[64,1024]{1,0:T(8,128)(2,1)S(1)}, bf16[64,1024]{1,0:T(8,128)(2,1)S(1)}, u32[]{:S(2)}, u32[]{:S(2)}) collective-permute-start(bf16[64,1024]{1,0:T(8,128)(2,1)S(1)} %add_convert_fusion.21), channel_id=1, source_target_pairs={{0,5},{1,4},{2,7},{3,6},{4,1},{5,0},{6,3},{7,2},{8,13},{9,12},{10,... | collective-permute-start | bytes 393224 | tf_op jit(solution)/shard_map/ppermute | solution.py:157
  302.2 7.7 %collective-permute-start.50 = (bf16[64,1024]{1,0:T(8,128)(2,1)S(1)}, bf16[64,1024]{1,0:T(8,128)(2,1)S(1)}, u32[]{:S(2)}, u32[]{:S(2)}) collective-permute-start(bf16[64,1024]{1,0:T(8,128)(2,1)S(1)} %add_convert_fusion.21), channel_id=1, source_target_pairs={{0,4},{1,5},{2,6},{3,7},{4,0},{5,1},{6,2},{7,3},{8,12},{9,13},{10,... | collective-permute-start | bytes 393224 | tf_op jit(solution)/shard_map/ppermute | solution.py:157
  310.0 10.2 %collective-permute-start.52 = (bf16[64,1024]{1,0:T(8,128)(2,1)S(1)}, bf16[64,1024]{1,0:T(8,128)(2,1)S(1)}, u32[]{:S(2)}, u32[]{:S(2)}) collective-permute-start(bf16[64,1024]{1,0:T(8,128)(2,1)S(1)} %add_convert_fusion.20), channel_id=1, source_target_pairs={{0,32},{1,33},{2,34},{3,35},{4,36},{5,37},{6,38},{7,39},{8,40},{9,... | collective-permute-start | bytes 393224 | tf_op jit(solution)/shard_map/ppermute | solution.py:157
  326.1 7.3 %collective-permute-start.55 = (bf16[64,1024]{1,0:T(8,128)(2,1)S(1)}, bf16[64,1024]{1,0:T(8,128)(2,1)S(1)}, u32[]{:S(2)}, u32[]{:S(2)}) collective-permute-start(bf16[64,1024]{1,0:T(8,128)(2,1)S(1)} %add_convert_fusion.19), channel_id=1, source_target_pairs={{0,5},{1,4},{2,7},{3,6},{4,1},{5,0},{6,3},{7,2},{8,13},{9,12},{10,... | collective-permute-start | bytes 393224 | tf_op jit(solution)/shard_map/ppermute | solution.py:157
  327.8 7.7 %collective-permute-start.56 = (bf16[64,1024]{1,0:T(8,128)(2,1)S(1)}, bf16[64,1024]{1,0:T(8,128)(2,1)S(1)}, u32[]{:S(2)}, u32[]{:S(2)}) collective-permute-start(bf16[64,1024]{1,0:T(8,128)(2,1)S(1)} %add_convert_fusion.19), channel_id=1, source_target_pairs={{0,4},{1,5},{2,6},{3,7},{4,0},{5,1},{6,2},{7,3},{8,12},{9,13},{10,... | collective-permute-start | bytes 393224 | tf_op jit(solution)/shard_map/ppermute | solution.py:157
  341.0 7.3 %collective-permute-start.60 = (bf16[64,1024]{1,0:T(8,128)(2,1)S(1)}, bf16[64,1024]{1,0:T(8,128)(2,1)S(1)}, u32[]{:S(2)}, u32[]{:S(2)}) collective-permute-start(bf16[64,1024]{1,0:T(8,128)(2,1)S(1)} %add_convert_fusion.17), channel_id=1, source_target_pairs={{0,5},{1,4},{2,7},{3,6},{4,1},{5,0},{6,3},{7,2},{8,13},{9,12},{10,... | collective-permute-start | bytes 393224 | tf_op jit(solution)/shard_map/ppermute | solution.py:157
  342.6 7.7 %collective-permute-start.61 = (bf16[64,1024]{1,0:T(8,128)(2,1)S(1)}, bf16[64,1024]{1,0:T(8,128)(2,1)S(1)}, u32[]{:S(2)}, u32[]{:S(2)}) collective-permute-start(bf16[64,1024]{1,0:T(8,128)(2,1)S(1)} %add_convert_fusion.17), channel_id=1, source_target_pairs={{0,4},{1,5},{2,6},{3,7},{4,0},{5,1},{6,2},{7,3},{8,12},{9,13},{10,... | collective-permute-start | bytes 393224 | tf_op jit(solution)/shard_map/ppermute | solution.py:157
  363.1 7.3 %collective-permute-start.66 = (bf16[64,1024]{1,0:T(8,128)(2,1)S(1)}, bf16[64,1024]{1,0:T(8,128)(2,1)S(1)}, u32[]{:S(2)}, u32[]{:S(2)}) collective-permute-start(bf16[64,1024]{1,0:T(8,128)(2,1)S(1)} %add_convert_fusion.15), channel_id=1, source_target_pairs={{0,5},{1,4},{2,7},{3,6},{4,1},{5,0},{6,3},{7,2},{8,13},{9,12},{10,... | collective-permute-start | bytes 393224 | tf_op jit(solution)/shard_map/ppermute | solution.py:157
  364.7 7.7 %collective-permute-start.67 = (bf16[64,1024]{1,0:T(8,128)(2,1)S(1)}, bf16[64,1024]{1,0:T(8,128)(2,1)S(1)}, u32[]{:S(2)}, u32[]{:S(2)}) collective-permute-start(bf16[64,1024]{1,0:T(8,128)(2,1)S(1)} %add_convert_fusion.15), channel_id=1, source_target_pairs={{0,4},{1,5},{2,6},{3,7},{4,0},{5,1},{6,2},{7,3},{8,12},{9,13},{10,... | collective-permute-start | bytes 393224 | tf_op jit(solution)/shard_map/ppermute | solution.py:157
  378.1 7.3 %collective-permute-start.71 = (bf16[64,1024]{1,0:T(8,128)(2,1)S(1)}, bf16[64,1024]{1,0:T(8,128)(2,1)S(1)}, u32[]{:S(2)}, u32[]{:S(2)}) collective-permute-start(bf16[64,1024]{1,0:T(8,128)(2,1)S(1)} %add_convert_fusion.13), channel_id=1, source_target_pairs={{0,5},{1,4},{2,7},{3,6},{4,1},{5,0},{6,3},{7,2},{8,13},{9,12},{10,... | collective-permute-start | bytes 393224 | tf_op jit(solution)/shard_map/ppermute | solution.py:157
  379.7 7.7 %collective-permute-start.72 = (bf16[64,1024]{1,0:T(8,128)(2,1)S(1)}, bf16[64,1024]{1,0:T(8,128)(2,1)S(1)}, u32[]{:S(2)}, u32[]{:S(2)}) collective-permute-start(bf16[64,1024]{1,0:T(8,128)(2,1)S(1)} %add_convert_fusion.13), channel_id=1, source_target_pairs={{0,4},{1,5},{2,6},{3,7},{4,0},{5,1},{6,2},{7,3},{8,12},{9,13},{10,... | collective-permute-start | bytes 393224 | tf_op jit(solution)/shard_map/ppermute | solution.py:157
  387.6 10.2 %collective-permute-start.74 = (bf16[64,1024]{1,0:T(8,128)(2,1)S(1)}, bf16[64,1024]{1,0:T(8,128)(2,1)S(1)}, u32[]{:S(2)}, u32[]{:S(2)}) collective-permute-start(bf16[64,1024]{1,0:T(8,128)(2,1)S(1)} %add_convert_fusion.12), channel_id=1, source_target_pairs={{0,32},{1,33},{2,34},{3,35},{4,36},{5,37},{6,38},{7,39},{8,40},{9,... | collective-permute-start | bytes 393224 | tf_op jit(solution)/shard_map/ppermute | solution.py:157
  405.3 7.7 %collective-permute-start.78 = (bf16[64,1024]{1,0:T(8,128)(2,1)S(1)}, bf16[64,1024]{1,0:T(8,128)(2,1)S(1)}, u32[]{:S(2)}, u32[]{:S(2)}) collective-permute-start(bf16[64,1024]{1,0:T(8,128)(2,1)S(1)} %add_convert_fusion.11), channel_id=1, source_target_pairs={{0,4},{1,5},{2,6},{3,7},{4,0},{5,1},{6,2},{7,3},{8,12},{9,13},{10,... | collective-permute-start | bytes 393224 | tf_op jit(solution)/shard_map/ppermute | solution.py:157
  420.1 7.7 %collective-permute-start.83 = (bf16[64,1024]{1,0:T(8,128)(2,1)S(1)}, bf16[64,1024]{1,0:T(8,128)(2,1)S(1)}, u32[]{:S(2)}, u32[]{:S(2)}) collective-permute-start(bf16[64,1024]{1,0:T(8,128)(2,1)S(1)} %add_convert_fusion.9), channel_id=1, source_target_pairs={{0,4},{1,5},{2,6},{3,7},{4,0},{5,1},{6,2},{7,3},{8,12},{9,13},{10,... | collective-permute-start | bytes 393224 | tf_op jit(solution)/shard_map/ppermute | solution.py:157
  428.5 29.1 %collective-permute-start.85 = (bf16[64,1024]{1,0:T(8,128)(2,1)S(1)}, bf16[64,1024]{1,0:T(8,128)(2,1)}, u32[]{:S(2)}, u32[]{:S(2)}) collective-permute-start(bf16[64,1024]{1,0:T(8,128)(2,1)S(1)} %add_convert_fusion.8), channel_id=1, source_target_pairs={{0,32},{1,33},{2,34},{3,35},{4,36},{5,37},{6,38},{7,39},{8,40},{9,... | collective-permute-start | bytes 393224 | tf_op jit(solution)/shard_map/ppermute | solution.py:157
  469.5 16.3 %collective-permute-start.87 = (bf16[64,1024]{1,0:T(8,128)(2,1)}, bf16[64,1024]{1,0:T(8,128)(2,1)}, u32[]{:S(2)}, u32[]{:S(2)}) collective-permute-start(bf16[64,1024]{1,0:T(8,128)(2,1)} %get-tuple-element.82), channel_id=1, source_target_pairs={{0,16},{1,17},{2,18},{3,19},{4,20},{5,21},{6,22},{7,23},{8,24},{9,... | collective-permute-start | bytes 393224 | tf_op jit(solution)/shard_map/ppermute | solution.py:157
  487.5 7.6 %collective-permute-start.88 = (bf16[64,1024]{1,0:T(8,128)(2,1)}, bf16[64,1024]{1,0:T(8,128)(2,1)}, u32[]{:S(2)}, u32[]{:S(2)}) collective-permute-start(bf16[64,1024]{1,0:T(8,128)(2,1)} %add_convert_fusion.7), channel_id=1, source_target_pairs={{0,5},{1,4},{2,7},{3,6},{4,1},{5,0},{6,3},{7,2},{8,13},{9,12},{10,... | collective-permute-start | bytes 393224 | tf_op jit(solution)/shard_map/ppermute | solution.py:157
  489.2 7.7 %collective-permute-start.89 = (bf16[64,1024]{1,0:T(8,128)(2,1)}, bf16[64,1024]{1,0:T(8,128)(2,1)}, u32[]{:S(2)}, u32[]{:S(2)}) collective-permute-start(bf16[64,1024]{1,0:T(8,128)(2,1)} %add_convert_fusion.7), channel_id=1, source_target_pairs={{0,4},{1,5},{2,6},{3,7},{4,0},{5,1},{6,2},{7,3},{8,12},{9,13},{10,... | collective-permute-start | bytes 393224 | tf_op jit(solution)/shard_map/ppermute | solution.py:157
  512.0 7.5 %collective-permute-start.94 = (bf16[64,1024]{1,0:T(8,128)(2,1)S(1)}, bf16[64,1024]{1,0:T(8,128)(2,1)S(1)}, u32[]{:S(2)}, u32[]{:S(2)}) collective-permute-start(bf16[64,1024]{1,0:T(8,128)(2,1)S(1)} %add_convert_fusion.5), channel_id=1, source_target_pairs={{0,4},{1,5},{2,6},{3,7},{4,0},{5,1},{6,2},{7,3},{8,12},{9,13},{10,... | collective-permute-start | bytes 393224 | tf_op jit(solution)/shard_map/ppermute | solution.py:157
  538.7 7.4 %collective-permute-start.99 = (bf16[64,1024]{1,0:T(8,128)(2,1)S(1)}, bf16[64,1024]{1,0:T(8,128)(2,1)S(1)}, u32[]{:S(2)}, u32[]{:S(2)}) collective-permute-start(bf16[64,1024]{1,0:T(8,128)(2,1)S(1)} %add_convert_fusion.3), channel_id=1, source_target_pairs={{0,5},{1,4},{2,7},{3,6},{4,1},{5,0},{6,3},{7,2},{8,13},{9,12},{10,... | collective-permute-start | bytes 393224 | tf_op jit(solution)/shard_map/ppermute | solution.py:157
  557.3 7.7 %collective-permute-start.105 = (bf16[64,1024]{1,0:T(8,128)(2,1)S(1)}, bf16[64,1024]{1,0:T(8,128)(2,1)S(1)}, u32[]{:S(2)}, u32[]{:S(2)}) collective-permute-start(bf16[64,1024]{1,0:T(8,128)(2,1)S(1)} %add_convert_fusion.1), channel_id=1, source_target_pairs={{0,4},{1,5},{2,6},{3,7},{4,0},{5,1},{6,2},{7,3},{8,12},{9,13},{10,... | collective-permute-start | bytes 393224 | tf_op jit(solution)/shard_map/ppermute | solution.py:157
  567.4 11.5 %collective-permute-start.109 = (bf16[2,16,1024]{2,1,0:T(8,128)(2,1)S(1)}, bf16[2,16,1024]{2,1,0:T(8,128)(2,1)S(1)}, u32[]{:S(2)}, u32[]{:S(2)}) collective-permute-start(bf16[2,16,1024]{2,1,0:T(8,128)(2,1)S(1)} %get-tuple-element.120), channel_id=1, source_target_pairs={{0,4},{1,5},{2,8},{3,9},{4,14},{5,15},{6,2},{7,3},{8,12},{9,13},{1... | collective-permute-start | bytes 196616 | tf_op jit(solution)/shard_map/ppermute | solution.py:157
  (103 other events, 908.5 us)
Sparse Core Ops, SparseCore 0:
  21.8 45.6 all-gather.1

commit v5 on v4

--- a/solution.py
+++ b/solution.py
@@ -184,11 +184,10 @@
     cut = low.shape[0] // 2
     own_a, own_b = jnp.where(first, kept, got), jnp.where(first, got, kept)
     x_a, y_a = over_x(own_a), over_y(own_a)
+    own_b, x_a, y_a = lax.optimization_barrier((own_b, x_a, y_a))
     weights_a = [own_a, x_a, y_a, over_y(x_a[:cut]), over_x(y_a[cut:])]
-    own_b, weights_a[3], weights_a[4] = lax.optimization_barrier(
-        (own_b, weights_a[3], weights_a[4])
-    )
     x_b, y_b = over_x(own_b), over_y(own_b)
+    weights_b = [own_b, x_b, y_b, over_y(x_b[:cut]), over_x(y_b[cut:])]
 
     inputs_all = lax.all_gather(inputs, "dp", axis=1, tiled=True)
     window_mine = lax.dynamic_slice_in_dim(inputs_all, start + HALF * core, HALF, 1)
@@ -202,18 +201,23 @@
         jnp.stack([plane, core, start]).astype(jnp.int32), batch_lengths.astype(jnp.int32)
     ])
 
+    def across(s, a, b, along_y):
+        return (s, a ^ 1, b) if along_y else (s, a, b ^ 1)
+
     def one_layer(turn, mine, other, gain, weights):
         keep, send = run_layer(turn, where_am_i, mine, other, gain, biases, weights)
         chip = (
             keep.astype(jnp.float32) + swap_cores(send).astype(jnp.float32)
         ).astype(jnp.bfloat16)
-        total = mine.astype(jnp.float32) + chip.astype(jnp.float32)
-        for piece in (
-            move(chip, lambda s, a, b: (s, a ^ 1, b ^ 1)),
-            move(chip, lambda s, a, b: (s, a ^ 1, b)),
-            move(chip, lambda s, a, b: (s, a, b ^ 1)),
-        ):
-            total = total + piece.astype(jnp.float32)
+        pair = (
+            chip.astype(jnp.float32)
+            + move(chip, lambda s, a, b: across(s, a, b, s % 2)).astype(jnp.float32)
+        ).astype(jnp.bfloat16)
+        total = (
+            mine.astype(jnp.float32)
+            + pair.astype(jnp.float32)
+            + move(pair, lambda s, a, b: across(s, a, b, 1 - s % 2)).astype(jnp.float32)
+        )
         return total.astype(jnp.bfloat16)
 
     side = jnp.where(member < SIDE // 2, group + 1, group - 1)
@@ -235,13 +239,9 @@
                 stash[layer][m] = jnp.where(plane == turn - m, found, stash[layer][m])
 
     mine, other = window_mine[0], window_other[0]
-    weights_b = None
     turns = planes + micro_count - 1
     for turn in range(turns):
         out_a = one_layer(turn, mine, other, gain_a, weights_a)
-        if weights_b is None:
-            x_b, y_b, out_a = lax.optimization_barrier((x_b, y_b, out_a))
-            weights_b = [own_b, x_b, y_b, over_y(x_b[:cut]), over_x(y_b[cut:])]
         out_b = one_layer(turn, out_a, swap_cores(out_a), gain_b, weights_b)
         if turn < turns - 1:
             onward = (

time: 596 us -> 609 us (1.022)
  waiting for transfers between devices: 321 us -> 383 us
  starting transfers between devices: 129 us -> 75 us
    ppermute x110 -> x92, waiting for transfers between devices: 321 us -> 383 us  [move(): return lax.ppermute(value, AXES, pairs)]
    ppermute x110 -> x92, starting transfers between devices: 129 us -> 75 us  [move(): return lax.ppermute(value, AXES, pairs)]
  transfers between devices with their start and end apart: 111 -> 93, of which waited for: 89 -> 83; matrix products, arithmetic and copies ran while one was open for 3% -> 4% of each run, Pallas kernels for 1% -> 1%
where the time goes in v5:
time: 609 us; the launch traced here: 599 us
  waiting for transfers between devices  383 us (63%)
  starting transfers between devices  75 us (12%)
  Pallas kernels  67.7 us (11%)
  between operations  34.1 us (6%)
  local copies, waits for them, and re-layouts  22.3 us (4%)
  other arithmetic  17.3 us (3%)
    ppermute x92, waiting for transfers between devices, move(): return lax.ppermute(value, AXES, pairs)  383 us
    ppermute x92, starting transfers between devices, move(): return lax.ppermute(value, AXES, pairs)  75 us
    pallas_call x18, Pallas kernels, run_layer(): pl.pallas_call(functools.partial(layer_kernel, turn), out_shape=(half, ha...  67.7 us
  transfers between devices with their start and end apart: 93, of which 83 were waited for; matrix products, arithmetic and copies ran while one was open for 4% of the time, Pallas kernels for 1%

profile of v5, /device:TPU:224, one launch (start us, length us, event | category | flops | bytes accessed | tf_op | source)
XLA Modules:
  0.0 599.3 jit_solution(4674666248394760746)
XLA Ops:
  24.1 46.3 %collective-permute-done.2.refs_1_ = bf16[4096,256]{1,0:T(8,128)(2,1)} collective-permute-done((bf16[4096,256]{1,0:T(8,128)(2,1)}, bf16[4096,256]{1,0:T(8,128)(2,1)}, u32[]{:S(2)}, u32[]{:S(2)}) %collective-permute-start.2) | collective-permute-done | bytes 2097184 | tf_op jit(solution)/shard_map/ppermute | solution.py:157
  88.7 54.8 %collective-permute-done.4.refs_3_ = bf16[2048,256]{1,0:T(8,128)(2,1)S(1)} collective-permute-done((bf16[2048,256]{1,0:T(8,128)(2,1)}, bf16[2048,256]{1,0:T(8,128)(2,1)S(1)}, u32[]{:S(2)}, u32[]{:S(2)}) %collective-permute-start.4) | collective-permute-done | bytes 1048608 | tf_op jit(solution)/shard_map/ppermute | solution.py:157
  155.2 5.0 collective-permute-done.7
  160.2 5.0 collective-permute-done.8
  166.9 7.9 %collective-permute-done.12.refs_3_ = bf16[2048,256]{1,0:T(8,128)(2,1)S(1)} collective-permute-done((bf16[2048,256]{1,0:T(8,128)(2,1)S(1)}, bf16[2048,256]{1,0:T(8,128)(2,1)S(1)}, u32[]{:S(2)}, u32[]{:S(2)}) %collective-permute-start.12) | collective-permute-done | bytes 1048608 | tf_op jit(solution)/shard_map/ppermute | solution.py:157
  183.1 5.0 collective-permute-done.15
  188.2 5.1 collective-permute-done.16
  195.0 5.5 collective-permute-start.17
  209.0 5.0 collective-permute-done.20
  214.1 5.0 collective-permute-done.21
  224.6 5.0 collective-permute-done.24
  229.7 5.0 collective-permute-done.25
  234.7 11.8 %collective-permute-start.26 = (bf16[64,1024]{1,0:T(8,128)(2,1)S(1)}, bf16[64,1024]{1,0:T(8,128)(2,1)S(1)}, u32[]{:S(2)}, u32[]{:S(2)}) collective-permute-start(bf16[64,1024]{1,0:T(8,128)(2,1)S(1)} %add_convert_fusion.42), channel_id=1, source_target_pairs={{0,32},{1,33},{2,34},{3,35},{4,36},{5,37},{6,38},{7,39},{8,40},{9,... | collective-permute-start | bytes 393224 | tf_op jit(solution)/shard_map/ppermute | solution.py:157
  255.1 5.0 collective-permute-done.29
  260.2 5.0 collective-permute-done.30
  270.9 5.0 collective-permute-done.33
  275.9 5.0 collective-permute-done.34
  293.3 5.0 collective-permute-done.38
  298.4 5.0 collective-permute-done.39
  308.8 5.0 collective-permute-done.42
  313.9 5.0 collective-permute-done.43
  318.9 7.0 %collective-permute-start.44 = (bf16[64,1024]{1,0:T(8,128)(2,1)S(1)}, bf16[64,1024]{1,0:T(8,128)(2,1)S(1)}, u32[]{:S(2)}, u32[]{:S(2)}) collective-permute-start(bf16[64,1024]{1,0:T(8,128)(2,1)S(1)} %add_convert_fusion.30), channel_id=1, source_target_pairs={{0,32},{1,33},{2,34},{3,35},{4,36},{5,37},{6,38},{7,39},{8,40},{9,... | collective-permute-start | bytes 393224 | tf_op jit(solution)/shard_map/ppermute | solution.py:157
  334.5 5.0 collective-permute-done.47
  339.6 5.0 collective-permute-done.48
  350.1 5.0 collective-permute-done.51
  355.1 5.0 collective-permute-done.52
  372.5 5.0 collective-permute-done.56
  377.6 5.0 collective-permute-done.57
  388.3 5.0 collective-permute-done.60
  393.3 5.0 collective-permute-done.61
  398.4 7.0 %collective-permute-start.62 = (bf16[64,1024]{1,0:T(8,128)(2,1)S(1)}, bf16[64,1024]{1,0:T(8,128)(2,1)S(1)}, u32[]{:S(2)}, u32[]{:S(2)}) collective-permute-start(bf16[64,1024]{1,0:T(8,128)(2,1)S(1)} %add_convert_fusion.18), channel_id=1, source_target_pairs={{0,32},{1,33},{2,34},{3,35},{4,36},{5,37},{6,38},{7,39},{8,40},{9,... | collective-permute-start | bytes 393224 | tf_op jit(solution)/shard_map/ppermute | solution.py:157
  413.9 5.0 collective-permute-done.65
  419.0 5.0 collective-permute-done.66
  429.4 5.0 collective-permute-done.69
  434.5 5.0 collective-permute-done.70
  443.3 23.6 %collective-permute-done.71.mine_ref = bf16[64,1024]{1,0:T(8,128)(2,1)S(1)} collective-permute-done((bf16[64,1024]{1,0:T(8,128)(2,1)S(1)}, bf16[64,1024]{1,0:T(8,128)(2,1)S(1)}, u32[]{:S(2)}, u32[]{:S(2)}) %collective-permute-start.71) | collective-permute-done | bytes 131104 | tf_op jit(solution)/shard_map/ppermute | solution.py:157
  468.2 7.1 %shard_map.114 = (bf16[64,1024]{1,0:T(8,128)(2,1)S(1)}, bf16[64,1024]{1,0:T(8,128)(2,1)S(1)}) custom-call(s32[5]{0:T(128)S(1)} %pad_add_fusion.1.place_ref, bf16[64,1024]{1,0:T(8,128)(2,1)S(1)} %collective-permute-done.71.mine_ref, bf16[64,1024]{1,0:T(8,128)(2,1)S(1)} %collective-permute-done.72.other_ref, f32[1,1024]{1,0:T(1,128)S(1)} %get-tuple-element.156.gain_ref, ...), custom_call_target="tpu_custom_call" | custom-call | flops 1073741824 | bytes 8388608 | tf_op jit(solution)/shard_map/pallas_call | solution.py:82
  477.0 5.0 collective-permute-done.74
  493.6 7.3 %shard_map.115 = (bf16[64,1024]{1,0:T(8,128)(2,1)S(1)}, bf16[64,1024]{1,0:T(8,128)(2,1)}) custom-call(s32[5]{0:T(128)S(1)} %pad_add_fusion.1.place_ref, bf16[64,1024]{1,0:T(8,128)(2,1)} %add_convert_fusion.9.mine_ref, bf16[64,1024]{1,0:T(8,128)(2,1)} %collective-permute-done.76.other_ref, f32[1,1024]{1,0:T(1,128)S(1)} %get-tuple-element.155.gain_ref, ...), custom_call_target="tpu_custom_call" | custom-call | flops 1073741824 | bytes 8388608 | tf_op jit(solution)/shard_map/pallas_call | solution.py:82
  532.7 5.2 collective-permute-done.80.mine_ref
  539.8 7.3 %shard_map.116 = (bf16[64,1024]{1,0:T(8,128)(2,1)S(1)}, bf16[64,1024]{1,0:T(8,128)(2,1)S(1)}) custom-call(s32[5]{0:T(128)S(1)} %pad_add_fusion.1.place_ref, bf16[64,1024]{1,0:T(8,128)(2,1)S(1)} %collective-permute-done.80.mine_ref, bf16[64,1024]{1,0:T(8,128)(2,1)S(1)} %collective-permute-done.81.other_ref, f32[1,1024]{1,0:T(1,128)S(1)} %get-tuple-element.156.gain_ref, ...), custom_call_target="tpu_custom_call" | custom-call | flops 1073741824 | bytes 8388608 | tf_op jit(solution)/shard_map/pallas_call | solution.py:82
  549.0 4.9 collective-permute-done.83
  554.0 4.9 collective-permute-done.84
  560.4 6.5 %shard_map.117 = (bf16[64,1024]{1,0:T(8,128)(2,1)S(1)}, bf16[64,1024]{1,0:T(8,128)(2,1)S(1)}) custom-call(s32[5]{0:T(128)S(1)} %pad_add_fusion.1.place_ref, bf16[64,1024]{1,0:T(8,128)(2,1)S(1)} %add_convert_fusion.3.mine_ref, bf16[64,1024]{1,0:T(8,128)(2,1)S(1)} %collective-permute-done.85.other_ref, f32[1,1024]{1,0:T(1,128)S(1)} %get-tuple-element.155.gain_ref, ...), custom_call_target="tpu_custom_call" | custom-call | flops 1073741824 | bytes 8388608 | tf_op jit(solution)/shard_map/pallas_call | solution.py:82
  568.6 4.9 collective-permute-done.87
  573.7 4.9 collective-permute-done.88
  580.9 4.9 collective-permute-start.91
  585.7 5.6 collective-permute-done.91
  (362 shorter events, 194.3 us)
Async XLA Ops:
  6.5 81.1 %all-gather.2.cloned.1.call-start = ((), (), s32[]{:S(2)}) async-start(), calls=%async_computation | async-start | bytes 1114112 | tf_op jit(solution)/shard_map/all_gather | solution.py:192
  15.9 54.5 %collective-permute-start.2 = (bf16[4096,256]{1,0:T(8,128)(2,1)}, bf16[4096,256]{1,0:T(8,128)(2,1)}, u32[]{:S(2)}, u32[]{:S(2)}) collective-permute-start(bf16[4096,256]{1,0:T(8,128)(2,1)} %get-tuple-element.102.refs_0_), channel_id=1, source_target_pairs={{0,3},{1,2},{2,1},{3,0},{4,7},{5,6},{6,5},{7,4},{8,11},{9,10},{10,... | collective-permute-start | bytes 6291464 | tf_op jit(solution)/shard_map/ppermute | solution.py:157
  18.7 54.3 %collective-permute-start.3 = (bf16[4096,256]{1,0:T(8,128)(2,1)}, bf16[4096,256]{1,0:T(8,128)(2,1)}, u32[]{:S(2)}, u32[]{:S(2)}) collective-permute-start(bf16[4096,256]{1,0:T(8,128)(2,1)} %get-tuple-element.102.refs_0_), channel_id=1, source_target_pairs={{0,12},{1,13},{2,14},{3,15},{4,8},{5,9},{6,10},{7,11},{8,4},{9,5},... | collective-permute-start | bytes 6291464 | tf_op jit(solution)/shard_map/ppermute | solution.py:157
  21.7 65.9 %collective-permute-start = (f32[1,1024]{1,0:T(1,128)S(1)}, f32[1,1024]{1,0:T(1,128)S(1)}, u32[]{:S(2)}, u32[]{:S(2)}) collective-permute-start(f32[1,1024]{1,0:T(1,128)S(1)} %copy-done.35), channel_id=1, source_target_pairs={{0,16},{1,17},{2,18},{3,19},{4,20},{5,21},{6,22},{7,23},{8,24},{9,... | collective-permute-start | bytes 12296 | tf_op jit(solution)/shard_map/ppermute | solution.py:157
  72.9 73.7 %collective-permute-start.10 = (bf16[4096,256]{1,0:T(8,128)(2,1)S(1)}, bf16[4096,256]{1,0:T(8,128)(2,1)}, u32[]{:S(2)}, u32[]{:S(2)}) collective-permute-start(bf16[4096,256]{1,0:T(8,128)(2,1)S(1)} %get-tuple-element.48.refs_0_), channel_id=1, source_target_pairs={{0,3},{1,2},{2,1},{3,0},{4,7},{5,6},{6,5},{7,4},{8,11},{9,10},{10,... | collective-permute-start | bytes 6291464 | tf_op jit(solution)/shard_map/ppermute | solution.py:157
  73.4 77.6 %collective-permute-start.11 = (bf16[4096,256]{1,0:T(8,128)(2,1)S(1)}, bf16[4096,256]{1,0:T(8,128)(2,1)}, u32[]{:S(2)}, u32[]{:S(2)}) collective-permute-start(bf16[4096,256]{1,0:T(8,128)(2,1)S(1)} %get-tuple-element.48.refs_0_), channel_id=1, source_target_pairs={{0,12},{1,13},{2,14},{3,15},{4,8},{5,9},{6,10},{7,11},{8,4},{9,5},... | collective-permute-start | bytes 6291464 | tf_op jit(solution)/shard_map/ppermute | solution.py:157
  80.0 63.5 %collective-permute-start.4 = (bf16[2048,256]{1,0:T(8,128)(2,1)}, bf16[2048,256]{1,0:T(8,128)(2,1)S(1)}, u32[]{:S(2)}, u32[]{:S(2)}) collective-permute-start(bf16[2048,256]{1,0:T(8,128)(2,1)} %slice.165), channel_id=1, source_target_pairs={{0,12},{1,13},{2,14},{3,15},{4,8},{5,9},{6,10},{7,11},{8,4},{9,5},... | collective-permute-start | bytes 3145736 | tf_op jit(solution)/shard_map/ppermute | solution.py:157
  82.5 60.9 %collective-permute-start.5 = (bf16[2048,256]{1,0:T(8,128)(2,1)}, bf16[2048,256]{1,0:T(8,128)(2,1)}, u32[]{:S(2)}, u32[]{:S(2)}) collective-permute-start(bf16[2048,256]{1,0:T(8,128)(2,1)} %slice.166), channel_id=1, source_target_pairs={{0,3},{1,2},{2,1},{3,0},{4,7},{5,6},{6,5},{7,4},{8,11},{9,10},{10,... | collective-permute-start | bytes 3145736 | tf_op jit(solution)/shard_map/ppermute | solution.py:157
  146.6 8.5 %collective-permute-start.6 = (bf16[64,1024]{1,0:T(8,128)(2,1)S(1)}, bf16[64,1024]{1,0:T(8,128)(2,1)S(1)}, u32[]{:S(2)}, u32[]{:S(2)}) collective-permute-start(bf16[64,1024]{1,0:T(8,128)(2,1)S(1)} %get-tuple-element.47), channel_id=1, source_target_pairs={{0,16},{1,17},{2,18},{3,19},{4,20},{5,21},{6,22},{7,23},{8,24},{9,... | collective-permute-start | bytes 393224 | tf_op jit(solution)/shard_map/ppermute | solution.py:157
  148.0 26.9 %collective-permute-start.12 = (bf16[2048,256]{1,0:T(8,128)(2,1)S(1)}, bf16[2048,256]{1,0:T(8,128)(2,1)S(1)}, u32[]{:S(2)}, u32[]{:S(2)}) collective-permute-start(bf16[2048,256]{1,0:T(8,128)(2,1)S(1)} %slice.188), channel_id=1, source_target_pairs={{0,12},{1,13},{2,14},{3,15},{4,8},{5,9},{6,10},{7,11},{8,4},{9,5},... | collective-permute-start | bytes 3145736 | tf_op jit(solution)/shard_map/ppermute | solution.py:157
  152.3 26.6 %collective-permute-start.13 = (bf16[2048,256]{1,0:T(8,128)(2,1)S(1)}, bf16[2048,256]{1,0:T(8,128)(2,1)S(1)}, u32[]{:S(2)}, u32[]{:S(2)}) collective-permute-start(bf16[2048,256]{1,0:T(8,128)(2,1)S(1)} %slice.189), channel_id=1, source_target_pairs={{0,3},{1,2},{2,1},{3,0},{4,7},{5,6},{6,5},{7,4},{8,11},{9,10},{10,... | collective-permute-start | bytes 3145736 | tf_op jit(solution)/shard_map/ppermute | solution.py:157
  155.1 5.1 collective-permute-start.7
  160.1 5.1 collective-permute-start.8
  188.1 5.2 collective-permute-start.16
  195.0 8.0 %collective-permute-start.17 = (bf16[64,1024]{1,0:T(8,128)(2,1)S(1)}, bf16[64,1024]{1,0:T(8,128)(2,1)S(1)}, u32[]{:S(2)}, u32[]{:S(2)}) collective-permute-start(bf16[64,1024]{1,0:T(8,128)(2,1)S(1)} %get-tuple-element.97), channel_id=1, source_target_pairs={{0,32},{1,33},{2,34},{3,35},{4,36},{5,37},{6,38},{7,39},{8,40},{9,... | collective-permute-start | bytes 393224 | tf_op jit(solution)/shard_map/ppermute | solution.py:157
  208.9 5.1 collective-permute-start.20
  214.0 5.1 collective-permute-start.21
  229.6 5.1 collective-permute-start.25
  234.7 14.3 %collective-permute-start.26 = (bf16[64,1024]{1,0:T(8,128)(2,1)S(1)}, bf16[64,1024]{1,0:T(8,128)(2,1)S(1)}, u32[]{:S(2)}, u32[]{:S(2)}) collective-permute-start(bf16[64,1024]{1,0:T(8,128)(2,1)S(1)} %add_convert_fusion.42), channel_id=1, source_target_pairs={{0,32},{1,33},{2,34},{3,35},{4,36},{5,37},{6,38},{7,39},{8,40},{9,... | collective-permute-start | bytes 393224 | tf_op jit(solution)/shard_map/ppermute | solution.py:157
  255.0 5.1 collective-permute-start.29
  260.1 5.1 collective-permute-start.30
  270.8 5.1 collective-permute-start.33
  275.8 5.1 collective-permute-start.34
  281.0 6.3 %collective-permute-start.35 = (bf16[64,1024]{1,0:T(8,128)(2,1)S(1)}, bf16[64,1024]{1,0:T(8,128)(2,1)S(1)}, u32[]{:S(2)}, u32[]{:S(2)}) collective-permute-start(bf16[64,1024]{1,0:T(8,128)(2,1)S(1)} %add_convert_fusion.36), channel_id=1, source_target_pairs={{0,32},{1,33},{2,34},{3,35},{4,36},{5,37},{6,38},{7,39},{8,40},{9,... | collective-permute-start | bytes 393224 | tf_op jit(solution)/shard_map/ppermute | solution.py:157
  293.2 5.1 collective-permute-start.38
  313.8 5.1 collective-permute-start.43
  318.9 9.5 %collective-permute-start.44 = (bf16[64,1024]{1,0:T(8,128)(2,1)S(1)}, bf16[64,1024]{1,0:T(8,128)(2,1)S(1)}, u32[]{:S(2)}, u32[]{:S(2)}) collective-permute-start(bf16[64,1024]{1,0:T(8,128)(2,1)S(1)} %add_convert_fusion.30), channel_id=1, source_target_pairs={{0,32},{1,33},{2,34},{3,35},{4,36},{5,37},{6,38},{7,39},{8,40},{9,... | collective-permute-start | bytes 393224 | tf_op jit(solution)/shard_map/ppermute | solution.py:157
  334.4 5.1 collective-permute-start.47
  355.1 5.1 collective-permute-start.52
  360.2 6.3 %collective-permute-start.53 = (bf16[64,1024]{1,0:T(8,128)(2,1)S(1)}, bf16[64,1024]{1,0:T(8,128)(2,1)S(1)}, u32[]{:S(2)}, u32[]{:S(2)}) collective-permute-start(bf16[64,1024]{1,0:T(8,128)(2,1)S(1)} %add_convert_fusion.24), channel_id=1, source_target_pairs={{0,32},{1,33},{2,34},{3,35},{4,36},{5,37},{6,38},{7,39},{8,40},{9,... | collective-permute-start | bytes 393224 | tf_op jit(solution)/shard_map/ppermute | solution.py:157
  372.4 5.1 collective-permute-start.56
  377.5 5.1 collective-permute-start.57
  388.2 5.1 collective-permute-start.60
  393.2 5.1 collective-permute-start.61
  398.4 9.5 %collective-permute-start.62 = (bf16[64,1024]{1,0:T(8,128)(2,1)S(1)}, bf16[64,1024]{1,0:T(8,128)(2,1)S(1)}, u32[]{:S(2)}, u32[]{:S(2)}) collective-permute-start(bf16[64,1024]{1,0:T(8,128)(2,1)S(1)} %add_convert_fusion.18), channel_id=1, source_target_pairs={{0,32},{1,33},{2,34},{3,35},{4,36},{5,37},{6,38},{7,39},{8,40},{9,... | collective-permute-start | bytes 393224 | tf_op jit(solution)/shard_map/ppermute | solution.py:157
  413.8 5.1 collective-permute-start.65
  429.3 5.1 collective-permute-start.69
  434.4 5.1 collective-permute-start.70
  439.6 27.3 %collective-permute-start.71 = (bf16[64,1024]{1,0:T(8,128)(2,1)S(1)}, bf16[64,1024]{1,0:T(8,128)(2,1)S(1)}, u32[]{:S(2)}, u32[]{:S(2)}) collective-permute-start(bf16[64,1024]{1,0:T(8,128)(2,1)S(1)} %add_convert_fusion.12), channel_id=1, source_target_pairs={{0,32},{1,33},{2,34},{3,35},{4,36},{5,37},{6,38},{7,39},{8,40},{9,... | collective-permute-start | bytes 393224 | tf_op jit(solution)/shard_map/ppermute | solution.py:157
  476.9 5.1 collective-permute-start.74
  501.6 16.1 %collective-permute-start.77 = (bf16[64,1024]{1,0:T(8,128)(2,1)}, bf16[64,1024]{1,0:T(8,128)(2,1)}, u32[]{:S(2)}, u32[]{:S(2)}) collective-permute-start(bf16[64,1024]{1,0:T(8,128)(2,1)} %get-tuple-element.78), channel_id=1, source_target_pairs={{0,16},{1,17},{2,18},{3,19},{4,20},{5,21},{6,22},{7,23},{8,24},{9,... | collective-permute-start | bytes 393224 | tf_op jit(solution)/shard_map/ppermute | solution.py:157
  519.4 5.3 collective-permute-start.78
  525.7 5.1 collective-permute-start.79
  531.7 6.3 %collective-permute-start.80 = (bf16[64,1024]{1,0:T(8,128)(2,1)S(1)}, bf16[64,1024]{1,0:T(8,128)(2,1)S(1)}, u32[]{:S(2)}, u32[]{:S(2)}) collective-permute-start(bf16[64,1024]{1,0:T(8,128)(2,1)S(1)} %add_convert_fusion.6), channel_id=1, source_target_pairs={{0,32},{1,33},{2,34},{3,35},{4,36},{5,37},{6,38},{7,39},{8,40},{9,... | collective-permute-start | bytes 393224 | tf_op jit(solution)/shard_map/ppermute | solution.py:157
  548.8 5.1 collective-permute-start.83
  573.5 5.1 collective-permute-start.88
  580.2 5.5 collective-permute-start.90
  580.9 10.4 %collective-permute-start.91 = (bf16[2,16,1024]{2,1,0:T(8,128)(2,1)S(1)}, bf16[2,16,1024]{2,1,0:T(8,128)(2,1)S(1)}, u32[]{:S(2)}, u32[]{:S(2)}) collective-permute-start(bf16[2,16,1024]{2,1,0:T(8,128)(2,1)S(1)} %get-tuple-element.114), channel_id=1, source_target_pairs={{0,4},{1,5},{2,8},{3,9},{4,14},{5,15},{6,2},{7,3},{8,12},{9,13},{1... | collective-permute-start | bytes 196616 | tf_op jit(solution)/shard_map/ppermute | solution.py:157
  (83 other events, 660.8 us)
Sparse Core Ops, SparseCore 0:
  21.8 45.6 all-gather.1

commit v6 on v4

--- a/solution.py
+++ b/solution.py
@@ -16,16 +16,13 @@
 
 
 def layer_kernel(turn, place_ref, mine_ref, other_ref, gain_ref, bias_ref, *refs):
-    own, from_x, from_y, top, bottom = refs[:5]
-    keep_ref, send_ref = refs[5:]
-    model, width = mine_ref.shape[1], own.shape[1]
+    weights, (keep_ref, send_ref) = refs[:8], refs[8:]
+    model, width = mine_ref.shape[1], weights[0].shape[1]
     plane, core, start = place_ref[0], place_ref[1], place_ref[2]
     micro = turn - plane
 
     def weight(j, n, row, rows):
-        if j < 3:
-            return (own, from_x, from_y)[j][pl.ds(n * model + row, rows)]
-        return (top if n < 2 else bottom)[pl.ds((n % 2) * model + row, rows)]
+        return weights[2 * j + n // 2][pl.ds((n % 2) * model + row, rows)]
 
     @pl.when((micro >= 0) & (micro < bias_ref.shape[0]))
     def _():
@@ -82,7 +79,7 @@
     return pl.pallas_call(
         functools.partial(layer_kernel, turn),
         out_shape=(half, half),
-        in_specs=[pl.BlockSpec(memory_space=pltpu.SMEM)] + [vmem] * 9,
+        in_specs=[pl.BlockSpec(memory_space=pltpu.SMEM)] + [vmem] * 12,
         out_specs=(vmem, vmem),
         compiler_params=pltpu.CompilerParams(vmem_limit_bytes=16 * 1024 * 1024),
         cost_estimate=pl.CostEstimate(
@@ -164,14 +161,15 @@
         cols = slice(h * width, (h + 1) * width)
         rows = w_output[0, cols]
         blocks = [rows[:, b * width : (b + 1) * width] for b in range(model // width)]
-        return jnp.concatenate(
-            [w_query[0, :, cols], w_key[0, :, cols], w_value[0, :, cols]] + blocks, axis=0
+        return (
+            jnp.concatenate([w_query[0, :, cols], w_key[0, :, cols]], axis=0),
+            jnp.concatenate([w_value[0, :, cols]] + blocks, axis=0),
         )
 
     first = core == 0
     low, high = pack(0), pack(1)
-    kept = jnp.where(first, low, high)
-    got = swap_cores(jnp.where(first, high, low))
+    kept = [jnp.where(first, p, q) for p, q in zip(low, high)]
+    got = [swap_cores(jnp.where(first, q, p)) for p, q in zip(low, high)]
     got_gain = swap_cores(norm_gain)
     gain_a, gain_b = jnp.where(first, norm_gain, got_gain), jnp.where(first, got_gain, norm_gain)
 
@@ -181,14 +179,17 @@
     def over_y(value):
         return move(value, lambda s, a, b: (s, a ^ 3, b))
 
-    cut = low.shape[0] // 2
-    own_a, own_b = jnp.where(first, kept, got), jnp.where(first, got, kept)
-    x_a, y_a = over_x(own_a), over_y(own_a)
-    weights_a = [own_a, x_a, y_a, over_y(x_a[:cut]), over_x(y_a[cut:])]
-    own_b, weights_a[3], weights_a[4] = lax.optimization_barrier(
-        (own_b, weights_a[3], weights_a[4])
-    )
-    x_b, y_b = over_x(own_b), over_y(own_b)
+    def gather(top, bottom):
+        x_top, y_bottom = over_x(top), over_y(bottom)
+        top, bottom, x_top, y_bottom = lax.optimization_barrier((top, bottom, x_top, y_bottom))
+        far_top, far_bottom = over_y(x_top), over_x(y_bottom)
+        y_top, x_bottom = over_y(top), over_x(bottom)
+        return [top, bottom, x_top, x_bottom, y_top, y_bottom, far_top, far_bottom]
+
+    weights_a = gather(*[jnp.where(first, p, q) for p, q in zip(kept, got)])
+    own_b = [jnp.where(first, q, p) for p, q in zip(kept, got)]
+    own_b, weights_a[6:] = lax.optimization_barrier((own_b, weights_a[6:]))
+    weights_b = gather(*own_b)
 
     inputs_all = lax.all_gather(inputs, "dp", axis=1, tiled=True)
     window_mine = lax.dynamic_slice_in_dim(inputs_all, start + HALF * core, HALF, 1)
@@ -235,13 +236,9 @@
                 stash[layer][m] = jnp.where(plane == turn - m, found, stash[layer][m])
 
     mine, other = window_mine[0], window_other[0]
-    weights_b = None
     turns = planes + micro_count - 1
     for turn in range(turns):
         out_a = one_layer(turn, mine, other, gain_a, weights_a)
-        if weights_b is None:
-            x_b, y_b, out_a = lax.optimization_barrier((x_b, y_b, out_a))
-            weights_b = [own_b, x_b, y_b, over_y(x_b[:cut]), over_x(y_b[cut:])]
         out_b = one_layer(turn, out_a, swap_cores(out_a), gain_b, weights_b)
         if turn < turns - 1:
             onward = (

time: 596 us -> 572 us (0.960)
  waiting for transfers between devices: 321 us -> 306 us
  Pallas kernels: 67.5 us -> 60.9 us
    ppermute x110 -> x115, waiting for transfers between devices: 321 us -> 306 us  [move(): return lax.ppermute(value, AXES, pairs)]
    slice x4 -> x0, local copies, waits for them, and re-layouts: 7.13 us -> none  [the longest x2 4.54 us: shards(): weights_a = [own_a, x_a, y_a, over_y(x_a[:cut]), over_x(y_a[cut:])]]
    pallas_call x18, Pallas kernels: 67.5 us -> 60.9 us  [run_layer(): pl.pallas_call(functools.partial(layer_kernel, turn), out_shape=(half, ha...]
    ppermute x110 -> x115, starting transfers between devices: 129 us -> 132 us  [move(): return lax.ppermute(value, AXES, pairs)]
  transfers between devices with their start and end apart: 111 -> 116, of which waited for: 89 -> 90; matrix products, arithmetic and copies ran while one was open for 3% -> 2% of each run, Pallas kernels for 1% -> 1%
where the time goes in v6:
time: 572 us; the launch traced here: 563 us
  waiting for transfers between devices  306 us (53%)
  starting transfers between devices  132 us (23%)
  Pallas kernels  60.9 us (11%)
  between operations  33.8 us (6%)
  other arithmetic  16.3 us (3%)
  local copies, waits for them, and re-layouts  13.5 us (2%)
    ppermute x115, waiting for transfers between devices, move(): return lax.ppermute(value, AXES, pairs)  306 us
    ppermute x115, starting transfers between devices, move(): return lax.ppermute(value, AXES, pairs)  132 us
    pallas_call x18, Pallas kernels, run_layer(): pl.pallas_call(functools.partial(layer_kernel, turn), out_shape=(half, ha...  60.9 us
  transfers between devices with their start and end apart: 116, of which 90 were waited for; matrix products, arithmetic and copies ran while one was open for 2% of the time, Pallas kernels for 1%

profile of v6, /device:TPU:224, one launch (start us, length us, event | category | flops | bytes accessed | tf_op | source)
XLA Modules:
  0.0 562.9 jit_solution(14831687139453230788)
XLA Ops:
  15.8 3.0 collective-permute-start.4
  19.2 20.1 %collective-permute-done.3.refs_2_ = bf16[2048,256]{1,0:T(8,128)(2,1)} collective-permute-done((bf16[2048,256]{1,0:T(8,128)(2,1)S(1)}, bf16[2048,256]{1,0:T(8,128)(2,1)}, u32[]{:S(2)}, u32[]{:S(2)}) %collective-permute-start.3) | collective-permute-done | bytes 1048608 | tf_op jit(solution)/shard_map/ppermute | solution.py:154
  39.3 4.1 collective-permute-done.4.refs_5_
  43.4 3.0 collective-permute-start.7
  54.4 20.8 %collective-permute-done.7.refs_6_ = bf16[2048,256]{1,0:T(8,128)(2,1)} collective-permute-done((bf16[2048,256]{1,0:T(8,128)(2,1)}, bf16[2048,256]{1,0:T(8,128)(2,1)}, u32[]{:S(2)}, u32[]{:S(2)}) %collective-permute-start.7) | collective-permute-done | bytes 1048608 | tf_op jit(solution)/shard_map/ppermute | solution.py:154
  75.2 3.0 collective-permute-done.8.refs_7_
  81.8 15.9 %collective-permute-done.6.refs_4_ = bf16[2048,256]{1,0:T(8,128)(2,1)} collective-permute-done((bf16[2048,256]{1,0:T(8,128)(2,1)S(1)}, bf16[2048,256]{1,0:T(8,128)(2,1)}, u32[]{:S(2)}, u32[]{:S(2)}) %collective-permute-start.6) | collective-permute-done | bytes 1048608 | tf_op jit(solution)/shard_map/ppermute | solution.py:154
  97.7 3.0 collective-permute-done.5.refs_3_
  100.6 3.1 shard_map.100
  103.9 16.9 %collective-permute-done.14.refs_2_ = bf16[2048,256]{1,0:T(8,128)(2,1)} collective-permute-done((bf16[2048,256]{1,0:T(8,128)(2,1)S(1)}, bf16[2048,256]{1,0:T(8,128)(2,1)}, u32[]{:S(2)}, u32[]{:S(2)}) %collective-permute-start.14) | collective-permute-done | bytes 1048608 | tf_op jit(solution)/shard_map/ppermute | solution.py:154
  123.3 2.9 collective-permute-start.18
  127.9 5.0 collective-permute-done.12
  132.9 6.2 %collective-permute-done.11 = bf16[64,1024]{1,0:T(8,128)(2,1)S(1)} collective-permute-done((bf16[64,1024]{1,0:T(8,128)(2,1)S(1)}, bf16[64,1024]{1,0:T(8,128)(2,1)S(1)}, u32[]{:S(2)}, u32[]{:S(2)}) %collective-permute-start.11) | collective-permute-done | bytes 131104 | tf_op jit(solution)/shard_map/ppermute | solution.py:154
  139.1 5.9 %collective-permute-done.10 = bf16[64,1024]{1,0:T(8,128)(2,1)S(1)} collective-permute-done((bf16[64,1024]{1,0:T(8,128)(2,1)S(1)}, bf16[64,1024]{1,0:T(8,128)(2,1)S(1)}, u32[]{:S(2)}, u32[]{:S(2)}) %collective-permute-start.10) | collective-permute-done | bytes 131104 | tf_op jit(solution)/shard_map/ppermute | solution.py:154
  149.0 18.3 %collective-permute-done.18.refs_6_ = bf16[2048,256]{1,0:T(8,128)(2,1)S(1)} collective-permute-done((bf16[2048,256]{1,0:T(8,128)(2,1)}, bf16[2048,256]{1,0:T(8,128)(2,1)S(1)}, u32[]{:S(2)}, u32[]{:S(2)}) %collective-permute-start.18) | collective-permute-done | bytes 1048608 | tf_op jit(solution)/shard_map/ppermute | solution.py:154
  171.8 3.4 collective-permute-start.21
  175.2 3.0 collective-permute-done.23
  184.1 3.0 collective-permute-done.24.mine_ref
  188.4 3.3 shard_map.102
  199.2 4.0 collective-permute-done.28
  211.4 2.9 collective-permute-done.34
  216.4 11.3 %collective-permute-start.35 = (bf16[64,1024]{1,0:T(8,128)(2,1)S(1)}, bf16[64,1024]{1,0:T(8,128)(2,1)S(1)}, u32[]{:S(2)}, u32[]{:S(2)}) collective-permute-start(bf16[64,1024]{1,0:T(8,128)(2,1)S(1)} %add_convert_fusion.28), channel_id=1, source_target_pairs={{0,32},{1,33},{2,34},{3,35},{4,36},{5,37},{6,38},{7,39},{8,40},{9,... | collective-permute-start | bytes 393224 | tf_op jit(solution)/shard_map/ppermute | solution.py:154
  231.7 3.1 shard_map.104
  241.9 4.4 collective-permute-done.39
  259.6 3.7 collective-permute-start.46
  267.1 3.1 shard_map.106
  277.6 3.9 collective-permute-done.50
  295.2 7.0 %collective-permute-start.57 = (bf16[64,1024]{1,0:T(8,128)(2,1)S(1)}, bf16[64,1024]{1,0:T(8,128)(2,1)S(1)}, u32[]{:S(2)}, u32[]{:S(2)}) collective-permute-start(bf16[64,1024]{1,0:T(8,128)(2,1)S(1)} %add_convert_fusion.20), channel_id=1, source_target_pairs={{0,32},{1,33},{2,34},{3,35},{4,36},{5,37},{6,38},{7,39},{8,40},{9,... | collective-permute-start | bytes 393224 | tf_op jit(solution)/shard_map/ppermute | solution.py:154
  306.0 3.1 shard_map.108
  316.5 3.9 collective-permute-done.61
  328.8 2.9 collective-permute-done.67
  333.9 3.7 collective-permute-start.68
  341.5 3.1 shard_map.110
  351.9 3.9 collective-permute-done.72
  369.4 7.0 %collective-permute-start.79 = (bf16[64,1024]{1,0:T(8,128)(2,1)S(1)}, bf16[64,1024]{1,0:T(8,128)(2,1)S(1)}, u32[]{:S(2)}, u32[]{:S(2)}) collective-permute-start(bf16[64,1024]{1,0:T(8,128)(2,1)S(1)} %add_convert_fusion.12), channel_id=1, source_target_pairs={{0,32},{1,33},{2,34},{3,35},{4,36},{5,37},{6,38},{7,39},{8,40},{9,... | collective-permute-start | bytes 393224 | tf_op jit(solution)/shard_map/ppermute | solution.py:154
  380.2 3.1 shard_map.112
  390.6 3.9 collective-permute-done.83
  408.9 3.7 collective-permute-start.90
  413.1 23.1 %collective-permute-done.90.mine_ref = bf16[64,1024]{1,0:T(8,128)(2,1)} collective-permute-done((bf16[64,1024]{1,0:T(8,128)(2,1)S(1)}, bf16[64,1024]{1,0:T(8,128)(2,1)}, u32[]{:S(2)}, u32[]{:S(2)}) %collective-permute-start.90) | collective-permute-done | bytes 131104 | tf_op jit(solution)/shard_map/ppermute | solution.py:154
  439.8 7.9 %shard_map.114 = (bf16[64,1024]{1,0:T(8,128)(2,1)S(1)}, bf16[64,1024]{1,0:T(8,128)(2,1)}) custom-call(s32[5]{0:T(128)S(1)} %pad_add_fusion.1.place_ref, bf16[64,1024]{1,0:T(8,128)(2,1)} %collective-permute-done.90.mine_ref, bf16[64,1024]{1,0:T(8,128)(2,1)} %collective-permute-done.91.other_ref, f32[1,1024]{1,0:T(1,128)S(1)} %get-tuple-element.176.gain_ref, ...), custom_call_target="tpu_custom_call" | custom-call | flops 1073741824 | bytes 8388608 | tf_op jit(solution)/shard_map/pallas_call | solution.py:79
  472.5 3.6 collective-permute-done.94
  482.4 5.8 %shard_map.115 = (bf16[64,1024]{1,0:T(8,128)(2,1)S(1)}, bf16[64,1024]{1,0:T(8,128)(2,1)S(1)}) custom-call(s32[5]{0:T(128)S(1)} %pad_add_fusion.1.place_ref, bf16[64,1024]{1,0:T(8,128)(2,1)S(1)} %add_convert_fusion.6.mine_ref, bf16[64,1024]{1,0:T(8,128)(2,1)S(1)} %collective-permute-done.96.other_ref, f32[1,1024]{1,0:T(1,128)S(1)} %get-tuple-element.175.gain_ref, ...), custom_call_target="tpu_custom_call" | custom-call | flops 1073741824 | bytes 8388608 | tf_op jit(solution)/shard_map/pallas_call | solution.py:79
  498.6 6.1 %collective-permute-done.101.mine_ref = bf16[64,1024]{1,0:T(8,128)(2,1)S(1)} collective-permute-done((bf16[64,1024]{1,0:T(8,128)(2,1)S(1)}, bf16[64,1024]{1,0:T(8,128)(2,1)S(1)}, u32[]{:S(2)}, u32[]{:S(2)}) %collective-permute-start.101) | collective-permute-done | bytes 131104 | tf_op jit(solution)/shard_map/ppermute | solution.py:154
  506.1 7.2 %shard_map.116 = (bf16[64,1024]{1,0:T(8,128)(2,1)S(1)}, bf16[64,1024]{1,0:T(8,128)(2,1)S(1)}) custom-call(s32[5]{0:T(128)S(1)} %pad_add_fusion.1.place_ref, bf16[64,1024]{1,0:T(8,128)(2,1)S(1)} %collective-permute-done.101.mine_ref, bf16[64,1024]{1,0:T(8,128)(2,1)S(1)} %collective-permute-done.102.other_ref, f32[1,1024]{1,0:T(1,128)S(1)} %get-tuple-element.176.gain_ref, ...), custom_call_target="tpu_custom_call" | custom-call | flops 1073741824 | bytes 8388608 | tf_op jit(solution)/shard_map/pallas_call | solution.py:79
  520.6 3.9 collective-permute-done.105
  526.1 5.8 %shard_map.117 = (bf16[64,1024]{1,0:T(8,128)(2,1)S(1)}, bf16[64,1024]{1,0:T(8,128)(2,1)S(1)}) custom-call(s32[5]{0:T(128)S(1)} %pad_add_fusion.1.place_ref, bf16[64,1024]{1,0:T(8,128)(2,1)S(1)} %add_convert_fusion.2.mine_ref, bf16[64,1024]{1,0:T(8,128)(2,1)S(1)} %collective-permute-done.107.other_ref, f32[1,1024]{1,0:T(1,128)S(1)} %get-tuple-element.175.gain_ref, ...), custom_call_target="tpu_custom_call" | custom-call | flops 1073741824 | bytes 8388608 | tf_op jit(solution)/shard_map/pallas_call | solution.py:79
  544.3 5.2 collective-permute-start.114
  549.5 5.6 collective-permute-done.114
  (405 shorter events, 229.4 us)
Async XLA Ops:
  6.5 74.2 %all-gather.2.cloned.1.call-start = ((), (), s32[]{:S(2)}) async-start(), calls=%async_computation | async-start | bytes 1114112 | tf_op jit(solution)/shard_map/all_gather | solution.py:194
  11.8 27.5 %collective-permute-start.3 = (bf16[2048,256]{1,0:T(8,128)(2,1)S(1)}, bf16[2048,256]{1,0:T(8,128)(2,1)}, u32[]{:S(2)}, u32[]{:S(2)}) collective-permute-start(bf16[2048,256]{1,0:T(8,128)(2,1)S(1)} %get-tuple-element.53.refs_0_), channel_id=1, source_target_pairs={{0,3},{1,2},{2,1},{3,0},{4,7},{5,6},{6,5},{7,4},{8,11},{9,10},{10,... | collective-permute-start | bytes 3145736 | tf_op jit(solution)/shard_map/ppermute | solution.py:154
  15.8 27.6 %collective-permute-start.4 = (bf16[2048,256]{1,0:T(8,128)(2,1)}, bf16[2048,256]{1,0:T(8,128)(2,1)}, u32[]{:S(2)}, u32[]{:S(2)}) collective-permute-start(bf16[2048,256]{1,0:T(8,128)(2,1)} %get-tuple-element.54.refs_1_), channel_id=1, source_target_pairs={{0,12},{1,13},{2,14},{3,15},{4,8},{5,9},{6,10},{7,11},{8,4},{9,5},... | collective-permute-start | bytes 3145736 | tf_op jit(solution)/shard_map/ppermute | solution.py:154
  18.9 61.9 %collective-permute-start = (f32[1,1024]{1,0:T(1,128)S(1)}, f32[1,1024]{1,0:T(1,128)S(1)}, u32[]{:S(2)}, u32[]{:S(2)}) collective-permute-start(f32[1,1024]{1,0:T(1,128)S(1)} %copy-done.44), channel_id=1, source_target_pairs={{0,16},{1,17},{2,18},{3,19},{4,20},{5,21},{6,22},{7,23},{8,24},{9,... | collective-permute-start | bytes 12296 | tf_op jit(solution)/shard_map/ppermute | solution.py:154
  43.4 31.8 %collective-permute-start.7 = (bf16[2048,256]{1,0:T(8,128)(2,1)}, bf16[2048,256]{1,0:T(8,128)(2,1)}, u32[]{:S(2)}, u32[]{:S(2)}) collective-permute-start(bf16[2048,256]{1,0:T(8,128)(2,1)} %collective-permute-done.3.refs_2_), channel_id=1, source_target_pairs={{0,12},{1,13},{2,14},{3,15},{4,8},{5,9},{6,10},{7,11},{8,4},{9,5},... | collective-permute-start | bytes 3145736 | tf_op jit(solution)/shard_map/ppermute | solution.py:154
  46.3 31.8 %collective-permute-start.8 = (bf16[2048,256]{1,0:T(8,128)(2,1)}, bf16[2048,256]{1,0:T(8,128)(2,1)}, u32[]{:S(2)}, u32[]{:S(2)}) collective-permute-start(bf16[2048,256]{1,0:T(8,128)(2,1)} %collective-permute-done.4.refs_5_), channel_id=1, source_target_pairs={{0,3},{1,2},{2,1},{3,0},{4,7},{5,6},{6,5},{7,4},{8,11},{9,10},{10,... | collective-permute-start | bytes 3145736 | tf_op jit(solution)/shard_map/ppermute | solution.py:154
  52.1 45.6 %collective-permute-start.6 = (bf16[2048,256]{1,0:T(8,128)(2,1)S(1)}, bf16[2048,256]{1,0:T(8,128)(2,1)}, u32[]{:S(2)}, u32[]{:S(2)}) collective-permute-start(bf16[2048,256]{1,0:T(8,128)(2,1)S(1)} %get-tuple-element.53.refs_0_), channel_id=1, source_target_pairs={{0,12},{1,13},{2,14},{3,15},{4,8},{5,9},{6,10},{7,11},{8,4},{9,5},... | collective-permute-start | bytes 3145736 | tf_op jit(solution)/shard_map/ppermute | solution.py:154
  52.4 48.3 %collective-permute-start.5 = (bf16[2048,256]{1,0:T(8,128)(2,1)}, bf16[2048,256]{1,0:T(8,128)(2,1)}, u32[]{:S(2)}, u32[]{:S(2)}) collective-permute-start(bf16[2048,256]{1,0:T(8,128)(2,1)} %get-tuple-element.54.refs_1_), channel_id=1, source_target_pairs={{0,3},{1,2},{2,1},{3,0},{4,7},{5,6},{6,5},{7,4},{8,11},{9,10},{10,... | collective-permute-start | bytes 3145736 | tf_op jit(solution)/shard_map/ppermute | solution.py:154
  78.2 42.6 %collective-permute-start.14 = (bf16[2048,256]{1,0:T(8,128)(2,1)S(1)}, bf16[2048,256]{1,0:T(8,128)(2,1)}, u32[]{:S(2)}, u32[]{:S(2)}) collective-permute-start(bf16[2048,256]{1,0:T(8,128)(2,1)S(1)} %get-tuple-element.63.refs_0_), channel_id=1, source_target_pairs={{0,3},{1,2},{2,1},{3,0},{4,7},{5,6},{6,5},{7,4},{8,11},{9,10},{10,... | collective-permute-start | bytes 3145736 | tf_op jit(solution)/shard_map/ppermute | solution.py:154
  79.5 41.3 %collective-permute-start.15 = (bf16[2048,256]{1,0:T(8,128)(2,1)S(1)}, bf16[2048,256]{1,0:T(8,128)(2,1)}, u32[]{:S(2)}, u32[]{:S(2)}) collective-permute-start(bf16[2048,256]{1,0:T(8,128)(2,1)S(1)} %get-tuple-element.64.refs_1_), channel_id=1, source_target_pairs={{0,12},{1,13},{2,14},{3,15},{4,8},{5,9},{6,10},{7,11},{8,4},{9,5},... | collective-permute-start | bytes 3145736 | tf_op jit(solution)/shard_map/ppermute | solution.py:154
  103.8 24.0 %collective-permute-start.9 = (bf16[64,1024]{1,0:T(8,128)(2,1)S(1)}, bf16[64,1024]{1,0:T(8,128)(2,1)S(1)}, u32[]{:S(2)}, u32[]{:S(2)}) collective-permute-start(bf16[64,1024]{1,0:T(8,128)(2,1)S(1)} %get-tuple-element.60), channel_id=1, source_target_pairs={{0,16},{1,17},{2,18},{3,19},{4,20},{5,21},{6,22},{7,23},{8,24},{9,... | collective-permute-start | bytes 393224 | tf_op jit(solution)/shard_map/ppermute | solution.py:154
  120.8 27.3 %collective-permute-start.17 = (bf16[2048,256]{1,0:T(8,128)(2,1)S(1)}, bf16[2048,256]{1,0:T(8,128)(2,1)S(1)}, u32[]{:S(2)}, u32[]{:S(2)}) collective-permute-start(bf16[2048,256]{1,0:T(8,128)(2,1)S(1)} %get-tuple-element.63.refs_0_), channel_id=1, source_target_pairs={{0,12},{1,13},{2,14},{3,15},{4,8},{5,9},{6,10},{7,11},{8,4},{9,5},... | collective-permute-start | bytes 3145736 | tf_op jit(solution)/shard_map/ppermute | solution.py:154
  121.2 27.8 %collective-permute-start.16 = (bf16[2048,256]{1,0:T(8,128)(2,1)S(1)}, bf16[2048,256]{1,0:T(8,128)(2,1)S(1)}, u32[]{:S(2)}, u32[]{:S(2)}) collective-permute-start(bf16[2048,256]{1,0:T(8,128)(2,1)S(1)} %get-tuple-element.64.refs_1_), channel_id=1, source_target_pairs={{0,3},{1,2},{2,1},{3,0},{4,7},{5,6},{6,5},{7,4},{8,11},{9,10},{10,... | collective-permute-start | bytes 3145736 | tf_op jit(solution)/shard_map/ppermute | solution.py:154
  123.3 44.0 %collective-permute-start.18 = (bf16[2048,256]{1,0:T(8,128)(2,1)}, bf16[2048,256]{1,0:T(8,128)(2,1)S(1)}, u32[]{:S(2)}, u32[]{:S(2)}) collective-permute-start(bf16[2048,256]{1,0:T(8,128)(2,1)} %collective-permute-done.14.refs_2_), channel_id=1, source_target_pairs={{0,12},{1,13},{2,14},{3,15},{4,8},{5,9},{6,10},{7,11},{8,4},{9,5},... | collective-permute-start | bytes 3145736 | tf_op jit(solution)/shard_map/ppermute | solution.py:154
  126.2 41.9 %collective-permute-start.19 = (bf16[2048,256]{1,0:T(8,128)(2,1)}, bf16[2048,256]{1,0:T(8,128)(2,1)S(1)}, u32[]{:S(2)}, u32[]{:S(2)}) collective-permute-start(bf16[2048,256]{1,0:T(8,128)(2,1)} %collective-permute-done.15.refs_5_), channel_id=1, source_target_pairs={{0,3},{1,2},{2,1},{3,0},{4,7},{5,6},{6,5},{7,4},{8,11},{9,10},{10,... | collective-permute-start | bytes 3145736 | tf_op jit(solution)/shard_map/ppermute | solution.py:154
  171.7 8.6 %collective-permute-start.22 = (bf16[64,1024]{1,0:T(8,128)(2,1)S(1)}, bf16[64,1024]{1,0:T(8,128)(2,1)}, u32[]{:S(2)}, u32[]{:S(2)}) collective-permute-start(bf16[64,1024]{1,0:T(8,128)(2,1)S(1)} %add_convert_fusion.33), channel_id=1, source_target_pairs={{0,4},{1,5},{2,6},{3,7},{4,0},{5,1},{6,2},{7,3},{8,12},{9,13},{10,... | collective-permute-start | bytes 393224 | tf_op jit(solution)/shard_map/ppermute | solution.py:154
  171.8 8.5 %collective-permute-start.21 = (bf16[64,1024]{1,0:T(8,128)(2,1)S(1)}, bf16[64,1024]{1,0:T(8,128)(2,1)}, u32[]{:S(2)}, u32[]{:S(2)}) collective-permute-start(bf16[64,1024]{1,0:T(8,128)(2,1)S(1)} %add_convert_fusion.33), channel_id=1, source_target_pairs={{0,5},{1,4},{2,7},{3,6},{4,1},{5,0},{6,3},{7,2},{8,13},{9,12},{10,... | collective-permute-start | bytes 393224 | tf_op jit(solution)/shard_map/ppermute | solution.py:154
  195.1 8.1 %collective-permute-start.28 = (bf16[64,1024]{1,0:T(8,128)(2,1)S(1)}, bf16[64,1024]{1,0:T(8,128)(2,1)S(1)}, u32[]{:S(2)}, u32[]{:S(2)}) collective-permute-start(bf16[64,1024]{1,0:T(8,128)(2,1)S(1)} %add_convert_fusion.31), channel_id=1, source_target_pairs={{0,4},{1,5},{2,6},{3,7},{4,0},{5,1},{6,2},{7,3},{8,12},{9,13},{10,... | collective-permute-start | bytes 393224 | tf_op jit(solution)/shard_map/ppermute | solution.py:154
  195.4 7.8 %collective-permute-start.27 = (bf16[64,1024]{1,0:T(8,128)(2,1)S(1)}, bf16[64,1024]{1,0:T(8,128)(2,1)S(1)}, u32[]{:S(2)}, u32[]{:S(2)}) collective-permute-start(bf16[64,1024]{1,0:T(8,128)(2,1)S(1)} %add_convert_fusion.31), channel_id=1, source_target_pairs={{0,5},{1,4},{2,7},{3,6},{4,1},{5,0},{6,3},{7,2},{8,13},{9,12},{10,... | collective-permute-start | bytes 393224 | tf_op jit(solution)/shard_map/ppermute | solution.py:154
  208.3 8.1 %collective-permute-start.33 = (bf16[64,1024]{1,0:T(8,128)(2,1)S(1)}, bf16[64,1024]{1,0:T(8,128)(2,1)S(1)}, u32[]{:S(2)}, u32[]{:S(2)}) collective-permute-start(bf16[64,1024]{1,0:T(8,128)(2,1)S(1)} %add_convert_fusion.29), channel_id=1, source_target_pairs={{0,4},{1,5},{2,6},{3,7},{4,0},{5,1},{6,2},{7,3},{8,12},{9,13},{10,... | collective-permute-start | bytes 393224 | tf_op jit(solution)/shard_map/ppermute | solution.py:154
  216.4 13.9 %collective-permute-start.35 = (bf16[64,1024]{1,0:T(8,128)(2,1)S(1)}, bf16[64,1024]{1,0:T(8,128)(2,1)S(1)}, u32[]{:S(2)}, u32[]{:S(2)}) collective-permute-start(bf16[64,1024]{1,0:T(8,128)(2,1)S(1)} %add_convert_fusion.28), channel_id=1, source_target_pairs={{0,32},{1,33},{2,34},{3,35},{4,36},{5,37},{6,38},{7,39},{8,40},{9,... | collective-permute-start | bytes 393224 | tf_op jit(solution)/shard_map/ppermute | solution.py:154
  238.0 8.3 %collective-permute-start.39 = (bf16[64,1024]{1,0:T(8,128)(2,1)S(1)}, bf16[64,1024]{1,0:T(8,128)(2,1)S(1)}, u32[]{:S(2)}, u32[]{:S(2)}) collective-permute-start(bf16[64,1024]{1,0:T(8,128)(2,1)S(1)} %add_convert_fusion.27), channel_id=1, source_target_pairs={{0,4},{1,5},{2,6},{3,7},{4,0},{5,1},{6,2},{7,3},{8,12},{9,13},{10,... | collective-permute-start | bytes 393224 | tf_op jit(solution)/shard_map/ppermute | solution.py:154
  238.5 7.8 %collective-permute-start.38 = (bf16[64,1024]{1,0:T(8,128)(2,1)S(1)}, bf16[64,1024]{1,0:T(8,128)(2,1)S(1)}, u32[]{:S(2)}, u32[]{:S(2)}) collective-permute-start(bf16[64,1024]{1,0:T(8,128)(2,1)S(1)} %add_convert_fusion.27), channel_id=1, source_target_pairs={{0,5},{1,4},{2,7},{3,6},{4,1},{5,0},{6,3},{7,2},{8,13},{9,12},{10,... | collective-permute-start | bytes 393224 | tf_op jit(solution)/shard_map/ppermute | solution.py:154
  251.4 8.1 %collective-permute-start.44 = (bf16[64,1024]{1,0:T(8,128)(2,1)S(1)}, bf16[64,1024]{1,0:T(8,128)(2,1)S(1)}, u32[]{:S(2)}, u32[]{:S(2)}) collective-permute-start(bf16[64,1024]{1,0:T(8,128)(2,1)S(1)} %add_convert_fusion.25), channel_id=1, source_target_pairs={{0,4},{1,5},{2,6},{3,7},{4,0},{5,1},{6,2},{7,3},{8,12},{9,13},{10,... | collective-permute-start | bytes 393224 | tf_op jit(solution)/shard_map/ppermute | solution.py:154
  273.5 8.1 %collective-permute-start.50 = (bf16[64,1024]{1,0:T(8,128)(2,1)S(1)}, bf16[64,1024]{1,0:T(8,128)(2,1)S(1)}, u32[]{:S(2)}, u32[]{:S(2)}) collective-permute-start(bf16[64,1024]{1,0:T(8,128)(2,1)S(1)} %add_convert_fusion.23), channel_id=1, source_target_pairs={{0,4},{1,5},{2,6},{3,7},{4,0},{5,1},{6,2},{7,3},{8,12},{9,13},{10,... | collective-permute-start | bytes 393224 | tf_op jit(solution)/shard_map/ppermute | solution.py:154
  273.8 7.8 %collective-permute-start.49 = (bf16[64,1024]{1,0:T(8,128)(2,1)S(1)}, bf16[64,1024]{1,0:T(8,128)(2,1)S(1)}, u32[]{:S(2)}, u32[]{:S(2)}) collective-permute-start(bf16[64,1024]{1,0:T(8,128)(2,1)S(1)} %add_convert_fusion.23), channel_id=1, source_target_pairs={{0,5},{1,4},{2,7},{3,6},{4,1},{5,0},{6,3},{7,2},{8,13},{9,12},{10,... | collective-permute-start | bytes 393224 | tf_op jit(solution)/shard_map/ppermute | solution.py:154
  287.0 8.1 %collective-permute-start.55 = (bf16[64,1024]{1,0:T(8,128)(2,1)S(1)}, bf16[64,1024]{1,0:T(8,128)(2,1)S(1)}, u32[]{:S(2)}, u32[]{:S(2)}) collective-permute-start(bf16[64,1024]{1,0:T(8,128)(2,1)S(1)} %add_convert_fusion.21), channel_id=1, source_target_pairs={{0,4},{1,5},{2,6},{3,7},{4,0},{5,1},{6,2},{7,3},{8,12},{9,13},{10,... | collective-permute-start | bytes 393224 | tf_op jit(solution)/shard_map/ppermute | solution.py:154
  288.4 6.7 %collective-permute-start.54 = (bf16[64,1024]{1,0:T(8,128)(2,1)S(1)}, bf16[64,1024]{1,0:T(8,128)(2,1)S(1)}, u32[]{:S(2)}, u32[]{:S(2)}) collective-permute-start(bf16[64,1024]{1,0:T(8,128)(2,1)S(1)} %add_convert_fusion.21), channel_id=1, source_target_pairs={{0,5},{1,4},{2,7},{3,6},{4,1},{5,0},{6,3},{7,2},{8,13},{9,12},{10,... | collective-permute-start | bytes 393224 | tf_op jit(solution)/shard_map/ppermute | solution.py:154
  295.2 9.5 %collective-permute-start.57 = (bf16[64,1024]{1,0:T(8,128)(2,1)S(1)}, bf16[64,1024]{1,0:T(8,128)(2,1)S(1)}, u32[]{:S(2)}, u32[]{:S(2)}) collective-permute-start(bf16[64,1024]{1,0:T(8,128)(2,1)S(1)} %add_convert_fusion.20), channel_id=1, source_target_pairs={{0,32},{1,33},{2,34},{3,35},{4,36},{5,37},{6,38},{7,39},{8,40},{9,... | collective-permute-start | bytes 393224 | tf_op jit(solution)/shard_map/ppermute | solution.py:154
  312.4 8.1 %collective-permute-start.61 = (bf16[64,1024]{1,0:T(8,128)(2,1)S(1)}, bf16[64,1024]{1,0:T(8,128)(2,1)S(1)}, u32[]{:S(2)}, u32[]{:S(2)}) collective-permute-start(bf16[64,1024]{1,0:T(8,128)(2,1)S(1)} %add_convert_fusion.19), channel_id=1, source_target_pairs={{0,4},{1,5},{2,6},{3,7},{4,0},{5,1},{6,2},{7,3},{8,12},{9,13},{10,... | collective-permute-start | bytes 393224 | tf_op jit(solution)/shard_map/ppermute | solution.py:154
  312.6 7.8 %collective-permute-start.60 = (bf16[64,1024]{1,0:T(8,128)(2,1)S(1)}, bf16[64,1024]{1,0:T(8,128)(2,1)S(1)}, u32[]{:S(2)}, u32[]{:S(2)}) collective-permute-start(bf16[64,1024]{1,0:T(8,128)(2,1)S(1)} %add_convert_fusion.19), channel_id=1, source_target_pairs={{0,5},{1,4},{2,7},{3,6},{4,1},{5,0},{6,3},{7,2},{8,13},{9,12},{10,... | collective-permute-start | bytes 393224 | tf_op jit(solution)/shard_map/ppermute | solution.py:154
  325.7 8.1 %collective-permute-start.66 = (bf16[64,1024]{1,0:T(8,128)(2,1)S(1)}, bf16[64,1024]{1,0:T(8,128)(2,1)S(1)}, u32[]{:S(2)}, u32[]{:S(2)}) collective-permute-start(bf16[64,1024]{1,0:T(8,128)(2,1)S(1)} %add_convert_fusion.17), channel_id=1, source_target_pairs={{0,4},{1,5},{2,6},{3,7},{4,0},{5,1},{6,2},{7,3},{8,12},{9,13},{10,... | collective-permute-start | bytes 393224 | tf_op jit(solution)/shard_map/ppermute | solution.py:154
  347.8 8.1 %collective-permute-start.72 = (bf16[64,1024]{1,0:T(8,128)(2,1)S(1)}, bf16[64,1024]{1,0:T(8,128)(2,1)S(1)}, u32[]{:S(2)}, u32[]{:S(2)}) collective-permute-start(bf16[64,1024]{1,0:T(8,128)(2,1)S(1)} %add_convert_fusion.15), channel_id=1, source_target_pairs={{0,4},{1,5},{2,6},{3,7},{4,0},{5,1},{6,2},{7,3},{8,12},{9,13},{10,... | collective-permute-start | bytes 393224 | tf_op jit(solution)/shard_map/ppermute | solution.py:154
  348.1 7.8 %collective-permute-start.71 = (bf16[64,1024]{1,0:T(8,128)(2,1)S(1)}, bf16[64,1024]{1,0:T(8,128)(2,1)S(1)}, u32[]{:S(2)}, u32[]{:S(2)}) collective-permute-start(bf16[64,1024]{1,0:T(8,128)(2,1)S(1)} %add_convert_fusion.15), channel_id=1, source_target_pairs={{0,5},{1,4},{2,7},{3,6},{4,1},{5,0},{6,3},{7,2},{8,13},{9,12},{10,... | collective-permute-start | bytes 393224 | tf_op jit(solution)/shard_map/ppermute | solution.py:154
  361.2 8.1 %collective-permute-start.77 = (bf16[64,1024]{1,0:T(8,128)(2,1)S(1)}, bf16[64,1024]{1,0:T(8,128)(2,1)S(1)}, u32[]{:S(2)}, u32[]{:S(2)}) collective-permute-start(bf16[64,1024]{1,0:T(8,128)(2,1)S(1)} %add_convert_fusion.13), channel_id=1, source_target_pairs={{0,4},{1,5},{2,6},{3,7},{4,0},{5,1},{6,2},{7,3},{8,12},{9,13},{10,... | collective-permute-start | bytes 393224 | tf_op jit(solution)/shard_map/ppermute | solution.py:154
  369.4 9.5 %collective-permute-start.79 = (bf16[64,1024]{1,0:T(8,128)(2,1)S(1)}, bf16[64,1024]{1,0:T(8,128)(2,1)S(1)}, u32[]{:S(2)}, u32[]{:S(2)}) collective-permute-start(bf16[64,1024]{1,0:T(8,128)(2,1)S(1)} %add_convert_fusion.12), channel_id=1, source_target_pairs={{0,32},{1,33},{2,34},{3,35},{4,36},{5,37},{6,38},{7,39},{8,40},{9,... | collective-permute-start | bytes 393224 | tf_op jit(solution)/shard_map/ppermute | solution.py:154
  386.5 8.1 %collective-permute-start.83 = (bf16[64,1024]{1,0:T(8,128)(2,1)S(1)}, bf16[64,1024]{1,0:T(8,128)(2,1)S(1)}, u32[]{:S(2)}, u32[]{:S(2)}) collective-permute-start(bf16[64,1024]{1,0:T(8,128)(2,1)S(1)} %add_convert_fusion.11), channel_id=1, source_target_pairs={{0,4},{1,5},{2,6},{3,7},{4,0},{5,1},{6,2},{7,3},{8,12},{9,13},{10,... | collective-permute-start | bytes 393224 | tf_op jit(solution)/shard_map/ppermute | solution.py:154
  386.8 7.8 %collective-permute-start.82 = (bf16[64,1024]{1,0:T(8,128)(2,1)S(1)}, bf16[64,1024]{1,0:T(8,128)(2,1)S(1)}, u32[]{:S(2)}, u32[]{:S(2)}) collective-permute-start(bf16[64,1024]{1,0:T(8,128)(2,1)S(1)} %add_convert_fusion.11), channel_id=1, source_target_pairs={{0,5},{1,4},{2,7},{3,6},{4,1},{5,0},{6,3},{7,2},{8,13},{9,12},{10,... | collective-permute-start | bytes 393224 | tf_op jit(solution)/shard_map/ppermute | solution.py:154
  400.1 8.1 %collective-permute-start.88 = (bf16[64,1024]{1,0:T(8,128)(2,1)S(1)}, bf16[64,1024]{1,0:T(8,128)(2,1)S(1)}, u32[]{:S(2)}, u32[]{:S(2)}) collective-permute-start(bf16[64,1024]{1,0:T(8,128)(2,1)S(1)} %add_convert_fusion.9), channel_id=1, source_target_pairs={{0,4},{1,5},{2,6},{3,7},{4,0},{5,1},{6,2},{7,3},{8,12},{9,13},{10,... | collective-permute-start | bytes 393224 | tf_op jit(solution)/shard_map/ppermute | solution.py:154
  408.9 27.4 %collective-permute-start.90 = (bf16[64,1024]{1,0:T(8,128)(2,1)S(1)}, bf16[64,1024]{1,0:T(8,128)(2,1)}, u32[]{:S(2)}, u32[]{:S(2)}) collective-permute-start(bf16[64,1024]{1,0:T(8,128)(2,1)S(1)} %add_convert_fusion.8), channel_id=1, source_target_pairs={{0,32},{1,33},{2,34},{3,35},{4,36},{5,37},{6,38},{7,39},{8,40},{9,... | collective-permute-start | bytes 393224 | tf_op jit(solution)/shard_map/ppermute | solution.py:154
  448.4 16.1 %collective-permute-start.92 = (bf16[64,1024]{1,0:T(8,128)(2,1)}, bf16[64,1024]{1,0:T(8,128)(2,1)}, u32[]{:S(2)}, u32[]{:S(2)}) collective-permute-start(bf16[64,1024]{1,0:T(8,128)(2,1)} %get-tuple-element.94), channel_id=1, source_target_pairs={{0,16},{1,17},{2,18},{3,19},{4,20},{5,21},{6,22},{7,23},{8,24},{9,... | collective-permute-start | bytes 393224 | tf_op jit(solution)/shard_map/ppermute | solution.py:154
  467.8 8.3 %collective-permute-start.94 = (bf16[64,1024]{1,0:T(8,128)(2,1)}, bf16[64,1024]{1,0:T(8,128)(2,1)}, u32[]{:S(2)}, u32[]{:S(2)}) collective-permute-start(bf16[64,1024]{1,0:T(8,128)(2,1)} %add_convert_fusion.7), channel_id=1, source_target_pairs={{0,4},{1,5},{2,6},{3,7},{4,0},{5,1},{6,2},{7,3},{8,12},{9,13},{10,... | collective-permute-start | bytes 393224 | tf_op jit(solution)/shard_map/ppermute | solution.py:154
  468.1 8.0 %collective-permute-start.93 = (bf16[64,1024]{1,0:T(8,128)(2,1)}, bf16[64,1024]{1,0:T(8,128)(2,1)}, u32[]{:S(2)}, u32[]{:S(2)}) collective-permute-start(bf16[64,1024]{1,0:T(8,128)(2,1)} %add_convert_fusion.7), channel_id=1, source_target_pairs={{0,5},{1,4},{2,7},{3,6},{4,1},{5,0},{6,3},{7,2},{8,13},{9,12},{10,... | collective-permute-start | bytes 393224 | tf_op jit(solution)/shard_map/ppermute | solution.py:154
  490.3 8.1 %collective-permute-start.99 = (bf16[64,1024]{1,0:T(8,128)(2,1)S(1)}, bf16[64,1024]{1,0:T(8,128)(2,1)S(1)}, u32[]{:S(2)}, u32[]{:S(2)}) collective-permute-start(bf16[64,1024]{1,0:T(8,128)(2,1)S(1)} %add_convert_fusion.5), channel_id=1, source_target_pairs={{0,4},{1,5},{2,6},{3,7},{4,0},{5,1},{6,2},{7,3},{8,12},{9,13},{10,... | collective-permute-start | bytes 393224 | tf_op jit(solution)/shard_map/ppermute | solution.py:154
  516.5 8.1 %collective-permute-start.105 = (bf16[64,1024]{1,0:T(8,128)(2,1)S(1)}, bf16[64,1024]{1,0:T(8,128)(2,1)S(1)}, u32[]{:S(2)}, u32[]{:S(2)}) collective-permute-start(bf16[64,1024]{1,0:T(8,128)(2,1)S(1)} %add_convert_fusion.3), channel_id=1, source_target_pairs={{0,4},{1,5},{2,6},{3,7},{4,0},{5,1},{6,2},{7,3},{8,12},{9,13},{10,... | collective-permute-start | bytes 393224 | tf_op jit(solution)/shard_map/ppermute | solution.py:154
  516.8 7.8 %collective-permute-start.104 = (bf16[64,1024]{1,0:T(8,128)(2,1)S(1)}, bf16[64,1024]{1,0:T(8,128)(2,1)S(1)}, u32[]{:S(2)}, u32[]{:S(2)}) collective-permute-start(bf16[64,1024]{1,0:T(8,128)(2,1)S(1)} %add_convert_fusion.3), channel_id=1, source_target_pairs={{0,5},{1,4},{2,7},{3,6},{4,1},{5,0},{6,3},{7,2},{8,13},{9,12},{10,... | collective-permute-start | bytes 393224 | tf_op jit(solution)/shard_map/ppermute | solution.py:154
  533.9 8.1 %collective-permute-start.110 = (bf16[64,1024]{1,0:T(8,128)(2,1)S(1)}, bf16[64,1024]{1,0:T(8,128)(2,1)S(1)}, u32[]{:S(2)}, u32[]{:S(2)}) collective-permute-start(bf16[64,1024]{1,0:T(8,128)(2,1)S(1)} %add_convert_fusion.1), channel_id=1, source_target_pairs={{0,4},{1,5},{2,6},{3,7},{4,0},{5,1},{6,2},{7,3},{8,12},{9,13},{10,... | collective-permute-start | bytes 393224 | tf_op jit(solution)/shard_map/ppermute | solution.py:154
  544.3 10.8 %collective-permute-start.114 = (bf16[2,16,1024]{2,1,0:T(8,128)(2,1)S(1)}, bf16[2,16,1024]{2,1,0:T(8,128)(2,1)S(1)}, u32[]{:S(2)}, u32[]{:S(2)}) collective-permute-start(bf16[2,16,1024]{2,1,0:T(8,128)(2,1)S(1)} %get-tuple-element.134), channel_id=1, source_target_pairs={{0,4},{1,5},{2,8},{3,9},{4,14},{5,15},{6,2},{7,3},{8,12},{9,13},{1... | collective-permute-start | bytes 196616 | tf_op jit(solution)/shard_map/ppermute | solution.py:154
  (115 other events, 861.9 us)
Sparse Core Ops, SparseCore 0:
  19.0 46.1 all-gather.1

commit v7 on v6

--- a/solution.py
+++ b/solution.py
@@ -89,6 +89,53 @@
     )(place, mine, other, gain, *resident)
 
 
+def rms_scale(hidden, norm_gain):
+    wide = hidden.astype(jnp.float32)
+    mean_square = jnp.mean(wide * wide, axis=-1, keepdims=True)
+    return (wide * lax.rsqrt(mean_square + 1e-06) * norm_gain).astype(jnp.bfloat16)
+
+
+def visible_keys(segments, prefixes, length):
+    seq_len = segments.shape[0]
+    count_seg = prefixes.shape[0]
+    position = jnp.arange(seq_len, dtype=jnp.int32)
+    member = segments[:, None] == jnp.arange(count_seg, dtype=jnp.int32)[None, :]
+    seg_start = jnp.min(jnp.where(member, position[:, None], jnp.int32(seq_len)), axis=0)
+    prefix_end = jnp.sum(jnp.where(member, (seg_start + prefixes)[None, :], jnp.int32(0)), axis=1)
+    key_ok = (position[None, :] <= position[:, None]) | (position[None, :] < prefix_end[None, :])
+    same_seg = segments[:, None] == segments[None, :]
+    live_keys = (position[None, :] < length) | (position[None, :] == position[:, None])
+    return same_seg & key_ok & live_keys
+
+
+def head_terms(hidden, gain, top, bottom, visible):
+    seq_len, model = hidden.shape
+    width = top.shape[1]
+    normed = rms_scale(hidden, gain)
+    queries, keyed, values = [
+        jnp.dot(normed, w, preferred_element_type=jnp.float32)
+        .astype(jnp.bfloat16)
+        .reshape(seq_len, width // DH, DH)
+        for w in (top[:model], top[model:], bottom[:model])
+    ]
+    scores = jnp.einsum(
+        "qhd,khd->hqk", queries, keyed, preferred_element_type=jnp.float32
+    ) * DH ** (-0.5)
+    scores = jnp.where(visible[None, :, :], scores, jnp.float32(-1e30))
+    expo = jnp.exp(scores - jnp.max(scores, axis=-1, keepdims=True))
+    share = (expo / jnp.sum(expo, axis=-1, keepdims=True)).astype(jnp.bfloat16)
+    context = jnp.einsum("hqk,khd->qhd", share, values, preferred_element_type=jnp.float32)
+    context = context.astype(jnp.bfloat16).reshape(seq_len, width)
+    blocks = bottom[model:].reshape(model // width, width, width)
+    return jnp.concatenate(
+        [
+            jnp.dot(context, blocks[b], preferred_element_type=jnp.float32)
+            for b in range(model // width)
+        ],
+        axis=1,
+    ).astype(jnp.bfloat16)
+
+
 def group_bounds(segments):
     seq_len = segments.shape[0]
     quarter = seq_len // SIDE
@@ -180,20 +227,53 @@
         return move(value, lambda s, a, b: (s, a ^ 3, b))
 
     def gather(top, bottom):
-        x_top, y_bottom = over_x(top), over_y(bottom)
-        top, bottom, x_top, y_bottom = lax.optimization_barrier((top, bottom, x_top, y_bottom))
+        x_top, y_bottom, x_bottom, y_top = over_x(top), over_y(bottom), over_x(bottom), over_y(top)
         far_top, far_bottom = over_y(x_top), over_x(y_bottom)
-        y_top, x_bottom = over_y(top), over_x(bottom)
         return [top, bottom, x_top, x_bottom, y_top, y_bottom, far_top, far_bottom]
 
-    weights_a = gather(*[jnp.where(first, p, q) for p, q in zip(kept, got)])
+    own_a = [jnp.where(first, p, q) for p, q in zip(kept, got)]
     own_b = [jnp.where(first, q, p) for p, q in zip(kept, got)]
-    own_b, weights_a[6:] = lax.optimization_barrier((own_b, weights_a[6:]))
-    weights_b = gather(*own_b)
-
-    inputs_all = lax.all_gather(inputs, "dp", axis=1, tiled=True)
-    window_mine = lax.dynamic_slice_in_dim(inputs_all, start + HALF * core, HALF, 1)
-    window_other = lax.dynamic_slice_in_dim(inputs_all, start + HALF * (1 - core), HALF, 1)
+    weights_a, weights_b = gather(*own_a), gather(*own_b)
+
+    def ours(pair):
+        return jnp.where(first, pair[0], pair[1])
+
+    def gather_rows(rows):
+        copies = jnp.broadcast_to(rows[None], (groups, row_count, model))
+        return lax.all_to_all(copies, "dp", 0, 0).reshape(seq_len, model)
+
+    def both(value):
+        other = swap_cores(value)
+        return [jnp.where(first, value, other), jnp.where(first, other, value)]
+
+    visible = [
+        visible_keys(segment_ids[m], prefix_lengths[m], batch_lengths[m])
+        for m in range(micro_count)
+    ]
+    slots = place * row_count + jnp.arange(row_count, dtype=jnp.int32)
+    live = (slots < ours(batch_lengths))[:, None]
+
+    def spread_layer(rows, full, gain, weights):
+        hidden = both(full)
+        terms = [
+            head_terms(hidden[m], gain, *weights, visible[m]) for m in range(micro_count)
+        ]
+        chip = (
+            ours(terms).astype(jnp.float32) + swap_cores(ours(terms[::-1])).astype(jnp.float32)
+        ).astype(jnp.bfloat16)
+        pieces = lax.all_to_all(chip.reshape(groups, row_count, model), "dp", 0, 0)
+        summed = jnp.sum(pieces.astype(jnp.float32), axis=0)
+        return (
+            rows.astype(jnp.float32) + jnp.where(live, summed, jnp.float32(0.0))
+        ).astype(jnp.bfloat16)
+
+    rows_in = ours(inputs)
+    rows_a = spread_layer(rows_in, gather_rows(rows_in), gain_a, own_a)
+    rows_b = spread_layer(rows_a, gather_rows(rows_a), gain_b, own_b)
+    full = gather_rows(move(rows_b, lambda s, a, b: (s + 2, a, b)))
+    stay = lax.dynamic_slice_in_dim(full, start + HALF * core, HALF, 0)
+    leave = swap_cores(lax.dynamic_slice_in_dim(full, start + HALF * (1 - core), HALF, 0))
+    window_mine = [jnp.where(first, stay, leave), jnp.where(first, leave, stay)]
 
     biases = jnp.stack([
         window_masks(segment_ids[m], prefix_lengths[m], batch_lengths[m], start, core)
@@ -232,20 +312,18 @@
     def keep_blocks(layer, turn, rows):
         found = blocks(rows)
         for m in range(micro_count):
-            if 0 <= turn - m < planes:
+            if 1 <= turn - m < planes:
                 stash[layer][m] = jnp.where(plane == turn - m, found, stash[layer][m])
 
-    mine, other = window_mine[0], window_other[0]
+    mine = window_mine[0]
     turns = planes + micro_count - 1
-    for turn in range(turns):
-        out_a = one_layer(turn, mine, other, gain_a, weights_a)
+    for turn in range(1, turns):
+        out_a = one_layer(turn, mine, swap_cores(mine), gain_a, weights_a)
         out_b = one_layer(turn, out_a, swap_cores(out_a), gain_b, weights_b)
         if turn < turns - 1:
-            onward = (
-                jnp.where(plane == planes - 1, window_mine[1], out_b) if turn == 0 else out_b
-            )
-            mine = move(onward, lambda s, a, b: (s + 2, a, b))
-            other = swap_cores(mine)
+            mine = move(out_b, lambda s, a, b: (s + 2, a, b))
+            if turn < micro_count:
+                mine = jnp.where(plane == 1, window_mine[turn], mine)
         keep_blocks(0, turn, out_a)
         keep_blocks(1, turn, out_b)
 
@@ -261,12 +339,14 @@
                 lambda s, a, b: owner(s, a, b, False))
     other = move(jnp.where(side_at // HALF == core, here[1], there[1]),
                  lambda s, a, b: owner(s, a, b, True))
-    slots = place * row_count + jnp.arange(row_count, dtype=jnp.int32)
+    kept_rows, got_rows = ours([rows_a, rows_b]), swap_cores(ours([rows_b, rows_a]))
+    early = [jnp.where(first, kept_rows, got_rows), jnp.where(first, got_rows, kept_rows)]
     picked = []
     for m in range(micro_count):
         bounds = group_bounds(segment_ids[m])
         holder = jnp.sum((slots[:, None] >= bounds[None, 1:]).astype(jnp.int32), axis=1)
-        picked.append(jnp.where((holder == y)[:, None], mine[m], other[m]))
+        late = jnp.where((holder == y)[:, None], mine[m], other[m])
+        picked.append(jnp.where(plane == 0, early[m], late))
     return jnp.stack(picked)[None]
 
 

time: 572 us -> 614 us (1.073)
  matrix products: 0 us -> 29.4 us
  local copies, waits for them, and re-layouts: 13.5 us -> 32.8 us
  Pallas kernels: 60.9 us -> 44.9 us
  waiting for transfers between devices: 306 us -> 291 us
  blocking collectives: 0 us -> 14.5 us
  other arithmetic: 16.3 us -> 30.5 us
  between operations: 33.8 us -> 22.9 us
    ppermute x115 -> x112, waiting for transfers between devices: 306 us -> 249 us  [move(): return lax.ppermute(value, AXES, pairs)]
    all_to_all x0 -> x4, waiting for transfers between devices: none -> 42.4 us  [the longest x2 25.3 us: gather_rows(): return lax.all_to_all(copies, 'dp', 0, 0).reshape(seq_len, model)]
    dot_general x0 -> x36, matrix products: none -> 25.1 us  [the longest x12 7.42 us: head_terms(): jnp.dot(normed, w, preferred_element_type=jnp.float32).astype(jnp.bfloat16)]
    all_to_all x0 -> x4, starting transfers between devices: none -> 20.2 us  [the longest x2 11.4 us: gather_rows(): return lax.all_to_all(copies, 'dp', 0, 0).reshape(seq_len, model)]
    pallas_call x18 -> x16, Pallas kernels: 60.9 us -> 44.9 us  [run_layer(): pl.pallas_call(functools.partial(layer_kernel, turn), out_shape=(half, ha...]
    ppermute x115 -> x112, starting transfers between devices: 132 us -> 117 us  [move(): return lax.ppermute(value, AXES, pairs)]
    all_to_all x0 -> x1, blocking collectives: none -> 14.5 us  [gather_rows(): return lax.all_to_all(copies, 'dp', 0, 0).reshape(seq_len, model)]
    unnamed x100 -> x198, local copies, waits for them, and re-layouts: 6.5 us -> 16.4 us
  transfers between devices with their start and end apart: 116 -> 116, of which waited for: 90 -> 80; matrix products, arithmetic and copies ran while one was open for 2% -> 5% of each run, Pallas kernels for 1% -> 0%
where the time goes in v7:
time: 614 us; the launch traced here: 604 us
  waiting for transfers between devices  291 us (47%)
  starting transfers between devices  137 us (22%)
  Pallas kernels  44.9 us (7%)
  local copies, waits for them, and re-layouts  32.8 us (5%)
  other arithmetic  30.5 us (5%)
  matrix products  29.4 us (5%)
  between operations  22.9 us (4%)
  blocking collectives  14.5 us (2%)
    ppermute x112, waiting for transfers between devices, move(): return lax.ppermute(value, AXES, pairs)  249 us
    ppermute x112, starting transfers between devices, move(): return lax.ppermute(value, AXES, pairs)  117 us
    pallas_call x16, Pallas kernels, run_layer(): pl.pallas_call(functools.partial(layer_kernel, turn), out_shape=(half, ha...  44.9 us
    all_to_all x2, waiting for transfers between devices, gather_rows(): return lax.all_to_all(copies, 'dp', 0, 0).reshape(seq_len, model)  25.3 us
    all_to_all x2, waiting for transfers between devices, spread_layer(): pieces = lax.all_to_all(chip.reshape(groups, row_count, model), 'dp', 0, 0)  17.1 us
    unnamed x198, local copies, waits for them, and re-layouts  16.4 us
    all_to_all x1, blocking collectives, gather_rows(): return lax.all_to_all(copies, 'dp', 0, 0).reshape(seq_len, model)  14.5 us
  transfers between devices with their start and end apart: 116, of which 80 were waited for; matrix products, arithmetic and copies ran while one was open for 5% of the time, Pallas kernels for 0%

profile of v7, /device:TPU:224, one launch (start us, length us, event | category | flops | bytes accessed | tf_op | source)
XLA Modules:
  0.0 603.6 jit_solution(16704361173754475673)
XLA Ops:
  1.7 7.0 %all-to-all-start = ((bf16[16,16,1024]{2,1,0:T(8,128)(2,1)}), bf16[16,16,1024]{2,1,0:T(8,128)(2,1)S(1)}, u32[]{:S(2)}, u32[]{:S(2)}) async-start(bf16[16,16,1024]{2,1,0:T(8,128)(2,1)} %broadcast_in_dim.236), calls=%async_computation | async-start | bytes 1048576 | tf_op jit(solution)/shard_map/all_to_all | solution.py:243
  17.1 3.8 all-to-all-done
  49.3 4.4 all-to-all-start.1
  55.0 11.1 %all-to-all-done.1 = bf16[16,16,1024]{2,1,0:T(8,128)(2,1)} async-done(((bf16[16,16,1024]{2,1,0:T(8,128)(2,1)}), bf16[16,16,1024]{2,1,0:T(8,128)(2,1)}, u32[]{:S(2)}, u32[]{:S(2)}) %all-to-all-start.1) | async-done | bytes 524320 | tf_op jit(solution)/shard_map/all_to_all | solution.py:264
  67.4 14.5 %all_to_all.25 = bf16[16,16,1024]{2,1,0:T(8,128)(2,1)} all-to-all(bf16[16,16,1024]{2,1,0:T(8,128)(2,1)S(1)} %broadcast_in_dim.252), channel_id=1, replica_groups=mesh['section'=16,'dp'=16] {'dp'}, dimensions={0} | all-to-all | bytes 1048576 | tf_op jit(solution)/shard_map/all_to_all | solution.py:243
  110.3 4.4 all-to-all-start.3
  114.7 3.0 collective-permute-start.11
  120.9 6.0 %all-to-all-done.3 = bf16[16,16,1024]{2,1,0:T(8,128)(2,1)} async-done(((bf16[16,16,1024]{2,1,0:T(8,128)(2,1)}), bf16[16,16,1024]{2,1,0:T(8,128)(2,1)}, u32[]{:S(2)}, u32[]{:S(2)}) %all-to-all-start.3) | async-done | bytes 524320 | tf_op jit(solution)/shard_map/all_to_all | solution.py:264
  129.5 3.9 collective-permute-done.8
  134.2 4.4 all-to-all-start.4
  141.0 2.9 collective-permute-start.12
  144.2 5.8 collective-permute-done.11.refs_2_
  154.5 21.5 %all-to-all-done.4 = bf16[16,16,1024]{2,1,0:T(8,128)(2,1)} async-done(((bf16[16,16,1024]{2,1,0:T(8,128)(2,1)}), bf16[16,16,1024]{2,1,0:T(8,128)(2,1)}, u32[]{:S(2)}, u32[]{:S(2)}) %all-to-all-start.4) | async-done | bytes 524320 | tf_op jit(solution)/shard_map/all_to_all | solution.py:243
  183.8 14.7 %collective-permute-done.15.refs_6_ = bf16[2048,256]{1,0:T(8,128)(2,1)} collective-permute-done((bf16[2048,256]{1,0:T(8,128)(2,1)}, bf16[2048,256]{1,0:T(8,128)(2,1)}, u32[]{:S(2)}, u32[]{:S(2)}) %collective-permute-start.15) | collective-permute-done | bytes 1048608 | tf_op jit(solution)/shard_map/ppermute | solution.py:201
  205.8 14.3 %collective-permute-done.22.refs_2_ = bf16[2048,256]{1,0:T(8,128)(2,1)S(1)} collective-permute-done((bf16[2048,256]{1,0:T(8,128)(2,1)S(1)}, bf16[2048,256]{1,0:T(8,128)(2,1)S(1)}, u32[]{:S(2)}, u32[]{:S(2)}) %collective-permute-start.22) | collective-permute-done | bytes 1048608 | tf_op jit(solution)/shard_map/ppermute | solution.py:201
  224.0 5.0 collective-permute-done.20
  229.1 4.8 collective-permute-done.19
  233.9 5.9 collective-permute-done.18
  240.0 3.3 collective-permute-done.24.refs_4_
  243.3 22.2 %collective-permute-done.26.refs_6_ = bf16[2048,256]{1,0:T(8,128)(2,1)S(1)} collective-permute-done((bf16[2048,256]{1,0:T(8,128)(2,1)S(1)}, bf16[2048,256]{1,0:T(8,128)(2,1)S(1)}, u32[]{:S(2)}, u32[]{:S(2)}) %collective-permute-start.26) | collective-permute-done | bytes 1048608 | tf_op jit(solution)/shard_map/ppermute | solution.py:201
  274.2 3.5 collective-permute-done.30
  279.3 4.5 collective-permute-done.32
  287.5 3.0 shard_map.102
  295.5 2.9 collective-permute-done.37
  308.3 2.9 collective-permute-done.42
  316.3 2.9 collective-permute-done.43.mine_ref
  328.5 2.9 collective-permute-done.48
  341.2 2.9 collective-permute-done.53
  347.0 8.4 %collective-permute-start.54 = (bf16[64,1024]{1,0:T(8,128)(2,1)S(1)}, bf16[64,1024]{1,0:T(8,128)(2,1)S(1)}, u32[]{:S(2)}, u32[]{:S(2)}) collective-permute-start(bf16[64,1024]{1,0:T(8,128)(2,1)S(1)} %add_convert_fusion.22), channel_id=1, source_target_pairs={{0,32},{1,33},{2,34},{3,35},{4,36},{5,37},{6,38},{7,39},{8,40},{9,... | collective-permute-start | bytes 393224 | tf_op jit(solution)/shard_map/ppermute | solution.py:201
  359.3 3.0 shard_map.106
  367.3 2.9 collective-permute-done.59
  380.1 2.9 collective-permute-done.64
  385.8 3.7 collective-permute-start.65
  393.4 3.2 shard_map.108
  401.7 2.9 collective-permute-done.70
  414.5 2.9 collective-permute-done.75
  420.2 7.0 %collective-permute-start.76 = (bf16[64,1024]{1,0:T(8,128)(2,1)S(1)}, bf16[64,1024]{1,0:T(8,128)(2,1)S(1)}, u32[]{:S(2)}, u32[]{:S(2)}) collective-permute-start(bf16[64,1024]{1,0:T(8,128)(2,1)S(1)} %add_convert_fusion.14), channel_id=1, source_target_pairs={{0,32},{1,33},{2,34},{3,35},{4,36},{5,37},{6,38},{7,39},{8,40},{9,... | collective-permute-start | bytes 393224 | tf_op jit(solution)/shard_map/ppermute | solution.py:201
  431.1 3.0 shard_map.110
  457.6 3.7 collective-permute-start.87
  461.4 24.9 %collective-permute-done.87.mine_ref = bf16[64,1024]{1,0:T(8,128)(2,1)S(1)} collective-permute-done((bf16[64,1024]{1,0:T(8,128)(2,1)S(1)}, bf16[64,1024]{1,0:T(8,128)(2,1)S(1)}, u32[]{:S(2)}, u32[]{:S(2)}) %collective-permute-start.87) | collective-permute-done | bytes 131104 | tf_op jit(solution)/shard_map/ppermute | solution.py:201
  487.6 7.1 %shard_map.112 = (bf16[64,1024]{1,0:T(8,128)(2,1)S(1)}, bf16[64,1024]{1,0:T(8,128)(2,1)S(1)}) custom-call(s32[5]{0:T(128)S(1)} %pad_add_fusion.1.place_ref, bf16[64,1024]{1,0:T(8,128)(2,1)S(1)} %collective-permute-done.87.mine_ref, bf16[64,1024]{1,0:T(8,128)(2,1)S(1)} %collective-permute-done.88.other_ref, f32[1,1024]{1,0:T(1,128)S(1)} %get-tuple-element.147.gain_ref, ...), custom_call_target="tpu_custom_call" | custom-call | flops 1073741824 | bytes 8388608 | tf_op jit(solution)/shard_map/pallas_call | solution.py:79
  529.9 5.1 shard_map.113
  543.0 3.0 collective-permute-done.96
  547.2 6.1 %collective-permute-done.98.mine_ref = bf16[64,1024]{1,0:T(8,128)(2,1)S(1)} collective-permute-done((bf16[64,1024]{1,0:T(8,128)(2,1)S(1)}, bf16[64,1024]{1,0:T(8,128)(2,1)S(1)}, u32[]{:S(2)}, u32[]{:S(2)}) %collective-permute-start.98) | collective-permute-done | bytes 131104 | tf_op jit(solution)/shard_map/ppermute | solution.py:201
  554.9 7.0 %shard_map.114 = (bf16[64,1024]{1,0:T(8,128)(2,1)S(1)}, bf16[64,1024]{1,0:T(8,128)(2,1)S(1)}) custom-call(s32[5]{0:T(128)S(1)} %pad_add_fusion.1.place_ref, bf16[64,1024]{1,0:T(8,128)(2,1)S(1)} %collective-permute-done.98.mine_ref, bf16[64,1024]{1,0:T(8,128)(2,1)S(1)} %collective-permute-done.99.other_ref, f32[1,1024]{1,0:T(1,128)S(1)} %get-tuple-element.147.gain_ref, ...), custom_call_target="tpu_custom_call" | custom-call | flops 1073741824 | bytes 8388608 | tf_op jit(solution)/shard_map/pallas_call | solution.py:79
  574.1 4.6 shard_map.115
  591.7 5.1 collective-permute-start.111
  596.8 5.6 collective-permute-done.111
  (567 shorter events, 280.9 us)
Async XLA Ops:
  0.0 23.9 %collective-permute-start.1 = (f32[1,1024]{1,0:T(1,128)}, f32[1,1024]{1,0:T(1,128)S(1)}, u32[]{:S(2)}, u32[]{:S(2)}) collective-permute-start(f32[1,1024]{1,0:T(1,128)} %param.11), channel_id=1, source_target_pairs={{0,16},{1,17},{2,18},{3,19},{4,20},{5,21},{6,22},{7,23},{8,24},{9,... | collective-permute-start | bytes 12296 | tf_op jit(solution)/shard_map/ppermute | solution.py:201
  1.7 19.2 %all-to-all-start = ((bf16[16,16,1024]{2,1,0:T(8,128)(2,1)}), bf16[16,16,1024]{2,1,0:T(8,128)(2,1)S(1)}, u32[]{:S(2)}, u32[]{:S(2)}) async-start(bf16[16,16,1024]{2,1,0:T(8,128)(2,1)} %broadcast_in_dim.236), calls=%async_computation | async-start | bytes 1048576 | tf_op jit(solution)/shard_map/all_to_all | solution.py:243
  11.9 13.8 %collective-permute-start.3 = (bf16[2048,256]{1,0:T(8,128)(2,1)}, bf16[2048,256]{1,0:T(8,128)(2,1)}, u32[]{:S(2)}, u32[]{:S(2)}) collective-permute-start(bf16[2048,256]{1,0:T(8,128)(2,1)} %broadcast_select_fusion.3), channel_id=1, source_target_pairs={{0,16},{1,17},{2,18},{3,19},{4,20},{5,21},{6,22},{7,23},{8,24},{9,... | collective-permute-start | bytes 3145736 | tf_op jit(solution)/shard_map/ppermute | solution.py:201
  15.0 19.2 %collective-permute-start.2 = (bf16[2048,256]{1,0:T(8,128)(2,1)}, bf16[2048,256]{1,0:T(8,128)(2,1)}, u32[]{:S(2)}, u32[]{:S(2)}) collective-permute-start(bf16[2048,256]{1,0:T(8,128)(2,1)} %broadcast_select_fusion.6), channel_id=1, source_target_pairs={{0,16},{1,17},{2,18},{3,19},{4,20},{5,21},{6,22},{7,23},{8,24},{9,... | collective-permute-start | bytes 3145736 | tf_op jit(solution)/shard_map/ppermute | solution.py:201
  49.3 16.7 %all-to-all-start.1 = ((bf16[16,16,1024]{2,1,0:T(8,128)(2,1)}), bf16[16,16,1024]{2,1,0:T(8,128)(2,1)}, u32[]{:S(2)}, u32[]{:S(2)}) async-start(bf16[16,16,1024]{2,1,0:T(8,128)(2,1)} %bitcast.268), calls=%async_computation.1 | async-start | bytes 1048576 | tf_op jit(solution)/shard_map/all_to_all | solution.py:264
  110.3 16.6 %all-to-all-start.3 = ((bf16[16,16,1024]{2,1,0:T(8,128)(2,1)}), bf16[16,16,1024]{2,1,0:T(8,128)(2,1)}, u32[]{:S(2)}, u32[]{:S(2)}) async-start(bf16[16,16,1024]{2,1,0:T(8,128)(2,1)} %bitcast.267), calls=%async_computation.3 | async-start | bytes 1048576 | tf_op jit(solution)/shard_map/all_to_all | solution.py:264
  114.7 35.2 %collective-permute-start.11 = (bf16[2048,256]{1,0:T(8,128)(2,1)}, bf16[2048,256]{1,0:T(8,128)(2,1)}, u32[]{:S(2)}, u32[]{:S(2)}) collective-permute-start(bf16[2048,256]{1,0:T(8,128)(2,1)} %copy-done), channel_id=1, source_target_pairs={{0,3},{1,2},{2,1},{3,0},{4,7},{5,6},{6,5},{7,4},{8,11},{9,10},{10,... | collective-permute-start | bytes 3145736 | tf_op jit(solution)/shard_map/ppermute | solution.py:201
  117.7 35.0 %collective-permute-start.14 = (bf16[2048,256]{1,0:T(8,128)(2,1)S(1)}, bf16[2048,256]{1,0:T(8,128)(2,1)}, u32[]{:S(2)}, u32[]{:S(2)}) collective-permute-start(bf16[2048,256]{1,0:T(8,128)(2,1)S(1)} %get-tuple-element.95.refs_1_), channel_id=1, source_target_pairs={{0,12},{1,13},{2,14},{3,15},{4,8},{5,9},{6,10},{7,11},{8,4},{9,5},... | collective-permute-start | bytes 3145736 | tf_op jit(solution)/shard_map/ppermute | solution.py:201
  120.4 56.7 %collective-permute-start.13 = (bf16[2048,256]{1,0:T(8,128)(2,1)}, bf16[2048,256]{1,0:T(8,128)(2,1)}, u32[]{:S(2)}, u32[]{:S(2)}) collective-permute-start(bf16[2048,256]{1,0:T(8,128)(2,1)} %copy-done), channel_id=1, source_target_pairs={{0,12},{1,13},{2,14},{3,15},{4,8},{5,9},{6,10},{7,11},{8,4},{9,5},... | collective-permute-start | bytes 3145736 | tf_op jit(solution)/shard_map/ppermute | solution.py:201
  134.2 41.7 %all-to-all-start.4 = ((bf16[16,16,1024]{2,1,0:T(8,128)(2,1)}), bf16[16,16,1024]{2,1,0:T(8,128)(2,1)}, u32[]{:S(2)}, u32[]{:S(2)}) async-start(bf16[16,16,1024]{2,1,0:T(8,128)(2,1)} %broadcast_in_dim.256), calls=%async_computation.4 | async-start | bytes 1048576 | tf_op jit(solution)/shard_map/all_to_all | solution.py:243
  141.0 41.8 %collective-permute-start.12 = (bf16[2048,256]{1,0:T(8,128)(2,1)S(1)}, bf16[2048,256]{1,0:T(8,128)(2,1)}, u32[]{:S(2)}, u32[]{:S(2)}) collective-permute-start(bf16[2048,256]{1,0:T(8,128)(2,1)S(1)} %get-tuple-element.95.refs_1_), channel_id=1, source_target_pairs={{0,3},{1,2},{2,1},{3,0},{4,7},{5,6},{6,5},{7,4},{8,11},{9,10},{10,... | collective-permute-start | bytes 3145736 | tf_op jit(solution)/shard_map/ppermute | solution.py:201
  149.9 48.5 %collective-permute-start.15 = (bf16[2048,256]{1,0:T(8,128)(2,1)}, bf16[2048,256]{1,0:T(8,128)(2,1)}, u32[]{:S(2)}, u32[]{:S(2)}) collective-permute-start(bf16[2048,256]{1,0:T(8,128)(2,1)} %collective-permute-done.11.refs_2_), channel_id=1, source_target_pairs={{0,12},{1,13},{2,14},{3,15},{4,8},{5,9},{6,10},{7,11},{8,4},{9,5},... | collective-permute-start | bytes 3145736 | tf_op jit(solution)/shard_map/ppermute | solution.py:201
  152.7 45.7 %collective-permute-start.16 = (bf16[2048,256]{1,0:T(8,128)(2,1)}, bf16[2048,256]{1,0:T(8,128)(2,1)}, u32[]{:S(2)}, u32[]{:S(2)}) collective-permute-start(bf16[2048,256]{1,0:T(8,128)(2,1)} %collective-permute-done.14.refs_5_), channel_id=1, source_target_pairs={{0,3},{1,2},{2,1},{3,0},{4,7},{5,6},{6,5},{7,4},{8,11},{9,10},{10,... | collective-permute-start | bytes 3145736 | tf_op jit(solution)/shard_map/ppermute | solution.py:201
  177.1 42.9 %collective-permute-start.22 = (bf16[2048,256]{1,0:T(8,128)(2,1)S(1)}, bf16[2048,256]{1,0:T(8,128)(2,1)S(1)}, u32[]{:S(2)}, u32[]{:S(2)}) collective-permute-start(bf16[2048,256]{1,0:T(8,128)(2,1)S(1)} %get-tuple-element.92.refs_0_), channel_id=1, source_target_pairs={{0,3},{1,2},{2,1},{3,0},{4,7},{5,6},{6,5},{7,4},{8,11},{9,10},{10,... | collective-permute-start | bytes 3145736 | tf_op jit(solution)/shard_map/ppermute | solution.py:201
  179.2 43.6 %collective-permute-start.25 = (bf16[2048,256]{1,0:T(8,128)(2,1)S(1)}, bf16[2048,256]{1,0:T(8,128)(2,1)S(1)}, u32[]{:S(2)}, u32[]{:S(2)}) collective-permute-start(bf16[2048,256]{1,0:T(8,128)(2,1)S(1)} %get-tuple-element.94.refs_1_), channel_id=1, source_target_pairs={{0,12},{1,13},{2,14},{3,15},{4,8},{5,9},{6,10},{7,11},{8,4},{9,5},... | collective-permute-start | bytes 3145736 | tf_op jit(solution)/shard_map/ppermute | solution.py:201
  182.9 15.5 %collective-permute-start.10 = (bf16[64,1024]{1,0:T(8,128)(2,1)S(1)}, bf16[64,1024]{1,0:T(8,128)(2,1)S(1)}, u32[]{:S(2)}, u32[]{:S(2)}) collective-permute-start(bf16[64,1024]{1,0:T(8,128)(2,1)S(1)} %broadcast_select_fusion.14.mine_ref), channel_id=1, source_target_pairs={{0,16},{1,17},{2,18},{3,19},{4,20},{5,21},{6,22},{7,23},{8,24},{9,... | collective-permute-start | bytes 393224 | tf_op jit(solution)/shard_map/ppermute | solution.py:201
  202.5 21.3 %collective-permute-start.17 = (bf16[64,1024]{1,0:T(8,128)(2,1)S(1)}, bf16[64,1024]{1,0:T(8,128)(2,1)S(1)}, u32[]{:S(2)}, u32[]{:S(2)}) collective-permute-start(bf16[64,1024]{1,0:T(8,128)(2,1)S(1)} %get-tuple-element.38), channel_id=1, source_target_pairs={{0,16},{1,17},{2,18},{3,19},{4,20},{5,21},{6,22},{7,23},{8,24},{9,... | collective-permute-start | bytes 393224 | tf_op jit(solution)/shard_map/ppermute | solution.py:201
  202.6 40.7 %collective-permute-start.24 = (bf16[2048,256]{1,0:T(8,128)(2,1)S(1)}, bf16[2048,256]{1,0:T(8,128)(2,1)S(1)}, u32[]{:S(2)}, u32[]{:S(2)}) collective-permute-start(bf16[2048,256]{1,0:T(8,128)(2,1)S(1)} %get-tuple-element.92.refs_0_), channel_id=1, source_target_pairs={{0,12},{1,13},{2,14},{3,15},{4,8},{5,9},{6,10},{7,11},{8,4},{9,5},... | collective-permute-start | bytes 3145736 | tf_op jit(solution)/shard_map/ppermute | solution.py:201
  204.7 38.6 %collective-permute-start.23 = (bf16[2048,256]{1,0:T(8,128)(2,1)S(1)}, bf16[2048,256]{1,0:T(8,128)(2,1)S(1)}, u32[]{:S(2)}, u32[]{:S(2)}) collective-permute-start(bf16[2048,256]{1,0:T(8,128)(2,1)S(1)} %get-tuple-element.94.refs_1_), channel_id=1, source_target_pairs={{0,3},{1,2},{2,1},{3,0},{4,7},{5,6},{6,5},{7,4},{8,11},{9,10},{10,... | collective-permute-start | bytes 3145736 | tf_op jit(solution)/shard_map/ppermute | solution.py:201
  220.1 45.4 %collective-permute-start.26 = (bf16[2048,256]{1,0:T(8,128)(2,1)S(1)}, bf16[2048,256]{1,0:T(8,128)(2,1)S(1)}, u32[]{:S(2)}, u32[]{:S(2)}) collective-permute-start(bf16[2048,256]{1,0:T(8,128)(2,1)S(1)} %collective-permute-done.22.refs_2_), channel_id=1, source_target_pairs={{0,12},{1,13},{2,14},{3,15},{4,8},{5,9},{6,10},{7,11},{8,4},{9,5},... | collective-permute-start | bytes 3145736 | tf_op jit(solution)/shard_map/ppermute | solution.py:201
  222.8 42.6 %collective-permute-start.27 = (bf16[2048,256]{1,0:T(8,128)(2,1)S(1)}, bf16[2048,256]{1,0:T(8,128)(2,1)S(1)}, u32[]{:S(2)}, u32[]{:S(2)}) collective-permute-start(bf16[2048,256]{1,0:T(8,128)(2,1)S(1)} %collective-permute-done.25.refs_5_), channel_id=1, source_target_pairs={{0,3},{1,2},{2,1},{3,0},{4,7},{5,6},{6,5},{7,4},{8,11},{9,10},{10,... | collective-permute-start | bytes 3145736 | tf_op jit(solution)/shard_map/ppermute | solution.py:201
  239.9 25.6 %collective-permute-start.21 = (bf16[64,1024]{1,0:T(8,128)(2,1)S(1)}, bf16[64,1024]{1,0:T(8,128)(2,1)S(1)}, u32[]{:S(2)}, u32[]{:S(2)}) collective-permute-start(bf16[64,1024]{1,0:T(8,128)(2,1)S(1)} %add_convert_fusion.32.mine_ref), channel_id=1, source_target_pairs={{0,16},{1,17},{2,18},{3,19},{4,20},{5,21},{6,22},{7,23},{8,24},{9,... | collective-permute-start | bytes 393224 | tf_op jit(solution)/shard_map/ppermute | solution.py:201
  269.3 8.5 %collective-permute-start.30 = (bf16[64,1024]{1,0:T(8,128)(2,1)S(1)}, bf16[64,1024]{1,0:T(8,128)(2,1)S(1)}, u32[]{:S(2)}, u32[]{:S(2)}) collective-permute-start(bf16[64,1024]{1,0:T(8,128)(2,1)S(1)} %add_convert_fusion.31), channel_id=1, source_target_pairs={{0,4},{1,5},{2,6},{3,7},{4,0},{5,1},{6,2},{7,3},{8,12},{9,13},{10,... | collective-permute-start | bytes 393224 | tf_op jit(solution)/shard_map/ppermute | solution.py:201
  269.9 7.8 %collective-permute-start.29 = (bf16[64,1024]{1,0:T(8,128)(2,1)S(1)}, bf16[64,1024]{1,0:T(8,128)(2,1)S(1)}, u32[]{:S(2)}, u32[]{:S(2)}) collective-permute-start(bf16[64,1024]{1,0:T(8,128)(2,1)S(1)} %add_convert_fusion.31), channel_id=1, source_target_pairs={{0,5},{1,4},{2,7},{3,6},{4,1},{5,0},{6,3},{7,2},{8,13},{9,12},{10,... | collective-permute-start | bytes 393224 | tf_op jit(solution)/shard_map/ppermute | solution.py:201
  293.0 8.1 %collective-permute-start.36 = (bf16[64,1024]{1,0:T(8,128)(2,1)S(1)}, bf16[64,1024]{1,0:T(8,128)(2,1)S(1)}, u32[]{:S(2)}, u32[]{:S(2)}) collective-permute-start(bf16[64,1024]{1,0:T(8,128)(2,1)S(1)} %add_convert_fusion.29), channel_id=1, source_target_pairs={{0,4},{1,5},{2,6},{3,7},{4,0},{5,1},{6,2},{7,3},{8,12},{9,13},{10,... | collective-permute-start | bytes 393224 | tf_op jit(solution)/shard_map/ppermute | solution.py:201
  293.6 7.5 %collective-permute-start.35 = (bf16[64,1024]{1,0:T(8,128)(2,1)S(1)}, bf16[64,1024]{1,0:T(8,128)(2,1)S(1)}, u32[]{:S(2)}, u32[]{:S(2)}) collective-permute-start(bf16[64,1024]{1,0:T(8,128)(2,1)S(1)} %add_convert_fusion.29), channel_id=1, source_target_pairs={{0,5},{1,4},{2,7},{3,6},{4,1},{5,0},{6,3},{7,2},{8,13},{9,12},{10,... | collective-permute-start | bytes 393224 | tf_op jit(solution)/shard_map/ppermute | solution.py:201
  305.8 8.1 %collective-permute-start.41 = (bf16[64,1024]{1,0:T(8,128)(2,1)S(1)}, bf16[64,1024]{1,0:T(8,128)(2,1)S(1)}, u32[]{:S(2)}, u32[]{:S(2)}) collective-permute-start(bf16[64,1024]{1,0:T(8,128)(2,1)S(1)} %add_convert_fusion.27), channel_id=1, source_target_pairs={{0,4},{1,5},{2,6},{3,7},{4,0},{5,1},{6,2},{7,3},{8,12},{9,13},{10,... | collective-permute-start | bytes 393224 | tf_op jit(solution)/shard_map/ppermute | solution.py:201
  326.0 8.1 %collective-permute-start.47 = (bf16[64,1024]{1,0:T(8,128)(2,1)S(1)}, bf16[64,1024]{1,0:T(8,128)(2,1)S(1)}, u32[]{:S(2)}, u32[]{:S(2)}) collective-permute-start(bf16[64,1024]{1,0:T(8,128)(2,1)S(1)} %add_convert_fusion.25), channel_id=1, source_target_pairs={{0,4},{1,5},{2,6},{3,7},{4,0},{5,1},{6,2},{7,3},{8,12},{9,13},{10,... | collective-permute-start | bytes 393224 | tf_op jit(solution)/shard_map/ppermute | solution.py:201
  326.7 7.4 %collective-permute-start.46 = (bf16[64,1024]{1,0:T(8,128)(2,1)S(1)}, bf16[64,1024]{1,0:T(8,128)(2,1)S(1)}, u32[]{:S(2)}, u32[]{:S(2)}) collective-permute-start(bf16[64,1024]{1,0:T(8,128)(2,1)S(1)} %add_convert_fusion.25), channel_id=1, source_target_pairs={{0,5},{1,4},{2,7},{3,6},{4,1},{5,0},{6,3},{7,2},{8,13},{9,12},{10,... | collective-permute-start | bytes 393224 | tf_op jit(solution)/shard_map/ppermute | solution.py:201
  338.8 8.1 %collective-permute-start.52 = (bf16[64,1024]{1,0:T(8,128)(2,1)S(1)}, bf16[64,1024]{1,0:T(8,128)(2,1)S(1)}, u32[]{:S(2)}, u32[]{:S(2)}) collective-permute-start(bf16[64,1024]{1,0:T(8,128)(2,1)S(1)} %add_convert_fusion.23), channel_id=1, source_target_pairs={{0,4},{1,5},{2,6},{3,7},{4,0},{5,1},{6,2},{7,3},{8,12},{9,13},{10,... | collective-permute-start | bytes 393224 | tf_op jit(solution)/shard_map/ppermute | solution.py:201
  347.0 11.0 %collective-permute-start.54 = (bf16[64,1024]{1,0:T(8,128)(2,1)S(1)}, bf16[64,1024]{1,0:T(8,128)(2,1)S(1)}, u32[]{:S(2)}, u32[]{:S(2)}) collective-permute-start(bf16[64,1024]{1,0:T(8,128)(2,1)S(1)} %add_convert_fusion.22), channel_id=1, source_target_pairs={{0,32},{1,33},{2,34},{3,35},{4,36},{5,37},{6,38},{7,39},{8,40},{9,... | collective-permute-start | bytes 393224 | tf_op jit(solution)/shard_map/ppermute | solution.py:201
  364.9 8.1 %collective-permute-start.58 = (bf16[64,1024]{1,0:T(8,128)(2,1)S(1)}, bf16[64,1024]{1,0:T(8,128)(2,1)S(1)}, u32[]{:S(2)}, u32[]{:S(2)}) collective-permute-start(bf16[64,1024]{1,0:T(8,128)(2,1)S(1)} %add_convert_fusion.21), channel_id=1, source_target_pairs={{0,4},{1,5},{2,6},{3,7},{4,0},{5,1},{6,2},{7,3},{8,12},{9,13},{10,... | collective-permute-start | bytes 393224 | tf_op jit(solution)/shard_map/ppermute | solution.py:201
  377.6 8.1 %collective-permute-start.63 = (bf16[64,1024]{1,0:T(8,128)(2,1)S(1)}, bf16[64,1024]{1,0:T(8,128)(2,1)S(1)}, u32[]{:S(2)}, u32[]{:S(2)}) collective-permute-start(bf16[64,1024]{1,0:T(8,128)(2,1)S(1)} %add_convert_fusion.19), channel_id=1, source_target_pairs={{0,4},{1,5},{2,6},{3,7},{4,0},{5,1},{6,2},{7,3},{8,12},{9,13},{10,... | collective-permute-start | bytes 393224 | tf_op jit(solution)/shard_map/ppermute | solution.py:201
  378.3 7.4 %collective-permute-start.62 = (bf16[64,1024]{1,0:T(8,128)(2,1)S(1)}, bf16[64,1024]{1,0:T(8,128)(2,1)S(1)}, u32[]{:S(2)}, u32[]{:S(2)}) collective-permute-start(bf16[64,1024]{1,0:T(8,128)(2,1)S(1)} %add_convert_fusion.19), channel_id=1, source_target_pairs={{0,5},{1,4},{2,7},{3,6},{4,1},{5,0},{6,3},{7,2},{8,13},{9,12},{10,... | collective-permute-start | bytes 393224 | tf_op jit(solution)/shard_map/ppermute | solution.py:201
  399.2 8.1 %collective-permute-start.69 = (bf16[64,1024]{1,0:T(8,128)(2,1)S(1)}, bf16[64,1024]{1,0:T(8,128)(2,1)S(1)}, u32[]{:S(2)}, u32[]{:S(2)}) collective-permute-start(bf16[64,1024]{1,0:T(8,128)(2,1)S(1)} %add_convert_fusion.17), channel_id=1, source_target_pairs={{0,4},{1,5},{2,6},{3,7},{4,0},{5,1},{6,2},{7,3},{8,12},{9,13},{10,... | collective-permute-start | bytes 393224 | tf_op jit(solution)/shard_map/ppermute | solution.py:201
  412.0 8.1 %collective-permute-start.74 = (bf16[64,1024]{1,0:T(8,128)(2,1)S(1)}, bf16[64,1024]{1,0:T(8,128)(2,1)S(1)}, u32[]{:S(2)}, u32[]{:S(2)}) collective-permute-start(bf16[64,1024]{1,0:T(8,128)(2,1)S(1)} %add_convert_fusion.15), channel_id=1, source_target_pairs={{0,4},{1,5},{2,6},{3,7},{4,0},{5,1},{6,2},{7,3},{8,12},{9,13},{10,... | collective-permute-start | bytes 393224 | tf_op jit(solution)/shard_map/ppermute | solution.py:201
  420.2 9.6 %collective-permute-start.76 = (bf16[64,1024]{1,0:T(8,128)(2,1)S(1)}, bf16[64,1024]{1,0:T(8,128)(2,1)S(1)}, u32[]{:S(2)}, u32[]{:S(2)}) collective-permute-start(bf16[64,1024]{1,0:T(8,128)(2,1)S(1)} %add_convert_fusion.14), channel_id=1, source_target_pairs={{0,32},{1,33},{2,34},{3,35},{4,36},{5,37},{6,38},{7,39},{8,40},{9,... | collective-permute-start | bytes 393224 | tf_op jit(solution)/shard_map/ppermute | solution.py:201
  436.7 8.1 %collective-permute-start.80 = (bf16[64,1024]{1,0:T(8,128)(2,1)S(1)}, bf16[64,1024]{1,0:T(8,128)(2,1)S(1)}, u32[]{:S(2)}, u32[]{:S(2)}) collective-permute-start(bf16[64,1024]{1,0:T(8,128)(2,1)S(1)} %add_convert_fusion.13), channel_id=1, source_target_pairs={{0,4},{1,5},{2,6},{3,7},{4,0},{5,1},{6,2},{7,3},{8,12},{9,13},{10,... | collective-permute-start | bytes 393224 | tf_op jit(solution)/shard_map/ppermute | solution.py:201
  449.4 8.1 %collective-permute-start.85 = (bf16[64,1024]{1,0:T(8,128)(2,1)S(1)}, bf16[64,1024]{1,0:T(8,128)(2,1)S(1)}, u32[]{:S(2)}, u32[]{:S(2)}) collective-permute-start(bf16[64,1024]{1,0:T(8,128)(2,1)S(1)} %add_convert_fusion.11), channel_id=1, source_target_pairs={{0,4},{1,5},{2,6},{3,7},{4,0},{5,1},{6,2},{7,3},{8,12},{9,13},{10,... | collective-permute-start | bytes 393224 | tf_op jit(solution)/shard_map/ppermute | solution.py:201
  457.6 28.6 %collective-permute-start.87 = (bf16[64,1024]{1,0:T(8,128)(2,1)S(1)}, bf16[64,1024]{1,0:T(8,128)(2,1)S(1)}, u32[]{:S(2)}, u32[]{:S(2)}) collective-permute-start(bf16[64,1024]{1,0:T(8,128)(2,1)S(1)} %add_convert_fusion.10), channel_id=1, source_target_pairs={{0,32},{1,33},{2,34},{3,35},{4,36},{5,37},{6,38},{7,39},{8,40},{9,... | collective-permute-start | bytes 393224 | tf_op jit(solution)/shard_map/ppermute | solution.py:201
  498.4 19.3 %collective-permute-start.92 = (bf16[64,1024]{1,0:T(8,128)(2,1)}, bf16[64,1024]{1,0:T(8,128)(2,1)}, u32[]{:S(2)}, u32[]{:S(2)}) collective-permute-start(bf16[64,1024]{1,0:T(8,128)(2,1)} %add_convert_fusion.9), channel_id=1, source_target_pairs={{0,1},{1,0},{2,3},{3,2},{4,5},{5,4},{6,7},{7,6},{8,9},{9,8},{10,11... | collective-permute-start | bytes 393224 | tf_op jit(solution)/shard_map/ppermute | solution.py:201
  499.4 18.3 %collective-permute-start.91 = (bf16[64,1024]{1,0:T(8,128)(2,1)}, bf16[64,1024]{1,0:T(8,128)(2,1)}, u32[]{:S(2)}, u32[]{:S(2)}) collective-permute-start(bf16[64,1024]{1,0:T(8,128)(2,1)} %add_convert_fusion.9), channel_id=1, source_target_pairs={{0,4},{1,5},{2,6},{3,7},{4,0},{5,1},{6,2},{7,3},{8,12},{9,13},{10,... | collective-permute-start | bytes 393224 | tf_op jit(solution)/shard_map/ppermute | solution.py:201
  500.2 17.5 %collective-permute-start.90 = (bf16[64,1024]{1,0:T(8,128)(2,1)}, bf16[64,1024]{1,0:T(8,128)(2,1)}, u32[]{:S(2)}, u32[]{:S(2)}) collective-permute-start(bf16[64,1024]{1,0:T(8,128)(2,1)} %add_convert_fusion.9), channel_id=1, source_target_pairs={{0,5},{1,4},{2,7},{3,6},{4,1},{5,0},{6,3},{7,2},{8,13},{9,12},{10,... | collective-permute-start | bytes 393224 | tf_op jit(solution)/shard_map/ppermute | solution.py:201
  537.7 8.3 %collective-permute-start.96 = (bf16[64,1024]{1,0:T(8,128)(2,1)S(1)}, bf16[64,1024]{1,0:T(8,128)(2,1)S(1)}, u32[]{:S(2)}, u32[]{:S(2)}) collective-permute-start(bf16[64,1024]{1,0:T(8,128)(2,1)S(1)} %add_convert_fusion.7), channel_id=1, source_target_pairs={{0,4},{1,5},{2,6},{3,7},{4,0},{5,1},{6,2},{7,3},{8,12},{9,13},{10,... | collective-permute-start | bytes 393224 | tf_op jit(solution)/shard_map/ppermute | solution.py:201
  538.5 7.5 %collective-permute-start.95 = (bf16[64,1024]{1,0:T(8,128)(2,1)S(1)}, bf16[64,1024]{1,0:T(8,128)(2,1)S(1)}, u32[]{:S(2)}, u32[]{:S(2)}) collective-permute-start(bf16[64,1024]{1,0:T(8,128)(2,1)S(1)} %add_convert_fusion.7), channel_id=1, source_target_pairs={{0,5},{1,4},{2,7},{3,6},{4,1},{5,0},{6,3},{7,2},{8,13},{9,12},{10,... | collective-permute-start | bytes 393224 | tf_op jit(solution)/shard_map/ppermute | solution.py:201
  564.5 8.1 %collective-permute-start.102 = (bf16[64,1024]{1,0:T(8,128)(2,1)S(1)}, bf16[64,1024]{1,0:T(8,128)(2,1)S(1)}, u32[]{:S(2)}, u32[]{:S(2)}) collective-permute-start(bf16[64,1024]{1,0:T(8,128)(2,1)S(1)} %add_convert_fusion.5), channel_id=1, source_target_pairs={{0,4},{1,5},{2,6},{3,7},{4,0},{5,1},{6,2},{7,3},{8,12},{9,13},{10,... | collective-permute-start | bytes 393224 | tf_op jit(solution)/shard_map/ppermute | solution.py:201
  581.3 8.1 %collective-permute-start.107 = (bf16[64,1024]{1,0:T(8,128)(2,1)S(1)}, bf16[64,1024]{1,0:T(8,128)(2,1)S(1)}, u32[]{:S(2)}, u32[]{:S(2)}) collective-permute-start(bf16[64,1024]{1,0:T(8,128)(2,1)S(1)} %add_convert_fusion.3), channel_id=1, source_target_pairs={{0,4},{1,5},{2,6},{3,7},{4,0},{5,1},{6,2},{7,3},{8,12},{9,13},{10,... | collective-permute-start | bytes 393224 | tf_op jit(solution)/shard_map/ppermute | solution.py:201
  591.7 10.7 %collective-permute-start.111 = (bf16[2,16,1024]{2,1,0:T(8,128)(2,1)S(1)}, bf16[2,16,1024]{2,1,0:T(8,128)(2,1)S(1)}, u32[]{:S(2)}, u32[]{:S(2)}) collective-permute-start(bf16[2,16,1024]{2,1,0:T(8,128)(2,1)S(1)} %get-tuple-element.109), channel_id=1, source_target_pairs={{0,4},{1,5},{2,8},{3,9},{4,14},{5,15},{6,2},{7,3},{8,12},{9,13},{1... | collective-permute-start | bytes 196616 | tf_op jit(solution)/shard_map/ppermute | solution.py:201
  (164 other events, 1381.2 us)

commit v8 on v6

--- a/solution.py
+++ b/solution.py
@@ -70,6 +70,28 @@
             send_ref[:, cols] = term[HALF:]
 
 
+def settle_kernel(top_ref, bottom_ref, top_out, bottom_out, sems):
+    copies = [
+        pltpu.make_async_copy(top_ref, top_out, sems.at[0]),
+        pltpu.make_async_copy(bottom_ref, bottom_out, sems.at[1]),
+    ]
+    for copy in copies:
+        copy.start()
+    for copy in copies:
+        copy.wait()
+
+
+def settle(pair):
+    return list(pl.pallas_call(
+        settle_kernel,
+        out_shape=tuple(pltpu.VMEM(v.shape, v.dtype) for v in pair),
+        in_specs=[pl.BlockSpec(memory_space=pl.ANY)] * 2,
+        out_specs=(pl.BlockSpec(memory_space=pltpu.VMEM),) * 2,
+        scratch_shapes=[pltpu.SemaphoreType.DMA((2,))],
+        compiler_params=pltpu.CompilerParams(vmem_limit_bytes=8 * 1024 * 1024),
+    )(*pair))
+
+
 def run_layer(turn, place, mine, other, gain, biases, weights):
     rows, model = mine.shape
     width = weights[0].shape[1]
@@ -179,17 +201,19 @@
     def over_y(value):
         return move(value, lambda s, a, b: (s, a ^ 3, b))
 
-    def gather(top, bottom):
-        x_top, y_bottom = over_x(top), over_y(bottom)
-        top, bottom, x_top, y_bottom = lax.optimization_barrier((top, bottom, x_top, y_bottom))
-        far_top, far_bottom = over_y(x_top), over_x(y_bottom)
-        y_top, x_bottom = over_y(top), over_x(bottom)
-        return [top, bottom, x_top, x_bottom, y_top, y_bottom, far_top, far_bottom]
-
-    weights_a = gather(*[jnp.where(first, p, q) for p, q in zip(kept, got)])
+    def near(top, bottom):
+        return [over_x(top), over_y(bottom), over_x(bottom), over_y(top)]
+
+    def shards_of(own, x_top, y_bottom, x_bottom, y_top):
+        far = [over_y(x_top), over_x(y_bottom)]
+        return settle(own) + [x_top, x_bottom, y_top, y_bottom] + far
+
+    own_a = [jnp.where(first, p, q) for p, q in zip(kept, got)]
     own_b = [jnp.where(first, q, p) for p, q in zip(kept, got)]
-    own_b, weights_a[6:] = lax.optimization_barrier((own_b, weights_a[6:]))
-    weights_b = gather(*own_b)
+    near_a = near(*own_a)
+    own_b, near_a[:2] = lax.optimization_barrier((own_b, near_a[:2]))
+    weights_a = shards_of(own_a, *near_a)
+    weights_b = shards_of(own_b, *near(*own_b))
 
     inputs_all = lax.all_gather(inputs, "dp", axis=1, tiled=True)
     window_mine = lax.dynamic_slice_in_dim(inputs_all, start + HALF * core, HALF, 1)
@@ -217,20 +241,15 @@
             total = total + piece.astype(jnp.float32)
         return total.astype(jnp.bfloat16)
 
+    own_at = quarter * group + row_count * member - start
     side = jnp.where(member < SIDE // 2, group + 1, group - 1)
-    own_at = (quarter * group + row_count * member - start) % WINDOW
     side_at = (quarter * side + row_count * member - start) % WINDOW
-
-    def blocks(rows):
-        return jnp.stack([
-            lax.dynamic_slice_in_dim(rows, at % HALF, row_count, 0) for at in (own_at, side_at)
-        ])
-
-    blank = jnp.zeros((2, row_count, model), jnp.bfloat16)
+    at = jnp.where(own_at // HALF == core, own_at, side_at) % HALF
+    blank = jnp.zeros((row_count, model), jnp.bfloat16)
     stash = [[blank] * micro_count, [blank] * micro_count]
 
-    def keep_blocks(layer, turn, rows):
-        found = blocks(rows)
+    def keep_block(layer, turn, rows):
+        found = lax.dynamic_slice_in_dim(rows, at, row_count, 0)
         for m in range(micro_count):
             if 0 <= turn - m < planes:
                 stash[layer][m] = jnp.where(plane == turn - m, found, stash[layer][m])
@@ -246,21 +265,24 @@
             )
             mine = move(onward, lambda s, a, b: (s + 2, a, b))
             other = swap_cores(mine)
-        keep_blocks(0, turn, out_a)
-        keep_blocks(1, turn, out_b)
-
-    stash_a, stash_b = [jnp.stack(rows, axis=1) for rows in stash]
+        keep_block(0, turn, out_a)
+        keep_block(1, turn, out_b)
+
+    def owner(s, a, b):
+        g, t = (a // 2) * 2 + b // 2, (a % 2) * 2 + b % 2
+        lower = t < SIDE // 2
+        own_half = (quarter * g + row_count * t - STARTS[g]) // HALF
+        to_core, to = (0 if lower else 1), g
+        if s % 2 != own_half:
+            to_core, to = 1 - to_core, (g + (1 if lower else -1)) % SIDE
+        return (s - s % 2 + to_core, to, t)
+
+    moved = move(jnp.stack([jnp.stack(rows) for rows in stash]), owner)
+    stash_a, stash_b = moved[0], moved[1]
     here = jnp.where(first, stash_a, stash_b)
     there = swap_cores(jnp.where(first, stash_b, stash_a))
-
-    def owner(s, a, b, shift):
-        g, t = (a // 2) * 2 + b // 2, (a % 2) * 2 + b % 2
-        return (s, g + (0 if not shift else 1 if t < SIDE // 2 else -1), t)
-
-    mine = move(jnp.where(own_at // HALF == core, here[0], there[0]),
-                lambda s, a, b: owner(s, a, b, False))
-    other = move(jnp.where(side_at // HALF == core, here[1], there[1]),
-                 lambda s, a, b: owner(s, a, b, True))
+    has_own = first == (x < SIDE // 2)
+    mine, other = jnp.where(has_own, here, there), jnp.where(has_own, there, here)
     slots = place * row_count + jnp.arange(row_count, dtype=jnp.int32)
     picked = []
     for m in range(micro_count):

time: 572 us -> 568 us (level)
  waiting for transfers between devices: 306 us -> 295 us
  Pallas kernels: 60.9 us -> 52.2 us
  local copies, waits for them, and re-layouts: 13.5 us -> 21.8 us
  other arithmetic: 16.3 us -> 22.5 us
    ppermute x115 -> x114, waiting for transfers between devices: 306 us -> 295 us  [move(): return lax.ppermute(value, AXES, pairs)]
    pallas_call x18, Pallas kernels: 60.9 us -> 50.4 us  [run_layer(): pl.pallas_call(functools.partial(layer_kernel, turn), out_shape=(half, ha...]
    unnamed x100 -> x128, local copies, waits for them, and re-layouts: 6.5 us -> 16.9 us
    ppermute x115 -> x114, starting transfers between devices: 132 us -> 132 us  [move(): return lax.ppermute(value, AXES, pairs)]
  transfers between devices with their start and end apart: 116 -> 115, of which waited for: 90 -> 85; matrix products, arithmetic and copies ran while one was open for 2% -> 3% of each run, Pallas kernels for 1% -> 1%
where the time goes in v8:
time: 568 us; the launch traced here: 558 us
  waiting for transfers between devices  295 us (52%)
  starting transfers between devices  132 us (23%)
  Pallas kernels  52.2 us (9%)
  between operations  34 us (6%)
  other arithmetic  22.5 us (4%)
  local copies, waits for them, and re-layouts  21.8 us (4%)
    ppermute x114, waiting for transfers between devices, move(): return lax.ppermute(value, AXES, pairs)  295 us
    ppermute x114, starting transfers between devices, move(): return lax.ppermute(value, AXES, pairs)  132 us
    pallas_call x18, Pallas kernels, run_layer(): pl.pallas_call(functools.partial(layer_kernel, turn), out_shape=(half, ha...  50.4 us
    unnamed x128, local copies, waits for them, and re-layouts  16.9 us
  transfers between devices with their start and end apart: 115, of which 85 were waited for; matrix products, arithmetic and copies ran while one was open for 3% of the time, Pallas kernels for 1%

profile of v8, /device:TPU:224, one launch (start us, length us, event | category | flops | bytes accessed | tf_op | source)
XLA Modules:
  0.0 557.6 jit_solution(14248612440875601808)
XLA Ops:
  15.4 3.0 collective-permute-start.4
  18.4 3.1 broadcast_select_fusion.1
  28.3 15.5 %collective-permute-done.4.refs_5_ = bf16[2048,256]{1,0:T(8,128)(2,1)S(1)} collective-permute-done((bf16[2048,256]{1,0:T(8,128)(2,1)}, bf16[2048,256]{1,0:T(8,128)(2,1)S(1)}, u32[]{:S(2)}, u32[]{:S(2)}) %collective-permute-start.4) | collective-permute-done | bytes 1048608 | tf_op jit(solution)/shard_map/ppermute | solution.py:176
  43.8 6.7 %collective-permute-done.3.refs_2_ = bf16[2048,256]{1,0:T(8,128)(2,1)S(1)} collective-permute-done((bf16[2048,256]{1,0:T(8,128)(2,1)}, bf16[2048,256]{1,0:T(8,128)(2,1)S(1)}, u32[]{:S(2)}, u32[]{:S(2)}) %collective-permute-start.3) | collective-permute-done | bytes 1048608 | tf_op jit(solution)/shard_map/ppermute | solution.py:176
  50.5 3.6 collective-permute-start.8
  54.9 21.8 %collective-permute-done.5.refs_3_ = bf16[2048,256]{1,0:T(8,128)(2,1)} collective-permute-done((bf16[2048,256]{1,0:T(8,128)(2,1)}, bf16[2048,256]{1,0:T(8,128)(2,1)}, u32[]{:S(2)}, u32[]{:S(2)}) %collective-permute-start.5) | collective-permute-done | bytes 1048608 | tf_op jit(solution)/shard_map/ppermute | solution.py:176
  83.1 10.0 %collective-permute-done.7.refs_6_ = bf16[2048,256]{1,0:T(8,128)(2,1)} collective-permute-done((bf16[2048,256]{1,0:T(8,128)(2,1)S(1)}, bf16[2048,256]{1,0:T(8,128)(2,1)}, u32[]{:S(2)}, u32[]{:S(2)}) %collective-permute-start.7) | collective-permute-done | bytes 1048608 | tf_op jit(solution)/shard_map/ppermute | solution.py:176
  93.1 6.1 %collective-permute-done.8.refs_7_ = bf16[2048,256]{1,0:T(8,128)(2,1)} collective-permute-done((bf16[2048,256]{1,0:T(8,128)(2,1)S(1)}, bf16[2048,256]{1,0:T(8,128)(2,1)}, u32[]{:S(2)}, u32[]{:S(2)}) %collective-permute-start.8) | collective-permute-done | bytes 1048608 | tf_op jit(solution)/shard_map/ppermute | solution.py:176
  107.4 14.2 %collective-permute-done.14.refs_2_ = bf16[2048,256]{1,0:T(8,128)(2,1)S(1)} collective-permute-done((bf16[2048,256]{1,0:T(8,128)(2,1)}, bf16[2048,256]{1,0:T(8,128)(2,1)S(1)}, u32[]{:S(2)}, u32[]{:S(2)}) %collective-permute-start.14) | collective-permute-done | bytes 1048608 | tf_op jit(solution)/shard_map/ppermute | solution.py:176
  124.7 6.0 %collective-permute-done.10 = bf16[64,1024]{1,0:T(8,128)(2,1)S(1)} collective-permute-done((bf16[64,1024]{1,0:T(8,128)(2,1)S(1)}, bf16[64,1024]{1,0:T(8,128)(2,1)S(1)}, u32[]{:S(2)}, u32[]{:S(2)}) %collective-permute-start.10) | collective-permute-done | bytes 131104 | tf_op jit(solution)/shard_map/ppermute | solution.py:176
  131.1 4.6 collective-permute-done.11
  135.7 5.0 collective-permute-done.12
  141.0 3.1 collective-permute-done.15.refs_3_
  144.1 15.5 %collective-permute-done.18.refs_6_ = bf16[2048,256]{1,0:T(8,128)(2,1)S(1)} collective-permute-done((bf16[2048,256]{1,0:T(8,128)(2,1)S(1)}, bf16[2048,256]{1,0:T(8,128)(2,1)S(1)}, u32[]{:S(2)}, u32[]{:S(2)}) %collective-permute-start.18) | collective-permute-done | bytes 1048608 | tf_op jit(solution)/shard_map/ppermute | solution.py:176
  159.6 5.8 %collective-permute-done.19.refs_7_ = bf16[2048,256]{1,0:T(8,128)(2,1)S(1)} collective-permute-done((bf16[2048,256]{1,0:T(8,128)(2,1)}, bf16[2048,256]{1,0:T(8,128)(2,1)S(1)}, u32[]{:S(2)}, u32[]{:S(2)}) %collective-permute-start.19) | collective-permute-done | bytes 1048608 | tf_op jit(solution)/shard_map/ppermute | solution.py:176
  172.7 4.0 collective-permute-done.21
  181.2 3.5 collective-permute-done.24.mine_ref
  194.9 3.8 collective-permute-done.27
  208.6 3.8 collective-permute-done.32
  214.5 10.8 %collective-permute-start.35 = (bf16[64,1024]{1,0:T(8,128)(2,1)S(1)}, bf16[64,1024]{1,0:T(8,128)(2,1)S(1)}, u32[]{:S(2)}, u32[]{:S(2)}) collective-permute-start(bf16[64,1024]{1,0:T(8,128)(2,1)S(1)} %add_convert_fusion.27), channel_id=1, source_target_pairs={{0,32},{1,33},{2,34},{3,35},{4,36},{5,37},{6,38},{7,39},{8,40},{9,... | collective-permute-start | bytes 393224 | tf_op jit(solution)/shard_map/ppermute | solution.py:176
  237.2 3.8 collective-permute-done.38
  250.9 3.8 collective-permute-done.43
  256.7 3.8 collective-permute-start.46
  260.5 2.9 collective-permute-done.46.mine_ref
  272.2 3.8 collective-permute-done.49
  285.8 3.8 collective-permute-done.54
  291.7 7.2 %collective-permute-start.57 = (bf16[64,1024]{1,0:T(8,128)(2,1)S(1)}, bf16[64,1024]{1,0:T(8,128)(2,1)S(1)}, u32[]{:S(2)}, u32[]{:S(2)}) collective-permute-start(bf16[64,1024]{1,0:T(8,128)(2,1)S(1)} %add_convert_fusion.19), channel_id=1, source_target_pairs={{0,32},{1,33},{2,34},{3,35},{4,36},{5,37},{6,38},{7,39},{8,40},{9,... | collective-permute-start | bytes 393224 | tf_op jit(solution)/shard_map/ppermute | solution.py:176
  298.9 2.9 collective-permute-done.57.mine_ref
  310.7 3.8 collective-permute-done.60
  324.3 3.8 collective-permute-done.65
  330.2 3.8 collective-permute-start.68
  333.9 2.9 collective-permute-done.68.mine_ref
  345.9 3.8 collective-permute-done.71
  359.5 3.8 collective-permute-done.76
  365.4 7.2 %collective-permute-start.79 = (bf16[64,1024]{1,0:T(8,128)(2,1)S(1)}, bf16[64,1024]{1,0:T(8,128)(2,1)S(1)}, u32[]{:S(2)}, u32[]{:S(2)}) collective-permute-start(bf16[64,1024]{1,0:T(8,128)(2,1)S(1)} %add_convert_fusion.11), channel_id=1, source_target_pairs={{0,32},{1,33},{2,34},{3,35},{4,36},{5,37},{6,38},{7,39},{8,40},{9,... | collective-permute-start | bytes 393224 | tf_op jit(solution)/shard_map/ppermute | solution.py:176
  372.6 2.9 collective-permute-done.79.mine_ref
  384.3 3.8 collective-permute-done.82
  397.9 3.8 collective-permute-done.87
  403.8 3.8 collective-permute-start.90
  407.6 25.5 %collective-permute-done.90.mine_ref = bf16[64,1024]{1,0:T(8,128)(2,1)S(1)} collective-permute-done((bf16[64,1024]{1,0:T(8,128)(2,1)S(1)}, bf16[64,1024]{1,0:T(8,128)(2,1)S(1)}, u32[]{:S(2)}, u32[]{:S(2)}) %collective-permute-start.90) | collective-permute-done | bytes 131104 | tf_op jit(solution)/shard_map/ppermute | solution.py:176
  434.4 6.4 %shard_map.116 = (bf16[64,1024]{1,0:T(8,128)(2,1)S(1)}, bf16[64,1024]{1,0:T(8,128)(2,1)S(1)}) custom-call(s32[5]{0:T(128)S(1)} %pad_add_fusion.1.place_ref, bf16[64,1024]{1,0:T(8,128)(2,1)S(1)} %collective-permute-done.90.mine_ref, bf16[64,1024]{1,0:T(8,128)(2,1)S(1)} %collective-permute-done.91.other_ref, f32[1,1024]{1,0:T(1,128)S(1)} %get-tuple-element.132.gain_ref, ...), custom_call_target="tpu_custom_call" | custom-call | flops 1073741824 | bytes 8388608 | tf_op jit(solution)/shard_map/pallas_call | solution.py:101
  445.9 3.8 collective-permute-done.93
  453.2 5.3 shard_map.117
  466.4 3.0 collective-permute-done.98
  471.0 5.9 %collective-permute-done.101.mine_ref = bf16[64,1024]{1,0:T(8,128)(2,1)S(1)} collective-permute-done((bf16[64,1024]{1,0:T(8,128)(2,1)S(1)}, bf16[64,1024]{1,0:T(8,128)(2,1)S(1)}, u32[]{:S(2)}, u32[]{:S(2)}) %collective-permute-start.101) | collective-permute-done | bytes 131104 | tf_op jit(solution)/shard_map/ppermute | solution.py:176
  478.9 6.5 %shard_map.118 = (bf16[64,1024]{1,0:T(8,128)(2,1)S(1)}, bf16[64,1024]{1,0:T(8,128)(2,1)S(1)}) custom-call(s32[5]{0:T(128)S(1)} %pad_add_fusion.1.place_ref, bf16[64,1024]{1,0:T(8,128)(2,1)S(1)} %collective-permute-done.101.mine_ref, bf16[64,1024]{1,0:T(8,128)(2,1)S(1)} %collective-permute-done.102.other_ref, f32[1,1024]{1,0:T(1,128)S(1)} %get-tuple-element.132.gain_ref, ...), custom_call_target="tpu_custom_call" | custom-call | flops 1073741824 | bytes 8388608 | tf_op jit(solution)/shard_map/pallas_call | solution.py:101
  517.1 5.9 %shard_map.119 = (bf16[64,1024]{1,0:T(8,128)(2,1)S(1)}, bf16[64,1024]{1,0:T(8,128)(2,1)}) custom-call(s32[5]{0:T(128)S(1)} %pad_add_fusion.1.place_ref, bf16[64,1024]{1,0:T(8,128)(2,1)S(1)} %copy-done.34, bf16[64,1024]{1,0:T(8,128)(2,1)S(1)} %copy-done.37, f32[1,1024]{1,0:T(1,128)S(1)} %get-tuple-element.131.gain_ref, ...), custom_call_target="tpu_custom_call" | custom-call | flops 1073741824 | bytes 8388608 | tf_op jit(solution)/shard_map/pallas_call | solution.py:101
  538.7 9.9 %collective-permute-start.113 = (bf16[2,16,1024]{2,1,0:T(8,128)(2,1)S(1)}, bf16[2,16,1024]{2,1,0:T(8,128)(2,1)S(1)}, u32[]{:S(2)}, u32[]{:S(2)}) collective-permute-start(bf16[2,16,1024]{2,1,0:T(8,128)(2,1)S(1)} %select_bitcast_fusion), channel_id=1, source_target_pairs={{0,16},{1,17},{2,18},{3,19},{4,20},{5,21},{6,22},{7,23},{8,24},{9,... | collective-permute-start | bytes 196616 | tf_op jit(solution)/shard_map/ppermute | solution.py:176
  (416 shorter events, 226.4 us)
Async XLA Ops:
  6.5 75.5 %all-gather.2.cloned.1.call-start = ((), (), s32[]{:S(2)}) async-start(), calls=%async_computation | async-start | bytes 1114112 | tf_op jit(solution)/shard_map/all_gather | solution.py:218
  11.8 43.1 %collective-permute-start = (f32[1,1024]{1,0:T(1,128)S(1)}, f32[1,1024]{1,0:T(1,128)S(1)}, u32[]{:S(2)}, u32[]{:S(2)}) collective-permute-start(f32[1,1024]{1,0:T(1,128)S(1)} %copy-done.58), channel_id=1, source_target_pairs={{0,16},{1,17},{2,18},{3,19},{4,20},{5,21},{6,22},{7,23},{8,24},{9,... | collective-permute-start | bytes 12296 | tf_op jit(solution)/shard_map/ppermute | solution.py:176
  15.4 28.5 %collective-permute-start.4 = (bf16[2048,256]{1,0:T(8,128)(2,1)}, bf16[2048,256]{1,0:T(8,128)(2,1)S(1)}, u32[]{:S(2)}, u32[]{:S(2)}) collective-permute-start(bf16[2048,256]{1,0:T(8,128)(2,1)} %get-tuple-element.112.bottom_ref), channel_id=1, source_target_pairs={{0,12},{1,13},{2,14},{3,15},{4,8},{5,9},{6,10},{7,11},{8,4},{9,5},... | collective-permute-start | bytes 3145736 | tf_op jit(solution)/shard_map/ppermute | solution.py:176
  21.5 29.1 %collective-permute-start.3 = (bf16[2048,256]{1,0:T(8,128)(2,1)}, bf16[2048,256]{1,0:T(8,128)(2,1)S(1)}, u32[]{:S(2)}, u32[]{:S(2)}) collective-permute-start(bf16[2048,256]{1,0:T(8,128)(2,1)} %get-tuple-element.114.top_ref), channel_id=1, source_target_pairs={{0,3},{1,2},{2,1},{3,0},{4,7},{5,6},{6,5},{7,4},{8,11},{9,10},{10,... | collective-permute-start | bytes 3145736 | tf_op jit(solution)/shard_map/ppermute | solution.py:176
  26.4 50.4 %collective-permute-start.5 = (bf16[2048,256]{1,0:T(8,128)(2,1)}, bf16[2048,256]{1,0:T(8,128)(2,1)}, u32[]{:S(2)}, u32[]{:S(2)}) collective-permute-start(bf16[2048,256]{1,0:T(8,128)(2,1)} %get-tuple-element.112.bottom_ref), channel_id=1, source_target_pairs={{0,3},{1,2},{2,1},{3,0},{4,7},{5,6},{6,5},{7,4},{8,11},{9,10},{10,... | collective-permute-start | bytes 3145736 | tf_op jit(solution)/shard_map/ppermute | solution.py:176
  28.1 55.0 %collective-permute-start.6 = (bf16[2048,256]{1,0:T(8,128)(2,1)}, bf16[2048,256]{1,0:T(8,128)(2,1)}, u32[]{:S(2)}, u32[]{:S(2)}) collective-permute-start(bf16[2048,256]{1,0:T(8,128)(2,1)} %get-tuple-element.114.top_ref), channel_id=1, source_target_pairs={{0,12},{1,13},{2,14},{3,15},{4,8},{5,9},{6,10},{7,11},{8,4},{9,5},... | collective-permute-start | bytes 3145736 | tf_op jit(solution)/shard_map/ppermute | solution.py:176
  50.5 42.6 %collective-permute-start.7 = (bf16[2048,256]{1,0:T(8,128)(2,1)S(1)}, bf16[2048,256]{1,0:T(8,128)(2,1)}, u32[]{:S(2)}, u32[]{:S(2)}) collective-permute-start(bf16[2048,256]{1,0:T(8,128)(2,1)S(1)} %collective-permute-done.3.refs_2_), channel_id=1, source_target_pairs={{0,12},{1,13},{2,14},{3,15},{4,8},{5,9},{6,10},{7,11},{8,4},{9,5},... | collective-permute-start | bytes 3145736 | tf_op jit(solution)/shard_map/ppermute | solution.py:176
  50.5 48.7 %collective-permute-start.8 = (bf16[2048,256]{1,0:T(8,128)(2,1)S(1)}, bf16[2048,256]{1,0:T(8,128)(2,1)}, u32[]{:S(2)}, u32[]{:S(2)}) collective-permute-start(bf16[2048,256]{1,0:T(8,128)(2,1)S(1)} %collective-permute-done.4.refs_5_), channel_id=1, source_target_pairs={{0,3},{1,2},{2,1},{3,0},{4,7},{5,6},{6,5},{7,4},{8,11},{9,10},{10,... | collective-permute-start | bytes 3145736 | tf_op jit(solution)/shard_map/ppermute | solution.py:176
  54.9 66.7 %collective-permute-start.14 = (bf16[2048,256]{1,0:T(8,128)(2,1)}, bf16[2048,256]{1,0:T(8,128)(2,1)S(1)}, u32[]{:S(2)}, u32[]{:S(2)}) collective-permute-start(bf16[2048,256]{1,0:T(8,128)(2,1)} %get-tuple-element.55.top_ref), channel_id=1, source_target_pairs={{0,3},{1,2},{2,1},{3,0},{4,7},{5,6},{6,5},{7,4},{8,11},{9,10},{10,... | collective-permute-start | bytes 3145736 | tf_op jit(solution)/shard_map/ppermute | solution.py:176
  76.8 45.0 %collective-permute-start.17 = (bf16[2048,256]{1,0:T(8,128)(2,1)}, bf16[2048,256]{1,0:T(8,128)(2,1)}, u32[]{:S(2)}, u32[]{:S(2)}) collective-permute-start(bf16[2048,256]{1,0:T(8,128)(2,1)} %get-tuple-element.56.bottom_ref), channel_id=1, source_target_pairs={{0,12},{1,13},{2,14},{3,15},{4,8},{5,9},{6,10},{7,11},{8,4},{9,5},... | collective-permute-start | bytes 3145736 | tf_op jit(solution)/shard_map/ppermute | solution.py:176
  104.1 20.5 %collective-permute-start.9 = (bf16[64,1024]{1,0:T(8,128)(2,1)S(1)}, bf16[64,1024]{1,0:T(8,128)(2,1)S(1)}, u32[]{:S(2)}, u32[]{:S(2)}) collective-permute-start(bf16[64,1024]{1,0:T(8,128)(2,1)S(1)} %get-tuple-element.54), channel_id=1, source_target_pairs={{0,16},{1,17},{2,18},{3,19},{4,20},{5,21},{6,22},{7,23},{8,24},{9,... | collective-permute-start | bytes 393224 | tf_op jit(solution)/shard_map/ppermute | solution.py:176
  104.2 39.9 %collective-permute-start.15 = (bf16[2048,256]{1,0:T(8,128)(2,1)S(1)}, bf16[2048,256]{1,0:T(8,128)(2,1)S(1)}, u32[]{:S(2)}, u32[]{:S(2)}) collective-permute-start(bf16[2048,256]{1,0:T(8,128)(2,1)S(1)} %copy-done.25), channel_id=1, source_target_pairs={{0,3},{1,2},{2,1},{3,0},{4,7},{5,6},{6,5},{7,4},{8,11},{9,10},{10,... | collective-permute-start | bytes 3145736 | tf_op jit(solution)/shard_map/ppermute | solution.py:176
  107.0 37.1 %collective-permute-start.16 = (bf16[2048,256]{1,0:T(8,128)(2,1)S(1)}, bf16[2048,256]{1,0:T(8,128)(2,1)S(1)}, u32[]{:S(2)}, u32[]{:S(2)}) collective-permute-start(bf16[2048,256]{1,0:T(8,128)(2,1)S(1)} %copy-done.26), channel_id=1, source_target_pairs={{0,12},{1,13},{2,14},{3,15},{4,8},{5,9},{6,10},{7,11},{8,4},{9,5},... | collective-permute-start | bytes 3145736 | tf_op jit(solution)/shard_map/ppermute | solution.py:176
  121.6 38.0 %collective-permute-start.18 = (bf16[2048,256]{1,0:T(8,128)(2,1)S(1)}, bf16[2048,256]{1,0:T(8,128)(2,1)S(1)}, u32[]{:S(2)}, u32[]{:S(2)}) collective-permute-start(bf16[2048,256]{1,0:T(8,128)(2,1)S(1)} %collective-permute-done.14.refs_2_), channel_id=1, source_target_pairs={{0,12},{1,13},{2,14},{3,15},{4,8},{5,9},{6,10},{7,11},{8,4},{9,5},... | collective-permute-start | bytes 3145736 | tf_op jit(solution)/shard_map/ppermute | solution.py:176
  121.8 43.5 %collective-permute-start.19 = (bf16[2048,256]{1,0:T(8,128)(2,1)}, bf16[2048,256]{1,0:T(8,128)(2,1)S(1)}, u32[]{:S(2)}, u32[]{:S(2)}) collective-permute-start(bf16[2048,256]{1,0:T(8,128)(2,1)} %collective-permute-done.17.refs_5_), channel_id=1, source_target_pairs={{0,3},{1,2},{2,1},{3,0},{4,7},{5,6},{6,5},{7,4},{8,11},{9,10},{10,... | collective-permute-start | bytes 3145736 | tf_op jit(solution)/shard_map/ppermute | solution.py:176
  169.2 7.5 %collective-permute-start.21 = (bf16[64,1024]{1,0:T(8,128)(2,1)}, bf16[64,1024]{1,0:T(8,128)(2,1)S(1)}, u32[]{:S(2)}, u32[]{:S(2)}) collective-permute-start(bf16[64,1024]{1,0:T(8,128)(2,1)} %add_convert_fusion.32), channel_id=1, source_target_pairs={{0,5},{1,4},{2,7},{3,6},{4,1},{5,0},{6,3},{7,2},{8,13},{9,12},{10,... | collective-permute-start | bytes 393224 | tf_op jit(solution)/shard_map/ppermute | solution.py:176
  169.2 8.7 %collective-permute-start.22 = (bf16[64,1024]{1,0:T(8,128)(2,1)}, bf16[64,1024]{1,0:T(8,128)(2,1)}, u32[]{:S(2)}, u32[]{:S(2)}) collective-permute-start(bf16[64,1024]{1,0:T(8,128)(2,1)} %add_convert_fusion.32), channel_id=1, source_target_pairs={{0,4},{1,5},{2,6},{3,7},{4,0},{5,1},{6,2},{7,3},{8,12},{9,13},{10,... | collective-permute-start | bytes 393224 | tf_op jit(solution)/shard_map/ppermute | solution.py:176
  191.4 7.3 %collective-permute-start.27 = (bf16[64,1024]{1,0:T(8,128)(2,1)S(1)}, bf16[64,1024]{1,0:T(8,128)(2,1)S(1)}, u32[]{:S(2)}, u32[]{:S(2)}) collective-permute-start(bf16[64,1024]{1,0:T(8,128)(2,1)S(1)} %add_convert_fusion.30), channel_id=1, source_target_pairs={{0,5},{1,4},{2,7},{3,6},{4,1},{5,0},{6,3},{7,2},{8,13},{9,12},{10,... | collective-permute-start | bytes 393224 | tf_op jit(solution)/shard_map/ppermute | solution.py:176
  193.1 7.6 %collective-permute-start.28 = (bf16[64,1024]{1,0:T(8,128)(2,1)S(1)}, bf16[64,1024]{1,0:T(8,128)(2,1)S(1)}, u32[]{:S(2)}, u32[]{:S(2)}) collective-permute-start(bf16[64,1024]{1,0:T(8,128)(2,1)S(1)} %add_convert_fusion.30), channel_id=1, source_target_pairs={{0,4},{1,5},{2,6},{3,7},{4,0},{5,1},{6,2},{7,3},{8,12},{9,13},{10,... | collective-permute-start | bytes 393224 | tf_op jit(solution)/shard_map/ppermute | solution.py:176
  205.1 7.3 %collective-permute-start.32 = (bf16[64,1024]{1,0:T(8,128)(2,1)S(1)}, bf16[64,1024]{1,0:T(8,128)(2,1)S(1)}, u32[]{:S(2)}, u32[]{:S(2)}) collective-permute-start(bf16[64,1024]{1,0:T(8,128)(2,1)S(1)} %add_convert_fusion.28), channel_id=1, source_target_pairs={{0,5},{1,4},{2,7},{3,6},{4,1},{5,0},{6,3},{7,2},{8,13},{9,12},{10,... | collective-permute-start | bytes 393224 | tf_op jit(solution)/shard_map/ppermute | solution.py:176
  206.8 7.6 %collective-permute-start.33 = (bf16[64,1024]{1,0:T(8,128)(2,1)S(1)}, bf16[64,1024]{1,0:T(8,128)(2,1)S(1)}, u32[]{:S(2)}, u32[]{:S(2)}) collective-permute-start(bf16[64,1024]{1,0:T(8,128)(2,1)S(1)} %add_convert_fusion.28), channel_id=1, source_target_pairs={{0,4},{1,5},{2,6},{3,7},{4,0},{5,1},{6,2},{7,3},{8,12},{9,13},{10,... | collective-permute-start | bytes 393224 | tf_op jit(solution)/shard_map/ppermute | solution.py:176
  214.5 13.7 %collective-permute-start.35 = (bf16[64,1024]{1,0:T(8,128)(2,1)S(1)}, bf16[64,1024]{1,0:T(8,128)(2,1)S(1)}, u32[]{:S(2)}, u32[]{:S(2)}) collective-permute-start(bf16[64,1024]{1,0:T(8,128)(2,1)S(1)} %add_convert_fusion.27), channel_id=1, source_target_pairs={{0,32},{1,33},{2,34},{3,35},{4,36},{5,37},{6,38},{7,39},{8,40},{9,... | collective-permute-start | bytes 393224 | tf_op jit(solution)/shard_map/ppermute | solution.py:176
  233.7 7.3 %collective-permute-start.38 = (bf16[64,1024]{1,0:T(8,128)(2,1)S(1)}, bf16[64,1024]{1,0:T(8,128)(2,1)S(1)}, u32[]{:S(2)}, u32[]{:S(2)}) collective-permute-start(bf16[64,1024]{1,0:T(8,128)(2,1)S(1)} %add_convert_fusion.26), channel_id=1, source_target_pairs={{0,5},{1,4},{2,7},{3,6},{4,1},{5,0},{6,3},{7,2},{8,13},{9,12},{10,... | collective-permute-start | bytes 393224 | tf_op jit(solution)/shard_map/ppermute | solution.py:176
  235.4 7.6 %collective-permute-start.39 = (bf16[64,1024]{1,0:T(8,128)(2,1)S(1)}, bf16[64,1024]{1,0:T(8,128)(2,1)S(1)}, u32[]{:S(2)}, u32[]{:S(2)}) collective-permute-start(bf16[64,1024]{1,0:T(8,128)(2,1)S(1)} %add_convert_fusion.26), channel_id=1, source_target_pairs={{0,4},{1,5},{2,6},{3,7},{4,0},{5,1},{6,2},{7,3},{8,12},{9,13},{10,... | collective-permute-start | bytes 393224 | tf_op jit(solution)/shard_map/ppermute | solution.py:176
  249.0 7.6 %collective-permute-start.44 = (bf16[64,1024]{1,0:T(8,128)(2,1)S(1)}, bf16[64,1024]{1,0:T(8,128)(2,1)S(1)}, u32[]{:S(2)}, u32[]{:S(2)}) collective-permute-start(bf16[64,1024]{1,0:T(8,128)(2,1)S(1)} %add_convert_fusion.24), channel_id=1, source_target_pairs={{0,4},{1,5},{2,6},{3,7},{4,0},{5,1},{6,2},{7,3},{8,12},{9,13},{10,... | collective-permute-start | bytes 393224 | tf_op jit(solution)/shard_map/ppermute | solution.py:176
  270.3 7.6 %collective-permute-start.50 = (bf16[64,1024]{1,0:T(8,128)(2,1)S(1)}, bf16[64,1024]{1,0:T(8,128)(2,1)S(1)}, u32[]{:S(2)}, u32[]{:S(2)}) collective-permute-start(bf16[64,1024]{1,0:T(8,128)(2,1)S(1)} %add_convert_fusion.22), channel_id=1, source_target_pairs={{0,4},{1,5},{2,6},{3,7},{4,0},{5,1},{6,2},{7,3},{8,12},{9,13},{10,... | collective-permute-start | bytes 393224 | tf_op jit(solution)/shard_map/ppermute | solution.py:176
  282.2 7.3 %collective-permute-start.54 = (bf16[64,1024]{1,0:T(8,128)(2,1)S(1)}, bf16[64,1024]{1,0:T(8,128)(2,1)S(1)}, u32[]{:S(2)}, u32[]{:S(2)}) collective-permute-start(bf16[64,1024]{1,0:T(8,128)(2,1)S(1)} %add_convert_fusion.20), channel_id=1, source_target_pairs={{0,5},{1,4},{2,7},{3,6},{4,1},{5,0},{6,3},{7,2},{8,13},{9,12},{10,... | collective-permute-start | bytes 393224 | tf_op jit(solution)/shard_map/ppermute | solution.py:176
  284.0 7.6 %collective-permute-start.55 = (bf16[64,1024]{1,0:T(8,128)(2,1)S(1)}, bf16[64,1024]{1,0:T(8,128)(2,1)S(1)}, u32[]{:S(2)}, u32[]{:S(2)}) collective-permute-start(bf16[64,1024]{1,0:T(8,128)(2,1)S(1)} %add_convert_fusion.20), channel_id=1, source_target_pairs={{0,4},{1,5},{2,6},{3,7},{4,0},{5,1},{6,2},{7,3},{8,12},{9,13},{10,... | collective-permute-start | bytes 393224 | tf_op jit(solution)/shard_map/ppermute | solution.py:176
  291.7 10.2 %collective-permute-start.57 = (bf16[64,1024]{1,0:T(8,128)(2,1)S(1)}, bf16[64,1024]{1,0:T(8,128)(2,1)S(1)}, u32[]{:S(2)}, u32[]{:S(2)}) collective-permute-start(bf16[64,1024]{1,0:T(8,128)(2,1)S(1)} %add_convert_fusion.19), channel_id=1, source_target_pairs={{0,32},{1,33},{2,34},{3,35},{4,36},{5,37},{6,38},{7,39},{8,40},{9,... | collective-permute-start | bytes 393224 | tf_op jit(solution)/shard_map/ppermute | solution.py:176
  307.1 7.3 %collective-permute-start.60 = (bf16[64,1024]{1,0:T(8,128)(2,1)S(1)}, bf16[64,1024]{1,0:T(8,128)(2,1)S(1)}, u32[]{:S(2)}, u32[]{:S(2)}) collective-permute-start(bf16[64,1024]{1,0:T(8,128)(2,1)S(1)} %add_convert_fusion.18), channel_id=1, source_target_pairs={{0,5},{1,4},{2,7},{3,6},{4,1},{5,0},{6,3},{7,2},{8,13},{9,12},{10,... | collective-permute-start | bytes 393224 | tf_op jit(solution)/shard_map/ppermute | solution.py:176
  308.8 7.6 %collective-permute-start.61 = (bf16[64,1024]{1,0:T(8,128)(2,1)S(1)}, bf16[64,1024]{1,0:T(8,128)(2,1)S(1)}, u32[]{:S(2)}, u32[]{:S(2)}) collective-permute-start(bf16[64,1024]{1,0:T(8,128)(2,1)S(1)} %add_convert_fusion.18), channel_id=1, source_target_pairs={{0,4},{1,5},{2,6},{3,7},{4,0},{5,1},{6,2},{7,3},{8,12},{9,13},{10,... | collective-permute-start | bytes 393224 | tf_op jit(solution)/shard_map/ppermute | solution.py:176
  322.4 7.6 %collective-permute-start.66 = (bf16[64,1024]{1,0:T(8,128)(2,1)S(1)}, bf16[64,1024]{1,0:T(8,128)(2,1)S(1)}, u32[]{:S(2)}, u32[]{:S(2)}) collective-permute-start(bf16[64,1024]{1,0:T(8,128)(2,1)S(1)} %add_convert_fusion.16), channel_id=1, source_target_pairs={{0,4},{1,5},{2,6},{3,7},{4,0},{5,1},{6,2},{7,3},{8,12},{9,13},{10,... | collective-permute-start | bytes 393224 | tf_op jit(solution)/shard_map/ppermute | solution.py:176
  344.0 7.6 %collective-permute-start.72 = (bf16[64,1024]{1,0:T(8,128)(2,1)S(1)}, bf16[64,1024]{1,0:T(8,128)(2,1)S(1)}, u32[]{:S(2)}, u32[]{:S(2)}) collective-permute-start(bf16[64,1024]{1,0:T(8,128)(2,1)S(1)} %add_convert_fusion.14), channel_id=1, source_target_pairs={{0,4},{1,5},{2,6},{3,7},{4,0},{5,1},{6,2},{7,3},{8,12},{9,13},{10,... | collective-permute-start | bytes 393224 | tf_op jit(solution)/shard_map/ppermute | solution.py:176
  357.6 7.6 %collective-permute-start.77 = (bf16[64,1024]{1,0:T(8,128)(2,1)S(1)}, bf16[64,1024]{1,0:T(8,128)(2,1)S(1)}, u32[]{:S(2)}, u32[]{:S(2)}) collective-permute-start(bf16[64,1024]{1,0:T(8,128)(2,1)S(1)} %add_convert_fusion.12), channel_id=1, source_target_pairs={{0,4},{1,5},{2,6},{3,7},{4,0},{5,1},{6,2},{7,3},{8,12},{9,13},{10,... | collective-permute-start | bytes 393224 | tf_op jit(solution)/shard_map/ppermute | solution.py:176
  365.4 10.2 %collective-permute-start.79 = (bf16[64,1024]{1,0:T(8,128)(2,1)S(1)}, bf16[64,1024]{1,0:T(8,128)(2,1)S(1)}, u32[]{:S(2)}, u32[]{:S(2)}) collective-permute-start(bf16[64,1024]{1,0:T(8,128)(2,1)S(1)} %add_convert_fusion.11), channel_id=1, source_target_pairs={{0,32},{1,33},{2,34},{3,35},{4,36},{5,37},{6,38},{7,39},{8,40},{9,... | collective-permute-start | bytes 393224 | tf_op jit(solution)/shard_map/ppermute | solution.py:176
  382.4 7.6 %collective-permute-start.83 = (bf16[64,1024]{1,0:T(8,128)(2,1)S(1)}, bf16[64,1024]{1,0:T(8,128)(2,1)S(1)}, u32[]{:S(2)}, u32[]{:S(2)}) collective-permute-start(bf16[64,1024]{1,0:T(8,128)(2,1)S(1)} %add_convert_fusion.10), channel_id=1, source_target_pairs={{0,4},{1,5},{2,6},{3,7},{4,0},{5,1},{6,2},{7,3},{8,12},{9,13},{10,... | collective-permute-start | bytes 393224 | tf_op jit(solution)/shard_map/ppermute | solution.py:176
  396.1 7.6 %collective-permute-start.88 = (bf16[64,1024]{1,0:T(8,128)(2,1)S(1)}, bf16[64,1024]{1,0:T(8,128)(2,1)S(1)}, u32[]{:S(2)}, u32[]{:S(2)}) collective-permute-start(bf16[64,1024]{1,0:T(8,128)(2,1)S(1)} %add_convert_fusion.8), channel_id=1, source_target_pairs={{0,4},{1,5},{2,6},{3,7},{4,0},{5,1},{6,2},{7,3},{8,12},{9,13},{10,... | collective-permute-start | bytes 393224 | tf_op jit(solution)/shard_map/ppermute | solution.py:176
  403.8 29.3 %collective-permute-start.90 = (bf16[64,1024]{1,0:T(8,128)(2,1)S(1)}, bf16[64,1024]{1,0:T(8,128)(2,1)S(1)}, u32[]{:S(2)}, u32[]{:S(2)}) collective-permute-start(bf16[64,1024]{1,0:T(8,128)(2,1)S(1)} %add_convert_fusion.7), channel_id=1, source_target_pairs={{0,32},{1,33},{2,34},{3,35},{4,36},{5,37},{6,38},{7,39},{8,40},{9,... | collective-permute-start | bytes 393224 | tf_op jit(solution)/shard_map/ppermute | solution.py:176
  444.1 7.6 %collective-permute-start.94 = (bf16[64,1024]{1,0:T(8,128)(2,1)S(1)}, bf16[64,1024]{1,0:T(8,128)(2,1)S(1)}, u32[]{:S(2)}, u32[]{:S(2)}) collective-permute-start(bf16[64,1024]{1,0:T(8,128)(2,1)S(1)} %add_convert_fusion.6), channel_id=1, source_target_pairs={{0,4},{1,5},{2,6},{3,7},{4,0},{5,1},{6,2},{7,3},{8,12},{9,13},{10,... | collective-permute-start | bytes 393224 | tf_op jit(solution)/shard_map/ppermute | solution.py:176
  461.7 7.7 %collective-permute-start.98 = (bf16[64,1024]{1,0:T(8,128)(2,1)S(1)}, bf16[64,1024]{1,0:T(8,128)(2,1)S(1)}, u32[]{:S(2)}, u32[]{:S(2)}) collective-permute-start(bf16[64,1024]{1,0:T(8,128)(2,1)S(1)} %add_convert_fusion.4), channel_id=1, source_target_pairs={{0,5},{1,4},{2,7},{3,6},{4,1},{5,0},{6,3},{7,2},{8,13},{9,12},{10,... | collective-permute-start | bytes 393224 | tf_op jit(solution)/shard_map/ppermute | solution.py:176
  463.0 7.8 %collective-permute-start.99 = (bf16[64,1024]{1,0:T(8,128)(2,1)S(1)}, bf16[64,1024]{1,0:T(8,128)(2,1)S(1)}, u32[]{:S(2)}, u32[]{:S(2)}) collective-permute-start(bf16[64,1024]{1,0:T(8,128)(2,1)S(1)} %add_convert_fusion.4), channel_id=1, source_target_pairs={{0,4},{1,5},{2,6},{3,7},{4,0},{5,1},{6,2},{7,3},{8,12},{9,13},{10,... | collective-permute-start | bytes 393224 | tf_op jit(solution)/shard_map/ppermute | solution.py:176
  487.0 12.2 %collective-permute-start.104 = (bf16[64,1024]{1,0:T(8,128)(2,1)S(1)}, bf16[64,1024]{1,0:T(8,128)(2,1)S(1)}, u32[]{:S(2)}, u32[]{:S(2)}) collective-permute-start(bf16[64,1024]{1,0:T(8,128)(2,1)S(1)} %add_convert_fusion.2), channel_id=1, source_target_pairs={{0,5},{1,4},{2,7},{3,6},{4,1},{5,0},{6,3},{7,2},{8,13},{9,12},{10,... | collective-permute-start | bytes 393224 | tf_op jit(solution)/shard_map/ppermute | solution.py:176
  488.7 10.5 %collective-permute-start.105 = (bf16[64,1024]{1,0:T(8,128)(2,1)S(1)}, bf16[64,1024]{1,0:T(8,128)(2,1)S(1)}, u32[]{:S(2)}, u32[]{:S(2)}) collective-permute-start(bf16[64,1024]{1,0:T(8,128)(2,1)S(1)} %add_convert_fusion.2), channel_id=1, source_target_pairs={{0,4},{1,5},{2,6},{3,7},{4,0},{5,1},{6,2},{7,3},{8,12},{9,13},{10,... | collective-permute-start | bytes 393224 | tf_op jit(solution)/shard_map/ppermute | solution.py:176
  489.3 9.9 %collective-permute-start.106 = (bf16[64,1024]{1,0:T(8,128)(2,1)S(1)}, bf16[64,1024]{1,0:T(8,128)(2,1)S(1)}, u32[]{:S(2)}, u32[]{:S(2)}) collective-permute-start(bf16[64,1024]{1,0:T(8,128)(2,1)S(1)} %add_convert_fusion.2), channel_id=1, source_target_pairs={{0,1},{1,0},{2,3},{3,2},{4,5},{5,4},{6,7},{7,6},{8,9},{9,8},{10,11... | collective-permute-start | bytes 393224 | tf_op jit(solution)/shard_map/ppermute | solution.py:176
  500.2 8.3 %collective-permute-start.107 = (bf16[64,1024]{1,0:T(8,128)(2,1)S(1)}, bf16[64,1024]{1,0:T(8,128)(2,1)S(1)}, u32[]{:S(2)}, u32[]{:S(2)}) collective-permute-start(bf16[64,1024]{1,0:T(8,128)(2,1)S(1)} %add_convert_fusion.1.mine_ref), channel_id=1, source_target_pairs={{0,16},{1,17},{2,18},{3,19},{4,20},{5,21},{6,22},{7,23},{8,24},{9,... | collective-permute-start | bytes 393224 | tf_op jit(solution)/shard_map/ppermute | solution.py:176
  527.7 7.4 %collective-permute-start.109 = (bf16[64,1024]{1,0:T(8,128)(2,1)S(1)}, bf16[64,1024]{1,0:T(8,128)(2,1)S(1)}, u32[]{:S(2)}, u32[]{:S(2)}) collective-permute-start(bf16[64,1024]{1,0:T(8,128)(2,1)S(1)} %add_convert_fusion), channel_id=1, source_target_pairs={{0,5},{1,4},{2,7},{3,6},{4,1},{5,0},{6,3},{7,2},{8,13},{9,12},{10,... | collective-permute-start | bytes 393224 | tf_op jit(solution)/shard_map/ppermute | solution.py:176
  529.3 7.6 %collective-permute-start.110 = (bf16[64,1024]{1,0:T(8,128)(2,1)S(1)}, bf16[64,1024]{1,0:T(8,128)(2,1)S(1)}, u32[]{:S(2)}, u32[]{:S(2)}) collective-permute-start(bf16[64,1024]{1,0:T(8,128)(2,1)S(1)} %add_convert_fusion), channel_id=1, source_target_pairs={{0,4},{1,5},{2,6},{3,7},{4,0},{5,1},{6,2},{7,3},{8,12},{9,13},{10,... | collective-permute-start | bytes 393224 | tf_op jit(solution)/shard_map/ppermute | solution.py:176
  538.7 10.8 %collective-permute-start.113 = (bf16[2,16,1024]{2,1,0:T(8,128)(2,1)S(1)}, bf16[2,16,1024]{2,1,0:T(8,128)(2,1)S(1)}, u32[]{:S(2)}, u32[]{:S(2)}) collective-permute-start(bf16[2,16,1024]{2,1,0:T(8,128)(2,1)S(1)} %select_bitcast_fusion), channel_id=1, source_target_pairs={{0,16},{1,17},{2,18},{3,19},{4,20},{5,21},{6,22},{7,23},{8,24},{9,... | collective-permute-start | bytes 196616 | tf_op jit(solution)/shard_map/ppermute | solution.py:176
  (128 other events, 829.3 us)
Sparse Core Ops, SparseCore 0:
  11.9 50.5 all-gather.1

commit v9 on v8

--- a/solution.py
+++ b/solution.py
@@ -88,7 +88,7 @@
         in_specs=[pl.BlockSpec(memory_space=pl.ANY)] * 2,
         out_specs=(pl.BlockSpec(memory_space=pltpu.VMEM),) * 2,
         scratch_shapes=[pltpu.SemaphoreType.DMA((2,))],
-        compiler_params=pltpu.CompilerParams(vmem_limit_bytes=8 * 1024 * 1024),
+        compiler_params=pltpu.CompilerParams(vmem_limit_bytes=6 * 1024 * 1024),
     )(*pair))
 
 
@@ -103,7 +103,7 @@
         out_shape=(half, half),
         in_specs=[pl.BlockSpec(memory_space=pltpu.SMEM)] + [vmem] * 12,
         out_specs=(vmem, vmem),
-        compiler_params=pltpu.CompilerParams(vmem_limit_bytes=16 * 1024 * 1024),
+        compiler_params=pltpu.CompilerParams(vmem_limit_bytes=6 * 1024 * 1024),
         cost_estimate=pl.CostEstimate(
             flops=2 * WINDOW * model * width * 16, bytes_accessed=16 * model * width * 2,
             transcendentals=WINDOW * WINDOW * 8,
@@ -219,6 +219,15 @@
     window_mine = lax.dynamic_slice_in_dim(inputs_all, start + HALF * core, HALF, 1)
     window_other = lax.dynamic_slice_in_dim(inputs_all, start + HALF * (1 - core), HALF, 1)
 
+    slots = place * row_count + jnp.arange(row_count, dtype=jnp.int32)
+    holders = [
+        jnp.sum(
+            (slots[:, None] >= group_bounds(segment_ids[m])[None, 1:]).astype(jnp.int32), axis=1
+        )
+        for m in range(micro_count)
+    ]
+    window_mine, holders = lax.optimization_barrier((window_mine, holders))
+
     biases = jnp.stack([
         window_masks(segment_ids[m], prefix_lengths[m], batch_lengths[m], start, core)
         for m in range(micro_count)
@@ -283,12 +292,9 @@
     there = swap_cores(jnp.where(first, stash_b, stash_a))
     has_own = first == (x < SIDE // 2)
     mine, other = jnp.where(has_own, here, there), jnp.where(has_own, there, here)
-    slots = place * row_count + jnp.arange(row_count, dtype=jnp.int32)
-    picked = []
-    for m in range(micro_count):
-        bounds = group_bounds(segment_ids[m])
-        holder = jnp.sum((slots[:, None] >= bounds[None, 1:]).astype(jnp.int32), axis=1)
-        picked.append(jnp.where((holder == y)[:, None], mine[m], other[m]))
+    picked = [
+        jnp.where((holders[m] == y)[:, None], mine[m], other[m]) for m in range(micro_count)
+    ]
     return jnp.stack(picked)[None]
 
 

time: 568 us -> 551 us (0.970)
  local copies, waits for them, and re-layouts: 21.8 us -> 11.7 us
    unnamed x128 -> x110, local copies, waits for them, and re-layouts: 16.9 us -> 5.79 us
  transfers between devices with their start and end apart: 115 -> 115, of which waited for: 85 -> 89; matrix products, arithmetic and copies ran while one was open for 3% -> 3% of each run, Pallas kernels for 1% -> 1%
where the time goes in v9:
time: 551 us; the launch traced here: 540 us
  waiting for transfers between devices  290 us (53%)
  starting transfers between devices  132 us (24%)
  Pallas kernels  51.5 us (9%)
  between operations  34 us (6%)
  other arithmetic  20.7 us (4%)
  local copies, waits for them, and re-layouts  11.7 us (2%)
    ppermute x114, waiting for transfers between devices, move(): return lax.ppermute(value, AXES, pairs)  290 us
    ppermute x114, starting transfers between devices, move(): return lax.ppermute(value, AXES, pairs)  132 us
    pallas_call x18, Pallas kernels, run_layer(): pl.pallas_call(functools.partial(layer_kernel, turn), out_shape=(half, ha...  49.8 us
  transfers between devices with their start and end apart: 115, of which 89 were waited for; matrix products, arithmetic and copies ran while one was open for 3% of the time, Pallas kernels for 1%

profile of v9, /device:TPU:224, one launch (start us, length us, event | category | flops | bytes accessed | tf_op | source)
XLA Modules:
  0.0 540.4 jit_solution(3866336651563138168)
XLA Ops:
  20.6 3.0 collective-permute-start.4
  23.6 3.1 broadcast_select_fusion.1
  48.3 8.9 %collective-permute-done.3.refs_2_ = bf16[2048,256]{1,0:T(8,128)(2,1)S(1)} collective-permute-done((bf16[2048,256]{1,0:T(8,128)(2,1)}, bf16[2048,256]{1,0:T(8,128)(2,1)S(1)}, u32[]{:S(2)}, u32[]{:S(2)}) %collective-permute-start.3) | collective-permute-done | bytes 1048608 | tf_op jit(solution)/shard_map/ppermute | solution.py:176
  57.2 3.0 collective-permute-start.8
  61.2 20.3 %collective-permute-done.5.refs_3_ = bf16[2048,256]{1,0:T(8,128)(2,1)S(1)} collective-permute-done((bf16[2048,256]{1,0:T(8,128)(2,1)}, bf16[2048,256]{1,0:T(8,128)(2,1)S(1)}, u32[]{:S(2)}, u32[]{:S(2)}) %collective-permute-start.5) | collective-permute-done | bytes 1048608 | tf_op jit(solution)/shard_map/ppermute | solution.py:176
  88.4 12.2 %collective-permute-done.7.refs_6_ = bf16[2048,256]{1,0:T(8,128)(2,1)} collective-permute-done((bf16[2048,256]{1,0:T(8,128)(2,1)S(1)}, bf16[2048,256]{1,0:T(8,128)(2,1)}, u32[]{:S(2)}, u32[]{:S(2)}) %collective-permute-start.7) | collective-permute-done | bytes 1048608 | tf_op jit(solution)/shard_map/ppermute | solution.py:176
  100.6 3.5 collective-permute-done.8.refs_7_
  110.8 15.8 %collective-permute-done.14.refs_2_ = bf16[2048,256]{1,0:T(8,128)(2,1)} collective-permute-done((bf16[2048,256]{1,0:T(8,128)(2,1)}, bf16[2048,256]{1,0:T(8,128)(2,1)}, u32[]{:S(2)}, u32[]{:S(2)}) %collective-permute-start.14) | collective-permute-done | bytes 1048608 | tf_op jit(solution)/shard_map/ppermute | solution.py:176
  129.8 5.9 %collective-permute-done.10 = bf16[64,1024]{1,0:T(8,128)(2,1)S(1)} collective-permute-done((bf16[64,1024]{1,0:T(8,128)(2,1)S(1)}, bf16[64,1024]{1,0:T(8,128)(2,1)S(1)}, u32[]{:S(2)}, u32[]{:S(2)}) %collective-permute-start.10) | collective-permute-done | bytes 131104 | tf_op jit(solution)/shard_map/ppermute | solution.py:176
  136.1 4.6 collective-permute-done.11
  140.7 5.0 collective-permute-done.12
  146.0 2.9 collective-permute-done.15.refs_3_
  149.0 18.3 %collective-permute-done.18.refs_6_ = bf16[2048,256]{1,0:T(8,128)(2,1)S(1)} collective-permute-done((bf16[2048,256]{1,0:T(8,128)(2,1)}, bf16[2048,256]{1,0:T(8,128)(2,1)S(1)}, u32[]{:S(2)}, u32[]{:S(2)}) %collective-permute-start.18) | collective-permute-done | bytes 1048608 | tf_op jit(solution)/shard_map/ppermute | solution.py:176
  167.3 3.0 collective-permute-done.19.refs_7_
  177.4 3.9 collective-permute-done.21
  186.1 3.2 collective-permute-done.24.mine_ref
  199.2 3.8 collective-permute-done.27
  213.3 3.8 collective-permute-done.32
  219.2 11.1 %collective-permute-start.35 = (bf16[64,1024]{1,0:T(8,128)(2,1)S(1)}, bf16[64,1024]{1,0:T(8,128)(2,1)S(1)}, u32[]{:S(2)}, u32[]{:S(2)}) collective-permute-start(bf16[64,1024]{1,0:T(8,128)(2,1)S(1)} %add_convert_fusion.27), channel_id=1, source_target_pairs={{0,32},{1,33},{2,34},{3,35},{4,36},{5,37},{6,38},{7,39},{8,40},{9,... | collective-permute-start | bytes 393224 | tf_op jit(solution)/shard_map/ppermute | solution.py:176
  230.2 2.9 collective-permute-done.35.mine_ref
  241.9 3.8 collective-permute-done.38
  255.8 3.8 collective-permute-done.43
  261.7 3.8 collective-permute-start.46
  265.4 2.9 collective-permute-done.46.mine_ref
  276.8 3.8 collective-permute-done.49
  290.8 3.8 collective-permute-done.54
  296.6 7.2 %collective-permute-start.57 = (bf16[64,1024]{1,0:T(8,128)(2,1)S(1)}, bf16[64,1024]{1,0:T(8,128)(2,1)S(1)}, u32[]{:S(2)}, u32[]{:S(2)}) collective-permute-start(bf16[64,1024]{1,0:T(8,128)(2,1)S(1)} %add_convert_fusion.19), channel_id=1, source_target_pairs={{0,32},{1,33},{2,34},{3,35},{4,36},{5,37},{6,38},{7,39},{8,40},{9,... | collective-permute-start | bytes 393224 | tf_op jit(solution)/shard_map/ppermute | solution.py:176
  303.9 2.9 collective-permute-done.57.mine_ref
  315.3 3.8 collective-permute-done.60
  329.3 3.8 collective-permute-done.65
  335.1 3.8 collective-permute-start.68
  338.9 2.9 collective-permute-done.68.mine_ref
  350.5 3.8 collective-permute-done.71
  364.5 3.8 collective-permute-done.76
  370.3 7.2 %collective-permute-start.79 = (bf16[64,1024]{1,0:T(8,128)(2,1)S(1)}, bf16[64,1024]{1,0:T(8,128)(2,1)S(1)}, u32[]{:S(2)}, u32[]{:S(2)}) collective-permute-start(bf16[64,1024]{1,0:T(8,128)(2,1)S(1)} %add_convert_fusion.11), channel_id=1, source_target_pairs={{0,32},{1,33},{2,34},{3,35},{4,36},{5,37},{6,38},{7,39},{8,40},{9,... | collective-permute-start | bytes 393224 | tf_op jit(solution)/shard_map/ppermute | solution.py:176
  389.0 3.8 collective-permute-done.82
  402.9 3.8 collective-permute-done.87
  408.8 3.8 collective-permute-start.90
  412.6 25.5 %collective-permute-done.90.mine_ref = bf16[64,1024]{1,0:T(8,128)(2,1)S(1)} collective-permute-done((bf16[64,1024]{1,0:T(8,128)(2,1)S(1)}, bf16[64,1024]{1,0:T(8,128)(2,1)S(1)}, u32[]{:S(2)}, u32[]{:S(2)}) %collective-permute-start.90) | collective-permute-done | bytes 131104 | tf_op jit(solution)/shard_map/ppermute | solution.py:176
  439.4 6.1 %shard_map.116 = (bf16[64,1024]{1,0:T(8,128)(2,1)S(1)}, bf16[64,1024]{1,0:T(8,128)(2,1)S(1)}) custom-call(s32[5]{0:T(128)S(1)} %pad_add_fusion.2.place_ref, bf16[64,1024]{1,0:T(8,128)(2,1)S(1)} %collective-permute-done.90.mine_ref, bf16[64,1024]{1,0:T(8,128)(2,1)S(1)} %collective-permute-done.91.other_ref, f32[1,1024]{1,0:T(1,128)S(1)} %get-tuple-element.136.gain_ref, ...), custom_call_target="tpu_custom_call" | custom-call | flops 1073741824 | bytes 8388608 | tf_op jit(solution)/shard_map/pallas_call | solution.py:101
  450.6 3.8 collective-permute-done.93
  457.9 5.6 %shard_map.117 = (bf16[64,1024]{1,0:T(8,128)(2,1)S(1)}, bf16[64,1024]{1,0:T(8,128)(2,1)S(1)}) custom-call(s32[5]{0:T(128)S(1)} %pad_add_fusion.2.place_ref, bf16[64,1024]{1,0:T(8,128)(2,1)S(1)} %add_convert_fusion.5.mine_ref, bf16[64,1024]{1,0:T(8,128)(2,1)S(1)} %collective-permute-done.96.other_ref, f32[1,1024]{1,0:T(1,128)S(1)} %get-tuple-element.135.gain_ref, ...), custom_call_target="tpu_custom_call" | custom-call | flops 1073741824 | bytes 8388608 | tf_op jit(solution)/shard_map/pallas_call | solution.py:101
  471.4 3.0 collective-permute-done.98
  476.0 5.9 %collective-permute-done.101.mine_ref = bf16[64,1024]{1,0:T(8,128)(2,1)S(1)} collective-permute-done((bf16[64,1024]{1,0:T(8,128)(2,1)S(1)}, bf16[64,1024]{1,0:T(8,128)(2,1)S(1)}, u32[]{:S(2)}, u32[]{:S(2)}) %collective-permute-start.101) | collective-permute-done | bytes 131104 | tf_op jit(solution)/shard_map/ppermute | solution.py:176
  483.3 6.2 %shard_map.118 = (bf16[64,1024]{1,0:T(8,128)(2,1)S(1)}, bf16[64,1024]{1,0:T(8,128)(2,1)S(1)}) custom-call(s32[5]{0:T(128)S(1)} %pad_add_fusion.2.place_ref, bf16[64,1024]{1,0:T(8,128)(2,1)S(1)} %collective-permute-done.101.mine_ref, bf16[64,1024]{1,0:T(8,128)(2,1)S(1)} %collective-permute-done.102.other_ref, f32[1,1024]{1,0:T(1,128)S(1)} %get-tuple-element.136.gain_ref, ...), custom_call_target="tpu_custom_call" | custom-call | flops 1073741824 | bytes 8388608 | tf_op jit(solution)/shard_map/pallas_call | solution.py:101
  494.5 3.8 collective-permute-done.104
  501.8 5.6 %shard_map.119 = (bf16[64,1024]{1,0:T(8,128)(2,1)S(1)}, bf16[64,1024]{1,0:T(8,128)(2,1)S(1)}) custom-call(s32[5]{0:T(128)S(1)} %pad_add_fusion.2.place_ref, bf16[64,1024]{1,0:T(8,128)(2,1)S(1)} %add_convert_fusion.1.mine_ref, bf16[64,1024]{1,0:T(8,128)(2,1)S(1)} %collective-permute-done.107.other_ref, f32[1,1024]{1,0:T(1,128)S(1)} %get-tuple-element.135.gain_ref, ...), custom_call_target="tpu_custom_call" | custom-call | flops 1073741824 | bytes 8388608 | tf_op jit(solution)/shard_map/pallas_call | solution.py:101
  521.5 9.9 %collective-permute-start.113 = (bf16[2,16,1024]{2,1,0:T(8,128)(2,1)S(1)}, bf16[2,16,1024]{2,1,0:T(8,128)(2,1)S(1)}, u32[]{:S(2)}, u32[]{:S(2)}) collective-permute-start(bf16[2,16,1024]{2,1,0:T(8,128)(2,1)S(1)} %select_bitcast_fusion), channel_id=1, source_target_pairs={{0,16},{1,17},{2,18},{3,19},{4,20},{5,21},{6,22},{7,23},{8,24},{9,... | collective-permute-start | bytes 196616 | tf_op jit(solution)/shard_map/ppermute | solution.py:176
  (400 shorter events, 220.5 us)
Async XLA Ops:
  6.5 79.8 %all-gather.2.cloned.1.call-start = ((), (), s32[]{:S(2)}) async-start(), calls=%async_computation | async-start | bytes 1114112 | tf_op jit(solution)/shard_map/all_gather | solution.py:218
  9.5 8.2 %collective-permute-start.2 = (bf16[2048,256]{1,0:T(8,128)(2,1)}, bf16[2048,256]{1,0:T(8,128)(2,1)}, u32[]{:S(2)}, u32[]{:S(2)}) collective-permute-start(bf16[2048,256]{1,0:T(8,128)(2,1)} %broadcast_select_fusion.3), channel_id=1, source_target_pairs={{0,16},{1,17},{2,18},{3,19},{4,20},{5,21},{6,22},{7,23},{8,24},{9,... | collective-permute-start | bytes 3145736 | tf_op jit(solution)/shard_map/ppermute | solution.py:176
  11.7 11.9 %collective-permute-start.1 = (bf16[2048,256]{1,0:T(8,128)(2,1)}, bf16[2048,256]{1,0:T(8,128)(2,1)}, u32[]{:S(2)}, u32[]{:S(2)}) collective-permute-start(bf16[2048,256]{1,0:T(8,128)(2,1)} %broadcast_select_fusion.6), channel_id=1, source_target_pairs={{0,16},{1,17},{2,18},{3,19},{4,20},{5,21},{6,22},{7,23},{8,24},{9,... | collective-permute-start | bytes 3145736 | tf_op jit(solution)/shard_map/ppermute | solution.py:176
  11.8 49.2 %collective-permute-start = (f32[1,1024]{1,0:T(1,128)S(1)}, f32[1,1024]{1,0:T(1,128)S(1)}, u32[]{:S(2)}, u32[]{:S(2)}) collective-permute-start(f32[1,1024]{1,0:T(1,128)S(1)} %copy-done.48), channel_id=1, source_target_pairs={{0,16},{1,17},{2,18},{3,19},{4,20},{5,21},{6,22},{7,23},{8,24},{9,... | collective-permute-start | bytes 12296 | tf_op jit(solution)/shard_map/ppermute | solution.py:176
  20.6 27.7 %collective-permute-start.4 = (bf16[2048,256]{1,0:T(8,128)(2,1)}, bf16[2048,256]{1,0:T(8,128)(2,1)S(1)}, u32[]{:S(2)}, u32[]{:S(2)}) collective-permute-start(bf16[2048,256]{1,0:T(8,128)(2,1)} %get-tuple-element.118.bottom_ref), channel_id=1, source_target_pairs={{0,12},{1,13},{2,14},{3,15},{4,8},{5,9},{6,10},{7,11},{8,4},{9,5},... | collective-permute-start | bytes 3145736 | tf_op jit(solution)/shard_map/ppermute | solution.py:176
  26.7 30.5 %collective-permute-start.3 = (bf16[2048,256]{1,0:T(8,128)(2,1)}, bf16[2048,256]{1,0:T(8,128)(2,1)S(1)}, u32[]{:S(2)}, u32[]{:S(2)}) collective-permute-start(bf16[2048,256]{1,0:T(8,128)(2,1)} %get-tuple-element.120.top_ref), channel_id=1, source_target_pairs={{0,3},{1,2},{2,1},{3,0},{4,7},{5,6},{6,5},{7,4},{8,11},{9,10},{10,... | collective-permute-start | bytes 3145736 | tf_op jit(solution)/shard_map/ppermute | solution.py:176
  37.0 44.6 %collective-permute-start.5 = (bf16[2048,256]{1,0:T(8,128)(2,1)}, bf16[2048,256]{1,0:T(8,128)(2,1)S(1)}, u32[]{:S(2)}, u32[]{:S(2)}) collective-permute-start(bf16[2048,256]{1,0:T(8,128)(2,1)} %get-tuple-element.118.bottom_ref), channel_id=1, source_target_pairs={{0,3},{1,2},{2,1},{3,0},{4,7},{5,6},{6,5},{7,4},{8,11},{9,10},{10,... | collective-permute-start | bytes 3145736 | tf_op jit(solution)/shard_map/ppermute | solution.py:176
  47.6 40.8 %collective-permute-start.6 = (bf16[2048,256]{1,0:T(8,128)(2,1)}, bf16[2048,256]{1,0:T(8,128)(2,1)}, u32[]{:S(2)}, u32[]{:S(2)}) collective-permute-start(bf16[2048,256]{1,0:T(8,128)(2,1)} %get-tuple-element.120.top_ref), channel_id=1, source_target_pairs={{0,12},{1,13},{2,14},{3,15},{4,8},{5,9},{6,10},{7,11},{8,4},{9,5},... | collective-permute-start | bytes 3145736 | tf_op jit(solution)/shard_map/ppermute | solution.py:176
  57.2 43.4 %collective-permute-start.7 = (bf16[2048,256]{1,0:T(8,128)(2,1)S(1)}, bf16[2048,256]{1,0:T(8,128)(2,1)}, u32[]{:S(2)}, u32[]{:S(2)}) collective-permute-start(bf16[2048,256]{1,0:T(8,128)(2,1)S(1)} %collective-permute-done.3.refs_2_), channel_id=1, source_target_pairs={{0,12},{1,13},{2,14},{3,15},{4,8},{5,9},{6,10},{7,11},{8,4},{9,5},... | collective-permute-start | bytes 3145736 | tf_op jit(solution)/shard_map/ppermute | solution.py:176
  57.2 46.9 %collective-permute-start.8 = (bf16[2048,256]{1,0:T(8,128)(2,1)S(1)}, bf16[2048,256]{1,0:T(8,128)(2,1)}, u32[]{:S(2)}, u32[]{:S(2)}) collective-permute-start(bf16[2048,256]{1,0:T(8,128)(2,1)S(1)} %collective-permute-done.4.refs_5_), channel_id=1, source_target_pairs={{0,3},{1,2},{2,1},{3,0},{4,7},{5,6},{6,5},{7,4},{8,11},{9,10},{10,... | collective-permute-start | bytes 3145736 | tf_op jit(solution)/shard_map/ppermute | solution.py:176
  61.0 65.6 %collective-permute-start.14 = (bf16[2048,256]{1,0:T(8,128)(2,1)}, bf16[2048,256]{1,0:T(8,128)(2,1)}, u32[]{:S(2)}, u32[]{:S(2)}) collective-permute-start(bf16[2048,256]{1,0:T(8,128)(2,1)} %get-tuple-element.60.top_ref), channel_id=1, source_target_pairs={{0,3},{1,2},{2,1},{3,0},{4,7},{5,6},{6,5},{7,4},{8,11},{9,10},{10,... | collective-permute-start | bytes 3145736 | tf_op jit(solution)/shard_map/ppermute | solution.py:176
  81.6 45.4 %collective-permute-start.17 = (bf16[2048,256]{1,0:T(8,128)(2,1)}, bf16[2048,256]{1,0:T(8,128)(2,1)}, u32[]{:S(2)}, u32[]{:S(2)}) collective-permute-start(bf16[2048,256]{1,0:T(8,128)(2,1)} %get-tuple-element.61.bottom_ref), channel_id=1, source_target_pairs={{0,12},{1,13},{2,14},{3,15},{4,8},{5,9},{6,10},{7,11},{8,4},{9,5},... | collective-permute-start | bytes 3145736 | tf_op jit(solution)/shard_map/ppermute | solution.py:176
  107.4 22.2 %collective-permute-start.9 = (bf16[64,1024]{1,0:T(8,128)(2,1)S(1)}, bf16[64,1024]{1,0:T(8,128)(2,1)S(1)}, u32[]{:S(2)}, u32[]{:S(2)}) collective-permute-start(bf16[64,1024]{1,0:T(8,128)(2,1)S(1)} %get-tuple-element.59), channel_id=1, source_target_pairs={{0,16},{1,17},{2,18},{3,19},{4,20},{5,21},{6,22},{7,23},{8,24},{9,... | collective-permute-start | bytes 393224 | tf_op jit(solution)/shard_map/ppermute | solution.py:176
  107.5 41.4 %collective-permute-start.15 = (bf16[2048,256]{1,0:T(8,128)(2,1)S(1)}, bf16[2048,256]{1,0:T(8,128)(2,1)S(1)}, u32[]{:S(2)}, u32[]{:S(2)}) collective-permute-start(bf16[2048,256]{1,0:T(8,128)(2,1)S(1)} %copy-done.19), channel_id=1, source_target_pairs={{0,3},{1,2},{2,1},{3,0},{4,7},{5,6},{6,5},{7,4},{8,11},{9,10},{10,... | collective-permute-start | bytes 3145736 | tf_op jit(solution)/shard_map/ppermute | solution.py:176
  110.3 38.7 %collective-permute-start.16 = (bf16[2048,256]{1,0:T(8,128)(2,1)S(1)}, bf16[2048,256]{1,0:T(8,128)(2,1)S(1)}, u32[]{:S(2)}, u32[]{:S(2)}) collective-permute-start(bf16[2048,256]{1,0:T(8,128)(2,1)S(1)} %copy-done.20), channel_id=1, source_target_pairs={{0,12},{1,13},{2,14},{3,15},{4,8},{5,9},{6,10},{7,11},{8,4},{9,5},... | collective-permute-start | bytes 3145736 | tf_op jit(solution)/shard_map/ppermute | solution.py:176
  126.6 40.7 %collective-permute-start.18 = (bf16[2048,256]{1,0:T(8,128)(2,1)}, bf16[2048,256]{1,0:T(8,128)(2,1)S(1)}, u32[]{:S(2)}, u32[]{:S(2)}) collective-permute-start(bf16[2048,256]{1,0:T(8,128)(2,1)} %collective-permute-done.14.refs_2_), channel_id=1, source_target_pairs={{0,12},{1,13},{2,14},{3,15},{4,8},{5,9},{6,10},{7,11},{8,4},{9,5},... | collective-permute-start | bytes 3145736 | tf_op jit(solution)/shard_map/ppermute | solution.py:176
  127.0 43.3 %collective-permute-start.19 = (bf16[2048,256]{1,0:T(8,128)(2,1)}, bf16[2048,256]{1,0:T(8,128)(2,1)S(1)}, u32[]{:S(2)}, u32[]{:S(2)}) collective-permute-start(bf16[2048,256]{1,0:T(8,128)(2,1)} %collective-permute-done.17.refs_5_), channel_id=1, source_target_pairs={{0,3},{1,2},{2,1},{3,0},{4,7},{5,6},{6,5},{7,4},{8,11},{9,10},{10,... | collective-permute-start | bytes 3145736 | tf_op jit(solution)/shard_map/ppermute | solution.py:176
  173.8 7.5 %collective-permute-start.21 = (bf16[64,1024]{1,0:T(8,128)(2,1)S(1)}, bf16[64,1024]{1,0:T(8,128)(2,1)}, u32[]{:S(2)}, u32[]{:S(2)}) collective-permute-start(bf16[64,1024]{1,0:T(8,128)(2,1)S(1)} %add_convert_fusion.32), channel_id=1, source_target_pairs={{0,5},{1,4},{2,7},{3,6},{4,1},{5,0},{6,3},{7,2},{8,13},{9,12},{10,... | collective-permute-start | bytes 393224 | tf_op jit(solution)/shard_map/ppermute | solution.py:176
  173.9 8.6 %collective-permute-start.22 = (bf16[64,1024]{1,0:T(8,128)(2,1)S(1)}, bf16[64,1024]{1,0:T(8,128)(2,1)}, u32[]{:S(2)}, u32[]{:S(2)}) collective-permute-start(bf16[64,1024]{1,0:T(8,128)(2,1)S(1)} %add_convert_fusion.32), channel_id=1, source_target_pairs={{0,4},{1,5},{2,6},{3,7},{4,0},{5,1},{6,2},{7,3},{8,12},{9,13},{10,... | collective-permute-start | bytes 393224 | tf_op jit(solution)/shard_map/ppermute | solution.py:176
  195.7 7.3 %collective-permute-start.27 = (bf16[64,1024]{1,0:T(8,128)(2,1)S(1)}, bf16[64,1024]{1,0:T(8,128)(2,1)S(1)}, u32[]{:S(2)}, u32[]{:S(2)}) collective-permute-start(bf16[64,1024]{1,0:T(8,128)(2,1)S(1)} %add_convert_fusion.30), channel_id=1, source_target_pairs={{0,5},{1,4},{2,7},{3,6},{4,1},{5,0},{6,3},{7,2},{8,13},{9,12},{10,... | collective-permute-start | bytes 393224 | tf_op jit(solution)/shard_map/ppermute | solution.py:176
  197.3 7.7 %collective-permute-start.28 = (bf16[64,1024]{1,0:T(8,128)(2,1)S(1)}, bf16[64,1024]{1,0:T(8,128)(2,1)S(1)}, u32[]{:S(2)}, u32[]{:S(2)}) collective-permute-start(bf16[64,1024]{1,0:T(8,128)(2,1)S(1)} %add_convert_fusion.30), channel_id=1, source_target_pairs={{0,4},{1,5},{2,6},{3,7},{4,0},{5,1},{6,2},{7,3},{8,12},{9,13},{10,... | collective-permute-start | bytes 393224 | tf_op jit(solution)/shard_map/ppermute | solution.py:176
  209.7 7.4 %collective-permute-start.32 = (bf16[64,1024]{1,0:T(8,128)(2,1)S(1)}, bf16[64,1024]{1,0:T(8,128)(2,1)S(1)}, u32[]{:S(2)}, u32[]{:S(2)}) collective-permute-start(bf16[64,1024]{1,0:T(8,128)(2,1)S(1)} %add_convert_fusion.28), channel_id=1, source_target_pairs={{0,5},{1,4},{2,7},{3,6},{4,1},{5,0},{6,3},{7,2},{8,13},{9,12},{10,... | collective-permute-start | bytes 393224 | tf_op jit(solution)/shard_map/ppermute | solution.py:176
  211.3 7.8 %collective-permute-start.33 = (bf16[64,1024]{1,0:T(8,128)(2,1)S(1)}, bf16[64,1024]{1,0:T(8,128)(2,1)S(1)}, u32[]{:S(2)}, u32[]{:S(2)}) collective-permute-start(bf16[64,1024]{1,0:T(8,128)(2,1)S(1)} %add_convert_fusion.28), channel_id=1, source_target_pairs={{0,4},{1,5},{2,6},{3,7},{4,0},{5,1},{6,2},{7,3},{8,12},{9,13},{10,... | collective-permute-start | bytes 393224 | tf_op jit(solution)/shard_map/ppermute | solution.py:176
  219.2 14.0 %collective-permute-start.35 = (bf16[64,1024]{1,0:T(8,128)(2,1)S(1)}, bf16[64,1024]{1,0:T(8,128)(2,1)S(1)}, u32[]{:S(2)}, u32[]{:S(2)}) collective-permute-start(bf16[64,1024]{1,0:T(8,128)(2,1)S(1)} %add_convert_fusion.27), channel_id=1, source_target_pairs={{0,32},{1,33},{2,34},{3,35},{4,36},{5,37},{6,38},{7,39},{8,40},{9,... | collective-permute-start | bytes 393224 | tf_op jit(solution)/shard_map/ppermute | solution.py:176
  238.3 7.3 %collective-permute-start.38 = (bf16[64,1024]{1,0:T(8,128)(2,1)S(1)}, bf16[64,1024]{1,0:T(8,128)(2,1)S(1)}, u32[]{:S(2)}, u32[]{:S(2)}) collective-permute-start(bf16[64,1024]{1,0:T(8,128)(2,1)S(1)} %add_convert_fusion.26), channel_id=1, source_target_pairs={{0,5},{1,4},{2,7},{3,6},{4,1},{5,0},{6,3},{7,2},{8,13},{9,12},{10,... | collective-permute-start | bytes 393224 | tf_op jit(solution)/shard_map/ppermute | solution.py:176
  240.0 7.7 %collective-permute-start.39 = (bf16[64,1024]{1,0:T(8,128)(2,1)S(1)}, bf16[64,1024]{1,0:T(8,128)(2,1)S(1)}, u32[]{:S(2)}, u32[]{:S(2)}) collective-permute-start(bf16[64,1024]{1,0:T(8,128)(2,1)S(1)} %add_convert_fusion.26), channel_id=1, source_target_pairs={{0,4},{1,5},{2,6},{3,7},{4,0},{5,1},{6,2},{7,3},{8,12},{9,13},{10,... | collective-permute-start | bytes 393224 | tf_op jit(solution)/shard_map/ppermute | solution.py:176
  252.2 7.3 %collective-permute-start.43 = (bf16[64,1024]{1,0:T(8,128)(2,1)S(1)}, bf16[64,1024]{1,0:T(8,128)(2,1)S(1)}, u32[]{:S(2)}, u32[]{:S(2)}) collective-permute-start(bf16[64,1024]{1,0:T(8,128)(2,1)S(1)} %add_convert_fusion.24), channel_id=1, source_target_pairs={{0,5},{1,4},{2,7},{3,6},{4,1},{5,0},{6,3},{7,2},{8,13},{9,12},{10,... | collective-permute-start | bytes 393224 | tf_op jit(solution)/shard_map/ppermute | solution.py:176
  253.9 7.7 %collective-permute-start.44 = (bf16[64,1024]{1,0:T(8,128)(2,1)S(1)}, bf16[64,1024]{1,0:T(8,128)(2,1)S(1)}, u32[]{:S(2)}, u32[]{:S(2)}) collective-permute-start(bf16[64,1024]{1,0:T(8,128)(2,1)S(1)} %add_convert_fusion.24), channel_id=1, source_target_pairs={{0,4},{1,5},{2,6},{3,7},{4,0},{5,1},{6,2},{7,3},{8,12},{9,13},{10,... | collective-permute-start | bytes 393224 | tf_op jit(solution)/shard_map/ppermute | solution.py:176
  273.3 7.3 %collective-permute-start.49 = (bf16[64,1024]{1,0:T(8,128)(2,1)S(1)}, bf16[64,1024]{1,0:T(8,128)(2,1)S(1)}, u32[]{:S(2)}, u32[]{:S(2)}) collective-permute-start(bf16[64,1024]{1,0:T(8,128)(2,1)S(1)} %add_convert_fusion.22), channel_id=1, source_target_pairs={{0,5},{1,4},{2,7},{3,6},{4,1},{5,0},{6,3},{7,2},{8,13},{9,12},{10,... | collective-permute-start | bytes 393224 | tf_op jit(solution)/shard_map/ppermute | solution.py:176
  274.9 7.7 %collective-permute-start.50 = (bf16[64,1024]{1,0:T(8,128)(2,1)S(1)}, bf16[64,1024]{1,0:T(8,128)(2,1)S(1)}, u32[]{:S(2)}, u32[]{:S(2)}) collective-permute-start(bf16[64,1024]{1,0:T(8,128)(2,1)S(1)} %add_convert_fusion.22), channel_id=1, source_target_pairs={{0,4},{1,5},{2,6},{3,7},{4,0},{5,1},{6,2},{7,3},{8,12},{9,13},{10,... | collective-permute-start | bytes 393224 | tf_op jit(solution)/shard_map/ppermute | solution.py:176
  287.2 7.3 %collective-permute-start.54 = (bf16[64,1024]{1,0:T(8,128)(2,1)S(1)}, bf16[64,1024]{1,0:T(8,128)(2,1)S(1)}, u32[]{:S(2)}, u32[]{:S(2)}) collective-permute-start(bf16[64,1024]{1,0:T(8,128)(2,1)S(1)} %add_convert_fusion.20), channel_id=1, source_target_pairs={{0,5},{1,4},{2,7},{3,6},{4,1},{5,0},{6,3},{7,2},{8,13},{9,12},{10,... | collective-permute-start | bytes 393224 | tf_op jit(solution)/shard_map/ppermute | solution.py:176
  288.8 7.7 %collective-permute-start.55 = (bf16[64,1024]{1,0:T(8,128)(2,1)S(1)}, bf16[64,1024]{1,0:T(8,128)(2,1)S(1)}, u32[]{:S(2)}, u32[]{:S(2)}) collective-permute-start(bf16[64,1024]{1,0:T(8,128)(2,1)S(1)} %add_convert_fusion.20), channel_id=1, source_target_pairs={{0,4},{1,5},{2,6},{3,7},{4,0},{5,1},{6,2},{7,3},{8,12},{9,13},{10,... | collective-permute-start | bytes 393224 | tf_op jit(solution)/shard_map/ppermute | solution.py:176
  296.6 10.2 %collective-permute-start.57 = (bf16[64,1024]{1,0:T(8,128)(2,1)S(1)}, bf16[64,1024]{1,0:T(8,128)(2,1)S(1)}, u32[]{:S(2)}, u32[]{:S(2)}) collective-permute-start(bf16[64,1024]{1,0:T(8,128)(2,1)S(1)} %add_convert_fusion.19), channel_id=1, source_target_pairs={{0,32},{1,33},{2,34},{3,35},{4,36},{5,37},{6,38},{7,39},{8,40},{9,... | collective-permute-start | bytes 393224 | tf_op jit(solution)/shard_map/ppermute | solution.py:176
  313.4 7.7 %collective-permute-start.61 = (bf16[64,1024]{1,0:T(8,128)(2,1)S(1)}, bf16[64,1024]{1,0:T(8,128)(2,1)S(1)}, u32[]{:S(2)}, u32[]{:S(2)}) collective-permute-start(bf16[64,1024]{1,0:T(8,128)(2,1)S(1)} %add_convert_fusion.18), channel_id=1, source_target_pairs={{0,4},{1,5},{2,6},{3,7},{4,0},{5,1},{6,2},{7,3},{8,12},{9,13},{10,... | collective-permute-start | bytes 393224 | tf_op jit(solution)/shard_map/ppermute | solution.py:176
  327.3 7.7 %collective-permute-start.66 = (bf16[64,1024]{1,0:T(8,128)(2,1)S(1)}, bf16[64,1024]{1,0:T(8,128)(2,1)S(1)}, u32[]{:S(2)}, u32[]{:S(2)}) collective-permute-start(bf16[64,1024]{1,0:T(8,128)(2,1)S(1)} %add_convert_fusion.16), channel_id=1, source_target_pairs={{0,4},{1,5},{2,6},{3,7},{4,0},{5,1},{6,2},{7,3},{8,12},{9,13},{10,... | collective-permute-start | bytes 393224 | tf_op jit(solution)/shard_map/ppermute | solution.py:176
  348.6 7.7 %collective-permute-start.72 = (bf16[64,1024]{1,0:T(8,128)(2,1)S(1)}, bf16[64,1024]{1,0:T(8,128)(2,1)S(1)}, u32[]{:S(2)}, u32[]{:S(2)}) collective-permute-start(bf16[64,1024]{1,0:T(8,128)(2,1)S(1)} %add_convert_fusion.14), channel_id=1, source_target_pairs={{0,4},{1,5},{2,6},{3,7},{4,0},{5,1},{6,2},{7,3},{8,12},{9,13},{10,... | collective-permute-start | bytes 393224 | tf_op jit(solution)/shard_map/ppermute | solution.py:176
  362.5 7.7 %collective-permute-start.77 = (bf16[64,1024]{1,0:T(8,128)(2,1)S(1)}, bf16[64,1024]{1,0:T(8,128)(2,1)S(1)}, u32[]{:S(2)}, u32[]{:S(2)}) collective-permute-start(bf16[64,1024]{1,0:T(8,128)(2,1)S(1)} %add_convert_fusion.12), channel_id=1, source_target_pairs={{0,4},{1,5},{2,6},{3,7},{4,0},{5,1},{6,2},{7,3},{8,12},{9,13},{10,... | collective-permute-start | bytes 393224 | tf_op jit(solution)/shard_map/ppermute | solution.py:176
  370.3 10.2 %collective-permute-start.79 = (bf16[64,1024]{1,0:T(8,128)(2,1)S(1)}, bf16[64,1024]{1,0:T(8,128)(2,1)S(1)}, u32[]{:S(2)}, u32[]{:S(2)}) collective-permute-start(bf16[64,1024]{1,0:T(8,128)(2,1)S(1)} %add_convert_fusion.11), channel_id=1, source_target_pairs={{0,32},{1,33},{2,34},{3,35},{4,36},{5,37},{6,38},{7,39},{8,40},{9,... | collective-permute-start | bytes 393224 | tf_op jit(solution)/shard_map/ppermute | solution.py:176
  387.1 7.7 %collective-permute-start.83 = (bf16[64,1024]{1,0:T(8,128)(2,1)S(1)}, bf16[64,1024]{1,0:T(8,128)(2,1)S(1)}, u32[]{:S(2)}, u32[]{:S(2)}) collective-permute-start(bf16[64,1024]{1,0:T(8,128)(2,1)S(1)} %add_convert_fusion.10), channel_id=1, source_target_pairs={{0,4},{1,5},{2,6},{3,7},{4,0},{5,1},{6,2},{7,3},{8,12},{9,13},{10,... | collective-permute-start | bytes 393224 | tf_op jit(solution)/shard_map/ppermute | solution.py:176
  401.0 7.7 %collective-permute-start.88 = (bf16[64,1024]{1,0:T(8,128)(2,1)S(1)}, bf16[64,1024]{1,0:T(8,128)(2,1)S(1)}, u32[]{:S(2)}, u32[]{:S(2)}) collective-permute-start(bf16[64,1024]{1,0:T(8,128)(2,1)S(1)} %add_convert_fusion.8), channel_id=1, source_target_pairs={{0,4},{1,5},{2,6},{3,7},{4,0},{5,1},{6,2},{7,3},{8,12},{9,13},{10,... | collective-permute-start | bytes 393224 | tf_op jit(solution)/shard_map/ppermute | solution.py:176
  408.8 29.3 %collective-permute-start.90 = (bf16[64,1024]{1,0:T(8,128)(2,1)S(1)}, bf16[64,1024]{1,0:T(8,128)(2,1)S(1)}, u32[]{:S(2)}, u32[]{:S(2)}) collective-permute-start(bf16[64,1024]{1,0:T(8,128)(2,1)S(1)} %add_convert_fusion.7), channel_id=1, source_target_pairs={{0,32},{1,33},{2,34},{3,35},{4,36},{5,37},{6,38},{7,39},{8,40},{9,... | collective-permute-start | bytes 393224 | tf_op jit(solution)/shard_map/ppermute | solution.py:176
  448.8 7.6 %collective-permute-start.94 = (bf16[64,1024]{1,0:T(8,128)(2,1)S(1)}, bf16[64,1024]{1,0:T(8,128)(2,1)S(1)}, u32[]{:S(2)}, u32[]{:S(2)}) collective-permute-start(bf16[64,1024]{1,0:T(8,128)(2,1)S(1)} %add_convert_fusion.6), channel_id=1, source_target_pairs={{0,4},{1,5},{2,6},{3,7},{4,0},{5,1},{6,2},{7,3},{8,12},{9,13},{10,... | collective-permute-start | bytes 393224 | tf_op jit(solution)/shard_map/ppermute | solution.py:176
  466.7 7.7 %collective-permute-start.98 = (bf16[64,1024]{1,0:T(8,128)(2,1)S(1)}, bf16[64,1024]{1,0:T(8,128)(2,1)S(1)}, u32[]{:S(2)}, u32[]{:S(2)}) collective-permute-start(bf16[64,1024]{1,0:T(8,128)(2,1)S(1)} %add_convert_fusion.4), channel_id=1, source_target_pairs={{0,5},{1,4},{2,7},{3,6},{4,1},{5,0},{6,3},{7,2},{8,13},{9,12},{10,... | collective-permute-start | bytes 393224 | tf_op jit(solution)/shard_map/ppermute | solution.py:176
  468.0 7.8 %collective-permute-start.99 = (bf16[64,1024]{1,0:T(8,128)(2,1)S(1)}, bf16[64,1024]{1,0:T(8,128)(2,1)S(1)}, u32[]{:S(2)}, u32[]{:S(2)}) collective-permute-start(bf16[64,1024]{1,0:T(8,128)(2,1)S(1)} %add_convert_fusion.4), channel_id=1, source_target_pairs={{0,4},{1,5},{2,6},{3,7},{4,0},{5,1},{6,2},{7,3},{8,12},{9,13},{10,... | collective-permute-start | bytes 393224 | tf_op jit(solution)/shard_map/ppermute | solution.py:176
  492.6 7.7 %collective-permute-start.105 = (bf16[64,1024]{1,0:T(8,128)(2,1)S(1)}, bf16[64,1024]{1,0:T(8,128)(2,1)S(1)}, u32[]{:S(2)}, u32[]{:S(2)}) collective-permute-start(bf16[64,1024]{1,0:T(8,128)(2,1)S(1)} %add_convert_fusion.2), channel_id=1, source_target_pairs={{0,4},{1,5},{2,6},{3,7},{4,0},{5,1},{6,2},{7,3},{8,12},{9,13},{10,... | collective-permute-start | bytes 393224 | tf_op jit(solution)/shard_map/ppermute | solution.py:176
  510.2 7.4 %collective-permute-start.109 = (bf16[64,1024]{1,0:T(8,128)(2,1)S(1)}, bf16[64,1024]{1,0:T(8,128)(2,1)S(1)}, u32[]{:S(2)}, u32[]{:S(2)}) collective-permute-start(bf16[64,1024]{1,0:T(8,128)(2,1)S(1)} %add_convert_fusion), channel_id=1, source_target_pairs={{0,5},{1,4},{2,7},{3,6},{4,1},{5,0},{6,3},{7,2},{8,13},{9,12},{10,... | collective-permute-start | bytes 393224 | tf_op jit(solution)/shard_map/ppermute | solution.py:176
  511.9 7.9 %collective-permute-start.110 = (bf16[64,1024]{1,0:T(8,128)(2,1)S(1)}, bf16[64,1024]{1,0:T(8,128)(2,1)S(1)}, u32[]{:S(2)}, u32[]{:S(2)}) collective-permute-start(bf16[64,1024]{1,0:T(8,128)(2,1)S(1)} %add_convert_fusion), channel_id=1, source_target_pairs={{0,4},{1,5},{2,6},{3,7},{4,0},{5,1},{6,2},{7,3},{8,12},{9,13},{10,... | collective-permute-start | bytes 393224 | tf_op jit(solution)/shard_map/ppermute | solution.py:176
  521.5 10.8 %collective-permute-start.113 = (bf16[2,16,1024]{2,1,0:T(8,128)(2,1)S(1)}, bf16[2,16,1024]{2,1,0:T(8,128)(2,1)S(1)}, u32[]{:S(2)}, u32[]{:S(2)}) collective-permute-start(bf16[2,16,1024]{2,1,0:T(8,128)(2,1)S(1)} %select_bitcast_fusion), channel_id=1, source_target_pairs={{0,16},{1,17},{2,18},{3,19},{4,20},{5,21},{6,22},{7,23},{8,24},{9,... | collective-permute-start | bytes 196616 | tf_op jit(solution)/shard_map/ppermute | solution.py:176
  (119 other events, 910.6 us)
Sparse Core Ops, SparseCore 0:
  11.9 50.1 all-gather.1

commit v10 on v9

--- a/solution.py
+++ b/solution.py
@@ -211,7 +211,7 @@
     own_a = [jnp.where(first, p, q) for p, q in zip(kept, got)]
     own_b = [jnp.where(first, q, p) for p, q in zip(kept, got)]
     near_a = near(*own_a)
-    own_b, near_a[:2] = lax.optimization_barrier((own_b, near_a[:2]))
+    own_b, near_a[:2], segments = lax.optimization_barrier((own_b, near_a[:2], segment_ids))
     weights_a = shards_of(own_a, *near_a)
     weights_b = shards_of(own_b, *near(*own_b))
 
@@ -222,7 +222,7 @@
     slots = place * row_count + jnp.arange(row_count, dtype=jnp.int32)
     holders = [
         jnp.sum(
-            (slots[:, None] >= group_bounds(segment_ids[m])[None, 1:]).astype(jnp.int32), axis=1
+            (slots[:, None] >= group_bounds(segments[m])[None, 1:]).astype(jnp.int32), axis=1
         )
         for m in range(micro_count)
     ]

time: 551 us -> 550 us (level)
  waiting for transfers between devices: 290 us -> 284 us
    ppermute x114, waiting for transfers between devices: 290 us -> 255 us  [move(): return lax.ppermute(value, AXES, pairs)]
    all_gather x1, waiting for transfers between devices: 0.01 us -> 28.2 us  [shards(): inputs_all = lax.all_gather(inputs, 'dp', axis=1, tiled=True)]
  transfers between devices with their start and end apart: 115 -> 115, of which waited for: 89 -> 87; matrix products, arithmetic and copies ran while one was open for 3% -> 4% of each run, Pallas kernels for 1% -> 1%
where the time goes in v10:
time: 550 us; the launch traced here: 540 us
  waiting for transfers between devices  284 us (52%)
  starting transfers between devices  135 us (25%)
  Pallas kernels  51.5 us (9%)
  between operations  34.5 us (6%)
  other arithmetic  20.4 us (4%)
  local copies, waits for them, and re-layouts  14.9 us (3%)
    ppermute x114, waiting for transfers between devices, move(): return lax.ppermute(value, AXES, pairs)  255 us
    ppermute x114, starting transfers between devices, move(): return lax.ppermute(value, AXES, pairs)  135 us
    pallas_call x18, Pallas kernels, run_layer(): pl.pallas_call(functools.partial(layer_kernel, turn), out_shape=(half, ha...  49.8 us
    all_gather x1, waiting for transfers between devices, shards(): inputs_all = lax.all_gather(inputs, 'dp', axis=1, tiled=True)  28.2 us
  transfers between devices with their start and end apart: 115, of which 87 were waited for; matrix products, arithmetic and copies ran while one was open for 4% of the time, Pallas kernels for 1%

profile of v10, /device:TPU:224, one launch (start us, length us, event | category | flops | bytes accessed | tf_op | source)
XLA Modules:
  0.0 540.2 jit_solution(18078460631605885002)
XLA Ops:
  17.7 2.9 broadcast_select_fusion
  20.6 3.0 collective-permute-start.3
  23.6 3.1 broadcast_select_fusion.1
  34.9 28.2 %all-gather.2.cloned.1.call-done = bf16[2,256,1024]{2,1,0:T(8,128)(2,1)} async-done(((bf16[2,16,1024]{2,1,0:T(8,128)(2,1)}), bf16[2,256,1024]{2,1,0:T(8,128)(2,1)}) %all-gather.2.cloned.1.call-update) | async-done | bytes 1048592 | tf_op jit(solution)/shard_map/all_gather | solution.py:218
  73.7 7.8 %collective-permute-done.5.refs_3_ = bf16[2048,256]{1,0:T(8,128)(2,1)S(1)} collective-permute-done((bf16[2048,256]{1,0:T(8,128)(2,1)}, bf16[2048,256]{1,0:T(8,128)(2,1)S(1)}, u32[]{:S(2)}, u32[]{:S(2)}) %collective-permute-start.5) | collective-permute-done | bytes 1048608 | tf_op jit(solution)/shard_map/ppermute | solution.py:176
  100.1 4.0 collective-permute-done.8.refs_7_
  111.9 14.6 %collective-permute-done.14.refs_2_ = bf16[2048,256]{1,0:T(8,128)(2,1)} collective-permute-done((bf16[2048,256]{1,0:T(8,128)(2,1)}, bf16[2048,256]{1,0:T(8,128)(2,1)}, u32[]{:S(2)}, u32[]{:S(2)}) %collective-permute-start.14) | collective-permute-done | bytes 1048608 | tf_op jit(solution)/shard_map/ppermute | solution.py:176
  129.7 5.9 %collective-permute-done.10 = bf16[64,1024]{1,0:T(8,128)(2,1)S(1)} collective-permute-done((bf16[64,1024]{1,0:T(8,128)(2,1)S(1)}, bf16[64,1024]{1,0:T(8,128)(2,1)S(1)}, u32[]{:S(2)}, u32[]{:S(2)}) %collective-permute-start.10) | collective-permute-done | bytes 131104 | tf_op jit(solution)/shard_map/ppermute | solution.py:176
  136.0 4.6 collective-permute-done.11
  140.6 5.0 collective-permute-done.12
  146.0 2.9 collective-permute-done.15.refs_3_
  148.9 15.9 %collective-permute-done.18.refs_6_ = bf16[2048,256]{1,0:T(8,128)(2,1)S(1)} collective-permute-done((bf16[2048,256]{1,0:T(8,128)(2,1)}, bf16[2048,256]{1,0:T(8,128)(2,1)S(1)}, u32[]{:S(2)}, u32[]{:S(2)}) %collective-permute-start.18) | collective-permute-done | bytes 1048608 | tf_op jit(solution)/shard_map/ppermute | solution.py:176
  164.8 5.4 %collective-permute-done.19.refs_7_ = bf16[2048,256]{1,0:T(8,128)(2,1)S(1)} collective-permute-done((bf16[2048,256]{1,0:T(8,128)(2,1)}, bf16[2048,256]{1,0:T(8,128)(2,1)S(1)}, u32[]{:S(2)}, u32[]{:S(2)}) %collective-permute-start.19) | collective-permute-done | bytes 1048608 | tf_op jit(solution)/shard_map/ppermute | solution.py:176
  177.3 3.9 collective-permute-done.21
  186.0 3.2 collective-permute-done.24.mine_ref
  199.1 3.8 collective-permute-done.27
  213.4 3.8 collective-permute-done.32
  219.3 10.8 %collective-permute-start.35 = (bf16[64,1024]{1,0:T(8,128)(2,1)S(1)}, bf16[64,1024]{1,0:T(8,128)(2,1)S(1)}, u32[]{:S(2)}, u32[]{:S(2)}) collective-permute-start(bf16[64,1024]{1,0:T(8,128)(2,1)S(1)} %add_convert_fusion.27), channel_id=1, source_target_pairs={{0,32},{1,33},{2,34},{3,35},{4,36},{5,37},{6,38},{7,39},{8,40},{9,... | collective-permute-start | bytes 393224 | tf_op jit(solution)/shard_map/ppermute | solution.py:176
  230.1 2.9 collective-permute-done.35.mine_ref
  241.8 3.8 collective-permute-done.38
  255.7 3.8 collective-permute-done.43
  261.6 3.8 collective-permute-start.46
  265.3 2.9 collective-permute-done.46.mine_ref
  276.7 3.8 collective-permute-done.49
  290.7 3.8 collective-permute-done.54
  296.5 7.2 %collective-permute-start.57 = (bf16[64,1024]{1,0:T(8,128)(2,1)S(1)}, bf16[64,1024]{1,0:T(8,128)(2,1)S(1)}, u32[]{:S(2)}, u32[]{:S(2)}) collective-permute-start(bf16[64,1024]{1,0:T(8,128)(2,1)S(1)} %add_convert_fusion.19), channel_id=1, source_target_pairs={{0,32},{1,33},{2,34},{3,35},{4,36},{5,37},{6,38},{7,39},{8,40},{9,... | collective-permute-start | bytes 393224 | tf_op jit(solution)/shard_map/ppermute | solution.py:176
  303.8 2.9 collective-permute-done.57.mine_ref
  315.2 3.8 collective-permute-done.60
  329.1 3.8 collective-permute-done.65
  335.0 3.8 collective-permute-start.68
  338.8 2.9 collective-permute-done.68.mine_ref
  350.4 3.8 collective-permute-done.71
  364.4 3.8 collective-permute-done.76
  370.2 7.2 %collective-permute-start.79 = (bf16[64,1024]{1,0:T(8,128)(2,1)S(1)}, bf16[64,1024]{1,0:T(8,128)(2,1)S(1)}, u32[]{:S(2)}, u32[]{:S(2)}) collective-permute-start(bf16[64,1024]{1,0:T(8,128)(2,1)S(1)} %add_convert_fusion.11), channel_id=1, source_target_pairs={{0,32},{1,33},{2,34},{3,35},{4,36},{5,37},{6,38},{7,39},{8,40},{9,... | collective-permute-start | bytes 393224 | tf_op jit(solution)/shard_map/ppermute | solution.py:176
  377.5 2.9 collective-permute-done.79.mine_ref
  388.9 3.8 collective-permute-done.82
  402.8 3.8 collective-permute-done.87
  408.7 3.8 collective-permute-start.90
  412.4 25.5 %collective-permute-done.90.mine_ref = bf16[64,1024]{1,0:T(8,128)(2,1)S(1)} collective-permute-done((bf16[64,1024]{1,0:T(8,128)(2,1)S(1)}, bf16[64,1024]{1,0:T(8,128)(2,1)S(1)}, u32[]{:S(2)}, u32[]{:S(2)}) %collective-permute-start.90) | collective-permute-done | bytes 131104 | tf_op jit(solution)/shard_map/ppermute | solution.py:176
  439.3 6.1 %shard_map.116 = (bf16[64,1024]{1,0:T(8,128)(2,1)S(1)}, bf16[64,1024]{1,0:T(8,128)(2,1)S(1)}) custom-call(s32[5]{0:T(128)S(1)} %pad_add_fusion.2.place_ref, bf16[64,1024]{1,0:T(8,128)(2,1)S(1)} %collective-permute-done.90.mine_ref, bf16[64,1024]{1,0:T(8,128)(2,1)S(1)} %collective-permute-done.91.other_ref, f32[1,1024]{1,0:T(1,128)S(1)} %get-tuple-element.138.gain_ref, ...), custom_call_target="tpu_custom_call" | custom-call | flops 1073741824 | bytes 8388608 | tf_op jit(solution)/shard_map/pallas_call | solution.py:101
  450.5 3.8 collective-permute-done.93
  457.8 5.6 %shard_map.117 = (bf16[64,1024]{1,0:T(8,128)(2,1)S(1)}, bf16[64,1024]{1,0:T(8,128)(2,1)S(1)}) custom-call(s32[5]{0:T(128)S(1)} %pad_add_fusion.2.place_ref, bf16[64,1024]{1,0:T(8,128)(2,1)S(1)} %add_convert_fusion.5.mine_ref, bf16[64,1024]{1,0:T(8,128)(2,1)S(1)} %collective-permute-done.96.other_ref, f32[1,1024]{1,0:T(1,128)S(1)} %get-tuple-element.137.gain_ref, ...), custom_call_target="tpu_custom_call" | custom-call | flops 1073741824 | bytes 8388608 | tf_op jit(solution)/shard_map/pallas_call | solution.py:101
  471.3 3.0 collective-permute-done.98
  475.8 5.9 %collective-permute-done.101.mine_ref = bf16[64,1024]{1,0:T(8,128)(2,1)S(1)} collective-permute-done((bf16[64,1024]{1,0:T(8,128)(2,1)S(1)}, bf16[64,1024]{1,0:T(8,128)(2,1)S(1)}, u32[]{:S(2)}, u32[]{:S(2)}) %collective-permute-start.101) | collective-permute-done | bytes 131104 | tf_op jit(solution)/shard_map/ppermute | solution.py:176
  483.1 6.2 %shard_map.118 = (bf16[64,1024]{1,0:T(8,128)(2,1)S(1)}, bf16[64,1024]{1,0:T(8,128)(2,1)S(1)}) custom-call(s32[5]{0:T(128)S(1)} %pad_add_fusion.2.place_ref, bf16[64,1024]{1,0:T(8,128)(2,1)S(1)} %collective-permute-done.101.mine_ref, bf16[64,1024]{1,0:T(8,128)(2,1)S(1)} %collective-permute-done.102.other_ref, f32[1,1024]{1,0:T(1,128)S(1)} %get-tuple-element.138.gain_ref, ...), custom_call_target="tpu_custom_call" | custom-call | flops 1073741824 | bytes 8388608 | tf_op jit(solution)/shard_map/pallas_call | solution.py:101
  494.3 3.8 collective-permute-done.104
  501.7 5.6 %shard_map.119 = (bf16[64,1024]{1,0:T(8,128)(2,1)S(1)}, bf16[64,1024]{1,0:T(8,128)(2,1)S(1)}) custom-call(s32[5]{0:T(128)S(1)} %pad_add_fusion.2.place_ref, bf16[64,1024]{1,0:T(8,128)(2,1)S(1)} %add_convert_fusion.1.mine_ref, bf16[64,1024]{1,0:T(8,128)(2,1)S(1)} %collective-permute-done.107.other_ref, f32[1,1024]{1,0:T(1,128)S(1)} %get-tuple-element.137.gain_ref, ...), custom_call_target="tpu_custom_call" | custom-call | flops 1073741824 | bytes 8388608 | tf_op jit(solution)/shard_map/pallas_call | solution.py:101
  521.4 9.9 %collective-permute-start.113 = (bf16[2,16,1024]{2,1,0:T(8,128)(2,1)S(1)}, bf16[2,16,1024]{2,1,0:T(8,128)(2,1)S(1)}, u32[]{:S(2)}, u32[]{:S(2)}) collective-permute-start(bf16[2,16,1024]{2,1,0:T(8,128)(2,1)S(1)} %select_bitcast_fusion), channel_id=1, source_target_pairs={{0,16},{1,17},{2,18},{3,19},{4,20},{5,21},{6,22},{7,23},{8,24},{9,... | collective-permute-start | bytes 196616 | tf_op jit(solution)/shard_map/ppermute | solution.py:176
  (403 shorter events, 223.6 us)
Async XLA Ops:
  6.5 56.5 %all-gather.2.cloned.1.call-start = ((), (), s32[]{:S(2)}) async-start(), calls=%async_computation | async-start | bytes 1114112 | tf_op jit(solution)/shard_map/all_gather | solution.py:218
  9.5 8.2 %collective-permute-start.1 = (bf16[2048,256]{1,0:T(8,128)(2,1)}, bf16[2048,256]{1,0:T(8,128)(2,1)}, u32[]{:S(2)}, u32[]{:S(2)}) collective-permute-start(bf16[2048,256]{1,0:T(8,128)(2,1)} %broadcast_select_fusion.4), channel_id=1, source_target_pairs={{0,16},{1,17},{2,18},{3,19},{4,20},{5,21},{6,22},{7,23},{8,24},{9,... | collective-permute-start | bytes 3145736 | tf_op jit(solution)/shard_map/ppermute | solution.py:176
  12.2 11.3 %collective-permute-start = (bf16[2048,256]{1,0:T(8,128)(2,1)}, bf16[2048,256]{1,0:T(8,128)(2,1)}, u32[]{:S(2)}, u32[]{:S(2)}) collective-permute-start(bf16[2048,256]{1,0:T(8,128)(2,1)} %broadcast_select_fusion.7), channel_id=1, source_target_pairs={{0,16},{1,17},{2,18},{3,19},{4,20},{5,21},{6,22},{7,23},{8,24},{9,... | collective-permute-start | bytes 3145736 | tf_op jit(solution)/shard_map/ppermute | solution.py:176
  12.3 18.7 %collective-permute-start.4 = (f32[1,1024]{1,0:T(1,128)S(1)}, f32[1,1024]{1,0:T(1,128)S(1)}, u32[]{:S(2)}, u32[]{:S(2)}) collective-permute-start(f32[1,1024]{1,0:T(1,128)S(1)} %copy-done.48), channel_id=1, source_target_pairs={{0,16},{1,17},{2,18},{3,19},{4,20},{5,21},{6,22},{7,23},{8,24},{9,... | collective-permute-start | bytes 12296 | tf_op jit(solution)/shard_map/ppermute | solution.py:176
  20.6 45.1 %collective-permute-start.3 = (bf16[2048,256]{1,0:T(8,128)(2,1)}, bf16[2048,256]{1,0:T(8,128)(2,1)S(1)}, u32[]{:S(2)}, u32[]{:S(2)}) collective-permute-start(bf16[2048,256]{1,0:T(8,128)(2,1)} %get-tuple-element.119.bottom_ref), channel_id=1, source_target_pairs={{0,12},{1,13},{2,14},{3,15},{4,8},{5,9},{6,10},{7,11},{8,4},{9,5},... | collective-permute-start | bytes 3145736 | tf_op jit(solution)/shard_map/ppermute | solution.py:176
  26.7 39.0 %collective-permute-start.2 = (bf16[2048,256]{1,0:T(8,128)(2,1)}, bf16[2048,256]{1,0:T(8,128)(2,1)S(1)}, u32[]{:S(2)}, u32[]{:S(2)}) collective-permute-start(bf16[2048,256]{1,0:T(8,128)(2,1)} %get-tuple-element.121.top_ref), channel_id=1, source_target_pairs={{0,3},{1,2},{2,1},{3,0},{4,7},{5,6},{6,5},{7,4},{8,11},{9,10},{10,... | collective-permute-start | bytes 3145736 | tf_op jit(solution)/shard_map/ppermute | solution.py:176
  29.6 51.8 %collective-permute-start.5 = (bf16[2048,256]{1,0:T(8,128)(2,1)}, bf16[2048,256]{1,0:T(8,128)(2,1)S(1)}, u32[]{:S(2)}, u32[]{:S(2)}) collective-permute-start(bf16[2048,256]{1,0:T(8,128)(2,1)} %get-tuple-element.119.bottom_ref), channel_id=1, source_target_pairs={{0,3},{1,2},{2,1},{3,0},{4,7},{5,6},{6,5},{7,4},{8,11},{9,10},{10,... | collective-permute-start | bytes 3145736 | tf_op jit(solution)/shard_map/ppermute | solution.py:176
  34.7 65.4 %collective-permute-start.6 = (bf16[2048,256]{1,0:T(8,128)(2,1)}, bf16[2048,256]{1,0:T(8,128)(2,1)}, u32[]{:S(2)}, u32[]{:S(2)}) collective-permute-start(bf16[2048,256]{1,0:T(8,128)(2,1)} %get-tuple-element.121.top_ref), channel_id=1, source_target_pairs={{0,12},{1,13},{2,14},{3,15},{4,8},{5,9},{6,10},{7,11},{8,4},{9,5},... | collective-permute-start | bytes 3145736 | tf_op jit(solution)/shard_map/ppermute | solution.py:176
  65.6 34.4 %collective-permute-start.7 = (bf16[2048,256]{1,0:T(8,128)(2,1)S(1)}, bf16[2048,256]{1,0:T(8,128)(2,1)}, u32[]{:S(2)}, u32[]{:S(2)}) collective-permute-start(bf16[2048,256]{1,0:T(8,128)(2,1)S(1)} %collective-permute-done.2.refs_2_), channel_id=1, source_target_pairs={{0,12},{1,13},{2,14},{3,15},{4,8},{5,9},{6,10},{7,11},{8,4},{9,5},... | collective-permute-start | bytes 3145736 | tf_op jit(solution)/shard_map/ppermute | solution.py:176
  68.5 35.6 %collective-permute-start.8 = (bf16[2048,256]{1,0:T(8,128)(2,1)S(1)}, bf16[2048,256]{1,0:T(8,128)(2,1)}, u32[]{:S(2)}, u32[]{:S(2)}) collective-permute-start(bf16[2048,256]{1,0:T(8,128)(2,1)S(1)} %collective-permute-done.3.refs_5_), channel_id=1, source_target_pairs={{0,3},{1,2},{2,1},{3,0},{4,7},{5,6},{6,5},{7,4},{8,11},{9,10},{10,... | collective-permute-start | bytes 3145736 | tf_op jit(solution)/shard_map/ppermute | solution.py:176
  70.9 55.6 %collective-permute-start.14 = (bf16[2048,256]{1,0:T(8,128)(2,1)}, bf16[2048,256]{1,0:T(8,128)(2,1)}, u32[]{:S(2)}, u32[]{:S(2)}) collective-permute-start(bf16[2048,256]{1,0:T(8,128)(2,1)} %get-tuple-element.62.top_ref), channel_id=1, source_target_pairs={{0,3},{1,2},{2,1},{3,0},{4,7},{5,6},{6,5},{7,4},{8,11},{9,10},{10,... | collective-permute-start | bytes 3145736 | tf_op jit(solution)/shard_map/ppermute | solution.py:176
  81.5 45.7 %collective-permute-start.17 = (bf16[2048,256]{1,0:T(8,128)(2,1)}, bf16[2048,256]{1,0:T(8,128)(2,1)}, u32[]{:S(2)}, u32[]{:S(2)}) collective-permute-start(bf16[2048,256]{1,0:T(8,128)(2,1)} %get-tuple-element.63.bottom_ref), channel_id=1, source_target_pairs={{0,12},{1,13},{2,14},{3,15},{4,8},{5,9},{6,10},{7,11},{8,4},{9,5},... | collective-permute-start | bytes 3145736 | tf_op jit(solution)/shard_map/ppermute | solution.py:176
  108.5 21.0 %collective-permute-start.9 = (bf16[64,1024]{1,0:T(8,128)(2,1)S(1)}, bf16[64,1024]{1,0:T(8,128)(2,1)S(1)}, u32[]{:S(2)}, u32[]{:S(2)}) collective-permute-start(bf16[64,1024]{1,0:T(8,128)(2,1)S(1)} %get-tuple-element.61), channel_id=1, source_target_pairs={{0,16},{1,17},{2,18},{3,19},{4,20},{5,21},{6,22},{7,23},{8,24},{9,... | collective-permute-start | bytes 393224 | tf_op jit(solution)/shard_map/ppermute | solution.py:176
  108.8 40.1 %collective-permute-start.15 = (bf16[2048,256]{1,0:T(8,128)(2,1)S(1)}, bf16[2048,256]{1,0:T(8,128)(2,1)S(1)}, u32[]{:S(2)}, u32[]{:S(2)}) collective-permute-start(bf16[2048,256]{1,0:T(8,128)(2,1)S(1)} %copy-done.19), channel_id=1, source_target_pairs={{0,3},{1,2},{2,1},{3,0},{4,7},{5,6},{6,5},{7,4},{8,11},{9,10},{10,... | collective-permute-start | bytes 3145736 | tf_op jit(solution)/shard_map/ppermute | solution.py:176
  111.6 37.3 %collective-permute-start.16 = (bf16[2048,256]{1,0:T(8,128)(2,1)S(1)}, bf16[2048,256]{1,0:T(8,128)(2,1)S(1)}, u32[]{:S(2)}, u32[]{:S(2)}) collective-permute-start(bf16[2048,256]{1,0:T(8,128)(2,1)S(1)} %copy-done.20), channel_id=1, source_target_pairs={{0,12},{1,13},{2,14},{3,15},{4,8},{5,9},{6,10},{7,11},{8,4},{9,5},... | collective-permute-start | bytes 3145736 | tf_op jit(solution)/shard_map/ppermute | solution.py:176
  126.5 38.3 %collective-permute-start.18 = (bf16[2048,256]{1,0:T(8,128)(2,1)}, bf16[2048,256]{1,0:T(8,128)(2,1)S(1)}, u32[]{:S(2)}, u32[]{:S(2)}) collective-permute-start(bf16[2048,256]{1,0:T(8,128)(2,1)} %collective-permute-done.14.refs_2_), channel_id=1, source_target_pairs={{0,12},{1,13},{2,14},{3,15},{4,8},{5,9},{6,10},{7,11},{8,4},{9,5},... | collective-permute-start | bytes 3145736 | tf_op jit(solution)/shard_map/ppermute | solution.py:176
  127.1 43.1 %collective-permute-start.19 = (bf16[2048,256]{1,0:T(8,128)(2,1)}, bf16[2048,256]{1,0:T(8,128)(2,1)S(1)}, u32[]{:S(2)}, u32[]{:S(2)}) collective-permute-start(bf16[2048,256]{1,0:T(8,128)(2,1)} %collective-permute-done.17.refs_5_), channel_id=1, source_target_pairs={{0,3},{1,2},{2,1},{3,0},{4,7},{5,6},{6,5},{7,4},{8,11},{9,10},{10,... | collective-permute-start | bytes 3145736 | tf_op jit(solution)/shard_map/ppermute | solution.py:176
  173.7 7.5 %collective-permute-start.21 = (bf16[64,1024]{1,0:T(8,128)(2,1)S(1)}, bf16[64,1024]{1,0:T(8,128)(2,1)}, u32[]{:S(2)}, u32[]{:S(2)}) collective-permute-start(bf16[64,1024]{1,0:T(8,128)(2,1)S(1)} %add_convert_fusion.32), channel_id=1, source_target_pairs={{0,5},{1,4},{2,7},{3,6},{4,1},{5,0},{6,3},{7,2},{8,13},{9,12},{10,... | collective-permute-start | bytes 393224 | tf_op jit(solution)/shard_map/ppermute | solution.py:176
  174.0 8.4 %collective-permute-start.22 = (bf16[64,1024]{1,0:T(8,128)(2,1)S(1)}, bf16[64,1024]{1,0:T(8,128)(2,1)}, u32[]{:S(2)}, u32[]{:S(2)}) collective-permute-start(bf16[64,1024]{1,0:T(8,128)(2,1)S(1)} %add_convert_fusion.32), channel_id=1, source_target_pairs={{0,4},{1,5},{2,6},{3,7},{4,0},{5,1},{6,2},{7,3},{8,12},{9,13},{10,... | collective-permute-start | bytes 393224 | tf_op jit(solution)/shard_map/ppermute | solution.py:176
  195.6 7.3 %collective-permute-start.27 = (bf16[64,1024]{1,0:T(8,128)(2,1)S(1)}, bf16[64,1024]{1,0:T(8,128)(2,1)S(1)}, u32[]{:S(2)}, u32[]{:S(2)}) collective-permute-start(bf16[64,1024]{1,0:T(8,128)(2,1)S(1)} %add_convert_fusion.30), channel_id=1, source_target_pairs={{0,5},{1,4},{2,7},{3,6},{4,1},{5,0},{6,3},{7,2},{8,13},{9,12},{10,... | collective-permute-start | bytes 393224 | tf_op jit(solution)/shard_map/ppermute | solution.py:176
  197.2 7.7 %collective-permute-start.28 = (bf16[64,1024]{1,0:T(8,128)(2,1)S(1)}, bf16[64,1024]{1,0:T(8,128)(2,1)S(1)}, u32[]{:S(2)}, u32[]{:S(2)}) collective-permute-start(bf16[64,1024]{1,0:T(8,128)(2,1)S(1)} %add_convert_fusion.30), channel_id=1, source_target_pairs={{0,4},{1,5},{2,6},{3,7},{4,0},{5,1},{6,2},{7,3},{8,12},{9,13},{10,... | collective-permute-start | bytes 393224 | tf_op jit(solution)/shard_map/ppermute | solution.py:176
  209.8 7.4 %collective-permute-start.32 = (bf16[64,1024]{1,0:T(8,128)(2,1)S(1)}, bf16[64,1024]{1,0:T(8,128)(2,1)S(1)}, u32[]{:S(2)}, u32[]{:S(2)}) collective-permute-start(bf16[64,1024]{1,0:T(8,128)(2,1)S(1)} %add_convert_fusion.28), channel_id=1, source_target_pairs={{0,5},{1,4},{2,7},{3,6},{4,1},{5,0},{6,3},{7,2},{8,13},{9,12},{10,... | collective-permute-start | bytes 393224 | tf_op jit(solution)/shard_map/ppermute | solution.py:176
  211.2 8.0 %collective-permute-start.33 = (bf16[64,1024]{1,0:T(8,128)(2,1)S(1)}, bf16[64,1024]{1,0:T(8,128)(2,1)S(1)}, u32[]{:S(2)}, u32[]{:S(2)}) collective-permute-start(bf16[64,1024]{1,0:T(8,128)(2,1)S(1)} %add_convert_fusion.28), channel_id=1, source_target_pairs={{0,4},{1,5},{2,6},{3,7},{4,0},{5,1},{6,2},{7,3},{8,12},{9,13},{10,... | collective-permute-start | bytes 393224 | tf_op jit(solution)/shard_map/ppermute | solution.py:176
  219.3 13.8 %collective-permute-start.35 = (bf16[64,1024]{1,0:T(8,128)(2,1)S(1)}, bf16[64,1024]{1,0:T(8,128)(2,1)S(1)}, u32[]{:S(2)}, u32[]{:S(2)}) collective-permute-start(bf16[64,1024]{1,0:T(8,128)(2,1)S(1)} %add_convert_fusion.27), channel_id=1, source_target_pairs={{0,32},{1,33},{2,34},{3,35},{4,36},{5,37},{6,38},{7,39},{8,40},{9,... | collective-permute-start | bytes 393224 | tf_op jit(solution)/shard_map/ppermute | solution.py:176
  238.2 7.3 %collective-permute-start.38 = (bf16[64,1024]{1,0:T(8,128)(2,1)S(1)}, bf16[64,1024]{1,0:T(8,128)(2,1)S(1)}, u32[]{:S(2)}, u32[]{:S(2)}) collective-permute-start(bf16[64,1024]{1,0:T(8,128)(2,1)S(1)} %add_convert_fusion.26), channel_id=1, source_target_pairs={{0,5},{1,4},{2,7},{3,6},{4,1},{5,0},{6,3},{7,2},{8,13},{9,12},{10,... | collective-permute-start | bytes 393224 | tf_op jit(solution)/shard_map/ppermute | solution.py:176
  239.9 7.7 %collective-permute-start.39 = (bf16[64,1024]{1,0:T(8,128)(2,1)S(1)}, bf16[64,1024]{1,0:T(8,128)(2,1)S(1)}, u32[]{:S(2)}, u32[]{:S(2)}) collective-permute-start(bf16[64,1024]{1,0:T(8,128)(2,1)S(1)} %add_convert_fusion.26), channel_id=1, source_target_pairs={{0,4},{1,5},{2,6},{3,7},{4,0},{5,1},{6,2},{7,3},{8,12},{9,13},{10,... | collective-permute-start | bytes 393224 | tf_op jit(solution)/shard_map/ppermute | solution.py:176
  253.8 7.7 %collective-permute-start.44 = (bf16[64,1024]{1,0:T(8,128)(2,1)S(1)}, bf16[64,1024]{1,0:T(8,128)(2,1)S(1)}, u32[]{:S(2)}, u32[]{:S(2)}) collective-permute-start(bf16[64,1024]{1,0:T(8,128)(2,1)S(1)} %add_convert_fusion.24), channel_id=1, source_target_pairs={{0,4},{1,5},{2,6},{3,7},{4,0},{5,1},{6,2},{7,3},{8,12},{9,13},{10,... | collective-permute-start | bytes 393224 | tf_op jit(solution)/shard_map/ppermute | solution.py:176
  273.2 7.3 %collective-permute-start.49 = (bf16[64,1024]{1,0:T(8,128)(2,1)S(1)}, bf16[64,1024]{1,0:T(8,128)(2,1)S(1)}, u32[]{:S(2)}, u32[]{:S(2)}) collective-permute-start(bf16[64,1024]{1,0:T(8,128)(2,1)S(1)} %add_convert_fusion.22), channel_id=1, source_target_pairs={{0,5},{1,4},{2,7},{3,6},{4,1},{5,0},{6,3},{7,2},{8,13},{9,12},{10,... | collective-permute-start | bytes 393224 | tf_op jit(solution)/shard_map/ppermute | solution.py:176
  274.8 7.7 %collective-permute-start.50 = (bf16[64,1024]{1,0:T(8,128)(2,1)S(1)}, bf16[64,1024]{1,0:T(8,128)(2,1)S(1)}, u32[]{:S(2)}, u32[]{:S(2)}) collective-permute-start(bf16[64,1024]{1,0:T(8,128)(2,1)S(1)} %add_convert_fusion.22), channel_id=1, source_target_pairs={{0,4},{1,5},{2,6},{3,7},{4,0},{5,1},{6,2},{7,3},{8,12},{9,13},{10,... | collective-permute-start | bytes 393224 | tf_op jit(solution)/shard_map/ppermute | solution.py:176
  287.1 7.3 %collective-permute-start.54 = (bf16[64,1024]{1,0:T(8,128)(2,1)S(1)}, bf16[64,1024]{1,0:T(8,128)(2,1)S(1)}, u32[]{:S(2)}, u32[]{:S(2)}) collective-permute-start(bf16[64,1024]{1,0:T(8,128)(2,1)S(1)} %add_convert_fusion.20), channel_id=1, source_target_pairs={{0,5},{1,4},{2,7},{3,6},{4,1},{5,0},{6,3},{7,2},{8,13},{9,12},{10,... | collective-permute-start | bytes 393224 | tf_op jit(solution)/shard_map/ppermute | solution.py:176
  288.7 7.7 %collective-permute-start.55 = (bf16[64,1024]{1,0:T(8,128)(2,1)S(1)}, bf16[64,1024]{1,0:T(8,128)(2,1)S(1)}, u32[]{:S(2)}, u32[]{:S(2)}) collective-permute-start(bf16[64,1024]{1,0:T(8,128)(2,1)S(1)} %add_convert_fusion.20), channel_id=1, source_target_pairs={{0,4},{1,5},{2,6},{3,7},{4,0},{5,1},{6,2},{7,3},{8,12},{9,13},{10,... | collective-permute-start | bytes 393224 | tf_op jit(solution)/shard_map/ppermute | solution.py:176
  296.5 10.2 %collective-permute-start.57 = (bf16[64,1024]{1,0:T(8,128)(2,1)S(1)}, bf16[64,1024]{1,0:T(8,128)(2,1)S(1)}, u32[]{:S(2)}, u32[]{:S(2)}) collective-permute-start(bf16[64,1024]{1,0:T(8,128)(2,1)S(1)} %add_convert_fusion.19), channel_id=1, source_target_pairs={{0,32},{1,33},{2,34},{3,35},{4,36},{5,37},{6,38},{7,39},{8,40},{9,... | collective-permute-start | bytes 393224 | tf_op jit(solution)/shard_map/ppermute | solution.py:176
  313.3 7.7 %collective-permute-start.61 = (bf16[64,1024]{1,0:T(8,128)(2,1)S(1)}, bf16[64,1024]{1,0:T(8,128)(2,1)S(1)}, u32[]{:S(2)}, u32[]{:S(2)}) collective-permute-start(bf16[64,1024]{1,0:T(8,128)(2,1)S(1)} %add_convert_fusion.18), channel_id=1, source_target_pairs={{0,4},{1,5},{2,6},{3,7},{4,0},{5,1},{6,2},{7,3},{8,12},{9,13},{10,... | collective-permute-start | bytes 393224 | tf_op jit(solution)/shard_map/ppermute | solution.py:176
  327.2 7.7 %collective-permute-start.66 = (bf16[64,1024]{1,0:T(8,128)(2,1)S(1)}, bf16[64,1024]{1,0:T(8,128)(2,1)S(1)}, u32[]{:S(2)}, u32[]{:S(2)}) collective-permute-start(bf16[64,1024]{1,0:T(8,128)(2,1)S(1)} %add_convert_fusion.16), channel_id=1, source_target_pairs={{0,4},{1,5},{2,6},{3,7},{4,0},{5,1},{6,2},{7,3},{8,12},{9,13},{10,... | collective-permute-start | bytes 393224 | tf_op jit(solution)/shard_map/ppermute | solution.py:176
  348.5 7.7 %collective-permute-start.72 = (bf16[64,1024]{1,0:T(8,128)(2,1)S(1)}, bf16[64,1024]{1,0:T(8,128)(2,1)S(1)}, u32[]{:S(2)}, u32[]{:S(2)}) collective-permute-start(bf16[64,1024]{1,0:T(8,128)(2,1)S(1)} %add_convert_fusion.14), channel_id=1, source_target_pairs={{0,4},{1,5},{2,6},{3,7},{4,0},{5,1},{6,2},{7,3},{8,12},{9,13},{10,... | collective-permute-start | bytes 393224 | tf_op jit(solution)/shard_map/ppermute | solution.py:176
  362.4 7.7 %collective-permute-start.77 = (bf16[64,1024]{1,0:T(8,128)(2,1)S(1)}, bf16[64,1024]{1,0:T(8,128)(2,1)S(1)}, u32[]{:S(2)}, u32[]{:S(2)}) collective-permute-start(bf16[64,1024]{1,0:T(8,128)(2,1)S(1)} %add_convert_fusion.12), channel_id=1, source_target_pairs={{0,4},{1,5},{2,6},{3,7},{4,0},{5,1},{6,2},{7,3},{8,12},{9,13},{10,... | collective-permute-start | bytes 393224 | tf_op jit(solution)/shard_map/ppermute | solution.py:176
  370.2 10.2 %collective-permute-start.79 = (bf16[64,1024]{1,0:T(8,128)(2,1)S(1)}, bf16[64,1024]{1,0:T(8,128)(2,1)S(1)}, u32[]{:S(2)}, u32[]{:S(2)}) collective-permute-start(bf16[64,1024]{1,0:T(8,128)(2,1)S(1)} %add_convert_fusion.11), channel_id=1, source_target_pairs={{0,32},{1,33},{2,34},{3,35},{4,36},{5,37},{6,38},{7,39},{8,40},{9,... | collective-permute-start | bytes 393224 | tf_op jit(solution)/shard_map/ppermute | solution.py:176
  385.3 7.3 %collective-permute-start.82 = (bf16[64,1024]{1,0:T(8,128)(2,1)S(1)}, bf16[64,1024]{1,0:T(8,128)(2,1)S(1)}, u32[]{:S(2)}, u32[]{:S(2)}) collective-permute-start(bf16[64,1024]{1,0:T(8,128)(2,1)S(1)} %add_convert_fusion.10), channel_id=1, source_target_pairs={{0,5},{1,4},{2,7},{3,6},{4,1},{5,0},{6,3},{7,2},{8,13},{9,12},{10,... | collective-permute-start | bytes 393224 | tf_op jit(solution)/shard_map/ppermute | solution.py:176
  386.9 7.7 %collective-permute-start.83 = (bf16[64,1024]{1,0:T(8,128)(2,1)S(1)}, bf16[64,1024]{1,0:T(8,128)(2,1)S(1)}, u32[]{:S(2)}, u32[]{:S(2)}) collective-permute-start(bf16[64,1024]{1,0:T(8,128)(2,1)S(1)} %add_convert_fusion.10), channel_id=1, source_target_pairs={{0,4},{1,5},{2,6},{3,7},{4,0},{5,1},{6,2},{7,3},{8,12},{9,13},{10,... | collective-permute-start | bytes 393224 | tf_op jit(solution)/shard_map/ppermute | solution.py:176
  400.9 7.7 %collective-permute-start.88 = (bf16[64,1024]{1,0:T(8,128)(2,1)S(1)}, bf16[64,1024]{1,0:T(8,128)(2,1)S(1)}, u32[]{:S(2)}, u32[]{:S(2)}) collective-permute-start(bf16[64,1024]{1,0:T(8,128)(2,1)S(1)} %add_convert_fusion.8), channel_id=1, source_target_pairs={{0,4},{1,5},{2,6},{3,7},{4,0},{5,1},{6,2},{7,3},{8,12},{9,13},{10,... | collective-permute-start | bytes 393224 | tf_op jit(solution)/shard_map/ppermute | solution.py:176
  408.7 29.2 %collective-permute-start.90 = (bf16[64,1024]{1,0:T(8,128)(2,1)S(1)}, bf16[64,1024]{1,0:T(8,128)(2,1)S(1)}, u32[]{:S(2)}, u32[]{:S(2)}) collective-permute-start(bf16[64,1024]{1,0:T(8,128)(2,1)S(1)} %add_convert_fusion.7), channel_id=1, source_target_pairs={{0,32},{1,33},{2,34},{3,35},{4,36},{5,37},{6,38},{7,39},{8,40},{9,... | collective-permute-start | bytes 393224 | tf_op jit(solution)/shard_map/ppermute | solution.py:176
  448.6 7.6 %collective-permute-start.94 = (bf16[64,1024]{1,0:T(8,128)(2,1)S(1)}, bf16[64,1024]{1,0:T(8,128)(2,1)S(1)}, u32[]{:S(2)}, u32[]{:S(2)}) collective-permute-start(bf16[64,1024]{1,0:T(8,128)(2,1)S(1)} %add_convert_fusion.6), channel_id=1, source_target_pairs={{0,4},{1,5},{2,6},{3,7},{4,0},{5,1},{6,2},{7,3},{8,12},{9,13},{10,... | collective-permute-start | bytes 393224 | tf_op jit(solution)/shard_map/ppermute | solution.py:176
  466.5 7.7 %collective-permute-start.98 = (bf16[64,1024]{1,0:T(8,128)(2,1)S(1)}, bf16[64,1024]{1,0:T(8,128)(2,1)S(1)}, u32[]{:S(2)}, u32[]{:S(2)}) collective-permute-start(bf16[64,1024]{1,0:T(8,128)(2,1)S(1)} %add_convert_fusion.4), channel_id=1, source_target_pairs={{0,5},{1,4},{2,7},{3,6},{4,1},{5,0},{6,3},{7,2},{8,13},{9,12},{10,... | collective-permute-start | bytes 393224 | tf_op jit(solution)/shard_map/ppermute | solution.py:176
  467.8 7.8 %collective-permute-start.99 = (bf16[64,1024]{1,0:T(8,128)(2,1)S(1)}, bf16[64,1024]{1,0:T(8,128)(2,1)S(1)}, u32[]{:S(2)}, u32[]{:S(2)}) collective-permute-start(bf16[64,1024]{1,0:T(8,128)(2,1)S(1)} %add_convert_fusion.4), channel_id=1, source_target_pairs={{0,4},{1,5},{2,6},{3,7},{4,0},{5,1},{6,2},{7,3},{8,12},{9,13},{10,... | collective-permute-start | bytes 393224 | tf_op jit(solution)/shard_map/ppermute | solution.py:176
  492.4 7.6 %collective-permute-start.105 = (bf16[64,1024]{1,0:T(8,128)(2,1)S(1)}, bf16[64,1024]{1,0:T(8,128)(2,1)S(1)}, u32[]{:S(2)}, u32[]{:S(2)}) collective-permute-start(bf16[64,1024]{1,0:T(8,128)(2,1)S(1)} %add_convert_fusion.2), channel_id=1, source_target_pairs={{0,4},{1,5},{2,6},{3,7},{4,0},{5,1},{6,2},{7,3},{8,12},{9,13},{10,... | collective-permute-start | bytes 393224 | tf_op jit(solution)/shard_map/ppermute | solution.py:176
  510.1 7.4 %collective-permute-start.109 = (bf16[64,1024]{1,0:T(8,128)(2,1)S(1)}, bf16[64,1024]{1,0:T(8,128)(2,1)S(1)}, u32[]{:S(2)}, u32[]{:S(2)}) collective-permute-start(bf16[64,1024]{1,0:T(8,128)(2,1)S(1)} %add_convert_fusion), channel_id=1, source_target_pairs={{0,5},{1,4},{2,7},{3,6},{4,1},{5,0},{6,3},{7,2},{8,13},{9,12},{10,... | collective-permute-start | bytes 393224 | tf_op jit(solution)/shard_map/ppermute | solution.py:176
  511.7 7.9 %collective-permute-start.110 = (bf16[64,1024]{1,0:T(8,128)(2,1)S(1)}, bf16[64,1024]{1,0:T(8,128)(2,1)S(1)}, u32[]{:S(2)}, u32[]{:S(2)}) collective-permute-start(bf16[64,1024]{1,0:T(8,128)(2,1)S(1)} %add_convert_fusion), channel_id=1, source_target_pairs={{0,4},{1,5},{2,6},{3,7},{4,0},{5,1},{6,2},{7,3},{8,12},{9,13},{10,... | collective-permute-start | bytes 393224 | tf_op jit(solution)/shard_map/ppermute | solution.py:176
  521.4 10.8 %collective-permute-start.113 = (bf16[2,16,1024]{2,1,0:T(8,128)(2,1)S(1)}, bf16[2,16,1024]{2,1,0:T(8,128)(2,1)S(1)}, u32[]{:S(2)}, u32[]{:S(2)}) collective-permute-start(bf16[2,16,1024]{2,1,0:T(8,128)(2,1)S(1)} %select_bitcast_fusion), channel_id=1, source_target_pairs={{0,16},{1,17},{2,18},{3,19},{4,20},{5,21},{6,22},{7,23},{8,24},{9,... | collective-permute-start | bytes 196616 | tf_op jit(solution)/shard_map/ppermute | solution.py:176
  (119 other events, 858.4 us)
Sparse Core Ops, SparseCore 0:
  12.4 50.6 all-gather.1
